TPU v7x, 32 devices: a whole 2x2x4 slice. The times are simulated.
32 devices in a mesh: layer: 4 (over y, core), phi: 8 (over z, x).
Axes of the slice: x: 2, y: 2, z: 4, core: 2. Of those that a mesh axis runs over, the one named last changes fastest.
Arguments:
- features: bfloat16 [8192, 256], P(('layer', 'phi')), may hold values from -6 to 6
- w_layers: bfloat16 [4, 256, 256], replicated, may hold values from -0.375 to 0.375
- b_layers: float32 [4, 256], replicated, may hold values from -1.5 to 1.5
- w_coord: bfloat16 [16, 256], replicated, may hold values from -0.09375 to 0.09375
- w_beta: bfloat16 [256], replicated, may hold values from -0.375 to 0.375
- point_hit: int32 [256], P(('layer', 'phi')), may hold values from 0 to 255
- track: int32 [8192], P(('layer', 'phi')), may hold values from 0 to 255
- noise: int32 [8192], P(('layer', 'phi')), may hold values 0 or 1
Outputs:
- grad_w_layers: float32 [4, 256, 256], replicated
- grad_b_layers: float32 [4, 256], replicated
- grad_w_coord: float32 [16, 256], replicated
- grad_w_beta: float32 [256], replicated
- loss: float32 [], replicated
Inputs may be any that keep to these rules, and one draw needn't show every extreme that they name: `point_hit`: an index among the 256 hits of the device holding the entry. A non-noise hit of track k is attracted to point k.
All inputs are finite; a program needn't handle non-finite values. No bound on the sum of `noise` on one device may be relied on, other than what follows from the above.
Results may differ from a plain program's by a relative error of at most 0.0013.
Values sent between devices are 32-bit elements; how exact they have to be, the bound alone decides.
No kernel may reach another device: no remote copies, remote signals or barrier semaphores. Data moves between devices by JAX's collectives and lax.ppermute only.
A program may use at most 64 MiB of HBM per device.

v0:
```python
import jax
import jax.numpy as jnp
from jax import lax
from jax.sharding import PartitionSpec as P

dist_eps = 0.0001
charge_floor = 0.5
block_cols = 512


def mlp_forward(features, w_layers, b_layers, w_coord, w_beta):
    hidden = features
    states = [features]
    preacts = []
    for layer_num in range(w_layers.shape[0]):
        pre = (
            jnp.dot(hidden, w_layers[layer_num], preferred_element_type=jnp.float32)
            + b_layers[layer_num]
        )
        preacts.append(pre)
        hidden = jax.nn.silu(pre).astype(jnp.bfloat16)
        states.append(hidden)
    coords = lax.dot_general(
        w_coord, hidden, (((1,), (1,)), ((), ())), preferred_element_type=jnp.float32
    )
    logits = jnp.dot(hidden, w_beta, preferred_element_type=jnp.float32)
    return (states, preacts, coords, logits)


def charges(logits):
    expz = jnp.exp(logits)
    spread = jnp.log1p(2.0 * expz)
    charge = 0.25 * spread * spread + charge_floor
    slope = 0.5 * spread * (2.0 * expz / (1.0 + 2.0 * expz))
    return (jax.nn.sigmoid(logits), charge, slope)


def pair_terms(coords, charge, track, live, point_rows, first, hits_all):
    point_y = point_rows[:-1]
    point_q = point_rows[-1]
    width = point_rows.shape[1]
    hit_sq = jnp.sum(coords * coords, 0)
    point_sq = jnp.sum(point_y * point_y, 0)
    cross = lax.dot_general(
        coords,
        point_y,
        (((0,), (0,)), ((), ())),
        precision=lax.Precision.HIGHEST,
        preferred_element_type=jnp.float32,
    )
    dist_sq = jnp.maximum(hit_sq[:, None] + point_sq[None, :] - 2.0 * cross, 0.0)
    dist = jnp.sqrt(dist_sq + dist_eps)
    index = first + lax.iota(jnp.int32, width)
    match = jnp.where((track[:, None] == index[None, :]) & (live[:, None] > 0), 1.0, 0.0)
    reach = jnp.maximum(1.0 - dist, 0.0)
    potential = match * dist_sq + (1.0 - match) * reach * reach
    pot_rows = jnp.sum(potential * point_q[None, :], 1)
    coef = (
        (charge / hits_all)[:, None]
        * point_q[None, :]
        * (2.0 * match - (1.0 - match) * 2.0 * reach / dist)
    )
    row_sums = jnp.sum(coef, 1)
    col_sums = jnp.sum(coef, 0)
    pulls = lax.dot_general(
        point_y,
        coef,
        (((1,), (1,)), ((), ())),
        precision=lax.Precision.HIGHEST,
        preferred_element_type=jnp.float32,
    )
    point_grad = point_y * col_sums[None, :] - lax.dot_general(
        coords,
        coef,
        (((1,), (0,)), ((), ())),
        precision=lax.Precision.HIGHEST,
        preferred_element_type=jnp.float32,
    )
    charge_grad = jnp.dot(charge, potential, precision=lax.Precision.HIGHEST) / hits_all
    return (row_sums, pot_rows, pulls, jnp.concatenate([point_grad, charge_grad[None, :]], 0))


def on_device(features, w_layers, b_layers, w_coord, w_beta, point_hit, track, noise):
    hit_count = features.shape[0]
    point_count = point_hit.shape[0]
    ndev = lax.axis_size("layer") * lax.axis_size("phi")
    total_points = point_count * ndev
    hits_all = hit_count * ndev * 1.0
    states, preacts, coords, logits = mlp_forward(features, w_layers, b_layers, w_coord, w_beta)
    beta_vals, charge, slope = charges(logits)
    selector = jnp.where(point_hit[:, None] == lax.iota(jnp.int32, hit_count)[None, :], 1.0, 0.0)
    own_y = lax.dot_general(
        coords,
        selector,
        (((1,), (1,)), ((), ())),
        precision=lax.Precision.HIGHEST,
        preferred_element_type=jnp.float32,
    )
    own_q = jnp.dot(selector, charge, precision=lax.Precision.HIGHEST)
    own_beta = jnp.dot(selector, beta_vals, precision=lax.Precision.HIGHEST)
    own_rows = jnp.concatenate([own_y, own_q[None, :]], 0)
    live = 1 - noise
    init = (
        jnp.zeros((hit_count,), jnp.float32),
        jnp.zeros((hit_count,), jnp.float32),
        jnp.zeros(coords.shape, jnp.float32),
        jnp.zeros((own_rows.shape[0], total_points), jnp.float32),
    )
    group_rows = lax.all_gather(own_rows, "phi", axis=1, tiled=True)
    piece = lax.all_gather(group_rows, "layer", axis=1, tiled=True)
    start = jnp.int32(0)
    width = piece.shape[1]

    def one_block(state, offset, cols):
        row_acc, pot_acc, pull_acc, grad_acc = state
        block = lax.dynamic_slice_in_dim(piece, offset, cols, 1)
        row_sums, pot_rows, pulls, point_grads = pair_terms(
            coords, charge, track, live, block, start + offset, hits_all
        )
        grad_acc = lax.dynamic_update_slice_in_dim(grad_acc, point_grads, start + offset, 1)
        return (row_acc + row_sums, pot_acc + pot_rows, pull_acc + pulls, grad_acc)

    full = width // block_cols
    rest = width - full * block_cols
    state = init
    if full > 0:
        state = lax.fori_loop(
            0, full, lambda step, inner: one_block(inner, step * block_cols, block_cols), state
        )
    if rest > 0:
        state = one_block(state, full * block_cols, rest)
    row_sums, pot_rows, pulls, point_grads = state
    partial_grads = lax.psum_scatter(point_grads, "layer", scatter_dimension=1, tiled=True)
    own_grads = lax.psum_scatter(partial_grads, "phi", scatter_dimension=1, tiled=True)
    coord_dim = coords.shape[0]
    coord_grad = coords * row_sums[None, :] - pulls
    coord_grad = coord_grad + jnp.dot(
        own_grads[:coord_dim], selector, precision=lax.Precision.HIGHEST
    )
    charge_grad = pot_rows / hits_all + jnp.dot(
        own_grads[coord_dim], selector, precision=lax.Precision.HIGHEST
    )
    noise_float = noise.astype(jnp.float32)
    beta_grad = noise_float / hits_all + jnp.sum(selector, 0) * (-1.0 / total_points)
    logit_grad = charge_grad * slope + beta_grad * beta_vals * (1.0 - beta_vals)
    loss_local = (
        jnp.sum(charge * pot_rows) / hits_all
        + jnp.sum(1.0 - own_beta) / total_points
        + jnp.sum(noise_float * beta_vals) / hits_all
    )
    coord_low = coord_grad.astype(jnp.bfloat16)
    logit_low = logit_grad.astype(jnp.bfloat16)
    hidden = states[-1]
    grad_coord_w = lax.dot_general(
        coord_low, hidden, (((1,), (0,)), ((), ())), preferred_element_type=jnp.float32
    )
    grad_beta_w = jnp.dot(logit_low, hidden, preferred_element_type=jnp.float32)
    upstream = lax.dot_general(
        coord_low, w_coord, (((0,), (0,)), ((), ())), preferred_element_type=jnp.float32
    )
    upstream = (
        upstream + logit_low.astype(jnp.float32)[:, None] * w_beta.astype(jnp.float32)[None, :]
    )
    count = w_layers.shape[0]
    weight_grads = [None] * count
    bias_grads = [None] * count
    for layer_num in range(count - 1, -1, -1):
        pre = preacts[layer_num]
        sig = jax.nn.sigmoid(pre)
        local = (upstream * sig * (1.0 + pre * (1.0 - sig))).astype(jnp.bfloat16)
        weight_grad = lax.dot_general(
            states[layer_num], local, (((0,), (0,)), ((), ())), preferred_element_type=jnp.float32
        )
        bias_grad = jnp.sum(local.astype(jnp.float32), 0)
        if layer_num > 0:
            upstream = lax.dot_general(
                local,
                w_layers[layer_num],
                (((1,), (1,)), ((), ())),
                preferred_element_type=jnp.float32,
            )
        weight_grads[layer_num] = weight_grad
        bias_grads[layer_num] = bias_grad
    grad_w_layers = jnp.stack(weight_grads)
    grad_b_layers = jnp.stack(bias_grads)
    grad_w_layers, grad_b_layers, grad_coord_w, grad_beta_w, loss_local = lax.psum(
        (grad_w_layers, grad_b_layers, grad_coord_w, grad_beta_w, loss_local), ("layer", "phi")
    )
    return (grad_w_layers, grad_b_layers, grad_coord_w, grad_beta_w, loss_local)


def solution(mesh):
    return jax.shard_map(
        on_device,
        mesh=mesh,
        in_specs=(
            P(("layer", "phi"), None),
            P(),
            P(),
            P(),
            P(),
            P(("layer", "phi")),
            P(("layer", "phi")),
            P(("layer", "phi")),
        ),
        out_specs=(P(), P(), P(), P(), P()),
        check_vma=False,
    )
```

profile of v0, /device:TPU:0, one launch (start us, length us, event | category | flops | bytes accessed | tf_op | source)
XLA Modules:
  0.0 253.2 jit_solution(7693284102866665003)
XLA Ops:
  7.2 0.0 copy-start
  7.2 0.0 copy-start.5
  7.2 0.0 copy-start.1
  7.2 0.0 reduce-scatter.5.cloned.1.call-start
  7.2 0.7 subtract_compare_fusion
  8.0 0.0 copy-done.5
  8.0 0.8 fusion.80
  8.8 0.0 copy-done
  8.8 1.1 convolution_add_fusion.3
  9.9 0.0 copy-done.1
  10.0 0.2 convolution_add_fusion.2
  10.2 0.2 convolution_add_fusion.1
  10.4 0.2 multiply_convert_fusion
  10.6 0.0 copy-start.2
  10.7 0.1 fusion.81
  10.8 0.0 copy-start.3
  10.8 0.7 copy-done.3
  11.5 0.6 multiply_reduce_fusion.3
  12.1 0.0 copy-done.2
  12.1 0.2 multiply_reduce_fusion.2
  12.3 0.0 copy-start.6
  12.3 0.6 copy-done.6
  13.0 0.2 fusion.39
  13.2 0.2 fusion.41
  13.4 0.1 pad_maximum_fusion.2
  13.5 32.2 %all_gather.6 = f32[17,64]{0,1:T(8,128)S(1)} all-gather(f32[17,8]{0,1:T(8,128)S(1)} %pad_maximum_fusion.2), channel_id=1, replica_groups=mesh['layer'=4,'phi'=8] {'phi'}, dimensions={1}, use_global_device_ids=true | all-gather | bytes 4896 | tf_op jit(solution)/shard_map/all_gather | solution.py:109
  45.6 0.1 copy.29
  45.7 5.2 %all-gather = f32[4,64,17]{1,2,0:T(8,128)S(1)} all-gather(f32[1,64,17]{1,2,0:T(8,128)S(1)} %copy.29), channel_id=1, replica_groups=mesh['layer'=4,'phi'=8] {'layer'}, dimensions={0}, use_global_device_ids=true | all-gather | bytes 21760 | tf_op jit(solution)/shard_map/all_gather | solution.py:110
  51.0 0.1 reshape.22
  51.1 0.0 copy-start.4
  51.1 0.7 copy-done.4
  51.8 0.8 multiply_reduce_fusion
  52.6 0.2 fusion.82
  52.8 0.2 convolution_subtract_fusion
  53.0 0.8 copy.40
  53.8 0.0 reduce-scatter.5.cloned.1.call-update
  53.8 0.0 all-reduce.4.cloned.1.call-start
  53.9 0.8 fusion.13
  54.7 0.3 convolution_subtract_fusion.1
  55.0 0.1 select_reduce_fusion
  55.1 0.0 copy-start.7
  55.1 0.7 copy-done.7
  55.8 0.6 dynamic-slice
  58.3 16.3 %reduce-scatter.5.cloned.1.call-done = f32[64,17]{1,0:T(8,128)} async-done(((f32[256,17]{1,0:T(8,128)}), f32[64,17]{1,0:T(8,128)}) %reduce-scatter.5.cloned.1.call-update) | async-done | bytes 4368
  74.6 0.8 copy.41
  75.4 37.1 %all-reduce = f32[17,64]{1,0:T(8,128)S(1)} all-reduce(f32[17,64]{1,0:T(8,128)S(1)} %copy.41), channel_id=3, replica_groups=mesh['layer'=4,'phi'=8] {'phi'}, use_global_device_ids=true, to_apply=%region_5.6.clone | all-reduce | flops 1088 | bytes 8704
  112.4 0.2 fusion.11
  112.7 0.2 fusion.36
  112.9 0.6 fusion.76
  113.5 0.2 convert_reduce_fusion
  113.7 0.3 convert_reduce_fusion.1
  114.0 0.2 convolution_bitcast_fusion
  114.2 0.3 convert_reduce_fusion.2
  114.5 0.2 convolution_bitcast_fusion.1
  114.7 0.3 convert_reduce_fusion.3
  115.0 0.2 convolution_bitcast_fusion.2
  115.9 0.2 convolution_bitcast_fusion.3
  116.2 1.0 pad_maximum_fusion
  117.2 0.0 all-reduce.4.cloned.1.call-update
  117.2 0.1 fusion.84
  117.4 0.1 fusion.83
  117.5 37.5 %all-reduce.1 = (f32[4,256]{1,0:T(4,128)}, f32[16,256]{1,0:T(8,128)}, f32[256]{0:T(256)}, f32[]{:T(128)}) all-reduce(f32[4,256]{1,0:T(4,128)S(1)} %pad_maximum_fusion.3, f32[16,256]{1,0:T(8,128)S(1)} %fusion.83, f32[256]{0:T(256)S(1)} %bitcast.117, f32[]{:T(128)S(6)} %add.170), channel_id=1, replica_groups=mesh['layer'=4,'phi'=8] {'layer','phi'}, use_global_device_ids=true, to_apply=%region_13.14 | all-reduce | flops 5377 | bytes 43016 | tf_op jit(solution)/shard_map/psum | solution.py:186
  155.1 88.7 %all-reduce.4.cloned.1.call-done = f32[4,256,256]{1,2,0:T(8,128)} async-done(((f32[4,256,256]{1,2,0:T(8,128)}), f32[4,256,256]{1,2,0:T(8,128)}) %all-reduce.4.cloned.1.call-update) | async-done | bytes 1048592 | tf_op jit(solution)/shard_map/psum | solution.py:186
  243.8 2.5 copy.35
  (9 shorter events, 0.1 us)
Async XLA Ops:
  7.2 1.7 copy-start
  7.2 0.8 copy-start.5
  7.2 2.8 %copy-start.1 = (bf16[4,256,256]{2,1,0:T(8,128)(2,1)S(1)}, bf16[4,256,256]{2,1,0:T(8,128)(2,1)}, u32[]{:S(2)}) copy-start(bf16[4,256,256]{2,1,0:T(8,128)(2,1)} %param.9) | copy-start | bytes 1572868
  7.2 67.4 %reduce-scatter.5.cloned.1.call-start = ((), (), s32[]{:S(2)}) async-start(), calls=%async_computation.2 | async-start | bytes 163840
  10.6 1.5 copy-start.2
  10.8 0.7 copy-start.3
  12.3 0.7 copy-start.6
  51.1 0.7 copy-start.4
  53.8 190.0 %all-reduce.4.cloned.1.call-start = ((), (), s32[]{:S(2)}) async-start(), calls=%async_computation.1 | async-start | bytes 2097152 | tf_op jit(solution)/shard_map/psum | solution.py:186
  55.1 0.7 copy-start.7
Sparse Core Ops, SparseCore 0:
  54.0 20.5 reduce-scatter.4
  117.3 126.4 all-reduce.3
where the time goes:
time: 254 us; the launch traced here: 253 us
  blocking collectives  112 us (44%)
  waiting for transfers between devices  105 us (41%)
  between operations  16.8 us (7%)
  local copies, waits for them, and re-layouts  8.46 us (3%)
  matrix products  7.46 us (3%)
  other arithmetic  3.3 us (1%)
    psum x1, waiting for transfers between devices, on_device(): lax.psum((grad_w_layers, grad_b_layers, grad_coord_w, grad_beta_w, loss_l...  88.7 us
    psum x1, blocking collectives, on_device(): lax.psum((grad_w_layers, grad_b_layers, grad_coord_w, grad_beta_w, loss_l...  37.5 us
    unnamed x1, blocking collectives  37.1 us
    all_gather x1, blocking collectives, on_device(): group_rows = lax.all_gather(own_rows, 'phi', axis=1, tiled=True)  32.2 us
    unnamed x3, waiting for transfers between devices  16.3 us
    unnamed x23, local copies, waits for them, and re-layouts  7.6 us
    all_gather x1, blocking collectives, on_device(): piece = lax.all_gather(group_rows, 'layer', axis=1, tiled=True)  5.23 us
  transfers between devices with their start and end apart: 2, of which 2 were waited for; matrix products, arithmetic and copies ran while one was open for 1% of the time, Pallas kernels for 0%

commit v1 on v0

v1 whole, which is shorter than its diff:
```python
import functools

import jax
import jax.numpy as jnp
from jax import lax
from jax.experimental import pallas as pl
from jax.experimental.pallas import tpu as pltpu
from jax.sharding import PartitionSpec as P

dist_eps = 0.0001
charge_floor = 0.5
AXES = ("layer", "phi")
VMEM = pl.BlockSpec(memory_space=pltpu.VMEM)
SMEM = pl.BlockSpec(memory_space=pltpu.SMEM)
HIGH = lax.Precision.HIGHEST
PARAMS = pltpu.CompilerParams(vmem_limit_bytes=48 * 1024 * 1024)


def matmul(a, b, ca=1, cb=0, precision=None):
    return lax.dot_general(
        a, b, (((ca,), (cb,)), ((), ())), precision=precision, preferred_element_type=jnp.float32
    )


def iota(shape, dim):
    return lax.broadcasted_iota(jnp.int32, shape, dim)


def head_rows(wc_ref, wb_ref):
    dim = wc_ref.shape[0]
    width = wc_ref.shape[1]
    beta_row = jnp.broadcast_to(wb_ref[...].astype(jnp.float32), (dim, width))
    tail = jnp.where(iota((dim, width), 0) == 0, beta_row, 0.0).astype(jnp.bfloat16)
    return jnp.concatenate([wc_ref[...], tail], 0)


def point_column(hit_ref, shift, shape):
    count = hit_ref.shape[0]
    rows = iota(shape, 0)
    col = jnp.zeros(shape, jnp.int32)
    for p in range(count):
        col = jnp.where(rows == (p + shift) % count, hit_ref[p], col)
    return col


def embed_kernel(
    pos_ref, hit_ref, feat_ref, w_ref, b_ref, wc_ref, wb_ref, track_ref, noise_ref,
    pay_ref, act_ref, aux_ref,
):
    dim = wc_ref.shape[0]
    hits = feat_ref.shape[0]
    points = hit_ref.shape[0]
    h = feat_ref[...]
    for l in range(w_ref.shape[0]):
        a = matmul(h, w_ref[l]) + b_ref[l : l + 1, :]
        act_ref[l] = a
        h = (a * jax.nn.sigmoid(a)).astype(jnp.bfloat16)
    xz = matmul(head_rows(wc_ref, wb_ref), h, 1, 1)
    z = xz[dim : dim + 1]
    expz = jnp.exp(z)
    spread = jnp.log1p(2.0 * expz)
    q = 0.25 * spread * spread + charge_floor
    slope = 0.5 * spread * (2.0 * expz / (1.0 + 2.0 * expz))
    beta = jax.nn.sigmoid(z)
    noise = noise_ref[...]
    label = jnp.where(noise == 0, track_ref[...], -1).astype(jnp.float32)
    rows8 = iota((8, hits), 0)
    aux_ref[...] = jnp.where(
        rows8 == 0, beta, jnp.where(rows8 == 1, slope, noise.astype(jnp.float32))
    )
    sel = iota((points, hits), 1) == point_column(hit_ref, 2, (points, hits))
    lane = iota((points, 128), 1)
    order = lax.rem(iota((points, 128), 0) + (points - 2), points)
    pts = jnp.where(lane == dim + 1, (pos_ref[0] * points + order).astype(jnp.float32), 0.0)
    for c in range(dim):
        v = jnp.sum(jnp.where(sel, xz[c : c + 1], 0.0), axis=1, keepdims=True)
        pts = jnp.where(lane == c, v, pts)
    v = jnp.sum(jnp.where(sel, q, 0.0), axis=1, keepdims=True)
    pts = jnp.where(lane == dim, v, pts)
    row = iota((points, 128), 0)
    moved = pltpu.roll(pts, 2, 0)
    left = jnp.where(row == 0, q[:, :128], jnp.where(row == 1, label[:, :128], pts))
    right = jnp.where(row == 0, q[:, 128:], jnp.where(row == 1, label[:, 128:], moved))
    pay_ref[0:dim, :] = xz[0:dim]
    pay_ref[dim : dim + 8, 0:128] = left
    pay_ref[dim : dim + 8, 128:256] = right


def residual_kernel(act_ref, feat_ref, w_ref, slope_ref, ht_ref, last_ref, wt_ref):
    layers = w_ref.shape[0]
    ht_ref[0] = feat_ref[...].T
    for l in range(layers):
        a = act_ref[l]
        sig = jax.nn.sigmoid(a)
        slope_ref[l] = sig * (1.0 + a * (1.0 - sig))
        h = (a * sig).astype(jnp.bfloat16)
        if l < layers - 1:
            ht_ref[l + 1] = h.T
            wt_ref[l] = w_ref[l + 1].T
        else:
            last_ref[...] = h


def point_tile(left, right):
    rows = iota(left.shape, 0)
    return jnp.where(rows < 2, pltpu.roll(right, 6, 0), left)


def pair_weights(dist_sq, match):
    shifted = dist_sq + dist_eps
    inv = lax.rsqrt(shifted)
    reach = jnp.maximum(1.0 - shifted * inv, 0.0)
    potential = jnp.where(match, dist_sq, reach * reach)
    weight = jnp.where(match, 2.0, -2.0 * jnp.maximum(inv - 1.0, 0.0))
    return potential, weight


def backward_kernel(
    hits_all, points_all, parts,
    pos_ref, hit_ref, pay_ref, aux_ref, slope_ref, ht_ref, last_ref, wt_ref, wc_ref, wb_ref, *rest,
):
    groups = rest[:parts]
    keep_ref, send_ref, xb, yb, gx_ref, stack, ext = rest[parts:]
    dim = wc_ref.shape[0]
    points = hit_ref.shape[0]
    hits = pay_ref.shape[1]
    layers = slope_ref.shape[0]
    full = (8, hits)
    own = pay_ref[dim : dim + 8, :]
    q_row = own[0:1]
    label_row = own[1:2]
    own = point_tile(own[:, :128], own[:, 128:])
    for c in range(dim):
        xb[c] = jnp.broadcast_to(pay_ref[c : c + 1, :], full)
        yb[c] = jnp.broadcast_to(own[:, c : c + 1], full)
    label_b = jnp.broadcast_to(label_row, full)
    index_b = jnp.broadcast_to(own[:, dim + 1 : dim + 2], full)
    zero = jnp.zeros(full, jnp.float32)

    def hit_side(ref):
        def body(j, carry):
            pot_acc, acc = carry
            tile = ref[j, dim : dim + 8, :]
            tile = point_tile(tile[:, :128], tile[:, 128:])
            diffs = []
            dist_sq = zero
            for c in range(dim):
                diff = xb[c] - tile[:, c : c + 1]
                diffs.append(diff)
                dist_sq = dist_sq + diff * diff
            point_q = tile[:, dim : dim + 1]
            potential, weight = pair_weights(dist_sq, label_b == tile[:, dim + 1 : dim + 2])
            weight = weight * point_q
            return pot_acc + potential * point_q, tuple(
                s + weight * diff for s, diff in zip(acc, diffs)
            )

        return body

    def point_side(ref):
        def body(j, carry):
            pot_acc, acc = carry
            diffs = []
            dist_sq = zero
            for c in range(dim):
                diff = yb[c] - ref[j, c : c + 1, :]
                diffs.append(diff)
                dist_sq = dist_sq + diff * diff
            hit_q = ref[j, dim : dim + 1, :]
            potential, weight = pair_weights(dist_sq, index_b == ref[j, dim + 1 : dim + 2, :])
            weight = weight * hit_q
            potential = potential * hit_q
            new = []
            for s, diff in zip(acc, diffs):
                term = weight * diff
                new.append(s + term[:, :128] + term[:, 128:])
            return pot_acc + potential[:, :128] + potential[:, 128:], tuple(new)

        return body

    carry = (zero, (zero,) * dim)
    for ref in groups:
        carry = lax.fori_loop(0, ref.shape[0], hit_side(ref), carry)
    pot_row = jnp.sum(carry[0], axis=0, keepdims=True)
    scaled = q_row * (1.0 / hits_all)
    for c in range(dim):
        gx_ref[c : c + 1, :] = jnp.sum(carry[1][c], axis=0, keepdims=True) * scaled

    half = jnp.zeros((8, 128), jnp.float32)
    carry = (half, (half,) * dim)
    for ref in groups:
        carry = lax.fori_loop(0, ref.shape[0], point_side(ref), carry)
    lane = iota((8, 128), 1)
    own_q = own[:, dim : dim + 1] * (1.0 / hits_all)
    grads = jnp.where(lane == dim + 1, 1.0, 0.0)
    for c in range(dim):
        v = jnp.sum(carry[1][c], axis=1, keepdims=True) * own_q
        grads = jnp.where(lane == c, v, grads)
    v = jnp.sum(carry[0], axis=1, keepdims=True) * (1.0 / hits_all)
    grads = jnp.where(lane == dim, v, grads)
    sel = iota(full, 1) == point_column(hit_ref, 2, full)
    added = matmul(grads, jnp.where(sel, 1.0, 0.0), 0, 0, HIGH)

    beta = aux_ref[0:1, :]
    noise = aux_ref[2:3, :]
    count = added[dim + 1 : dim + 2]
    grad_q = pot_row * (1.0 / hits_all) + added[dim : dim + 1]
    grad_b = noise * (1.0 / hits_all) - count * (1.0 / points_all)
    grad_z = grad_q * aux_ref[1:2, :] + grad_b * beta * (1.0 - beta)
    per_hit = q_row * pot_row * (1.0 / hits_all) + noise * beta * (1.0 / hits_all)
    per_hit = per_hit - count * beta * (1.0 / points_all)
    loss = jnp.sum(per_hit, axis=1, keepdims=True) + points * 1.0 / points_all

    grad_x = gx_ref[...] + added[0:dim]
    tail = jnp.where(iota((dim, hits), 0) == 0, grad_z, 0.0)
    low = jnp.concatenate([grad_x, tail], 0).astype(jnp.bfloat16)
    head = head_rows(wc_ref, wb_ref)
    grad_head = matmul(low, last_ref[...])
    up = matmul(low, head, 0, 0)
    ext[...] = jnp.zeros(ext.shape, jnp.float32)
    cols = [slice(0, 128), slice(128, 256)]
    base = 2 * layers
    for h, col in enumerate(cols):
        ext[base + h * dim : base + (h + 1) * dim, :] = grad_head[0:dim, col]
        ext[base + 2 * dim + h : base + 2 * dim + h + 1, :] = grad_head[dim : dim + 1, col]
    ext[base + 2 * dim + 2 : base + 2 * dim + 3, :] = jnp.broadcast_to(loss, (1, 128))
    blocks = stack.shape[0]
    rows = layers * hits // blocks
    per_layer = blocks // layers
    for l in range(layers - 1, -1, -1):
        err = (up * slope_ref[l]).astype(jnp.bfloat16)
        if l > 0:
            up = matmul(err, wt_ref[l - 1])
        grad_w = matmul(ht_ref[l], err)
        bias = jnp.sum(err.astype(jnp.float32), axis=0, keepdims=True)
        for h, col in enumerate(cols):
            ext[h * layers + l : h * layers + l + 1, :] = bias[:, col]
            for s in range(per_layer):
                stack[l * per_layer + s, h * rows : (h + 1) * rows, :] = grad_w[
                    s * rows : (s + 1) * rows, col
                ]
    for b in range(blocks):
        stack[b, 2 * rows : 2 * rows + 8, :] = ext[8 * b : 8 * b + 8, :]
    me = pos_ref[1]
    for j in range(blocks // 2):
        keep_ref[j] = stack[jnp.bitwise_xor(me, j)]
        send_ref[j] = stack[jnp.bitwise_xor(me, j + blocks // 2)]


def finish_kernel(pos_ref, *refs):
    quarter = refs[:-7]
    other, gw_ref, gb_ref, gc_ref, gbeta_ref, loss_ref, ext = refs[-7:]
    blocks = 2 * len(quarter)
    rows = gw_ref.shape[1]
    dim = gc_ref.shape[0]
    layers = gb_ref.shape[0]
    me = pos_ref[1]
    for r in range(blocks):
        if r < len(quarter):
            block = quarter[r][...]
        else:
            block = other[r - len(quarter)]
        place = jnp.bitwise_xor(me, r)
        gw_ref[place, :, 0:128] = block[0:rows]
        gw_ref[place, :, 128:256] = block[rows : 2 * rows]
        ext[place] = block[2 * rows :]
    flat = [ext[b] for b in range(blocks)]
    flat = jnp.concatenate(flat, 0)
    base = 2 * layers
    for h, col in enumerate([slice(0, 128), slice(128, 256)]):
        gb_ref[:, col] = flat[h * layers : (h + 1) * layers]
        gc_ref[:, col] = flat[base + h * dim : base + (h + 1) * dim]
        gbeta_ref[:, col] = flat[base + 2 * dim + h : base + 2 * dim + h + 1]
    loss_ref[...] = flat[base + 2 * dim + 2 : base + 2 * dim + 3, 0:1]


def bits_of(size):
    return [1 << t for t in range(size.bit_length() - 1)]


def on_device(layer_size, phi_size, features, w_layers, b_layers, w_coord, w_beta, point_hit, track, noise):
    ndev = layer_size * phi_size
    hits, width = features.shape
    layers = w_layers.shape[0]
    dim = w_coord.shape[0]
    points = point_hit.shape[0]
    hits_all = hits * ndev * 1.0
    points_all = points * ndev * 1.0
    f32 = jnp.float32
    core = phi_size
    plane = [1, 2 * phi_size]
    others = [b for b in bits_of(ndev) if b != core and b not in plane]

    def swap(x, mask):
        return lax.ppermute(x, AXES, [(i, i ^ mask) for i in range(ndev)])

    me = lax.axis_index("layer") * phi_size + lax.axis_index("phi")
    slot = (me // core) % 2 * 4 + (me // plane[1]) % 2 * 2 + me % 2
    pos = jnp.stack([me, slot]).astype(jnp.int32)
    w_beta = w_beta.reshape(1, width)
    track = track.reshape(1, hits)
    noise = noise.reshape(1, hits)

    pay, act, aux = pl.pallas_call(
        embed_kernel,
        out_shape=(
            jax.ShapeDtypeStruct((dim + 8, hits), f32),
            jax.ShapeDtypeStruct((layers, hits, width), f32),
            jax.ShapeDtypeStruct((8, hits), f32),
        ),
        in_specs=[SMEM, SMEM] + [VMEM] * 7,
        out_specs=(VMEM,) * 3,
        compiler_params=PARAMS,
        name="embed",
    )(pos, point_hit, features, w_layers, b_layers, w_coord, w_beta, track, noise)

    slope, ht, last, wt = pl.pallas_call(
        residual_kernel,
        out_shape=(
            jax.ShapeDtypeStruct((layers, hits, width), f32),
            jax.ShapeDtypeStruct((layers, width, hits), jnp.bfloat16),
            jax.ShapeDtypeStruct((hits, width), jnp.bfloat16),
            jax.ShapeDtypeStruct((layers - 1, width, width), jnp.bfloat16),
        ),
        in_specs=[VMEM] * 3,
        out_specs=(VMEM,) * 4,
        compiler_params=PARAMS,
        cost_estimate=pl.CostEstimate(
            flops=20 * layers * hits * width, bytes_accessed=6 * layers * hits * width,
            transcendentals=layers * hits * width,
        ),
        name="residuals",
    )(act, features, w_layers)

    rows_all = pay[None]
    stages = [others[i : i + 2] for i in range(0, len(others), 2)] + [plane]
    for stage in stages:
        masks = stage + ([stage[0] ^ stage[1]] if len(stage) > 1 else [])
        rows_all = jnp.concatenate([rows_all] + [swap(rows_all, m) for m in masks], 0)
    rows_far = swap(rows_all, core)

    blocks = 8
    block_rows = 2 * (layers * width // blocks) + 8
    half = jax.ShapeDtypeStruct((blocks // 2, block_rows, 128), f32)
    keep, send = pl.pallas_call(
        functools.partial(backward_kernel, hits_all, points_all, 2),
        out_shape=(half, half),
        in_specs=[SMEM, SMEM] + [VMEM] * 10,
        out_specs=(VMEM, VMEM),
        scratch_shapes=[
            pltpu.VMEM((dim, 8, hits), f32),
            pltpu.VMEM((dim, 8, hits), f32),
            pltpu.VMEM((dim, hits), f32),
            pltpu.VMEM((blocks, block_rows, 128), f32),
            pltpu.VMEM((8 * blocks, 128), f32),
        ],
        compiler_params=PARAMS,
        name="pairs_backward",
    )(pos, point_hit, pay, aux, slope, ht, last, wt, w_coord, w_beta, rows_all, rows_far)

    total = keep + swap(send, core)
    masks = [plane[0], plane[1], plane[0] ^ plane[1]]
    mine = total[0]
    arrived = [swap(total[r + 1], m) for r, m in enumerate(masks)]
    mine = (mine + arrived[0]) + (arrived[1] + arrived[2])
    for m in others:
        mine = mine + swap(mine, m)
    quarter = [mine] + [swap(mine, m) for m in masks]
    far = swap(jnp.stack(quarter), core)

    gw, gb, gc, gbeta, loss = pl.pallas_call(
        finish_kernel,
        out_shape=(
            jax.ShapeDtypeStruct((blocks, layers * width // blocks, width), f32),
            jax.ShapeDtypeStruct((layers, width), f32),
            jax.ShapeDtypeStruct((dim, width), f32),
            jax.ShapeDtypeStruct((1, width), f32),
            jax.ShapeDtypeStruct((1, 1), f32),
        ),
        in_specs=[SMEM] + [VMEM] * 5,
        out_specs=(VMEM,) * 5,
        scratch_shapes=[pltpu.VMEM((blocks, 8, 128), f32)],
        compiler_params=PARAMS,
        name="finish",
    )(pos, *quarter, far)
    return (
        gw.reshape(layers, width, width),
        gb,
        gc,
        gbeta.reshape(width),
        loss.reshape(()),
    )


def solution(mesh):
    split = P(AXES)
    return jax.shard_map(
        functools.partial(on_device, mesh.shape["layer"], mesh.shape["phi"]),
        mesh=mesh,
        in_specs=(P(AXES, None), P(), P(), P(), P(), split, split, split),
        out_specs=(P(), P(), P(), P(), P()),
        check_vma=False,
    )
```

time: 254 us -> 71.1 us (0.28)
  blocking collectives: 112 us -> 0 us
  waiting for transfers between devices: 105 us -> 36.6 us
  starting transfers between devices: 0.08 us -> 18.9 us
  between operations: 16.8 us -> 0.82 us
  Pallas kernels: 0 us -> 11 us
  matrix products: 7.46 us -> 0 us
  local copies, waits for them, and re-layouts: 8.46 us -> 3.19 us
  other arithmetic: 3.3 us -> 0.27 us
    psum x1 -> x0, waiting for transfers between devices: 88.7 us -> none  [on_device(): lax.psum((grad_w_layers, grad_b_layers, grad_coord_w, grad_beta_w, loss_l...]
    psum x1 -> x0, blocking collectives: 37.5 us -> none  [on_device(): lax.psum((grad_w_layers, grad_b_layers, grad_coord_w, grad_beta_w, loss_l...]
    all_gather x2 -> x0, blocking collectives: 37.4 us -> none  [the longest x1 32.2 us: on_device(): group_rows = lax.all_gather(own_rows, 'phi', axis=1, tiled=True)]
    unnamed x1 -> x0, blocking collectives: 37.1 us -> none
    ppermute x0 -> x17, waiting for transfers between devices: none -> 36.6 us  [swap(): return lax.ppermute(x, AXES, [(i, i ^ mask) for i in range(ndev)])]
    ppermute x0 -> x17, starting transfers between devices: none -> 18.9 us  [swap(): return lax.ppermute(x, AXES, [(i, i ^ mask) for i in range(ndev)])]
    unnamed x3 -> x0, waiting for transfers between devices: 16.3 us -> none
    pallas_call x0 -> x4, Pallas kernels: none -> 11 us  [the longest x1 7.64 us: on_device(): pl.pallas_call(functools.partial(backward_kernel, hits_all, points_all, 2...]
  transfers between devices with their start and end apart: 2 -> 17, of which waited for: 2 -> 13; matrix products, arithmetic and copies ran while one was open for 1% -> 0% of each run, Pallas kernels for 0% -> 1%
where the time goes in v1:
time: 71.1 us; the launch traced here: 70.8 us
  waiting for transfers between devices  36.6 us (51%)
  starting transfers between devices  18.9 us (27%)
  Pallas kernels  11 us (15%)
  local copies, waits for them, and re-layouts  3.19 us (4%)
  between operations  0.82 us (1%)
    ppermute x17, waiting for transfers between devices, swap(): return lax.ppermute(x, AXES, [(i, i ^ mask) for i in range(ndev)])  36.6 us
    ppermute x17, starting transfers between devices, swap(): return lax.ppermute(x, AXES, [(i, i ^ mask) for i in range(ndev)])  18.9 us
    pallas_call x1, Pallas kernels, on_device(): pl.pallas_call(functools.partial(backward_kernel, hits_all, points_all, 2...  7.64 us
    unnamed x22, local copies, waits for them, and re-layouts  2.49 us
    pallas_call x1, Pallas kernels, on_device(): pl.pallas_call(finish_kernel, out_shape=(jax.ShapeDtypeStruct((blocks, la...  1.59 us
  transfers between devices with their start and end apart: 17, of which 13 were waited for; matrix products, arithmetic and copies ran while one was open for 0% of the time, Pallas kernels for 1%

profile of v1, /device:TPU:0, one launch (start us, length us, event | category | flops | bytes accessed | tf_op | source)
XLA Modules:
  0.0 70.8 jit_solution(10575667678238655280)
XLA Ops:
  0.6 0.0 copy-start.2
  0.7 0.7 reshape.28.wb_ref
  1.4 0.0 copy-start.3
  1.4 0.1 pad_add_fusion.pos_ref
  1.4 0.0 copy-start.7
  1.4 0.0 copy-start.5
  1.4 0.0 copy-start.6
  1.4 0.1 copy-done.2
  1.5 0.5 copy-done.3
  2.1 0.1 copy-done.7
  2.1 0.0 copy-done.5
  2.1 0.0 copy-done.6
  2.2 0.0 copy-start
  2.2 1.0 %copy-done = bf16[4,256,256]{2,1,0:T(8,128)(2,1)S(1)} copy-done((bf16[4,256,256]{2,1,0:T(8,128)(2,1)S(1)}, bf16[4,256,256]{2,1,0:T(8,128)(2,1)}, u32[]{:S(2)}) %copy-start) | copy-done | bytes 524312
  3.2 0.0 copy-start.4
  3.2 0.7 copy-done.4
  3.9 1.4 %embed.1 = (f32[24,256]{1,0:T(8,128)S(1)}, f32[4,256,256]{2,1,0:T(8,128)S(1)}, f32[8,256]{1,0:T(8,128)S(1)}) custom-call(s32[2]{0:T(128)S(1)} %pad_add_fusion.pos_ref, s32[8]{0:T(128)S(1)} %copy-done.5, bf16[256,256]{1,0:T(8,128)(2,1)S(1)} %copy-done.2, bf16[4,256,256]{2,1,0:T(8,128)(2,1)S(1)} %copy-done, f32[4,256]{1,0:T(4,128)S(1)} %copy-done.4, ...), custom_call_target="tpu_custom_call" | custom-call | tf_op jit(solution)/shard_map/embed/pallas_call | solution.py:304
  5.3 0.0 copy-start.1
  5.3 5.1 %collective-permute-start.2 = (f32[1,24,256]{2,1,0:T(8,128)S(1)}, f32[1,24,256]{2,1,0:T(8,128)S(1)}, u32[]{:S(2)}, u32[]{:S(2)}) collective-permute-start(f32[1,24,256]{2,1,0:T(8,128)S(1)} %bitcast.29), channel_id=1, source_target_pairs={{0,6},{1,7},{2,4},{3,5},{4,2},{5,3},{6,0},{7,1},{8,14},{9,15},{10,... | collective-permute-start | bytes 73736 | tf_op jit(solution)/shard_map/ppermute | solution.py:295
  10.4 0.0 collective-permute-start.1
  10.4 0.6 collective-permute-start
  11.0 1.2 %collective-permute-done.2 = f32[1,24,256]{2,1,0:T(8,128)S(1)} collective-permute-done((f32[1,24,256]{2,1,0:T(8,128)S(1)}, f32[1,24,256]{2,1,0:T(8,128)S(1)}, u32[]{:S(2)}, u32[]{:S(2)}) %collective-permute-start.2) | collective-permute-done | bytes 24608 | tf_op jit(solution)/shard_map/ppermute | solution.py:295
  12.2 2.9 %collective-permute-done.1 = f32[1,24,256]{2,1,0:T(8,128)S(1)} collective-permute-done((f32[1,24,256]{2,1,0:T(8,128)S(1)}, f32[1,24,256]{2,1,0:T(8,128)S(1)}, u32[]{:S(2)}, u32[]{:S(2)}) %collective-permute-start.1) | collective-permute-done | bytes 24608 | tf_op jit(solution)/shard_map/ppermute | solution.py:295
  15.1 0.0 collective-permute-done
  15.1 2.5 %collective-permute-start.5 = (f32[4,24,256]{2,1,0:T(8,128)S(1)}, f32[4,24,256]{2,1,0:T(8,128)S(1)}, u32[]{:S(2)}, u32[]{:S(2)}) collective-permute-start(f32[4,24,256]{2,1,0:T(8,128)S(1)} %pad_maximum_fusion.1), channel_id=1, source_target_pairs={{0,17},{1,16},{2,19},{3,18},{4,21},{5,20},{6,23},{7,22},{8,25},{9,... | collective-permute-start | bytes 294920 | tf_op jit(solution)/shard_map/ppermute | solution.py:295
  17.6 0.5 collective-permute-start.4
  18.1 0.5 collective-permute-start.3
  18.7 4.1 %collective-permute-done.3 = f32[4,24,256]{2,1,0:T(8,128)S(1)} collective-permute-done((f32[4,24,256]{2,1,0:T(8,128)S(1)}, f32[4,24,256]{2,1,0:T(8,128)S(1)}, u32[]{:S(2)}, u32[]{:S(2)}) %collective-permute-start.3) | collective-permute-done | bytes 98336 | tf_op jit(solution)/shard_map/ppermute | solution.py:295
  22.8 0.0 collective-permute-done.4
  22.8 0.0 collective-permute-done.5
  22.8 0.1 collective-permute-start.6
  22.9 0.0 copy-done.1
  22.9 0.4 residuals.1
  23.3 1.3 %collective-permute-done.6.rest_1_ = f32[16,24,256]{2,1,0:T(8,128)S(1)} collective-permute-done((f32[16,24,256]{2,1,0:T(8,128)S(1)}, f32[16,24,256]{2,1,0:T(8,128)S(1)}, u32[]{:S(2)}, u32[]{:S(2)}) %collective-permute-start.6) | collective-permute-done | bytes 393248 | tf_op jit(solution)/shard_map/ppermute | solution.py:295
  24.6 7.6 %pairs_backward.1 = (f32[4,264,128]{2,1,0:T(8,128)S(1)}, f32[4,264,128]{2,1,0:T(8,128)S(1)}) custom-call(s32[2]{0:T(128)S(1)} %pad_add_fusion.pos_ref, s32[8]{0:T(128)S(1)} %copy-done.5, f32[24,256]{1,0:T(8,128)S(1)} %get-tuple-element.19.pay_ref, f32[8,256]{1,0:T(8,128)S(1)} %get-tuple-element.20.aux_ref, f32[4,256,256]{2,1,0:T(8,128)S(1)} %get-tuple-element.22.slope_ref, ...), custom_call_target="tpu_custom_call" | custom-call | tf_op jit(solution)/shard_map/pairs_backward/pallas_call | solution.py:345
  32.3 0.2 collective-permute-start.7
  32.5 1.8 %collective-permute-done.7 = f32[4,264,128]{2,1,0:T(8,128)S(1)} collective-permute-done((f32[4,264,128]{2,1,0:T(8,128)S(1)}, f32[4,264,128]{2,1,0:T(8,128)S(1)}, u32[]{:S(2)}, u32[]{:S(2)}) %collective-permute-start.7) | collective-permute-done | bytes 540704 | tf_op jit(solution)/shard_map/ppermute | solution.py:295
  34.3 0.1 add.45
  34.4 1.6 %collective-permute-start.10 = (f32[264,128]{1,0:T(8,128)S(1)}, f32[264,128]{1,0:T(8,128)S(1)}, u32[]{:S(2)}, u32[]{:S(2)}) collective-permute-start(f32[264,128]{1,0:T(8,128)S(1)} %get-tuple-element.33), channel_id=1, source_target_pairs={{0,17},{1,16},{2,19},{3,18},{4,21},{5,20},{6,23},{7,22},{8,25},{9,... | collective-permute-start | bytes 405512 | tf_op jit(solution)/shard_map/ppermute | solution.py:295
  35.9 0.6 collective-permute-start.9
  36.5 1.4 %collective-permute-start.8 = (f32[264,128]{1,0:T(8,128)S(1)}, f32[264,128]{1,0:T(8,128)S(1)}, u32[]{:S(2)}, u32[]{:S(2)}) collective-permute-start(f32[264,128]{1,0:T(8,128)S(1)} %get-tuple-element.35), channel_id=1, source_target_pairs={{0,1},{1,0},{2,3},{3,2},{4,5},{5,4},{6,7},{7,6},{8,9},{9,8},{10,11... | collective-permute-start | bytes 405512 | tf_op jit(solution)/shard_map/ppermute | solution.py:295
  37.9 3.9 %collective-permute-done.10 = f32[264,128]{1,0:T(8,128)S(1)} collective-permute-done((f32[264,128]{1,0:T(8,128)S(1)}, f32[264,128]{1,0:T(8,128)S(1)}, u32[]{:S(2)}, u32[]{:S(2)}) %collective-permute-start.10) | collective-permute-done | bytes 135200 | tf_op jit(solution)/shard_map/ppermute | solution.py:295
  41.8 2.1 %collective-permute-done.9 = f32[264,128]{1,0:T(8,128)S(1)} collective-permute-done((f32[264,128]{1,0:T(8,128)S(1)}, f32[264,128]{1,0:T(8,128)S(1)}, u32[]{:S(2)}, u32[]{:S(2)}) %collective-permute-start.9) | collective-permute-done | bytes 135200 | tf_op jit(solution)/shard_map/ppermute | solution.py:295
  43.9 0.1 collective-permute-done.8
  44.0 0.1 collective-permute-start.11
  44.1 5.4 %collective-permute-done.11 = f32[264,128]{1,0:T(8,128)S(1)} collective-permute-done((f32[264,128]{1,0:T(8,128)S(1)}, f32[264,128]{1,0:T(8,128)S(1)}, u32[]{:S(2)}, u32[]{:S(2)}) %collective-permute-start.11) | collective-permute-done | bytes 135200 | tf_op jit(solution)/shard_map/ppermute | solution.py:295
  49.5 2.1 %collective-permute-start.12 = (f32[264,128]{1,0:T(8,128)S(1)}, f32[264,128]{1,0:T(8,128)S(1)}, u32[]{:S(2)}, u32[]{:S(2)}) collective-permute-start(f32[264,128]{1,0:T(8,128)S(1)} %add.49), channel_id=1, source_target_pairs={{0,4},{1,5},{2,6},{3,7},{4,0},{5,1},{6,2},{7,3},{8,12},{9,13},{10,... | collective-permute-start | bytes 405512 | tf_op jit(solution)/shard_map/ppermute | solution.py:295
  51.6 6.3 %collective-permute-done.12 = f32[264,128]{1,0:T(8,128)S(1)} collective-permute-done((f32[264,128]{1,0:T(8,128)S(1)}, f32[264,128]{1,0:T(8,128)S(1)}, u32[]{:S(2)}, u32[]{:S(2)}) %collective-permute-start.12) | collective-permute-done | bytes 135200 | tf_op jit(solution)/shard_map/ppermute | solution.py:295
  57.9 1.7 %collective-permute-start.15 = (f32[264,128]{1,0:T(8,128)S(1)}, f32[264,128]{1,0:T(8,128)S(1)}, u32[]{:S(2)}, u32[]{:S(2)}) collective-permute-start(f32[264,128]{1,0:T(8,128)S(1)} %add.50.refs_0_), channel_id=1, source_target_pairs={{0,17},{1,16},{2,19},{3,18},{4,21},{5,20},{6,23},{7,22},{8,25},{9,... | collective-permute-start | bytes 405512 | tf_op jit(solution)/shard_map/ppermute | solution.py:295
  59.6 0.5 collective-permute-start.14
  60.1 1.4 %collective-permute-start.13 = (f32[264,128]{1,0:T(8,128)S(1)}, f32[264,128]{1,0:T(8,128)S(1)}, u32[]{:S(2)}, u32[]{:S(2)}) collective-permute-start(f32[264,128]{1,0:T(8,128)S(1)} %add.50.refs_0_), channel_id=1, source_target_pairs={{0,1},{1,0},{2,3},{3,2},{4,5},{5,4},{6,7},{7,6},{8,9},{9,8},{10,11... | collective-permute-start | bytes 405512 | tf_op jit(solution)/shard_map/ppermute | solution.py:295
  61.5 3.9 %collective-permute-done.15.refs_3_ = f32[264,128]{1,0:T(8,128)S(1)} collective-permute-done((f32[264,128]{1,0:T(8,128)S(1)}, f32[264,128]{1,0:T(8,128)S(1)}, u32[]{:S(2)}, u32[]{:S(2)}) %collective-permute-start.15) | collective-permute-done | bytes 135200 | tf_op jit(solution)/shard_map/ppermute | solution.py:295
  65.3 1.8 %collective-permute-done.14.refs_2_ = f32[264,128]{1,0:T(8,128)S(1)} collective-permute-done((f32[264,128]{1,0:T(8,128)S(1)}, f32[264,128]{1,0:T(8,128)S(1)}, u32[]{:S(2)}, u32[]{:S(2)}) %collective-permute-start.14) | collective-permute-done | bytes 135200 | tf_op jit(solution)/shard_map/ppermute | solution.py:295
  67.2 0.0 collective-permute-done.13.refs_1_
  67.2 0.1 pad_maximum_fusion
  67.2 0.1 collective-permute-start.16
  67.3 1.9 %collective-permute-done.16.refs_4_ = f32[4,264,128]{2,1,0:T(8,128)S(1)} collective-permute-done((f32[4,264,128]{2,1,0:T(8,128)S(1)}, f32[4,264,128]{2,1,0:T(8,128)S(1)}, u32[]{:S(2)}, u32[]{:S(2)}) %collective-permute-start.16) | collective-permute-done | bytes 540704 | tf_op jit(solution)/shard_map/ppermute | solution.py:295
  69.2 1.6 %finish.1 = (f32[8,128,256]{2,1,0:T(8,128)}, f32[4,256]{1,0:T(4,128)}, f32[16,256]{1,0:T(8,128)}, f32[1,256]{1,0:T(1,128)}, f32[1,1]{1,0:T(1,128)}) custom-call(s32[2]{0:T(128)S(1)} %pad_add_fusion.pos_ref, f32[264,128]{1,0:T(8,128)S(1)} %add.50.refs_0_, f32[264,128]{1,0:T(8,128)S(1)} %collective-permute-done.13.refs_1_, ...), custom_call_target="tpu_custom_call" | custom-call | tf_op jit(solution)/shard_map/finish/pallas_call | solution.py:371
  (12 shorter events, 0.1 us)
Async XLA Ops:
  0.6 0.9 %copy-start.2 = (bf16[256,256]{1,0:T(8,128)(2,1)S(1)}, bf16[256,256]{1,0:T(8,128)(2,1)}, u32[]{:S(2)}) copy-start(bf16[256,256]{1,0:T(8,128)(2,1)} %feat_ref.3) | copy-start | bytes 393220
  1.4 0.7 %copy-start.3 = (bf16[16,256]{1,0:T(8,128)(2,1)S(1)}, bf16[16,256]{1,0:T(8,128)(2,1)}, u32[]{:S(2)}) copy-start(bf16[16,256]{1,0:T(8,128)(2,1)} %wc_ref.3) | copy-start | bytes 24580
  1.4 0.7 copy-start.7
  1.4 0.7 copy-start.5
  1.4 0.7 %copy-start.6 = (s32[256]{0:T(256)S(1)}, s32[256]{0:T(256)}, u32[]{:S(2)}) copy-start(s32[256]{0:T(256)} %param.14) | copy-start | bytes 3076
  2.2 1.0 %copy-start = (bf16[4,256,256]{2,1,0:T(8,128)(2,1)S(1)}, bf16[4,256,256]{2,1,0:T(8,128)(2,1)}, u32[]{:S(2)}) copy-start(bf16[4,256,256]{2,1,0:T(8,128)(2,1)} %w_ref.3) | copy-start | bytes 1572868
  3.2 0.7 copy-start.4
  5.3 17.7 %copy-start.1 = (bf16[4,256,256]{2,1,0:T(8,128)(2,1)S(1)}, bf16[4,256,256]{2,1,0:T(8,128)(2,1)}, u32[]{:S(2)}) copy-start(bf16[4,256,256]{2,1,0:T(8,128)(2,1)} %w_ref.3) | copy-start | bytes 1572868
  5.3 6.9 %collective-permute-start.2 = (f32[1,24,256]{2,1,0:T(8,128)S(1)}, f32[1,24,256]{2,1,0:T(8,128)S(1)}, u32[]{:S(2)}, u32[]{:S(2)}) collective-permute-start(f32[1,24,256]{2,1,0:T(8,128)S(1)} %bitcast.29), channel_id=1, source_target_pairs={{0,6},{1,7},{2,4},{3,5},{4,2},{5,3},{6,0},{7,1},{8,14},{9,15},{10,... | collective-permute-start | bytes 73736 | tf_op jit(solution)/shard_map/ppermute | solution.py:295
  10.4 4.7 %collective-permute-start.1 = (f32[1,24,256]{2,1,0:T(8,128)S(1)}, f32[1,24,256]{2,1,0:T(8,128)S(1)}, u32[]{:S(2)}, u32[]{:S(2)}) collective-permute-start(f32[1,24,256]{2,1,0:T(8,128)S(1)} %bitcast.30), channel_id=1, source_target_pairs={{0,4},{1,5},{2,6},{3,7},{4,0},{5,1},{6,2},{7,3},{8,12},{9,13},{10,... | collective-permute-start | bytes 73736 | tf_op jit(solution)/shard_map/ppermute | solution.py:295
  10.4 4.7 %collective-permute-start = (f32[1,24,256]{2,1,0:T(8,128)S(1)}, f32[1,24,256]{2,1,0:T(8,128)S(1)}, u32[]{:S(2)}, u32[]{:S(2)}) collective-permute-start(f32[1,24,256]{2,1,0:T(8,128)S(1)} %bitcast.31), channel_id=1, source_target_pairs={{0,2},{1,3},{2,0},{3,1},{4,6},{5,7},{6,4},{7,5},{8,10},{9,11},{10,... | collective-permute-start | bytes 73736 | tf_op jit(solution)/shard_map/ppermute | solution.py:295
  15.1 7.7 %collective-permute-start.5 = (f32[4,24,256]{2,1,0:T(8,128)S(1)}, f32[4,24,256]{2,1,0:T(8,128)S(1)}, u32[]{:S(2)}, u32[]{:S(2)}) collective-permute-start(f32[4,24,256]{2,1,0:T(8,128)S(1)} %pad_maximum_fusion.1), channel_id=1, source_target_pairs={{0,17},{1,16},{2,19},{3,18},{4,21},{5,20},{6,23},{7,22},{8,25},{9,... | collective-permute-start | bytes 294920 | tf_op jit(solution)/shard_map/ppermute | solution.py:295
  17.6 5.1 %collective-permute-start.4 = (f32[4,24,256]{2,1,0:T(8,128)S(1)}, f32[4,24,256]{2,1,0:T(8,128)S(1)}, u32[]{:S(2)}, u32[]{:S(2)}) collective-permute-start(f32[4,24,256]{2,1,0:T(8,128)S(1)} %pad_maximum_fusion.1), channel_id=1, source_target_pairs={{0,16},{1,17},{2,18},{3,19},{4,20},{5,21},{6,22},{7,23},{8,24},{9,... | collective-permute-start | bytes 294920 | tf_op jit(solution)/shard_map/ppermute | solution.py:295
  18.1 4.6 %collective-permute-start.3 = (f32[4,24,256]{2,1,0:T(8,128)S(1)}, f32[4,24,256]{2,1,0:T(8,128)S(1)}, u32[]{:S(2)}, u32[]{:S(2)}) collective-permute-start(f32[4,24,256]{2,1,0:T(8,128)S(1)} %pad_maximum_fusion.1), channel_id=1, source_target_pairs={{0,1},{1,0},{2,3},{3,2},{4,5},{5,4},{6,7},{7,6},{8,9},{9,8},{10,11... | collective-permute-start | bytes 294920 | tf_op jit(solution)/shard_map/ppermute | solution.py:295
  22.8 1.8 %collective-permute-start.6 = (f32[16,24,256]{2,1,0:T(8,128)S(1)}, f32[16,24,256]{2,1,0:T(8,128)S(1)}, u32[]{:S(2)}, u32[]{:S(2)}) collective-permute-start(f32[16,24,256]{2,1,0:T(8,128)S(1)} %constant_dynamic-update-slice_fusion.rest_0_), channel_id=1, source_target_pairs={{0,8},{1,9},{2,10},{3,11},{4,12},{5,13},{6,14},{7,15},{8,0},{9,1},... | collective-permute-start | bytes 1179656 | tf_op jit(solution)/shard_map/ppermute | solution.py:295
  32.3 2.0 %collective-permute-start.7 = (f32[4,264,128]{2,1,0:T(8,128)S(1)}, f32[4,264,128]{2,1,0:T(8,128)S(1)}, u32[]{:S(2)}, u32[]{:S(2)}) collective-permute-start(f32[4,264,128]{2,1,0:T(8,128)S(1)} %get-tuple-element.27), channel_id=1, source_target_pairs={{0,8},{1,9},{2,10},{3,11},{4,12},{5,13},{6,14},{7,15},{8,0},{9,1},... | collective-permute-start | bytes 1622024 | tf_op jit(solution)/shard_map/ppermute | solution.py:295
  34.4 7.4 %collective-permute-start.10 = (f32[264,128]{1,0:T(8,128)S(1)}, f32[264,128]{1,0:T(8,128)S(1)}, u32[]{:S(2)}, u32[]{:S(2)}) collective-permute-start(f32[264,128]{1,0:T(8,128)S(1)} %get-tuple-element.33), channel_id=1, source_target_pairs={{0,17},{1,16},{2,19},{3,18},{4,21},{5,20},{6,23},{7,22},{8,25},{9,... | collective-permute-start | bytes 405512 | tf_op jit(solution)/shard_map/ppermute | solution.py:295
  35.9 7.9 %collective-permute-start.9 = (f32[264,128]{1,0:T(8,128)S(1)}, f32[264,128]{1,0:T(8,128)S(1)}, u32[]{:S(2)}, u32[]{:S(2)}) collective-permute-start(f32[264,128]{1,0:T(8,128)S(1)} %get-tuple-element.34), channel_id=1, source_target_pairs={{0,16},{1,17},{2,18},{3,19},{4,20},{5,21},{6,22},{7,23},{8,24},{9,... | collective-permute-start | bytes 405512 | tf_op jit(solution)/shard_map/ppermute | solution.py:295
  36.5 7.5 %collective-permute-start.8 = (f32[264,128]{1,0:T(8,128)S(1)}, f32[264,128]{1,0:T(8,128)S(1)}, u32[]{:S(2)}, u32[]{:S(2)}) collective-permute-start(f32[264,128]{1,0:T(8,128)S(1)} %get-tuple-element.35), channel_id=1, source_target_pairs={{0,1},{1,0},{2,3},{3,2},{4,5},{5,4},{6,7},{7,6},{8,9},{9,8},{10,11... | collective-permute-start | bytes 405512 | tf_op jit(solution)/shard_map/ppermute | solution.py:295
  44.0 5.5 %collective-permute-start.11 = (f32[264,128]{1,0:T(8,128)S(1)}, f32[264,128]{1,0:T(8,128)S(1)}, u32[]{:S(2)}, u32[]{:S(2)}) collective-permute-start(f32[264,128]{1,0:T(8,128)S(1)} %fusion.1), channel_id=1, source_target_pairs={{0,2},{1,3},{2,0},{3,1},{4,6},{5,7},{6,4},{7,5},{8,10},{9,11},{10,... | collective-permute-start | bytes 405512 | tf_op jit(solution)/shard_map/ppermute | solution.py:295
  49.5 8.4 %collective-permute-start.12 = (f32[264,128]{1,0:T(8,128)S(1)}, f32[264,128]{1,0:T(8,128)S(1)}, u32[]{:S(2)}, u32[]{:S(2)}) collective-permute-start(f32[264,128]{1,0:T(8,128)S(1)} %add.49), channel_id=1, source_target_pairs={{0,4},{1,5},{2,6},{3,7},{4,0},{5,1},{6,2},{7,3},{8,12},{9,13},{10,... | collective-permute-start | bytes 405512 | tf_op jit(solution)/shard_map/ppermute | solution.py:295
  57.9 7.4 %collective-permute-start.15 = (f32[264,128]{1,0:T(8,128)S(1)}, f32[264,128]{1,0:T(8,128)S(1)}, u32[]{:S(2)}, u32[]{:S(2)}) collective-permute-start(f32[264,128]{1,0:T(8,128)S(1)} %add.50.refs_0_), channel_id=1, source_target_pairs={{0,17},{1,16},{2,19},{3,18},{4,21},{5,20},{6,23},{7,22},{8,25},{9,... | collective-permute-start | bytes 405512 | tf_op jit(solution)/shard_map/ppermute | solution.py:295
  59.6 7.6 %collective-permute-start.14 = (f32[264,128]{1,0:T(8,128)S(1)}, f32[264,128]{1,0:T(8,128)S(1)}, u32[]{:S(2)}, u32[]{:S(2)}) collective-permute-start(f32[264,128]{1,0:T(8,128)S(1)} %add.50.refs_0_), channel_id=1, source_target_pairs={{0,16},{1,17},{2,18},{3,19},{4,20},{5,21},{6,22},{7,23},{8,24},{9,... | collective-permute-start | bytes 405512 | tf_op jit(solution)/shard_map/ppermute | solution.py:295
  60.1 7.1 %collective-permute-start.13 = (f32[264,128]{1,0:T(8,128)S(1)}, f32[264,128]{1,0:T(8,128)S(1)}, u32[]{:S(2)}, u32[]{:S(2)}) collective-permute-start(f32[264,128]{1,0:T(8,128)S(1)} %add.50.refs_0_), channel_id=1, source_target_pairs={{0,1},{1,0},{2,3},{3,2},{4,5},{5,4},{6,7},{7,6},{8,9},{9,8},{10,11... | collective-permute-start | bytes 405512 | tf_op jit(solution)/shard_map/ppermute | solution.py:295
  67.2 2.0 %collective-permute-start.16 = (f32[4,264,128]{2,1,0:T(8,128)S(1)}, f32[4,264,128]{2,1,0:T(8,128)S(1)}, u32[]{:S(2)}, u32[]{:S(2)}) collective-permute-start(f32[4,264,128]{2,1,0:T(8,128)S(1)} %pad_maximum_fusion), channel_id=1, source_target_pairs={{0,8},{1,9},{2,10},{3,11},{4,12},{5,13},{6,14},{7,15},{8,0},{9,1},... | collective-permute-start | bytes 1622024 | tf_op jit(solution)/shard_map/ppermute | solution.py:295

commit v2 on v1

v2 whole, which is shorter than its diff:
```python
import functools

import jax
import jax.numpy as jnp
from jax import lax
from jax.experimental import pallas as pl
from jax.experimental.pallas import tpu as pltpu
from jax.sharding import PartitionSpec as P

dist_eps = 0.0001
charge_floor = 0.5
AXES = ("layer", "phi")
VMEM = pl.BlockSpec(memory_space=pltpu.VMEM)
HBM = pl.BlockSpec(memory_space=pltpu.HBM)
UNROLL = 4
EMBED_VMEM = 63400000
HIGH = lax.Precision.HIGHEST
PARAMS = pltpu.CompilerParams(vmem_limit_bytes=48 * 1024 * 1024)


def matmul(a, b, ca=1, cb=0, precision=None):
    return lax.dot_general(
        a, b, (((ca,), (cb,)), ((), ())), precision=precision, preferred_element_type=jnp.float32
    )


def iota(shape, dim):
    return lax.broadcasted_iota(jnp.int32, shape, dim)


def head_rows(wc_ref, wb_ref):
    dim = wc_ref.shape[0]
    width = wc_ref.shape[1]
    beta_row = jnp.broadcast_to(wb_ref[...].astype(jnp.float32).reshape(1, width), (dim, width))
    tail = jnp.where(iota((dim, width), 0) == 0, beta_row, 0.0).astype(jnp.bfloat16)
    return jnp.concatenate([wc_ref[...], tail], 0)


def flat_index(axis_sizes):
    return lax.axis_index("layer") * axis_sizes[1] + lax.axis_index("phi")


def block_index(axis_sizes):
    me = flat_index(axis_sizes)
    core = lax.shift_right_logical(me, axis_sizes[1].bit_length() - 1) & 1
    upper = lax.shift_right_logical(me, axis_sizes[1].bit_length()) & 1
    return core * 4 + upper * 2 + (me & 1)


def embed_kernel(
    sizes,
    hit_hbm, feat_hbm, w_hbm, b_hbm, wc_hbm, wb_hbm, track_hbm, noise_hbm,
    pay_ref, aux_ref,
    hit_ref, feat_ref, w_ref, b_ref, wc_ref, wb_ref, track_ref, noise_ref, sems,
):
    dim = wc_ref.shape[0]
    hits = feat_ref.shape[0]
    points = hit_ref.shape[0]
    layers = w_ref.shape[0]
    pairs = [(feat_hbm, feat_ref)] + [(w_hbm.at[l], w_ref.at[l]) for l in range(layers)]
    pairs = pairs[:2] + [(b_hbm, b_ref)] + pairs[2:]
    pairs += [(wc_hbm, wc_ref), (wb_hbm, wb_ref), (track_hbm, track_ref)]
    pairs += [(noise_hbm, noise_ref), (hit_hbm, hit_ref)]
    copies = [
        pltpu.make_async_copy(src, dst, sems.at[i]) for i, (src, dst) in enumerate(pairs)
    ]
    for copy in copies:
        copy.start()
    for copy in copies[:3]:
        copy.wait()
    h = feat_ref[...]
    for l in range(layers):
        if l > 0:
            copies[l + 2].wait()
        a = matmul(h, w_ref[l]) + b_ref[l : l + 1, :]
        h = (a * jax.nn.sigmoid(a)).astype(jnp.bfloat16)
    for copy in copies[layers + 2 :]:
        copy.wait()
    xz = matmul(head_rows(wc_ref, wb_ref), h, 1, 1)
    z = xz[dim : dim + 1]
    expz = jnp.exp(z)
    spread = jnp.log1p(2.0 * expz)
    q = 0.25 * spread * spread + charge_floor
    slope = 0.5 * spread * (2.0 * expz / (1.0 + 2.0 * expz))
    beta = jax.nn.sigmoid(z)
    noise = noise_ref[...]
    label = jnp.where(noise == 0, track_ref[...], -1).astype(jnp.float32)
    rows8 = iota((8, hits), 0)
    aux_ref[0:8, :] = jnp.where(
        rows8 == 0, beta, jnp.where(rows8 == 1, slope, noise.astype(jnp.float32))
    )
    col = jnp.zeros((points, hits), jnp.int32)
    for p in range(points):
        col = jnp.where(rows8 == (p + 2) % points, hit_ref[p], col)
    sel = iota((points, hits), 1) == col
    aux_ref[8:16, :] = jnp.where(sel, 1.0, 0.0)
    lane = iota((points, 128), 1)
    row = iota((points, 128), 0)
    order = jnp.where(row < 2, row + points - 2, row - 2)
    pts = jnp.where(lane == dim + 1, (flat_index(sizes) * points + order).astype(jnp.float32), 0.0)
    for c in range(dim):
        v = jnp.sum(jnp.where(sel, xz[c : c + 1], 0.0), axis=1, keepdims=True)
        pts = jnp.where(lane == c, v, pts)
    v = jnp.sum(jnp.where(sel, q, 0.0), axis=1, keepdims=True)
    pts = jnp.where(lane == dim, v, pts)
    moved = pltpu.roll(pts, 2, 0)
    left = jnp.where(row == 0, q[:, :128], jnp.where(row == 1, label[:, :128], pts))
    right = jnp.where(row == 0, q[:, 128:], jnp.where(row == 1, label[:, 128:], moved))
    pay_ref[0:dim, :] = xz[0:dim]
    pay_ref[dim : dim + 8, 0:128] = left
    pay_ref[dim : dim + 8, 128:256] = right


def residual_kernel(
    feat_ref, w_ref, b_ref, wc_ref, wb_ref, slope_ref, ht_ref, last_ref, wt_ref, head_ref
):
    head_ref[...] = head_rows(wc_ref, wb_ref)
    layers = w_ref.shape[0]
    h = feat_ref[...]
    ht_ref[0] = h.T
    for l in range(layers):
        a = matmul(h, w_ref[l]) + b_ref[l : l + 1, :]
        sig = jax.nn.sigmoid(a)
        slope_ref[l] = sig * (1.0 + a * (1.0 - sig))
        h = (a * sig).astype(jnp.bfloat16)
        if l < layers - 1:
            ht_ref[l + 1] = h.T
            wt_ref[l] = w_ref[l + 1].T
        else:
            last_ref[...] = h


def point_tile(left, right):
    rows = iota(left.shape, 0)
    return jnp.where(rows < 2, pltpu.roll(right, 6, 0), left)


def pair_weights(dist_sq, match):
    shifted = dist_sq + dist_eps
    inv = lax.rsqrt(shifted)
    reach = jnp.maximum(1.0 - shifted * inv, 0.0)
    potential = jnp.where(match, dist_sq, reach * reach)
    weight = jnp.where(match, 2.0, -2.0 * jnp.maximum(inv - 1.0, 0.0))
    return potential, weight


def spread_kernel(pay_ref, copy_ref, own_ref, xb, yb):
    dim = xb.shape[0]
    full = xb.shape[1:]
    copy_ref[...] = pay_ref[...]
    own = pay_ref[dim : dim + 8, :]
    own = point_tile(own[:, :128], own[:, 128:])
    own_ref[...] = own
    for c in range(dim):
        xb[c] = jnp.broadcast_to(pay_ref[c : c + 1, :], full)
        yb[c] = jnp.broadcast_to(own[:, c : c + 1], full)


def pair_sums(pay_ref, own, ref, xb, yb, hit_acc, point_acc):
    dim = xb.shape[0]
    full = xb.shape[1:]
    label_b = jnp.broadcast_to(pay_ref[dim + 1 : dim + 2, :], full)
    index_b = jnp.broadcast_to(own[:, dim + 1 : dim + 2], full)
    zero = jnp.zeros(full, jnp.float32)

    def hit_side(j, acc):
        tile = ref[j, dim : dim + 8, :]
        tile = point_tile(tile[:, :128], tile[:, 128:])
        diffs = []
        dist_sq = zero
        for c in range(dim):
            diff = xb[c] - tile[:, c : c + 1]
            diffs.append(diff)
            dist_sq = dist_sq + diff * diff
        point_q = tile[:, dim : dim + 1]
        potential, weight = pair_weights(dist_sq, label_b == tile[:, dim + 1 : dim + 2])
        weight = weight * point_q
        terms = [weight * diff for diff in diffs] + [potential * point_q]
        return tuple(s + term for s, term in zip(acc, terms))

    def point_side(j, acc):
        diffs = []
        dist_sq = zero
        for c in range(dim):
            diff = yb[c] - ref[j, c : c + 1, :]
            diffs.append(diff)
            dist_sq = dist_sq + diff * diff
        hit_q = ref[j, dim : dim + 1, :]
        potential, weight = pair_weights(dist_sq, index_b == ref[j, dim + 1 : dim + 2, :])
        weight = weight * hit_q
        terms = [weight * diff for diff in diffs] + [potential * hit_q]
        return tuple(s + term[:, :128] + term[:, 128:] for s, term in zip(acc, terms))

    hit_acc = lax.fori_loop(0, ref.shape[0], hit_side, hit_acc, unroll=UNROLL)
    point_acc = lax.fori_loop(0, ref.shape[0], point_side, point_acc, unroll=UNROLL)
    return hit_acc, point_acc


def near_kernel(pay_ref, own_ref, xb, yb, rows_ref, hit_ref, point_ref):
    dim = xb.shape[0]
    own = own_ref[...]
    hit_acc = (jnp.zeros(hit_ref.shape[1:], jnp.float32),) * (dim + 1)
    point_acc = (jnp.zeros(point_ref.shape[1:], jnp.float32),) * (dim + 1)
    hit_acc, point_acc = pair_sums(pay_ref, own, rows_ref, xb, yb, hit_acc, point_acc)
    for c in range(dim + 1):
        hit_ref[c] = hit_acc[c]
        point_ref[c] = point_acc[c]


def backward_kernel(
    sizes, hits_all, points_all,
    pay_ref, own_ref, xb, yb, aux_ref, slope_ref, ht_ref, last_ref, wt_ref, head_ref, rows_ref, hit_ref, point_ref,
    keep_ref, send_ref, gx_ref, stack, ext,
):
    dim = xb.shape[0]
    hits = pay_ref.shape[1]
    layers = slope_ref.shape[0]
    points = own_ref.shape[0]
    own = own_ref[...]
    q_row = pay_ref[dim : dim + 1, :]
    hit_acc = tuple(hit_ref[c] for c in range(dim + 1))
    point_acc = tuple(point_ref[c] for c in range(dim + 1))
    hit_acc, point_acc = pair_sums(pay_ref, own, rows_ref, xb, yb, hit_acc, point_acc)

    pot_row = jnp.sum(hit_acc[dim], axis=0, keepdims=True)
    scaled = q_row * (1.0 / hits_all)
    for c in range(dim):
        gx_ref[c : c + 1, :] = jnp.sum(hit_acc[c], axis=0, keepdims=True) * scaled
    lane = iota((8, 128), 1)
    own_q = own[:, dim : dim + 1] * (1.0 / hits_all)
    grads = jnp.where(lane == dim + 1, 1.0, 0.0)
    for c in range(dim):
        v = jnp.sum(point_acc[c], axis=1, keepdims=True) * own_q
        grads = jnp.where(lane == c, v, grads)
    v = jnp.sum(point_acc[dim], axis=1, keepdims=True) * (1.0 / hits_all)
    grads = jnp.where(lane == dim, v, grads)
    added = matmul(grads, aux_ref[8:16, :], 0, 0, HIGH)

    beta = aux_ref[0:1, :]
    noise = aux_ref[2:3, :]
    count = added[dim + 1 : dim + 2]
    grad_q = pot_row * (1.0 / hits_all) + added[dim : dim + 1]
    grad_b = noise * (1.0 / hits_all) - count * (1.0 / points_all)
    grad_z = grad_q * aux_ref[1:2, :] + grad_b * beta * (1.0 - beta)
    per_hit = q_row * pot_row * (1.0 / hits_all) + noise * beta * (1.0 / hits_all)
    per_hit = per_hit - count * beta * (1.0 / points_all)
    loss = jnp.sum(per_hit, axis=1, keepdims=True) + points * 1.0 / points_all

    grad_x = gx_ref[...] + added[0:dim]
    tail = jnp.where(iota((dim, hits), 0) == 0, grad_z, 0.0)
    low = jnp.concatenate([grad_x, tail], 0).astype(jnp.bfloat16)
    head = head_ref[...]
    grad_head = matmul(low, last_ref[...])
    up = matmul(low, head, 0, 0)
    ext[...] = jnp.zeros(ext.shape, jnp.float32)
    cols = [slice(0, 128), slice(128, 256)]
    base = 2 * layers
    for h, col in enumerate(cols):
        ext[base + h * dim : base + (h + 1) * dim, :] = grad_head[0:dim, col]
        ext[base + 2 * dim + h : base + 2 * dim + h + 1, :] = grad_head[dim : dim + 1, col]
    ext[base + 2 * dim + 2 : base + 2 * dim + 3, :] = jnp.broadcast_to(loss, (1, 128))
    blocks = stack.shape[0]
    rows = layers * hits // blocks
    per_layer = blocks // layers
    for l in range(layers - 1, -1, -1):
        err = (up * slope_ref[l]).astype(jnp.bfloat16)
        if l > 0:
            up = matmul(err, wt_ref[l - 1])
        grad_w = matmul(ht_ref[l], err)
        bias = jnp.sum(err.astype(jnp.float32), axis=0, keepdims=True)
        for h, col in enumerate(cols):
            ext[h * layers + l : h * layers + l + 1, :] = bias[:, col]
            for s in range(per_layer):
                stack[l * per_layer + s, h * rows : (h + 1) * rows, :] = grad_w[
                    s * rows : (s + 1) * rows, col
                ]
    for b in range(blocks):
        stack[b, 2 * rows : 2 * rows + 8, :] = ext[8 * b : 8 * b + 8, :]
    me = block_index(sizes)
    for j in range(blocks // 2):
        keep_ref[j] = stack[jnp.bitwise_xor(me, j)]
        send_ref[j] = stack[jnp.bitwise_xor(me, j + blocks // 2)]


def place_copies(sizes, blocks, first, gw_ref, sems):
    rows = gw_ref.shape[1]
    me = block_index(sizes)
    copies = []
    for r, block in enumerate(blocks):
        place = jnp.bitwise_xor(me, first + r)
        for h in range(2):
            copies.append(
                pltpu.make_async_copy(
                    block.at[pl.ds(h * rows, rows)],
                    gw_ref.at[place, :, pl.ds(h * 128, 128)],
                    sems.at[2 * r + h],
                )
            )
    for copy in copies:
        copy.start()
    return copies


def place_near_kernel(sizes, *refs):
    blocks = refs[:4]
    gw_ref, ext_ref, sems = refs[4:]
    rows = gw_ref.shape[1]
    copies = place_copies(sizes, blocks, 0, gw_ref, sems)
    for r, block in enumerate(blocks):
        ext_ref[r] = block[2 * rows :, :]
    for copy in copies:
        copy.wait()


def place_far_kernel(
    sizes, far_ref, near_ref, gw_in, gw_ref, *rest
):
    outs, scratch, (ext, sems, small_sems) = rest[:4], rest[4:8], rest[8:]
    gb_ref, gc_ref, gbeta_ref, loss_ref = scratch
    rows = gw_ref.shape[1]
    half = far_ref.shape[0]
    dim = gc_ref.shape[0]
    layers = gb_ref.shape[0]
    blocks = [far_ref.at[r] for r in range(half)]
    copies = place_copies(sizes, blocks, half, gw_ref, sems)
    me = block_index(sizes)
    for r in range(half):
        ext[jnp.bitwise_xor(me, r)] = near_ref[r]
        ext[jnp.bitwise_xor(me, half + r)] = far_ref[r, 2 * rows :, :]
    flat = jnp.concatenate([ext[b] for b in range(2 * half)], 0)
    base = 2 * layers
    for h, col in enumerate([slice(0, 128), slice(128, 256)]):
        gb_ref[:, col] = flat[h * layers : (h + 1) * layers]
        gc_ref[:, col] = flat[base + h * dim : base + (h + 1) * dim]
        gbeta_ref[:, col] = flat[base + 2 * dim + h : base + 2 * dim + h + 1]
    loss_ref[...] = flat[base + 2 * dim + 2 : base + 2 * dim + 3, 0:1]
    for i in range(4):
        copies.append(pltpu.make_async_copy(scratch[i], outs[i], small_sems.at[i]))
        copies[-1].start()
    for copy in copies:
        copy.wait()


def bits_of(size):
    return [1 << t for t in range(size.bit_length() - 1)]


def on_device(layer_size, phi_size, features, w_layers, b_layers, w_coord, w_beta, point_hit, track, noise):
    ndev = layer_size * phi_size
    hits, width = features.shape
    layers = w_layers.shape[0]
    dim = w_coord.shape[0]
    points = point_hit.shape[0]
    hits_all = hits * ndev * 1.0
    points_all = points * ndev * 1.0
    f32 = jnp.float32
    core = phi_size
    plane = [1, 2 * phi_size]
    others = [b for b in bits_of(ndev) if b != core and b not in plane]

    def swap(x, mask):
        return lax.ppermute(x, AXES, [(i, i ^ mask) for i in range(ndev)])

    sizes = (layer_size, phi_size)
    track = track.reshape(1, hits)
    noise = noise.reshape(1, hits)
    low = jnp.bfloat16

    pay, aux = pl.pallas_call(
        functools.partial(embed_kernel, sizes),
        out_shape=(
            jax.ShapeDtypeStruct((dim + 8, hits), f32),
            jax.ShapeDtypeStruct((16, hits), f32),
        ),
        in_specs=[HBM] * 8,
        out_specs=(VMEM,) * 2,
        scratch_shapes=[
            pltpu.SMEM((points,), jnp.int32),
            pltpu.VMEM((hits, width), low),
            pltpu.VMEM((layers, width, width), low),
            pltpu.VMEM((layers, width), f32),
            pltpu.VMEM((dim, width), low),
            pltpu.VMEM(w_beta.shape, low),
            pltpu.VMEM((1, hits), jnp.int32),
            pltpu.VMEM((1, hits), jnp.int32),
            pltpu.SemaphoreType.DMA((layers + 7,)),
        ],
        compiler_params=pltpu.CompilerParams(vmem_limit_bytes=EMBED_VMEM),
        name="embed",
    )(point_hit, features, w_layers, b_layers, w_coord, w_beta, track, noise)

    def residuals(early):
        return pl.pallas_call(
            residual_kernel,
            out_shape=(
                jax.ShapeDtypeStruct((layers, hits, width), f32),
                jax.ShapeDtypeStruct((layers, width, hits), low),
                jax.ShapeDtypeStruct((hits, width), low),
                jax.ShapeDtypeStruct((layers - 1, width, width), low),
                jax.ShapeDtypeStruct((2 * dim, width), low),
            ),
            in_specs=[VMEM] * 5,
            out_specs=(VMEM,) * 5,
            compiler_params=PARAMS,
            cost_estimate=pl.CostEstimate(
                flops=20 * layers * hits * width, bytes_accessed=6 * layers * hits * width,
                transcendentals=layers * hits * width,
            ),
            name="residuals",
        )(*early)

    pay_own, own, xb, yb = pl.pallas_call(
        spread_kernel,
        out_shape=(
            jax.ShapeDtypeStruct((dim + 8, hits), f32),
            jax.ShapeDtypeStruct((8, 128), f32),
            jax.ShapeDtypeStruct((dim, 8, hits), f32),
            jax.ShapeDtypeStruct((dim, 8, hits), f32),
        ),
        in_specs=[VMEM],
        out_specs=(VMEM,) * 4,
        compiler_params=PARAMS,
        cost_estimate=pl.CostEstimate(flops=0, bytes_accessed=80 * dim * hits, transcendentals=0),
        name="spread",
    )(pay)
    rows_all = pay[None]
    kept = pay_own[None]
    stages = [others[i : i + 2] for i in range(0, len(others), 2)] + [plane]
    for stage in stages:
        masks = stage + ([stage[0] ^ stage[1]] if len(stage) > 1 else [])
        if stage is plane:
            rows_all, *early = lax.optimization_barrier((rows_all, features, w_layers, b_layers))
            kept = rows_all
        arrived = [swap(rows_all, m) for m in masks]
        kept = rows_all = jnp.concatenate([kept] + arrived, 0)
    slope, ht, last, wt, head = residuals(early + [w_coord, w_beta])
    rows_all, slope = lax.optimization_barrier((rows_all, slope))
    rows_far = swap(rows_all, core)

    partial_sums = (
        jax.ShapeDtypeStruct((dim + 1, 8, hits), f32),
        jax.ShapeDtypeStruct((dim + 1, 8, 128), f32),
    )
    hit_sums, point_sums = pl.pallas_call(
        near_kernel,
        out_shape=partial_sums,
        in_specs=[VMEM] * 5,
        out_specs=(VMEM, VMEM),
        compiler_params=PARAMS,
        cost_estimate=pl.CostEstimate(
            flops=200 * points * hits * ndev, bytes_accessed=ndev * hits * 64,
            transcendentals=2 * points * hits * ndev,
        ),
        name="near_pairs",
    )(pay_own, own, xb, yb, rows_all)

    blocks = 8
    block_rows = 2 * (layers * width // blocks) + 8
    half = jax.ShapeDtypeStruct((blocks // 2, block_rows, 128), f32)
    keep, send = pl.pallas_call(
        functools.partial(backward_kernel, sizes, hits_all, points_all),
        out_shape=(half, half),
        in_specs=[VMEM] * 13,
        out_specs=(VMEM, VMEM),
        scratch_shapes=[
            pltpu.VMEM((dim, hits), f32),
            pltpu.VMEM((blocks, block_rows, 128), f32),
            pltpu.VMEM((8 * blocks, 128), f32),
        ],
        compiler_params=PARAMS,
        name="pairs_backward",
    )(pay_own, own, xb, yb, aux, slope, ht, last, wt, head, rows_far, hit_sums, point_sums)

    total = keep + swap(send, core)
    masks = [plane[0], plane[1], plane[0] ^ plane[1]]
    mine = total[0]
    arrived = [swap(total[r + 1], m) for r, m in enumerate(masks)]
    mine = (mine + arrived[0]) + (arrived[1] + arrived[2])
    for m in others:
        mine = mine + swap(mine, m)
    quarter = [mine] + [swap(mine, m) for m in masks]
    far = swap(jnp.stack(quarter), core)

    weights = jax.ShapeDtypeStruct((blocks, layers * width // blocks, width), f32)
    gw, near_ext = pl.pallas_call(
        functools.partial(place_near_kernel, sizes),
        out_shape=(weights, jax.ShapeDtypeStruct((blocks // 2, 8, 128), f32)),
        in_specs=[VMEM] * 4,
        out_specs=(HBM, VMEM),
        scratch_shapes=[pltpu.SemaphoreType.DMA((blocks,))],
        compiler_params=PARAMS,
        cost_estimate=pl.CostEstimate(flops=0, bytes_accessed=4 * layers * width * width, transcendentals=0),
        name="place_near",
    )(*quarter)
    gw, gb, gc, gbeta, loss = pl.pallas_call(
        functools.partial(place_far_kernel, sizes),
        out_shape=(
            weights,
            jax.ShapeDtypeStruct((layers, width), f32),
            jax.ShapeDtypeStruct((dim, width), f32),
            jax.ShapeDtypeStruct((1, width), f32),
            jax.ShapeDtypeStruct((1, 1), f32),
        ),
        in_specs=[VMEM, VMEM, HBM],
        out_specs=(HBM,) * 5,
        scratch_shapes=[
            pltpu.VMEM((layers, width), f32),
            pltpu.VMEM((dim, width), f32),
            pltpu.VMEM((1, width), f32),
            pltpu.VMEM((1, 1), f32),
            pltpu.VMEM((blocks, 8, 128), f32),
            pltpu.SemaphoreType.DMA((blocks,)),
            pltpu.SemaphoreType.DMA((4,)),
        ],
        input_output_aliases={2: 0},
        compiler_params=PARAMS,
        name="place_far",
    )(far, near_ext, gw)
    return (
        gw.reshape(layers, width, width),
        gb,
        gc,
        gbeta.reshape(width),
        loss.reshape(()),
    )


def solution(mesh):
    split = P(AXES)
    return jax.shard_map(
        functools.partial(on_device, mesh.shape["layer"], mesh.shape["phi"]),
        mesh=mesh,
        in_specs=(P(AXES, None), P(), P(), P(), P(), split, split, split),
        out_specs=(P(), P(), P(), P(), P()),
        check_vma=False,
    )
```

time: 71.1 us -> 64.3 us (0.904)
  waiting for transfers between devices: 36.6 us -> 33.4 us
  local copies, waits for them, and re-layouts: 3.19 us -> 0.83 us
  Pallas kernels: 11 us -> 9.84 us
    ppermute x17, waiting for transfers between devices: 36.6 us -> 33.4 us  [swap(): return lax.ppermute(x, AXES, [(i, i ^ mask) for i in range(ndev)])]
    unnamed x22 -> x14, local copies, waits for them, and re-layouts: 2.49 us -> 0.8 us
    pallas_call x4 -> x7, Pallas kernels: 11 us -> 9.84 us  [the longest x1 2.93 us: on_device(): pl.pallas_call(functools.partial(embed_kernel, sizes), out_shape=(jax.Sha...]
  transfers between devices with their start and end apart: 17 -> 17, of which waited for: 13 -> 15; matrix products, arithmetic and copies ran while one was open for 0% -> 0% of each run, Pallas kernels for 1% -> 5%
where the time goes in v2:
time: 64.3 us; the launch traced here: 64.1 us
  waiting for transfers between devices  33.4 us (52%)
  starting transfers between devices  19.1 us (30%)
  Pallas kernels  9.84 us (15%)
  local copies, waits for them, and re-layouts  0.83 us (1%)
  between operations  0.78 us (1%)
    ppermute x17, waiting for transfers between devices, swap(): return lax.ppermute(x, AXES, [(i, i ^ mask) for i in range(ndev)])  33.4 us
    ppermute x17, starting transfers between devices, swap(): return lax.ppermute(x, AXES, [(i, i ^ mask) for i in range(ndev)])  19.1 us
    pallas_call x1, Pallas kernels, on_device(): pl.pallas_call(functools.partial(embed_kernel, sizes), out_shape=(jax.Sha...  2.93 us
    pallas_call x1, Pallas kernels, on_device(): pl.pallas_call(functools.partial(backward_kernel, sizes, hits_all, points...  2.93 us
    pallas_call x1, Pallas kernels, on_device(): pl.pallas_call(near_kernel, out_shape=partial_sums, in_specs=[VMEM] * 5,...  1.49 us
  transfers between devices with their start and end apart: 17, of which 15 were waited for; matrix products, arithmetic and copies ran while one was open for 0% of the time, Pallas kernels for 5%

profile of v2, /device:TPU:0, one launch (start us, length us, event | category | flops | bytes accessed | tf_op | source)
XLA Modules:
  0.0 64.1 jit_solution(13887999672867933018)
XLA Ops:
  0.6 0.0 copy-start
  0.6 2.9 %embed.1 = (f32[24,256]{1,0:T(8,128)}, f32[16,256]{1,0:T(8,128)}) custom-call(s32[8]{0:T(128)} %hit_hbm.1, bf16[256,256]{1,0:T(8,128)(2,1)} %feat_ref, bf16[4,256,256]{2,1,0:T(8,128)(2,1)} %w_ref, f32[4,256]{1,0:T(4,128)} %b_ref, bf16[16,256]{1,0:T(8,128)(2,1)} %wc_ref.1, bf16[256]{0:T(256)(128)(2,1)} %wb_ref.1, s32[1,256]{1,0:T(1,128)} %bitcast.32, ...), custom_call_target="tpu_custom_call" | custom-call | tf_op jit(solution)/shard_map/embed/pallas_call | solution.py:369
  3.6 0.0 copy-start.1
  3.6 5.1 %collective-permute-start.2 = (f32[1,24,256]{2,1,0:T(8,128)}, f32[1,24,256]{2,1,0:T(8,128)S(1)}, u32[]{:S(2)}, u32[]{:S(2)}) collective-permute-start(f32[1,24,256]{2,1,0:T(8,128)} %bitcast.28), channel_id=1, source_target_pairs={{0,6},{1,7},{2,4},{3,5},{4,2},{5,3},{6,0},{7,1},{8,14},{9,15},{10,... | collective-permute-start | bytes 73736 | tf_op jit(solution)/shard_map/ppermute | solution.py:362
  8.7 0.0 collective-permute-start.1
  8.7 0.6 collective-permute-start
  9.4 0.0 copy-start.3
  9.4 0.8 %copy-done.3 = f32[24,256]{1,0:T(8,128)S(1)} copy-done((f32[24,256]{1,0:T(8,128)S(1)}, f32[24,256]{1,0:T(8,128)}, u32[]{:S(2)}) %copy-start.3) | copy-done | bytes 24600
  10.1 0.1 spread.1
  10.2 0.5 collective-permute-done.2
  10.7 2.9 %collective-permute-done.1 = f32[1,24,256]{2,1,0:T(8,128)S(1)} collective-permute-done((f32[1,24,256]{2,1,0:T(8,128)}, f32[1,24,256]{2,1,0:T(8,128)S(1)}, u32[]{:S(2)}, u32[]{:S(2)}) %collective-permute-start.1) | collective-permute-done | bytes 24608 | tf_op jit(solution)/shard_map/ppermute | solution.py:362
  13.6 0.0 collective-permute-done
  13.6 0.0 copy-start.2
  13.7 0.0 copy-start.5
  13.7 0.0 copy-start.6
  13.7 2.5 %collective-permute-start.5 = (f32[4,24,256]{2,1,0:T(8,128)S(1)}, f32[4,24,256]{2,1,0:T(8,128)S(1)}, u32[]{:S(2)}, u32[]{:S(2)}) collective-permute-start(f32[4,24,256]{2,1,0:T(8,128)S(1)} %pad_maximum_fusion.2), channel_id=1, source_target_pairs={{0,17},{1,16},{2,19},{3,18},{4,21},{5,20},{6,23},{7,22},{8,25},{9,... | collective-permute-start | bytes 294920 | tf_op jit(solution)/shard_map/ppermute | solution.py:362
  16.2 0.5 collective-permute-start.4
  16.7 0.5 collective-permute-start.3
  17.2 0.0 copy-done
  17.2 0.0 copy-done.1
  17.2 0.0 copy-done.2
  17.2 0.0 copy-done.5
  17.2 0.0 copy-done.6
  17.3 0.6 %residuals.1 = (f32[4,256,256]{2,1,0:T(8,128)S(1)}, bf16[4,256,256]{2,1,0:T(8,128)(2,1)S(1)}, bf16[256,256]{1,0:T(8,128)(2,1)S(1)}, bf16[3,256,256]{2,1,0:T(8,128)(2,1)S(1)}, bf16[32,256]{1,0:T(8,128)(2,1)S(1)}) custom-call(bf16[256,256]{1,0:T(8,128)(2,1)S(1)} %copy-done.1, bf16[4,256,256]{2,1,0:T(8,128)(2,1)S(1)} %copy-done, f32[4,256]{1,0:T(4,128)S(1)} %copy-done.5, ...), custom_call_target="tpu_custom_call" | custom-call | flops 5242880 | bytes 1572864 | tf_op jit(solution)/shard_map/residuals/pallas_call | solution.py:393
  17.9 2.4 %collective-permute-done.5 = f32[4,24,256]{2,1,0:T(8,128)S(1)} collective-permute-done((f32[4,24,256]{2,1,0:T(8,128)S(1)}, f32[4,24,256]{2,1,0:T(8,128)S(1)}, u32[]{:S(2)}, u32[]{:S(2)}) %collective-permute-start.5) | collective-permute-done | bytes 98336 | tf_op jit(solution)/shard_map/ppermute | solution.py:362
  20.3 0.8 %collective-permute-done.4 = f32[4,24,256]{2,1,0:T(8,128)S(1)} collective-permute-done((f32[4,24,256]{2,1,0:T(8,128)S(1)}, f32[4,24,256]{2,1,0:T(8,128)S(1)}, u32[]{:S(2)}, u32[]{:S(2)}) %collective-permute-start.4) | collective-permute-done | bytes 98336 | tf_op jit(solution)/shard_map/ppermute | solution.py:362
  21.1 0.2 collective-permute-done.3
  21.3 0.1 collective-permute-start.6
  21.4 0.0 copy-start.4
  21.4 1.5 %near_pairs.1 = (f32[17,8,256]{2,1,0:T(8,128)S(1)}, f32[17,8,128]{2,1,0:T(8,128)S(1)}) custom-call(f32[24,256]{1,0:T(8,128)S(1)} %get-tuple-element.34.pay_ref, f32[8,128]{1,0:T(8,128)S(1)} %get-tuple-element.35.own_ref, f32[16,8,256]{2,1,0:T(8,128)S(1)} %get-tuple-element.36.xb, f32[16,8,256]{2,1,0:T(8,128)S(1)} %get-tuple-element.37.yb, ...), custom_call_target="tpu_custom_call" | custom-call | flops 13107200 | bytes 524288 | tf_op jit(solution)/shard_map/near_pairs/pallas_call | solution.py:444
  22.9 0.2 collective-permute-done.6.rows_ref
  23.1 0.0 copy-done.4
  23.1 2.9 %pairs_backward.1 = (f32[4,264,128]{2,1,0:T(8,128)S(1)}, f32[4,264,128]{2,1,0:T(8,128)S(1)}) custom-call(f32[24,256]{1,0:T(8,128)S(1)} %get-tuple-element.34.pay_ref, f32[8,128]{1,0:T(8,128)S(1)} %get-tuple-element.35.own_ref, f32[16,8,256]{2,1,0:T(8,128)S(1)} %get-tuple-element.36.xb, f32[16,8,256]{2,1,0:T(8,128)S(1)} %get-tuple-element.37.yb, ...), custom_call_target="tpu_custom_call" | custom-call | tf_op jit(solution)/shard_map/pairs_backward/pallas_call | solution.py:460
  26.1 0.4 collective-permute-start.7
  26.4 1.6 %collective-permute-done.7 = f32[4,264,128]{2,1,0:T(8,128)S(1)} collective-permute-done((f32[4,264,128]{2,1,0:T(8,128)S(1)}, f32[4,264,128]{2,1,0:T(8,128)S(1)}, u32[]{:S(2)}, u32[]{:S(2)}) %collective-permute-start.7) | collective-permute-done | bytes 540704 | tf_op jit(solution)/shard_map/ppermute | solution.py:362
  28.1 0.1 add.18
  28.2 1.6 %collective-permute-start.10 = (f32[264,128]{1,0:T(8,128)S(1)}, f32[264,128]{1,0:T(8,128)S(1)}, u32[]{:S(2)}, u32[]{:S(2)}) collective-permute-start(f32[264,128]{1,0:T(8,128)S(1)} %get-tuple-element.61), channel_id=1, source_target_pairs={{0,17},{1,16},{2,19},{3,18},{4,21},{5,20},{6,23},{7,22},{8,25},{9,... | collective-permute-start | bytes 405512 | tf_op jit(solution)/shard_map/ppermute | solution.py:362
  29.7 0.6 collective-permute-start.9
  30.3 1.4 %collective-permute-start.8 = (f32[264,128]{1,0:T(8,128)S(1)}, f32[264,128]{1,0:T(8,128)S(1)}, u32[]{:S(2)}, u32[]{:S(2)}) collective-permute-start(f32[264,128]{1,0:T(8,128)S(1)} %get-tuple-element.63), channel_id=1, source_target_pairs={{0,1},{1,0},{2,3},{3,2},{4,5},{5,4},{6,7},{7,6},{8,9},{9,8},{10,11... | collective-permute-start | bytes 405512 | tf_op jit(solution)/shard_map/ppermute | solution.py:362
  31.7 3.9 %collective-permute-done.10 = f32[264,128]{1,0:T(8,128)S(1)} collective-permute-done((f32[264,128]{1,0:T(8,128)S(1)}, f32[264,128]{1,0:T(8,128)S(1)}, u32[]{:S(2)}, u32[]{:S(2)}) %collective-permute-start.10) | collective-permute-done | bytes 135200 | tf_op jit(solution)/shard_map/ppermute | solution.py:362
  35.6 2.2 %collective-permute-done.9 = f32[264,128]{1,0:T(8,128)S(1)} collective-permute-done((f32[264,128]{1,0:T(8,128)S(1)}, f32[264,128]{1,0:T(8,128)S(1)}, u32[]{:S(2)}, u32[]{:S(2)}) %collective-permute-start.9) | collective-permute-done | bytes 135200 | tf_op jit(solution)/shard_map/ppermute | solution.py:362
  37.8 0.1 collective-permute-done.8
  38.0 0.1 collective-permute-start.11
  38.1 5.4 %collective-permute-done.11 = f32[264,128]{1,0:T(8,128)S(1)} collective-permute-done((f32[264,128]{1,0:T(8,128)S(1)}, f32[264,128]{1,0:T(8,128)S(1)}, u32[]{:S(2)}, u32[]{:S(2)}) %collective-permute-start.11) | collective-permute-done | bytes 135200 | tf_op jit(solution)/shard_map/ppermute | solution.py:362
  43.5 2.1 %collective-permute-start.12 = (f32[264,128]{1,0:T(8,128)S(1)}, f32[264,128]{1,0:T(8,128)S(1)}, u32[]{:S(2)}, u32[]{:S(2)}) collective-permute-start(f32[264,128]{1,0:T(8,128)S(1)} %add.22), channel_id=1, source_target_pairs={{0,4},{1,5},{2,6},{3,7},{4,0},{5,1},{6,2},{7,3},{8,12},{9,13},{10,... | collective-permute-start | bytes 405512 | tf_op jit(solution)/shard_map/ppermute | solution.py:362
  45.6 6.3 %collective-permute-done.12 = f32[264,128]{1,0:T(8,128)S(1)} collective-permute-done((f32[264,128]{1,0:T(8,128)S(1)}, f32[264,128]{1,0:T(8,128)S(1)}, u32[]{:S(2)}, u32[]{:S(2)}) %collective-permute-start.12) | collective-permute-done | bytes 135200 | tf_op jit(solution)/shard_map/ppermute | solution.py:362
  51.9 1.7 %collective-permute-start.15 = (f32[264,128]{1,0:T(8,128)S(1)}, f32[264,128]{1,0:T(8,128)S(1)}, u32[]{:S(2)}, u32[]{:S(2)}) collective-permute-start(f32[264,128]{1,0:T(8,128)S(1)} %add.23.refs_0_), channel_id=1, source_target_pairs={{0,17},{1,16},{2,19},{3,18},{4,21},{5,20},{6,23},{7,22},{8,25},{9,... | collective-permute-start | bytes 405512 | tf_op jit(solution)/shard_map/ppermute | solution.py:362
  53.6 0.5 collective-permute-start.14
  54.1 1.4 %collective-permute-start.13 = (f32[264,128]{1,0:T(8,128)S(1)}, f32[264,128]{1,0:T(8,128)S(1)}, u32[]{:S(2)}, u32[]{:S(2)}) collective-permute-start(f32[264,128]{1,0:T(8,128)S(1)} %add.23.refs_0_), channel_id=1, source_target_pairs={{0,1},{1,0},{2,3},{3,2},{4,5},{5,4},{6,7},{7,6},{8,9},{9,8},{10,11... | collective-permute-start | bytes 405512 | tf_op jit(solution)/shard_map/ppermute | solution.py:362
  55.5 3.9 %collective-permute-done.15.refs_3_ = f32[264,128]{1,0:T(8,128)S(1)} collective-permute-done((f32[264,128]{1,0:T(8,128)S(1)}, f32[264,128]{1,0:T(8,128)S(1)}, u32[]{:S(2)}, u32[]{:S(2)}) %collective-permute-start.15) | collective-permute-done | bytes 135200 | tf_op jit(solution)/shard_map/ppermute | solution.py:362
  59.3 1.8 %collective-permute-done.14.refs_2_ = f32[264,128]{1,0:T(8,128)S(1)} collective-permute-done((f32[264,128]{1,0:T(8,128)S(1)}, f32[264,128]{1,0:T(8,128)S(1)}, u32[]{:S(2)}, u32[]{:S(2)}) %collective-permute-start.14) | collective-permute-done | bytes 135200 | tf_op jit(solution)/shard_map/ppermute | solution.py:362
  61.2 0.0 collective-permute-done.13.refs_1_
  61.2 0.1 pad_maximum_fusion
  61.2 0.1 collective-permute-start.16
  61.3 0.9 %place_near.1 = (f32[8,128,256]{2,1,0:T(8,128)}, f32[4,8,128]{2,1,0:T(8,128)S(1)}) custom-call(f32[264,128]{1,0:T(8,128)S(1)} %add.23.refs_0_, f32[264,128]{1,0:T(8,128)S(1)} %collective-permute-done.13.refs_1_, f32[264,128]{1,0:T(8,128)S(1)} %collective-permute-done.14.refs_2_, f32[264,128]{1,0:T(8,128)S(1)} %collective-permute-done.15.refs_3_), custom_call_target="tpu_custom_call" | custom-call | bytes 1048576 | tf_op jit(solution)/shard_map/place_near/pallas_call | solution.py:485
  62.2 1.1 %collective-permute-done.16.far_ref = f32[4,264,128]{2,1,0:T(8,128)S(1)} collective-permute-done((f32[4,264,128]{2,1,0:T(8,128)S(1)}, f32[4,264,128]{2,1,0:T(8,128)S(1)}, u32[]{:S(2)}, u32[]{:S(2)}) %collective-permute-start.16) | collective-permute-done | bytes 540704 | tf_op jit(solution)/shard_map/ppermute | solution.py:362
  63.2 0.9 %place_far.1 = (f32[8,128,256]{2,1,0:T(8,128)}, f32[4,256]{1,0:T(4,128)}, f32[16,256]{1,0:T(8,128)}, f32[1,256]{1,0:T(1,128)}, f32[1,1]{1,0:T(1,128)}) custom-call(f32[4,264,128]{2,1,0:T(8,128)S(1)} %collective-permute-done.16.far_ref, f32[4,8,128]{2,1,0:T(8,128)S(1)} %get-tuple-element.54.near_ref, ...), custom_call_target="tpu_custom_call", output_to_operand_aliasing={{0}: (2, {})} | custom-call | tf_op jit(solution)/shard_map/place_far/pallas_call | solution.py:495
  (6 shorter events, 0.1 us)
Async XLA Ops:
  0.6 16.6 %copy-start = (bf16[4,256,256]{2,1,0:T(8,128)(2,1)S(1)}, bf16[4,256,256]{2,1,0:T(8,128)(2,1)}, u32[]{:S(2)}) copy-start(bf16[4,256,256]{2,1,0:T(8,128)(2,1)} %w_ref) | copy-start | bytes 1572868
  3.6 13.7 %copy-start.1 = (bf16[256,256]{1,0:T(8,128)(2,1)S(1)}, bf16[256,256]{1,0:T(8,128)(2,1)}, u32[]{:S(2)}) copy-start(bf16[256,256]{1,0:T(8,128)(2,1)} %feat_ref) | copy-start | bytes 393220
  3.6 7.1 %collective-permute-start.2 = (f32[1,24,256]{2,1,0:T(8,128)}, f32[1,24,256]{2,1,0:T(8,128)S(1)}, u32[]{:S(2)}, u32[]{:S(2)}) collective-permute-start(f32[1,24,256]{2,1,0:T(8,128)} %bitcast.28), channel_id=1, source_target_pairs={{0,6},{1,7},{2,4},{3,5},{4,2},{5,3},{6,0},{7,1},{8,14},{9,15},{10,... | collective-permute-start | bytes 73736 | tf_op jit(solution)/shard_map/ppermute | solution.py:362
  8.7 4.9 %collective-permute-start.1 = (f32[1,24,256]{2,1,0:T(8,128)}, f32[1,24,256]{2,1,0:T(8,128)S(1)}, u32[]{:S(2)}, u32[]{:S(2)}) collective-permute-start(f32[1,24,256]{2,1,0:T(8,128)} %bitcast.29), channel_id=1, source_target_pairs={{0,4},{1,5},{2,6},{3,7},{4,0},{5,1},{6,2},{7,3},{8,12},{9,13},{10,... | collective-permute-start | bytes 73736 | tf_op jit(solution)/shard_map/ppermute | solution.py:362
  8.7 4.9 %collective-permute-start = (f32[1,24,256]{2,1,0:T(8,128)}, f32[1,24,256]{2,1,0:T(8,128)S(1)}, u32[]{:S(2)}, u32[]{:S(2)}) collective-permute-start(f32[1,24,256]{2,1,0:T(8,128)} %bitcast.30), channel_id=1, source_target_pairs={{0,2},{1,3},{2,0},{3,1},{4,6},{5,7},{6,4},{7,5},{8,10},{9,11},{10,... | collective-permute-start | bytes 73736 | tf_op jit(solution)/shard_map/ppermute | solution.py:362
  9.4 0.8 %copy-start.3 = (f32[24,256]{1,0:T(8,128)S(1)}, f32[24,256]{1,0:T(8,128)}, u32[]{:S(2)}) copy-start(f32[24,256]{1,0:T(8,128)} %get-tuple-element.33.pay_ref) | copy-start | bytes 73732
  13.6 3.6 %copy-start.2 = (bf16[16,256]{1,0:T(8,128)(2,1)S(1)}, bf16[16,256]{1,0:T(8,128)(2,1)}, u32[]{:S(2)}) copy-start(bf16[16,256]{1,0:T(8,128)(2,1)} %wc_ref.1) | copy-start | bytes 24580
  13.7 3.6 %copy-start.5 = (f32[4,256]{1,0:T(4,128)S(1)}, f32[4,256]{1,0:T(4,128)}, u32[]{:S(2)}) copy-start(f32[4,256]{1,0:T(4,128)} %b_ref) | copy-start | bytes 12292
  13.7 3.6 %copy-start.6 = (bf16[256]{0:T(256)(128)(2,1)S(1)}, bf16[256]{0:T(256)(128)(2,1)}, u32[]{:S(2)}) copy-start(bf16[256]{0:T(256)(128)(2,1)} %wb_ref.1) | copy-start | bytes 1540
  13.7 6.6 %collective-permute-start.5 = (f32[4,24,256]{2,1,0:T(8,128)S(1)}, f32[4,24,256]{2,1,0:T(8,128)S(1)}, u32[]{:S(2)}, u32[]{:S(2)}) collective-permute-start(f32[4,24,256]{2,1,0:T(8,128)S(1)} %pad_maximum_fusion.2), channel_id=1, source_target_pairs={{0,17},{1,16},{2,19},{3,18},{4,21},{5,20},{6,23},{7,22},{8,25},{9,... | collective-permute-start | bytes 294920 | tf_op jit(solution)/shard_map/ppermute | solution.py:362
  16.2 4.9 %collective-permute-start.4 = (f32[4,24,256]{2,1,0:T(8,128)S(1)}, f32[4,24,256]{2,1,0:T(8,128)S(1)}, u32[]{:S(2)}, u32[]{:S(2)}) collective-permute-start(f32[4,24,256]{2,1,0:T(8,128)S(1)} %pad_maximum_fusion.2), channel_id=1, source_target_pairs={{0,16},{1,17},{2,18},{3,19},{4,20},{5,21},{6,22},{7,23},{8,24},{9,... | collective-permute-start | bytes 294920 | tf_op jit(solution)/shard_map/ppermute | solution.py:362
  16.7 4.6 %collective-permute-start.3 = (f32[4,24,256]{2,1,0:T(8,128)S(1)}, f32[4,24,256]{2,1,0:T(8,128)S(1)}, u32[]{:S(2)}, u32[]{:S(2)}) collective-permute-start(f32[4,24,256]{2,1,0:T(8,128)S(1)} %pad_maximum_fusion.2), channel_id=1, source_target_pairs={{0,1},{1,0},{2,3},{3,2},{4,5},{5,4},{6,7},{7,6},{8,9},{9,8},{10,11... | collective-permute-start | bytes 294920 | tf_op jit(solution)/shard_map/ppermute | solution.py:362
  21.3 1.8 %collective-permute-start.6 = (f32[16,24,256]{2,1,0:T(8,128)S(1)}, f32[16,24,256]{2,1,0:T(8,128)S(1)}, u32[]{:S(2)}, u32[]{:S(2)}) collective-permute-start(f32[16,24,256]{2,1,0:T(8,128)S(1)} %pad_maximum_fusion.1.rows_ref), channel_id=1, source_target_pairs={{0,8},{1,9},{2,10},{3,11},{4,12},{5,13},{6,14},{7,15},{8,0},{9,1},... | collective-permute-start | bytes 1179656 | tf_op jit(solution)/shard_map/ppermute | solution.py:362
  21.4 1.7 %copy-start.4 = (f32[16,256]{1,0:T(8,128)S(1)}, f32[16,256]{1,0:T(8,128)}, u32[]{:S(2)}) copy-start(f32[16,256]{1,0:T(8,128)} %get-tuple-element.38.aux_ref) | copy-start | bytes 49156
  26.1 2.0 %collective-permute-start.7 = (f32[4,264,128]{2,1,0:T(8,128)S(1)}, f32[4,264,128]{2,1,0:T(8,128)S(1)}, u32[]{:S(2)}, u32[]{:S(2)}) collective-permute-start(f32[4,264,128]{2,1,0:T(8,128)S(1)} %get-tuple-element.53), channel_id=1, source_target_pairs={{0,8},{1,9},{2,10},{3,11},{4,12},{5,13},{6,14},{7,15},{8,0},{9,1},... | collective-permute-start | bytes 1622024 | tf_op jit(solution)/shard_map/ppermute | solution.py:362
  28.2 7.4 %collective-permute-start.10 = (f32[264,128]{1,0:T(8,128)S(1)}, f32[264,128]{1,0:T(8,128)S(1)}, u32[]{:S(2)}, u32[]{:S(2)}) collective-permute-start(f32[264,128]{1,0:T(8,128)S(1)} %get-tuple-element.61), channel_id=1, source_target_pairs={{0,17},{1,16},{2,19},{3,18},{4,21},{5,20},{6,23},{7,22},{8,25},{9,... | collective-permute-start | bytes 405512 | tf_op jit(solution)/shard_map/ppermute | solution.py:362
  29.7 8.1 %collective-permute-start.9 = (f32[264,128]{1,0:T(8,128)S(1)}, f32[264,128]{1,0:T(8,128)S(1)}, u32[]{:S(2)}, u32[]{:S(2)}) collective-permute-start(f32[264,128]{1,0:T(8,128)S(1)} %get-tuple-element.62), channel_id=1, source_target_pairs={{0,16},{1,17},{2,18},{3,19},{4,20},{5,21},{6,22},{7,23},{8,24},{9,... | collective-permute-start | bytes 405512 | tf_op jit(solution)/shard_map/ppermute | solution.py:362
  30.3 7.6 %collective-permute-start.8 = (f32[264,128]{1,0:T(8,128)S(1)}, f32[264,128]{1,0:T(8,128)S(1)}, u32[]{:S(2)}, u32[]{:S(2)}) collective-permute-start(f32[264,128]{1,0:T(8,128)S(1)} %get-tuple-element.63), channel_id=1, source_target_pairs={{0,1},{1,0},{2,3},{3,2},{4,5},{5,4},{6,7},{7,6},{8,9},{9,8},{10,11... | collective-permute-start | bytes 405512 | tf_op jit(solution)/shard_map/ppermute | solution.py:362
  38.0 5.5 %collective-permute-start.11 = (f32[264,128]{1,0:T(8,128)S(1)}, f32[264,128]{1,0:T(8,128)S(1)}, u32[]{:S(2)}, u32[]{:S(2)}) collective-permute-start(f32[264,128]{1,0:T(8,128)S(1)} %fusion.1), channel_id=1, source_target_pairs={{0,2},{1,3},{2,0},{3,1},{4,6},{5,7},{6,4},{7,5},{8,10},{9,11},{10,... | collective-permute-start | bytes 405512 | tf_op jit(solution)/shard_map/ppermute | solution.py:362
  43.5 8.4 %collective-permute-start.12 = (f32[264,128]{1,0:T(8,128)S(1)}, f32[264,128]{1,0:T(8,128)S(1)}, u32[]{:S(2)}, u32[]{:S(2)}) collective-permute-start(f32[264,128]{1,0:T(8,128)S(1)} %add.22), channel_id=1, source_target_pairs={{0,4},{1,5},{2,6},{3,7},{4,0},{5,1},{6,2},{7,3},{8,12},{9,13},{10,... | collective-permute-start | bytes 405512 | tf_op jit(solution)/shard_map/ppermute | solution.py:362
  51.9 7.4 %collective-permute-start.15 = (f32[264,128]{1,0:T(8,128)S(1)}, f32[264,128]{1,0:T(8,128)S(1)}, u32[]{:S(2)}, u32[]{:S(2)}) collective-permute-start(f32[264,128]{1,0:T(8,128)S(1)} %add.23.refs_0_), channel_id=1, source_target_pairs={{0,17},{1,16},{2,19},{3,18},{4,21},{5,20},{6,23},{7,22},{8,25},{9,... | collective-permute-start | bytes 405512 | tf_op jit(solution)/shard_map/ppermute | solution.py:362
  53.6 7.6 %collective-permute-start.14 = (f32[264,128]{1,0:T(8,128)S(1)}, f32[264,128]{1,0:T(8,128)S(1)}, u32[]{:S(2)}, u32[]{:S(2)}) collective-permute-start(f32[264,128]{1,0:T(8,128)S(1)} %add.23.refs_0_), channel_id=1, source_target_pairs={{0,16},{1,17},{2,18},{3,19},{4,20},{5,21},{6,22},{7,23},{8,24},{9,... | collective-permute-start | bytes 405512 | tf_op jit(solution)/shard_map/ppermute | solution.py:362
  54.1 7.1 %collective-permute-start.13 = (f32[264,128]{1,0:T(8,128)S(1)}, f32[264,128]{1,0:T(8,128)S(1)}, u32[]{:S(2)}, u32[]{:S(2)}) collective-permute-start(f32[264,128]{1,0:T(8,128)S(1)} %add.23.refs_0_), channel_id=1, source_target_pairs={{0,1},{1,0},{2,3},{3,2},{4,5},{5,4},{6,7},{7,6},{8,9},{9,8},{10,11... | collective-permute-start | bytes 405512 | tf_op jit(solution)/shard_map/ppermute | solution.py:362
  61.2 2.0 %collective-permute-start.16 = (f32[4,264,128]{2,1,0:T(8,128)S(1)}, f32[4,264,128]{2,1,0:T(8,128)S(1)}, u32[]{:S(2)}, u32[]{:S(2)}) collective-permute-start(f32[4,264,128]{2,1,0:T(8,128)S(1)} %pad_maximum_fusion), channel_id=1, source_target_pairs={{0,8},{1,9},{2,10},{3,11},{4,12},{5,13},{6,14},{7,15},{8,0},{9,1},... | collective-permute-start | bytes 1622024 | tf_op jit(solution)/shard_map/ppermute | solution.py:362

commit v3 on v2

--- a/solution.py
+++ b/solution.py
@@ -427,7 +427,7 @@
     kept = pay_own[None]
     stages = [others[i : i + 2] for i in range(0, len(others), 2)] + [plane]
     for stage in stages:
-        masks = stage + ([stage[0] ^ stage[1]] if len(stage) > 1 else [])
+        masks = stage[:1] + ([stage[0] ^ stage[1]] if len(stage) > 1 else []) + stage[1:]
         if stage is plane:
             rows_all, *early = lax.optimization_barrier((rows_all, features, w_layers, b_layers))
             kept = rows_all
@@ -474,11 +474,12 @@
     total = keep + swap(send, core)
     masks = [plane[0], plane[1], plane[0] ^ plane[1]]
     mine = total[0]
-    arrived = [swap(total[r + 1], m) for r, m in enumerate(masks)]
-    mine = (mine + arrived[0]) + (arrived[1] + arrived[2])
-    for m in others:
-        mine = mine + swap(mine, m)
-    quarter = [mine] + [swap(mine, m) for m in masks]
+    arrived = [swap(total[r + 1], masks[r]) for r in (2, 1, 0)]
+    mine = (mine + arrived[2]) + (arrived[1] + arrived[0])
+    for i, m in enumerate(others):
+        mine = mine + swap(mine, m ^ others[0] if i > 0 else m)
+    quarter = [swap(mine, masks[r]) for r in (2, 1, 0)] + [mine]
+    quarter = quarter[::-1]
     far = swap(jnp.stack(quarter), core)
 
     weights = jax.ShapeDtypeStruct((blocks, layers * width // blocks, width), f32)

time: 64.3 us -> 61.1 us (0.950)
  waiting for transfers between devices: 33.4 us -> 30.2 us
    ppermute x17, waiting for transfers between devices: 33.4 us -> 30.2 us  [swap(): return lax.ppermute(x, AXES, [(i, i ^ mask) for i in range(ndev)])]
where the time goes in v3:
time: 61.1 us; the launch traced here: 60.9 us
  waiting for transfers between devices  30.2 us (49%)
  starting transfers between devices  19 us (31%)
  Pallas kernels  9.84 us (16%)
  local copies, waits for them, and re-layouts  0.83 us (1%)
  between operations  0.79 us (1%)
    ppermute x17, waiting for transfers between devices, swap(): return lax.ppermute(x, AXES, [(i, i ^ mask) for i in range(ndev)])  30.2 us
    ppermute x17, starting transfers between devices, swap(): return lax.ppermute(x, AXES, [(i, i ^ mask) for i in range(ndev)])  19 us
    pallas_call x1, Pallas kernels, on_device(): pl.pallas_call(functools.partial(embed_kernel, sizes), out_shape=(jax.Sha...  2.93 us
    pallas_call x1, Pallas kernels, on_device(): pl.pallas_call(functools.partial(backward_kernel, sizes, hits_all, points...  2.93 us
    pallas_call x1, Pallas kernels, on_device(): pl.pallas_call(near_kernel, out_shape=partial_sums, in_specs=[VMEM] * 5,...  1.49 us
  transfers between devices with their start and end apart: 17, of which 15 were waited for; matrix products, arithmetic and copies ran while one was open for 0% of the time, Pallas kernels for 5%

profile of v3, /device:TPU:0, one launch (start us, length us, event | category | flops | bytes accessed | tf_op | source)
XLA Modules:
  0.0 60.9 jit_solution(8963476064984502713)
XLA Ops:
  0.6 0.0 copy-start
  0.6 2.9 %embed.1 = (f32[24,256]{1,0:T(8,128)}, f32[16,256]{1,0:T(8,128)}) custom-call(s32[8]{0:T(128)} %hit_hbm.1, bf16[256,256]{1,0:T(8,128)(2,1)} %feat_ref, bf16[4,256,256]{2,1,0:T(8,128)(2,1)} %w_ref, f32[4,256]{1,0:T(4,128)} %b_ref, bf16[16,256]{1,0:T(8,128)(2,1)} %wc_ref.1, bf16[256]{0:T(256)(128)(2,1)} %wb_ref.1, s32[1,256]{1,0:T(1,128)} %bitcast.32, ...), custom_call_target="tpu_custom_call" | custom-call | tf_op jit(solution)/shard_map/embed/pallas_call | solution.py:369
  3.6 0.0 copy-start.1
  3.6 4.1 %collective-permute-start.2 = (f32[1,24,256]{2,1,0:T(8,128)}, f32[1,24,256]{2,1,0:T(8,128)S(1)}, u32[]{:S(2)}, u32[]{:S(2)}) collective-permute-start(f32[1,24,256]{2,1,0:T(8,128)} %bitcast.28), channel_id=1, source_target_pairs={{0,4},{1,5},{2,6},{3,7},{4,0},{5,1},{6,2},{7,3},{8,12},{9,13},{10,... | collective-permute-start | bytes 73736 | tf_op jit(solution)/shard_map/ppermute | solution.py:362
  7.7 1.3 %collective-permute-start.1 = (f32[1,24,256]{2,1,0:T(8,128)}, f32[1,24,256]{2,1,0:T(8,128)S(1)}, u32[]{:S(2)}, u32[]{:S(2)}) collective-permute-start(f32[1,24,256]{2,1,0:T(8,128)} %bitcast.29), channel_id=1, source_target_pairs={{0,6},{1,7},{2,4},{3,5},{4,2},{5,3},{6,0},{7,1},{8,14},{9,15},{10,... | collective-permute-start | bytes 73736 | tf_op jit(solution)/shard_map/ppermute | solution.py:362
  9.0 0.2 collective-permute-start
  9.3 0.0 copy-start.3
  9.3 0.8 %copy-done.3 = f32[24,256]{1,0:T(8,128)S(1)} copy-done((f32[24,256]{1,0:T(8,128)S(1)}, f32[24,256]{1,0:T(8,128)}, u32[]{:S(2)}) %copy-start.3) | copy-done | bytes 24600
  10.0 0.1 spread.1
  10.1 0.0 collective-permute-done.2
  10.1 3.4 %collective-permute-done.1 = f32[1,24,256]{2,1,0:T(8,128)S(1)} collective-permute-done((f32[1,24,256]{2,1,0:T(8,128)}, f32[1,24,256]{2,1,0:T(8,128)S(1)}, u32[]{:S(2)}, u32[]{:S(2)}) %collective-permute-start.1) | collective-permute-done | bytes 24608 | tf_op jit(solution)/shard_map/ppermute | solution.py:362
  13.5 0.0 collective-permute-done
  13.5 0.0 copy-start.2
  13.5 0.0 copy-start.5
  13.5 0.0 copy-start.6
  13.6 1.6 %collective-permute-start.5 = (f32[4,24,256]{2,1,0:T(8,128)S(1)}, f32[4,24,256]{2,1,0:T(8,128)S(1)}, u32[]{:S(2)}, u32[]{:S(2)}) collective-permute-start(f32[4,24,256]{2,1,0:T(8,128)S(1)} %pad_maximum_fusion.2), channel_id=1, source_target_pairs={{0,16},{1,17},{2,18},{3,19},{4,20},{5,21},{6,22},{7,23},{8,24},{9,... | collective-permute-start | bytes 294920 | tf_op jit(solution)/shard_map/ppermute | solution.py:362
  15.2 1.4 %collective-permute-start.4 = (f32[4,24,256]{2,1,0:T(8,128)S(1)}, f32[4,24,256]{2,1,0:T(8,128)S(1)}, u32[]{:S(2)}, u32[]{:S(2)}) collective-permute-start(f32[4,24,256]{2,1,0:T(8,128)S(1)} %pad_maximum_fusion.2), channel_id=1, source_target_pairs={{0,17},{1,16},{2,19},{3,18},{4,21},{5,20},{6,23},{7,22},{8,25},{9,... | collective-permute-start | bytes 294920 | tf_op jit(solution)/shard_map/ppermute | solution.py:362
  16.6 0.5 collective-permute-start.3
  17.1 0.0 copy-done
  17.1 0.0 copy-done.1
  17.1 0.0 copy-done.2
  17.1 0.0 copy-done.5
  17.1 0.0 copy-done.6
  17.1 0.6 %residuals.1 = (f32[4,256,256]{2,1,0:T(8,128)S(1)}, bf16[4,256,256]{2,1,0:T(8,128)(2,1)S(1)}, bf16[256,256]{1,0:T(8,128)(2,1)S(1)}, bf16[3,256,256]{2,1,0:T(8,128)(2,1)S(1)}, bf16[32,256]{1,0:T(8,128)(2,1)S(1)}) custom-call(bf16[256,256]{1,0:T(8,128)(2,1)S(1)} %copy-done.1, bf16[4,256,256]{2,1,0:T(8,128)(2,1)S(1)} %copy-done, f32[4,256]{1,0:T(4,128)S(1)} %copy-done.5, ...), custom_call_target="tpu_custom_call" | custom-call | flops 5242880 | bytes 1572864 | tf_op jit(solution)/shard_map/residuals/pallas_call | solution.py:393
  17.8 1.1 %collective-permute-done.5 = f32[4,24,256]{2,1,0:T(8,128)S(1)} collective-permute-done((f32[4,24,256]{2,1,0:T(8,128)S(1)}, f32[4,24,256]{2,1,0:T(8,128)S(1)}, u32[]{:S(2)}, u32[]{:S(2)}) %collective-permute-start.5) | collective-permute-done | bytes 98336 | tf_op jit(solution)/shard_map/ppermute | solution.py:362
  18.9 1.8 %collective-permute-done.4 = f32[4,24,256]{2,1,0:T(8,128)S(1)} collective-permute-done((f32[4,24,256]{2,1,0:T(8,128)S(1)}, f32[4,24,256]{2,1,0:T(8,128)S(1)}, u32[]{:S(2)}, u32[]{:S(2)}) %collective-permute-start.4) | collective-permute-done | bytes 98336 | tf_op jit(solution)/shard_map/ppermute | solution.py:362
  20.7 0.5 collective-permute-done.3
  21.2 0.1 collective-permute-start.6
  21.3 0.0 copy-start.4
  21.3 1.5 %near_pairs.1 = (f32[17,8,256]{2,1,0:T(8,128)S(1)}, f32[17,8,128]{2,1,0:T(8,128)S(1)}) custom-call(f32[24,256]{1,0:T(8,128)S(1)} %get-tuple-element.34.pay_ref, f32[8,128]{1,0:T(8,128)S(1)} %get-tuple-element.35.own_ref, f32[16,8,256]{2,1,0:T(8,128)S(1)} %get-tuple-element.36.xb, f32[16,8,256]{2,1,0:T(8,128)S(1)} %get-tuple-element.37.yb, ...), custom_call_target="tpu_custom_call" | custom-call | flops 13107200 | bytes 524288 | tf_op jit(solution)/shard_map/near_pairs/pallas_call | solution.py:444
  22.8 0.2 collective-permute-done.6.rows_ref
  23.0 0.0 copy-done.4
  23.0 2.9 %pairs_backward.1 = (f32[4,264,128]{2,1,0:T(8,128)S(1)}, f32[4,264,128]{2,1,0:T(8,128)S(1)}) custom-call(f32[24,256]{1,0:T(8,128)S(1)} %get-tuple-element.34.pay_ref, f32[8,128]{1,0:T(8,128)S(1)} %get-tuple-element.35.own_ref, f32[16,8,256]{2,1,0:T(8,128)S(1)} %get-tuple-element.36.xb, f32[16,8,256]{2,1,0:T(8,128)S(1)} %get-tuple-element.37.yb, ...), custom_call_target="tpu_custom_call" | custom-call | tf_op jit(solution)/shard_map/pairs_backward/pallas_call | solution.py:460
  26.0 0.4 collective-permute-start.7
  26.3 1.6 %collective-permute-done.7 = f32[4,264,128]{2,1,0:T(8,128)S(1)} collective-permute-done((f32[4,264,128]{2,1,0:T(8,128)S(1)}, f32[4,264,128]{2,1,0:T(8,128)S(1)}, u32[]{:S(2)}, u32[]{:S(2)}) %collective-permute-start.7) | collective-permute-done | bytes 540704 | tf_op jit(solution)/shard_map/ppermute | solution.py:362
  28.0 0.1 add.18
  28.1 2.1 %collective-permute-start.10 = (f32[264,128]{1,0:T(8,128)S(1)}, f32[264,128]{1,0:T(8,128)S(1)}, u32[]{:S(2)}, u32[]{:S(2)}) collective-permute-start(f32[264,128]{1,0:T(8,128)S(1)} %get-tuple-element.61), channel_id=1, source_target_pairs={{0,17},{1,16},{2,19},{3,18},{4,21},{5,20},{6,23},{7,22},{8,25},{9,... | collective-permute-start | bytes 405512 | tf_op jit(solution)/shard_map/ppermute | solution.py:362
  30.1 0.5 collective-permute-start.9
  30.7 1.0 %collective-permute-start.8 = (f32[264,128]{1,0:T(8,128)S(1)}, f32[264,128]{1,0:T(8,128)S(1)}, u32[]{:S(2)}, u32[]{:S(2)}) collective-permute-start(f32[264,128]{1,0:T(8,128)S(1)} %get-tuple-element.63), channel_id=1, source_target_pairs={{0,1},{1,0},{2,3},{3,2},{4,5},{5,4},{6,7},{7,6},{8,9},{9,8},{10,11... | collective-permute-start | bytes 405512 | tf_op jit(solution)/shard_map/ppermute | solution.py:362
  31.6 3.8 %collective-permute-done.10 = f32[264,128]{1,0:T(8,128)S(1)} collective-permute-done((f32[264,128]{1,0:T(8,128)S(1)}, f32[264,128]{1,0:T(8,128)S(1)}, u32[]{:S(2)}, u32[]{:S(2)}) %collective-permute-start.10) | collective-permute-done | bytes 135200 | tf_op jit(solution)/shard_map/ppermute | solution.py:362
  35.4 2.3 %collective-permute-done.9 = f32[264,128]{1,0:T(8,128)S(1)} collective-permute-done((f32[264,128]{1,0:T(8,128)S(1)}, f32[264,128]{1,0:T(8,128)S(1)}, u32[]{:S(2)}, u32[]{:S(2)}) %collective-permute-start.9) | collective-permute-done | bytes 135200 | tf_op jit(solution)/shard_map/ppermute | solution.py:362
  37.7 0.1 collective-permute-done.8
  37.9 0.1 collective-permute-start.11
  37.9 5.4 %collective-permute-done.11 = f32[264,128]{1,0:T(8,128)S(1)} collective-permute-done((f32[264,128]{1,0:T(8,128)S(1)}, f32[264,128]{1,0:T(8,128)S(1)}, u32[]{:S(2)}, u32[]{:S(2)}) %collective-permute-start.11) | collective-permute-done | bytes 135200 | tf_op jit(solution)/shard_map/ppermute | solution.py:362
  43.4 2.1 %collective-permute-start.12 = (f32[264,128]{1,0:T(8,128)S(1)}, f32[264,128]{1,0:T(8,128)S(1)}, u32[]{:S(2)}, u32[]{:S(2)}) collective-permute-start(f32[264,128]{1,0:T(8,128)S(1)} %add.22), channel_id=1, source_target_pairs={{0,6},{1,7},{2,4},{3,5},{4,2},{5,3},{6,0},{7,1},{8,14},{9,15},{10,... | collective-permute-start | bytes 405512 | tf_op jit(solution)/shard_map/ppermute | solution.py:362
  45.4 4.9 %collective-permute-done.12 = f32[264,128]{1,0:T(8,128)S(1)} collective-permute-done((f32[264,128]{1,0:T(8,128)S(1)}, f32[264,128]{1,0:T(8,128)S(1)}, u32[]{:S(2)}, u32[]{:S(2)}) %collective-permute-start.12) | collective-permute-done | bytes 135200 | tf_op jit(solution)/shard_map/ppermute | solution.py:362
  50.3 1.6 %collective-permute-start.15 = (f32[264,128]{1,0:T(8,128)S(1)}, f32[264,128]{1,0:T(8,128)S(1)}, u32[]{:S(2)}, u32[]{:S(2)}) collective-permute-start(f32[264,128]{1,0:T(8,128)S(1)} %add.23.refs_0_), channel_id=1, source_target_pairs={{0,17},{1,16},{2,19},{3,18},{4,21},{5,20},{6,23},{7,22},{8,25},{9,... | collective-permute-start | bytes 405512 | tf_op jit(solution)/shard_map/ppermute | solution.py:362
  51.9 1.0 %collective-permute-start.14 = (f32[264,128]{1,0:T(8,128)S(1)}, f32[264,128]{1,0:T(8,128)S(1)}, u32[]{:S(2)}, u32[]{:S(2)}) collective-permute-start(f32[264,128]{1,0:T(8,128)S(1)} %add.23.refs_0_), channel_id=1, source_target_pairs={{0,16},{1,17},{2,18},{3,19},{4,20},{5,21},{6,22},{7,23},{8,24},{9,... | collective-permute-start | bytes 405512 | tf_op jit(solution)/shard_map/ppermute | solution.py:362
  52.9 1.0 %collective-permute-start.13 = (f32[264,128]{1,0:T(8,128)S(1)}, f32[264,128]{1,0:T(8,128)S(1)}, u32[]{:S(2)}, u32[]{:S(2)}) collective-permute-start(f32[264,128]{1,0:T(8,128)S(1)} %add.23.refs_0_), channel_id=1, source_target_pairs={{0,1},{1,0},{2,3},{3,2},{4,5},{5,4},{6,7},{7,6},{8,9},{9,8},{10,11... | collective-permute-start | bytes 405512 | tf_op jit(solution)/shard_map/ppermute | solution.py:362
  53.9 2.5 %collective-permute-done.15.refs_3_ = f32[264,128]{1,0:T(8,128)S(1)} collective-permute-done((f32[264,128]{1,0:T(8,128)S(1)}, f32[264,128]{1,0:T(8,128)S(1)}, u32[]{:S(2)}, u32[]{:S(2)}) %collective-permute-start.15) | collective-permute-done | bytes 135200 | tf_op jit(solution)/shard_map/ppermute | solution.py:362
  56.4 1.4 %collective-permute-done.14.refs_2_ = f32[264,128]{1,0:T(8,128)S(1)} collective-permute-done((f32[264,128]{1,0:T(8,128)S(1)}, f32[264,128]{1,0:T(8,128)S(1)}, u32[]{:S(2)}, u32[]{:S(2)}) %collective-permute-start.14) | collective-permute-done | bytes 135200 | tf_op jit(solution)/shard_map/ppermute | solution.py:362
  57.7 0.2 collective-permute-done.13.refs_1_
  57.9 0.1 pad_maximum_fusion
  58.0 0.1 collective-permute-start.16
  58.0 0.9 %place_near.1 = (f32[8,128,256]{2,1,0:T(8,128)}, f32[4,8,128]{2,1,0:T(8,128)S(1)}) custom-call(f32[264,128]{1,0:T(8,128)S(1)} %add.23.refs_0_, f32[264,128]{1,0:T(8,128)S(1)} %collective-permute-done.13.refs_1_, f32[264,128]{1,0:T(8,128)S(1)} %collective-permute-done.14.refs_2_, f32[264,128]{1,0:T(8,128)S(1)} %collective-permute-done.15.refs_3_), custom_call_target="tpu_custom_call" | custom-call | bytes 1048576 | tf_op jit(solution)/shard_map/place_near/pallas_call | solution.py:486
  58.9 1.1 %collective-permute-done.16.far_ref = f32[4,264,128]{2,1,0:T(8,128)S(1)} collective-permute-done((f32[4,264,128]{2,1,0:T(8,128)S(1)}, f32[4,264,128]{2,1,0:T(8,128)S(1)}, u32[]{:S(2)}, u32[]{:S(2)}) %collective-permute-start.16) | collective-permute-done | bytes 540704 | tf_op jit(solution)/shard_map/ppermute | solution.py:362
  60.0 0.9 %place_far.1 = (f32[8,128,256]{2,1,0:T(8,128)}, f32[4,256]{1,0:T(4,128)}, f32[16,256]{1,0:T(8,128)}, f32[1,256]{1,0:T(1,128)}, f32[1,1]{1,0:T(1,128)}) custom-call(f32[4,264,128]{2,1,0:T(8,128)S(1)} %collective-permute-done.16.far_ref, f32[4,8,128]{2,1,0:T(8,128)S(1)} %get-tuple-element.54.near_ref, ...), custom_call_target="tpu_custom_call", output_to_operand_aliasing={{0}: (2, {})} | custom-call | tf_op jit(solution)/shard_map/place_far/pallas_call | solution.py:496
  (6 shorter events, 0.1 us)
Async XLA Ops:
  0.6 16.5 %copy-start = (bf16[4,256,256]{2,1,0:T(8,128)(2,1)S(1)}, bf16[4,256,256]{2,1,0:T(8,128)(2,1)}, u32[]{:S(2)}) copy-start(bf16[4,256,256]{2,1,0:T(8,128)(2,1)} %w_ref) | copy-start | bytes 1572868
  3.6 13.5 %copy-start.1 = (bf16[256,256]{1,0:T(8,128)(2,1)S(1)}, bf16[256,256]{1,0:T(8,128)(2,1)}, u32[]{:S(2)}) copy-start(bf16[256,256]{1,0:T(8,128)(2,1)} %feat_ref) | copy-start | bytes 393220
  3.6 6.5 %collective-permute-start.2 = (f32[1,24,256]{2,1,0:T(8,128)}, f32[1,24,256]{2,1,0:T(8,128)S(1)}, u32[]{:S(2)}, u32[]{:S(2)}) collective-permute-start(f32[1,24,256]{2,1,0:T(8,128)} %bitcast.28), channel_id=1, source_target_pairs={{0,4},{1,5},{2,6},{3,7},{4,0},{5,1},{6,2},{7,3},{8,12},{9,13},{10,... | collective-permute-start | bytes 73736 | tf_op jit(solution)/shard_map/ppermute | solution.py:362
  7.7 5.8 %collective-permute-start.1 = (f32[1,24,256]{2,1,0:T(8,128)}, f32[1,24,256]{2,1,0:T(8,128)S(1)}, u32[]{:S(2)}, u32[]{:S(2)}) collective-permute-start(f32[1,24,256]{2,1,0:T(8,128)} %bitcast.29), channel_id=1, source_target_pairs={{0,6},{1,7},{2,4},{3,5},{4,2},{5,3},{6,0},{7,1},{8,14},{9,15},{10,... | collective-permute-start | bytes 73736 | tf_op jit(solution)/shard_map/ppermute | solution.py:362
  9.0 4.5 %collective-permute-start = (f32[1,24,256]{2,1,0:T(8,128)}, f32[1,24,256]{2,1,0:T(8,128)S(1)}, u32[]{:S(2)}, u32[]{:S(2)}) collective-permute-start(f32[1,24,256]{2,1,0:T(8,128)} %bitcast.30), channel_id=1, source_target_pairs={{0,2},{1,3},{2,0},{3,1},{4,6},{5,7},{6,4},{7,5},{8,10},{9,11},{10,... | collective-permute-start | bytes 73736 | tf_op jit(solution)/shard_map/ppermute | solution.py:362
  9.3 0.8 %copy-start.3 = (f32[24,256]{1,0:T(8,128)S(1)}, f32[24,256]{1,0:T(8,128)}, u32[]{:S(2)}) copy-start(f32[24,256]{1,0:T(8,128)} %get-tuple-element.33.pay_ref) | copy-start | bytes 73732
  13.5 3.6 %copy-start.2 = (bf16[16,256]{1,0:T(8,128)(2,1)S(1)}, bf16[16,256]{1,0:T(8,128)(2,1)}, u32[]{:S(2)}) copy-start(bf16[16,256]{1,0:T(8,128)(2,1)} %wc_ref.1) | copy-start | bytes 24580
  13.5 3.6 %copy-start.5 = (f32[4,256]{1,0:T(4,128)S(1)}, f32[4,256]{1,0:T(4,128)}, u32[]{:S(2)}) copy-start(f32[4,256]{1,0:T(4,128)} %b_ref) | copy-start | bytes 12292
  13.5 3.6 %copy-start.6 = (bf16[256]{0:T(256)(128)(2,1)S(1)}, bf16[256]{0:T(256)(128)(2,1)}, u32[]{:S(2)}) copy-start(bf16[256]{0:T(256)(128)(2,1)} %wb_ref.1) | copy-start | bytes 1540
  13.6 5.3 %collective-permute-start.5 = (f32[4,24,256]{2,1,0:T(8,128)S(1)}, f32[4,24,256]{2,1,0:T(8,128)S(1)}, u32[]{:S(2)}, u32[]{:S(2)}) collective-permute-start(f32[4,24,256]{2,1,0:T(8,128)S(1)} %pad_maximum_fusion.2), channel_id=1, source_target_pairs={{0,16},{1,17},{2,18},{3,19},{4,20},{5,21},{6,22},{7,23},{8,24},{9,... | collective-permute-start | bytes 294920 | tf_op jit(solution)/shard_map/ppermute | solution.py:362
  15.2 5.5 %collective-permute-start.4 = (f32[4,24,256]{2,1,0:T(8,128)S(1)}, f32[4,24,256]{2,1,0:T(8,128)S(1)}, u32[]{:S(2)}, u32[]{:S(2)}) collective-permute-start(f32[4,24,256]{2,1,0:T(8,128)S(1)} %pad_maximum_fusion.2), channel_id=1, source_target_pairs={{0,17},{1,16},{2,19},{3,18},{4,21},{5,20},{6,23},{7,22},{8,25},{9,... | collective-permute-start | bytes 294920 | tf_op jit(solution)/shard_map/ppermute | solution.py:362
  16.6 4.6 %collective-permute-start.3 = (f32[4,24,256]{2,1,0:T(8,128)S(1)}, f32[4,24,256]{2,1,0:T(8,128)S(1)}, u32[]{:S(2)}, u32[]{:S(2)}) collective-permute-start(f32[4,24,256]{2,1,0:T(8,128)S(1)} %pad_maximum_fusion.2), channel_id=1, source_target_pairs={{0,1},{1,0},{2,3},{3,2},{4,5},{5,4},{6,7},{7,6},{8,9},{9,8},{10,11... | collective-permute-start | bytes 294920 | tf_op jit(solution)/shard_map/ppermute | solution.py:362
  21.2 1.8 %collective-permute-start.6 = (f32[16,24,256]{2,1,0:T(8,128)S(1)}, f32[16,24,256]{2,1,0:T(8,128)S(1)}, u32[]{:S(2)}, u32[]{:S(2)}) collective-permute-start(f32[16,24,256]{2,1,0:T(8,128)S(1)} %pad_maximum_fusion.1.rows_ref), channel_id=1, source_target_pairs={{0,8},{1,9},{2,10},{3,11},{4,12},{5,13},{6,14},{7,15},{8,0},{9,1},... | collective-permute-start | bytes 1179656 | tf_op jit(solution)/shard_map/ppermute | solution.py:362
  21.3 1.7 %copy-start.4 = (f32[16,256]{1,0:T(8,128)S(1)}, f32[16,256]{1,0:T(8,128)}, u32[]{:S(2)}) copy-start(f32[16,256]{1,0:T(8,128)} %get-tuple-element.38.aux_ref) | copy-start | bytes 49156
  26.0 2.0 %collective-permute-start.7 = (f32[4,264,128]{2,1,0:T(8,128)S(1)}, f32[4,264,128]{2,1,0:T(8,128)S(1)}, u32[]{:S(2)}, u32[]{:S(2)}) collective-permute-start(f32[4,264,128]{2,1,0:T(8,128)S(1)} %get-tuple-element.53), channel_id=1, source_target_pairs={{0,8},{1,9},{2,10},{3,11},{4,12},{5,13},{6,14},{7,15},{8,0},{9,1},... | collective-permute-start | bytes 1622024 | tf_op jit(solution)/shard_map/ppermute | solution.py:362
  28.1 7.4 %collective-permute-start.10 = (f32[264,128]{1,0:T(8,128)S(1)}, f32[264,128]{1,0:T(8,128)S(1)}, u32[]{:S(2)}, u32[]{:S(2)}) collective-permute-start(f32[264,128]{1,0:T(8,128)S(1)} %get-tuple-element.61), channel_id=1, source_target_pairs={{0,17},{1,16},{2,19},{3,18},{4,21},{5,20},{6,23},{7,22},{8,25},{9,... | collective-permute-start | bytes 405512 | tf_op jit(solution)/shard_map/ppermute | solution.py:362
  30.1 7.6 %collective-permute-start.9 = (f32[264,128]{1,0:T(8,128)S(1)}, f32[264,128]{1,0:T(8,128)S(1)}, u32[]{:S(2)}, u32[]{:S(2)}) collective-permute-start(f32[264,128]{1,0:T(8,128)S(1)} %get-tuple-element.62), channel_id=1, source_target_pairs={{0,16},{1,17},{2,18},{3,19},{4,20},{5,21},{6,22},{7,23},{8,24},{9,... | collective-permute-start | bytes 405512 | tf_op jit(solution)/shard_map/ppermute | solution.py:362
  30.7 7.2 %collective-permute-start.8 = (f32[264,128]{1,0:T(8,128)S(1)}, f32[264,128]{1,0:T(8,128)S(1)}, u32[]{:S(2)}, u32[]{:S(2)}) collective-permute-start(f32[264,128]{1,0:T(8,128)S(1)} %get-tuple-element.63), channel_id=1, source_target_pairs={{0,1},{1,0},{2,3},{3,2},{4,5},{5,4},{6,7},{7,6},{8,9},{9,8},{10,11... | collective-permute-start | bytes 405512 | tf_op jit(solution)/shard_map/ppermute | solution.py:362
  37.9 5.5 %collective-permute-start.11 = (f32[264,128]{1,0:T(8,128)S(1)}, f32[264,128]{1,0:T(8,128)S(1)}, u32[]{:S(2)}, u32[]{:S(2)}) collective-permute-start(f32[264,128]{1,0:T(8,128)S(1)} %fusion.1), channel_id=1, source_target_pairs={{0,2},{1,3},{2,0},{3,1},{4,6},{5,7},{6,4},{7,5},{8,10},{9,11},{10,... | collective-permute-start | bytes 405512 | tf_op jit(solution)/shard_map/ppermute | solution.py:362
  43.4 6.9 %collective-permute-start.12 = (f32[264,128]{1,0:T(8,128)S(1)}, f32[264,128]{1,0:T(8,128)S(1)}, u32[]{:S(2)}, u32[]{:S(2)}) collective-permute-start(f32[264,128]{1,0:T(8,128)S(1)} %add.22), channel_id=1, source_target_pairs={{0,6},{1,7},{2,4},{3,5},{4,2},{5,3},{6,0},{7,1},{8,14},{9,15},{10,... | collective-permute-start | bytes 405512 | tf_op jit(solution)/shard_map/ppermute | solution.py:362
  50.3 6.1 %collective-permute-start.15 = (f32[264,128]{1,0:T(8,128)S(1)}, f32[264,128]{1,0:T(8,128)S(1)}, u32[]{:S(2)}, u32[]{:S(2)}) collective-permute-start(f32[264,128]{1,0:T(8,128)S(1)} %add.23.refs_0_), channel_id=1, source_target_pairs={{0,17},{1,16},{2,19},{3,18},{4,21},{5,20},{6,23},{7,22},{8,25},{9,... | collective-permute-start | bytes 405512 | tf_op jit(solution)/shard_map/ppermute | solution.py:362
  51.9 5.8 %collective-permute-start.14 = (f32[264,128]{1,0:T(8,128)S(1)}, f32[264,128]{1,0:T(8,128)S(1)}, u32[]{:S(2)}, u32[]{:S(2)}) collective-permute-start(f32[264,128]{1,0:T(8,128)S(1)} %add.23.refs_0_), channel_id=1, source_target_pairs={{0,16},{1,17},{2,18},{3,19},{4,20},{5,21},{6,22},{7,23},{8,24},{9,... | collective-permute-start | bytes 405512 | tf_op jit(solution)/shard_map/ppermute | solution.py:362
  52.9 5.0 %collective-permute-start.13 = (f32[264,128]{1,0:T(8,128)S(1)}, f32[264,128]{1,0:T(8,128)S(1)}, u32[]{:S(2)}, u32[]{:S(2)}) collective-permute-start(f32[264,128]{1,0:T(8,128)S(1)} %add.23.refs_0_), channel_id=1, source_target_pairs={{0,1},{1,0},{2,3},{3,2},{4,5},{5,4},{6,7},{7,6},{8,9},{9,8},{10,11... | collective-permute-start | bytes 405512 | tf_op jit(solution)/shard_map/ppermute | solution.py:362
  58.0 2.0 %collective-permute-start.16 = (f32[4,264,128]{2,1,0:T(8,128)S(1)}, f32[4,264,128]{2,1,0:T(8,128)S(1)}, u32[]{:S(2)}, u32[]{:S(2)}) collective-permute-start(f32[4,264,128]{2,1,0:T(8,128)S(1)} %pad_maximum_fusion), channel_id=1, source_target_pairs={{0,8},{1,9},{2,10},{3,11},{4,12},{5,13},{6,14},{7,15},{8,0},{9,1},... | collective-permute-start | bytes 1622024 | tf_op jit(solution)/shard_map/ppermute | solution.py:362

commit v4 on v2

--- a/solution.py
+++ b/solution.py
@@ -12,7 +12,7 @@
 AXES = ("layer", "phi")
 VMEM = pl.BlockSpec(memory_space=pltpu.VMEM)
 HBM = pl.BlockSpec(memory_space=pltpu.HBM)
-UNROLL = 4
+UNROLL = 16
 EMBED_VMEM = 63400000
 HIGH = lax.Precision.HIGHEST
 PARAMS = pltpu.CompilerParams(vmem_limit_bytes=48 * 1024 * 1024)
@@ -40,11 +40,14 @@
     return lax.axis_index("layer") * axis_sizes[1] + lax.axis_index("phi")
 
 
-def block_index(axis_sizes):
+def block_places(axis_sizes):
     me = flat_index(axis_sizes)
-    core = lax.shift_right_logical(me, axis_sizes[1].bit_length() - 1) & 1
-    upper = lax.shift_right_logical(me, axis_sizes[1].bit_length()) & 1
-    return core * 4 + upper * 2 + (me & 1)
+    shift = axis_sizes[1].bit_length() - 1
+    core = lax.shift_right_logical(me, shift) & 1
+    flat = (lax.shift_right_logical(me, shift + 1) & 1) * 2 + (me & 1)
+    line = lax.shift_right_logical(me, 1) & 3
+    mine = flat + core * (line - flat)
+    return (core * 4, mine), (4 - core * 4, flat + line - mine)
 
 
 def embed_kernel(
@@ -191,8 +194,10 @@
         terms = [weight * diff for diff in diffs] + [potential * hit_q]
         return tuple(s + term[:, :128] + term[:, 128:] for s, term in zip(acc, terms))
 
-    hit_acc = lax.fori_loop(0, ref.shape[0], hit_side, hit_acc, unroll=UNROLL)
-    point_acc = lax.fori_loop(0, ref.shape[0], point_side, point_acc, unroll=UNROLL)
+    count = ref.shape[0]
+    unroll = min(count, UNROLL)
+    hit_acc = lax.fori_loop(0, count, hit_side, hit_acc, unroll=unroll)
+    point_acc = lax.fori_loop(0, count, point_side, point_acc, unroll=unroll)
     return hit_acc, point_acc
 
 
@@ -276,23 +281,21 @@
                 ]
     for b in range(blocks):
         stack[b, 2 * rows : 2 * rows + 8, :] = ext[8 * b : 8 * b + 8, :]
-    me = block_index(sizes)
-    for j in range(blocks // 2):
-        keep_ref[j] = stack[jnp.bitwise_xor(me, j)]
-        send_ref[j] = stack[jnp.bitwise_xor(me, j + blocks // 2)]
-
-
-def place_copies(sizes, blocks, first, gw_ref, sems):
+    for out_ref, (first, place) in zip((keep_ref, send_ref), block_places(sizes)):
+        for j in range(blocks // 2):
+            out_ref[j] = stack[first + jnp.bitwise_xor(place, j)]
+
+
+def place_copies(blocks, first, place, gw_ref, sems):
     rows = gw_ref.shape[1]
-    me = block_index(sizes)
     copies = []
     for r, block in enumerate(blocks):
-        place = jnp.bitwise_xor(me, first + r)
+        slot = first + jnp.bitwise_xor(place, r)
         for h in range(2):
             copies.append(
                 pltpu.make_async_copy(
                     block.at[pl.ds(h * rows, rows)],
-                    gw_ref.at[place, :, pl.ds(h * 128, 128)],
+                    gw_ref.at[slot, :, pl.ds(h * 128, 128)],
                     sems.at[2 * r + h],
                 )
             )
@@ -305,7 +308,7 @@
     blocks = refs[:4]
     gw_ref, ext_ref, sems = refs[4:]
     rows = gw_ref.shape[1]
-    copies = place_copies(sizes, blocks, 0, gw_ref, sems)
+    copies = place_copies(blocks, *block_places(sizes)[0], gw_ref, sems)
     for r, block in enumerate(blocks):
         ext_ref[r] = block[2 * rows :, :]
     for copy in copies:
@@ -322,11 +325,11 @@
     dim = gc_ref.shape[0]
     layers = gb_ref.shape[0]
     blocks = [far_ref.at[r] for r in range(half)]
-    copies = place_copies(sizes, blocks, half, gw_ref, sems)
-    me = block_index(sizes)
+    (near_first, near_place), (far_first, far_place) = block_places(sizes)
+    copies = place_copies(blocks, far_first, far_place, gw_ref, sems)
     for r in range(half):
-        ext[jnp.bitwise_xor(me, r)] = near_ref[r]
-        ext[jnp.bitwise_xor(me, half + r)] = far_ref[r, 2 * rows :, :]
+        ext[near_first + jnp.bitwise_xor(near_place, r)] = near_ref[r]
+        ext[far_first + jnp.bitwise_xor(far_place, r)] = far_ref[r, 2 * rows :, :]
     flat = jnp.concatenate([ext[b] for b in range(2 * half)], 0)
     base = 2 * layers
     for h, col in enumerate([slice(0, 128), slice(128, 256)]):
@@ -358,8 +361,14 @@
     plane = [1, 2 * phi_size]
     others = [b for b in bits_of(ndev) if b != core and b not in plane]
 
-    def swap(x, mask):
-        return lax.ppermute(x, AXES, [(i, i ^ mask) for i in range(ndev)])
+    line = others[:2]
+    others = others[2:]
+    flat_masks = [plane[0], plane[1], plane[0] ^ plane[1]]
+    line_masks = [line[0], line[1], line[0] ^ line[1]]
+
+    def swap(x, mask, other=None):
+        masks = (mask, mask if other is None else other)
+        return lax.ppermute(x, AXES, [(i, i ^ masks[i // core & 1]) for i in range(ndev)])
 
     sizes = (layer_size, phi_size)
     track = track.reshape(1, hits)
@@ -425,14 +434,13 @@
     )(pay)
     rows_all = pay[None]
     kept = pay_own[None]
-    stages = [others[i : i + 2] for i in range(0, len(others), 2)] + [plane]
-    for stage in stages:
-        masks = stage + ([stage[0] ^ stage[1]] if len(stage) > 1 else [])
-        if stage is plane:
-            rows_all, *early = lax.optimization_barrier((rows_all, features, w_layers, b_layers))
-            kept = rows_all
-        arrived = [swap(rows_all, m) for m in masks]
-        kept = rows_all = jnp.concatenate([kept] + arrived, 0)
+    for m in others:
+        kept = rows_all = jnp.concatenate([kept, swap(rows_all, m)], 0)
+    arrived = [swap(rows_all, m) for m in (line[0], line[0] ^ line[1], line[1])]
+    rows_all = jnp.concatenate([kept] + arrived, 0)
+    rows_all, *early = lax.optimization_barrier((rows_all, features, w_layers, b_layers))
+    arrived = [swap(rows_all, m) for m in (plane[0], plane[0] ^ plane[1], plane[1])]
+    rows_all = jnp.concatenate([rows_all] + arrived, 0)
     slope, ht, last, wt, head = residuals(early + [w_coord, w_beta])
     rows_all, slope = lax.optimization_barrier((rows_all, slope))
     rows_far = swap(rows_all, core)
@@ -472,13 +480,14 @@
     )(pay_own, own, xb, yb, aux, slope, ht, last, wt, head, rows_far, hit_sums, point_sums)
 
     total = keep + swap(send, core)
-    masks = [plane[0], plane[1], plane[0] ^ plane[1]]
     mine = total[0]
-    arrived = [swap(total[r + 1], m) for r, m in enumerate(masks)]
+    arrived = [swap(total[r + 1], a, b) for r, (a, b) in enumerate(zip(flat_masks, line_masks))]
     mine = (mine + arrived[0]) + (arrived[1] + arrived[2])
+    mine = mine + swap(mine, line[0], plane[0])
+    mine = mine + swap(mine, line[0] ^ line[1], plane[1])
     for m in others:
         mine = mine + swap(mine, m)
-    quarter = [mine] + [swap(mine, m) for m in masks]
+    quarter = [mine] + [swap(mine, a, b) for a, b in zip(flat_masks, line_masks)]
     far = swap(jnp.stack(quarter), core)
 
     weights = jax.ShapeDtypeStruct((blocks, layers * width // blocks, width), f32)

time: 64.3 us -> 57.6 us (0.90)
  waiting for transfers between devices: 33.4 us -> 28 us
  Pallas kernels: 9.84 us -> 8.74 us
    ppermute x17, waiting for transfers between devices: 33.4 us -> 28 us  [swap(): lax.ppermute(x, AXES, [(i, i ^ masks[i // core & 1]) for i in range(ndev)])]
    pallas_call x1, Pallas kernels: 2.93 us -> 2.2 us  [on_device(): pl.pallas_call(functools.partial(backward_kernel, sizes, hits_all, points...]
where the time goes in v4:
time: 57.6 us; the launch traced here: 57.4 us
  waiting for transfers between devices  28 us (49%)
  starting transfers between devices  18.8 us (33%)
  Pallas kernels  8.74 us (15%)
  local copies, waits for them, and re-layouts  0.83 us (1%)
  between operations  0.79 us (1%)
    ppermute x17, waiting for transfers between devices, swap(): lax.ppermute(x, AXES, [(i, i ^ masks[i // core & 1]) for i in range(ndev)])  28 us
    ppermute x17, starting transfers between devices, swap(): lax.ppermute(x, AXES, [(i, i ^ masks[i // core & 1]) for i in range(ndev)])  18.8 us
    pallas_call x1, Pallas kernels, on_device(): pl.pallas_call(functools.partial(embed_kernel, sizes), out_shape=(jax.Sha...  2.93 us
    pallas_call x1, Pallas kernels, on_device(): pl.pallas_call(functools.partial(backward_kernel, sizes, hits_all, points...  2.2 us
  transfers between devices with their start and end apart: 17, of which 15 were waited for; matrix products, arithmetic and copies ran while one was open for 0% of the time, Pallas kernels for 5%

profile of v4, /device:TPU:0, one launch (start us, length us, event | category | flops | bytes accessed | tf_op | source)
XLA Modules:
  0.0 57.4 jit_solution(1080377583919674184)
XLA Ops:
  0.6 0.0 copy-start
  0.6 2.9 %embed.1 = (f32[24,256]{1,0:T(8,128)}, f32[16,256]{1,0:T(8,128)}) custom-call(s32[8]{0:T(128)} %hit_hbm.1, bf16[256,256]{1,0:T(8,128)(2,1)} %feat_ref, bf16[4,256,256]{2,1,0:T(8,128)(2,1)} %w_ref, f32[4,256]{1,0:T(4,128)} %b_ref, bf16[16,256]{1,0:T(8,128)(2,1)} %wc_ref.1, bf16[256]{0:T(256)(128)(2,1)} %wb_ref.1, s32[1,256]{1,0:T(1,128)} %bitcast.32, ...), custom_call_target="tpu_custom_call" | custom-call | tf_op jit(solution)/shard_map/embed/pallas_call | solution.py:378
  3.6 0.0 copy-start.1
  3.6 4.1 %collective-permute-start.2 = (f32[1,24,256]{2,1,0:T(8,128)}, f32[1,24,256]{2,1,0:T(8,128)S(1)}, u32[]{:S(2)}, u32[]{:S(2)}) collective-permute-start(f32[1,24,256]{2,1,0:T(8,128)} %bitcast.28), channel_id=1, source_target_pairs={{0,4},{1,5},{2,6},{3,7},{4,0},{5,1},{6,2},{7,3},{8,12},{9,13},{10,... | collective-permute-start | bytes 73736 | tf_op jit(solution)/shard_map/ppermute | solution.py:371
  7.7 1.3 %collective-permute-start.1 = (f32[1,24,256]{2,1,0:T(8,128)}, f32[1,24,256]{2,1,0:T(8,128)S(1)}, u32[]{:S(2)}, u32[]{:S(2)}) collective-permute-start(f32[1,24,256]{2,1,0:T(8,128)} %bitcast.29), channel_id=1, source_target_pairs={{0,6},{1,7},{2,4},{3,5},{4,2},{5,3},{6,0},{7,1},{8,14},{9,15},{10,... | collective-permute-start | bytes 73736 | tf_op jit(solution)/shard_map/ppermute | solution.py:371
  9.0 0.2 collective-permute-start
  9.3 0.0 copy-start.3
  9.3 0.8 %copy-done.3 = f32[24,256]{1,0:T(8,128)S(1)} copy-done((f32[24,256]{1,0:T(8,128)S(1)}, f32[24,256]{1,0:T(8,128)}, u32[]{:S(2)}) %copy-start.3) | copy-done | bytes 24600
  10.0 0.1 spread.1
  10.1 0.0 collective-permute-done.2
  10.1 3.4 %collective-permute-done.1 = f32[1,24,256]{2,1,0:T(8,128)S(1)} collective-permute-done((f32[1,24,256]{2,1,0:T(8,128)}, f32[1,24,256]{2,1,0:T(8,128)S(1)}, u32[]{:S(2)}, u32[]{:S(2)}) %collective-permute-start.1) | collective-permute-done | bytes 24608 | tf_op jit(solution)/shard_map/ppermute | solution.py:371
  13.5 0.0 collective-permute-done
  13.5 0.0 copy-start.2
  13.5 0.0 copy-start.5
  13.5 0.0 copy-start.6
  13.6 1.6 %collective-permute-start.5 = (f32[4,24,256]{2,1,0:T(8,128)S(1)}, f32[4,24,256]{2,1,0:T(8,128)S(1)}, u32[]{:S(2)}, u32[]{:S(2)}) collective-permute-start(f32[4,24,256]{2,1,0:T(8,128)S(1)} %pad_maximum_fusion.2), channel_id=1, source_target_pairs={{0,16},{1,17},{2,18},{3,19},{4,20},{5,21},{6,22},{7,23},{8,24},{9,... | collective-permute-start | bytes 294920 | tf_op jit(solution)/shard_map/ppermute | solution.py:371
  15.2 1.4 %collective-permute-start.4 = (f32[4,24,256]{2,1,0:T(8,128)S(1)}, f32[4,24,256]{2,1,0:T(8,128)S(1)}, u32[]{:S(2)}, u32[]{:S(2)}) collective-permute-start(f32[4,24,256]{2,1,0:T(8,128)S(1)} %pad_maximum_fusion.2), channel_id=1, source_target_pairs={{0,17},{1,16},{2,19},{3,18},{4,21},{5,20},{6,23},{7,22},{8,25},{9,... | collective-permute-start | bytes 294920 | tf_op jit(solution)/shard_map/ppermute | solution.py:371
  16.6 0.5 collective-permute-start.3
  17.1 0.0 copy-done
  17.1 0.0 copy-done.1
  17.1 0.0 copy-done.2
  17.1 0.0 copy-done.5
  17.1 0.0 copy-done.6
  17.1 0.6 %residuals.1 = (f32[4,256,256]{2,1,0:T(8,128)S(1)}, bf16[4,256,256]{2,1,0:T(8,128)(2,1)S(1)}, bf16[256,256]{1,0:T(8,128)(2,1)S(1)}, bf16[3,256,256]{2,1,0:T(8,128)(2,1)S(1)}, bf16[32,256]{1,0:T(8,128)(2,1)S(1)}) custom-call(bf16[256,256]{1,0:T(8,128)(2,1)S(1)} %copy-done.1, bf16[4,256,256]{2,1,0:T(8,128)(2,1)S(1)} %copy-done, f32[4,256]{1,0:T(4,128)S(1)} %copy-done.5, ...), custom_call_target="tpu_custom_call" | custom-call | flops 5242880 | bytes 1572864 | tf_op jit(solution)/shard_map/residuals/pallas_call | solution.py:402
  17.8 1.1 %collective-permute-done.5 = f32[4,24,256]{2,1,0:T(8,128)S(1)} collective-permute-done((f32[4,24,256]{2,1,0:T(8,128)S(1)}, f32[4,24,256]{2,1,0:T(8,128)S(1)}, u32[]{:S(2)}, u32[]{:S(2)}) %collective-permute-start.5) | collective-permute-done | bytes 98336 | tf_op jit(solution)/shard_map/ppermute | solution.py:371
  18.9 1.8 %collective-permute-done.4 = f32[4,24,256]{2,1,0:T(8,128)S(1)} collective-permute-done((f32[4,24,256]{2,1,0:T(8,128)S(1)}, f32[4,24,256]{2,1,0:T(8,128)S(1)}, u32[]{:S(2)}, u32[]{:S(2)}) %collective-permute-start.4) | collective-permute-done | bytes 98336 | tf_op jit(solution)/shard_map/ppermute | solution.py:371
  20.7 0.5 collective-permute-done.3
  21.2 0.1 collective-permute-start.6
  21.3 0.0 copy-start.4
  21.3 1.1 %near_pairs.1 = (f32[17,8,256]{2,1,0:T(8,128)S(1)}, f32[17,8,128]{2,1,0:T(8,128)S(1)}) custom-call(f32[24,256]{1,0:T(8,128)S(1)} %get-tuple-element.34.pay_ref, f32[8,128]{1,0:T(8,128)S(1)} %get-tuple-element.35.own_ref, f32[16,8,256]{2,1,0:T(8,128)S(1)} %get-tuple-element.36.xb, f32[16,8,256]{2,1,0:T(8,128)S(1)} %get-tuple-element.37.yb, ...), custom_call_target="tpu_custom_call" | custom-call | flops 13107200 | bytes 524288 | tf_op jit(solution)/shard_map/near_pairs/pallas_call | solution.py:452
  22.4 0.6 collective-permute-done.6.rows_ref
  23.0 0.0 copy-done.4
  23.0 2.2 %pairs_backward.1 = (f32[4,264,128]{2,1,0:T(8,128)S(1)}, f32[4,264,128]{2,1,0:T(8,128)S(1)}) custom-call(f32[24,256]{1,0:T(8,128)S(1)} %get-tuple-element.34.pay_ref, f32[8,128]{1,0:T(8,128)S(1)} %get-tuple-element.35.own_ref, f32[16,8,256]{2,1,0:T(8,128)S(1)} %get-tuple-element.36.xb, f32[16,8,256]{2,1,0:T(8,128)S(1)} %get-tuple-element.37.yb, ...), custom_call_target="tpu_custom_call" | custom-call | tf_op jit(solution)/shard_map/pairs_backward/pallas_call | solution.py:468
  25.2 0.2 collective-permute-start.7
  25.4 1.8 %collective-permute-done.7 = f32[4,264,128]{2,1,0:T(8,128)S(1)} collective-permute-done((f32[4,264,128]{2,1,0:T(8,128)S(1)}, f32[4,264,128]{2,1,0:T(8,128)S(1)}, u32[]{:S(2)}, u32[]{:S(2)}) %collective-permute-start.7) | collective-permute-done | bytes 540704 | tf_op jit(solution)/shard_map/ppermute | solution.py:371
  27.2 0.1 add.18
  27.3 2.1 %collective-permute-start.10 = (f32[264,128]{1,0:T(8,128)S(1)}, f32[264,128]{1,0:T(8,128)S(1)}, u32[]{:S(2)}, u32[]{:S(2)}) collective-permute-start(f32[264,128]{1,0:T(8,128)S(1)} %get-tuple-element.61), channel_id=1, source_target_pairs={{0,17},{1,16},{2,19},{3,18},{4,21},{5,20},{6,23},{7,22},{8,14},{9,... | collective-permute-start | bytes 405512 | tf_op jit(solution)/shard_map/ppermute | solution.py:371
  29.4 0.5 collective-permute-start.9
  29.9 1.0 %collective-permute-start.8 = (f32[264,128]{1,0:T(8,128)S(1)}, f32[264,128]{1,0:T(8,128)S(1)}, u32[]{:S(2)}, u32[]{:S(2)}) collective-permute-start(f32[264,128]{1,0:T(8,128)S(1)} %get-tuple-element.63), channel_id=1, source_target_pairs={{0,1},{1,0},{2,3},{3,2},{4,5},{5,4},{6,7},{7,6},{8,10},{9,11},{10,... | collective-permute-start | bytes 405512 | tf_op jit(solution)/shard_map/ppermute | solution.py:371
  30.9 2.5 %collective-permute-done.10 = f32[264,128]{1,0:T(8,128)S(1)} collective-permute-done((f32[264,128]{1,0:T(8,128)S(1)}, f32[264,128]{1,0:T(8,128)S(1)}, u32[]{:S(2)}, u32[]{:S(2)}) %collective-permute-start.10) | collective-permute-done | bytes 135200 | tf_op jit(solution)/shard_map/ppermute | solution.py:371
  33.3 1.4 %collective-permute-done.9 = f32[264,128]{1,0:T(8,128)S(1)} collective-permute-done((f32[264,128]{1,0:T(8,128)S(1)}, f32[264,128]{1,0:T(8,128)S(1)}, u32[]{:S(2)}, u32[]{:S(2)}) %collective-permute-start.9) | collective-permute-done | bytes 135200 | tf_op jit(solution)/shard_map/ppermute | solution.py:371
  34.8 0.2 collective-permute-done.8
  35.0 0.1 collective-permute-start.11
  35.1 5.0 %collective-permute-done.11 = f32[264,128]{1,0:T(8,128)S(1)} collective-permute-done((f32[264,128]{1,0:T(8,128)S(1)}, f32[264,128]{1,0:T(8,128)S(1)}, u32[]{:S(2)}, u32[]{:S(2)}) %collective-permute-start.11) | collective-permute-done | bytes 135200 | tf_op jit(solution)/shard_map/ppermute | solution.py:371
  40.1 2.1 %collective-permute-start.12 = (f32[264,128]{1,0:T(8,128)S(1)}, f32[264,128]{1,0:T(8,128)S(1)}, u32[]{:S(2)}, u32[]{:S(2)}) collective-permute-start(f32[264,128]{1,0:T(8,128)S(1)} %add.22), channel_id=1, source_target_pairs={{0,6},{1,7},{2,4},{3,5},{4,2},{5,3},{6,0},{7,1},{8,24},{9,25},{10,... | collective-permute-start | bytes 405512 | tf_op jit(solution)/shard_map/ppermute | solution.py:371
  42.1 4.8 %collective-permute-done.12 = f32[264,128]{1,0:T(8,128)S(1)} collective-permute-done((f32[264,128]{1,0:T(8,128)S(1)}, f32[264,128]{1,0:T(8,128)S(1)}, u32[]{:S(2)}, u32[]{:S(2)}) %collective-permute-start.12) | collective-permute-done | bytes 135200 | tf_op jit(solution)/shard_map/ppermute | solution.py:371
  47.0 2.0 %collective-permute-start.15 = (f32[264,128]{1,0:T(8,128)S(1)}, f32[264,128]{1,0:T(8,128)S(1)}, u32[]{:S(2)}, u32[]{:S(2)}) collective-permute-start(f32[264,128]{1,0:T(8,128)S(1)} %add.23.refs_0_), channel_id=1, source_target_pairs={{0,17},{1,16},{2,19},{3,18},{4,21},{5,20},{6,23},{7,22},{8,14},{9,... | collective-permute-start | bytes 405512 | tf_op jit(solution)/shard_map/ppermute | solution.py:371
  49.0 0.5 collective-permute-start.14
  49.5 1.1 %collective-permute-start.13 = (f32[264,128]{1,0:T(8,128)S(1)}, f32[264,128]{1,0:T(8,128)S(1)}, u32[]{:S(2)}, u32[]{:S(2)}) collective-permute-start(f32[264,128]{1,0:T(8,128)S(1)} %add.23.refs_0_), channel_id=1, source_target_pairs={{0,1},{1,0},{2,3},{3,2},{4,5},{5,4},{6,7},{7,6},{8,10},{9,11},{10,... | collective-permute-start | bytes 405512 | tf_op jit(solution)/shard_map/ppermute | solution.py:371
  50.5 2.5 %collective-permute-done.15.refs_3_ = f32[264,128]{1,0:T(8,128)S(1)} collective-permute-done((f32[264,128]{1,0:T(8,128)S(1)}, f32[264,128]{1,0:T(8,128)S(1)}, u32[]{:S(2)}, u32[]{:S(2)}) %collective-permute-start.15) | collective-permute-done | bytes 135200 | tf_op jit(solution)/shard_map/ppermute | solution.py:371
  53.0 1.4 %collective-permute-done.14.refs_2_ = f32[264,128]{1,0:T(8,128)S(1)} collective-permute-done((f32[264,128]{1,0:T(8,128)S(1)}, f32[264,128]{1,0:T(8,128)S(1)}, u32[]{:S(2)}, u32[]{:S(2)}) %collective-permute-start.14) | collective-permute-done | bytes 135200 | tf_op jit(solution)/shard_map/ppermute | solution.py:371
  54.4 0.1 collective-permute-done.13.refs_1_
  54.5 0.1 pad_maximum_fusion
  54.5 0.1 collective-permute-start.16
  54.6 0.9 %place_near.1 = (f32[8,128,256]{2,1,0:T(8,128)}, f32[4,8,128]{2,1,0:T(8,128)S(1)}) custom-call(f32[264,128]{1,0:T(8,128)S(1)} %add.23.refs_0_, f32[264,128]{1,0:T(8,128)S(1)} %collective-permute-done.13.refs_1_, f32[264,128]{1,0:T(8,128)S(1)} %collective-permute-done.14.refs_2_, f32[264,128]{1,0:T(8,128)S(1)} %collective-permute-done.15.refs_3_), custom_call_target="tpu_custom_call" | custom-call | bytes 1048576 | tf_op jit(solution)/shard_map/place_near/pallas_call | solution.py:494
  55.5 1.0 %collective-permute-done.16.far_ref = f32[4,264,128]{2,1,0:T(8,128)S(1)} collective-permute-done((f32[4,264,128]{2,1,0:T(8,128)S(1)}, f32[4,264,128]{2,1,0:T(8,128)S(1)}, u32[]{:S(2)}, u32[]{:S(2)}) %collective-permute-start.16) | collective-permute-done | bytes 540704 | tf_op jit(solution)/shard_map/ppermute | solution.py:371
  56.5 0.9 %place_far.1 = (f32[8,128,256]{2,1,0:T(8,128)}, f32[4,256]{1,0:T(4,128)}, f32[16,256]{1,0:T(8,128)}, f32[1,256]{1,0:T(1,128)}, f32[1,1]{1,0:T(1,128)}) custom-call(f32[4,264,128]{2,1,0:T(8,128)S(1)} %collective-permute-done.16.far_ref, f32[4,8,128]{2,1,0:T(8,128)S(1)} %get-tuple-element.54.near_ref, ...), custom_call_target="tpu_custom_call", output_to_operand_aliasing={{0}: (2, {})} | custom-call | tf_op jit(solution)/shard_map/place_far/pallas_call | solution.py:504
  (6 shorter events, 0.1 us)
Async XLA Ops:
  0.6 16.5 %copy-start = (bf16[4,256,256]{2,1,0:T(8,128)(2,1)S(1)}, bf16[4,256,256]{2,1,0:T(8,128)(2,1)}, u32[]{:S(2)}) copy-start(bf16[4,256,256]{2,1,0:T(8,128)(2,1)} %w_ref) | copy-start | bytes 1572868
  3.6 13.5 %copy-start.1 = (bf16[256,256]{1,0:T(8,128)(2,1)S(1)}, bf16[256,256]{1,0:T(8,128)(2,1)}, u32[]{:S(2)}) copy-start(bf16[256,256]{1,0:T(8,128)(2,1)} %feat_ref) | copy-start | bytes 393220
  3.6 6.5 %collective-permute-start.2 = (f32[1,24,256]{2,1,0:T(8,128)}, f32[1,24,256]{2,1,0:T(8,128)S(1)}, u32[]{:S(2)}, u32[]{:S(2)}) collective-permute-start(f32[1,24,256]{2,1,0:T(8,128)} %bitcast.28), channel_id=1, source_target_pairs={{0,4},{1,5},{2,6},{3,7},{4,0},{5,1},{6,2},{7,3},{8,12},{9,13},{10,... | collective-permute-start | bytes 73736 | tf_op jit(solution)/shard_map/ppermute | solution.py:371
  7.7 5.8 %collective-permute-start.1 = (f32[1,24,256]{2,1,0:T(8,128)}, f32[1,24,256]{2,1,0:T(8,128)S(1)}, u32[]{:S(2)}, u32[]{:S(2)}) collective-permute-start(f32[1,24,256]{2,1,0:T(8,128)} %bitcast.29), channel_id=1, source_target_pairs={{0,6},{1,7},{2,4},{3,5},{4,2},{5,3},{6,0},{7,1},{8,14},{9,15},{10,... | collective-permute-start | bytes 73736 | tf_op jit(solution)/shard_map/ppermute | solution.py:371
  9.0 4.5 %collective-permute-start = (f32[1,24,256]{2,1,0:T(8,128)}, f32[1,24,256]{2,1,0:T(8,128)S(1)}, u32[]{:S(2)}, u32[]{:S(2)}) collective-permute-start(f32[1,24,256]{2,1,0:T(8,128)} %bitcast.30), channel_id=1, source_target_pairs={{0,2},{1,3},{2,0},{3,1},{4,6},{5,7},{6,4},{7,5},{8,10},{9,11},{10,... | collective-permute-start | bytes 73736 | tf_op jit(solution)/shard_map/ppermute | solution.py:371
  9.3 0.8 %copy-start.3 = (f32[24,256]{1,0:T(8,128)S(1)}, f32[24,256]{1,0:T(8,128)}, u32[]{:S(2)}) copy-start(f32[24,256]{1,0:T(8,128)} %get-tuple-element.33.pay_ref) | copy-start | bytes 73732
  13.5 3.6 %copy-start.2 = (bf16[16,256]{1,0:T(8,128)(2,1)S(1)}, bf16[16,256]{1,0:T(8,128)(2,1)}, u32[]{:S(2)}) copy-start(bf16[16,256]{1,0:T(8,128)(2,1)} %wc_ref.1) | copy-start | bytes 24580
  13.5 3.6 %copy-start.5 = (f32[4,256]{1,0:T(4,128)S(1)}, f32[4,256]{1,0:T(4,128)}, u32[]{:S(2)}) copy-start(f32[4,256]{1,0:T(4,128)} %b_ref) | copy-start | bytes 12292
  13.5 3.6 %copy-start.6 = (bf16[256]{0:T(256)(128)(2,1)S(1)}, bf16[256]{0:T(256)(128)(2,1)}, u32[]{:S(2)}) copy-start(bf16[256]{0:T(256)(128)(2,1)} %wb_ref.1) | copy-start | bytes 1540
  13.6 5.3 %collective-permute-start.5 = (f32[4,24,256]{2,1,0:T(8,128)S(1)}, f32[4,24,256]{2,1,0:T(8,128)S(1)}, u32[]{:S(2)}, u32[]{:S(2)}) collective-permute-start(f32[4,24,256]{2,1,0:T(8,128)S(1)} %pad_maximum_fusion.2), channel_id=1, source_target_pairs={{0,16},{1,17},{2,18},{3,19},{4,20},{5,21},{6,22},{7,23},{8,24},{9,... | collective-permute-start | bytes 294920 | tf_op jit(solution)/shard_map/ppermute | solution.py:371
  15.2 5.5 %collective-permute-start.4 = (f32[4,24,256]{2,1,0:T(8,128)S(1)}, f32[4,24,256]{2,1,0:T(8,128)S(1)}, u32[]{:S(2)}, u32[]{:S(2)}) collective-permute-start(f32[4,24,256]{2,1,0:T(8,128)S(1)} %pad_maximum_fusion.2), channel_id=1, source_target_pairs={{0,17},{1,16},{2,19},{3,18},{4,21},{5,20},{6,23},{7,22},{8,25},{9,... | collective-permute-start | bytes 294920 | tf_op jit(solution)/shard_map/ppermute | solution.py:371
  16.6 4.6 %collective-permute-start.3 = (f32[4,24,256]{2,1,0:T(8,128)S(1)}, f32[4,24,256]{2,1,0:T(8,128)S(1)}, u32[]{:S(2)}, u32[]{:S(2)}) collective-permute-start(f32[4,24,256]{2,1,0:T(8,128)S(1)} %pad_maximum_fusion.2), channel_id=1, source_target_pairs={{0,1},{1,0},{2,3},{3,2},{4,5},{5,4},{6,7},{7,6},{8,9},{9,8},{10,11... | collective-permute-start | bytes 294920 | tf_op jit(solution)/shard_map/ppermute | solution.py:371
  21.2 1.8 %collective-permute-start.6 = (f32[16,24,256]{2,1,0:T(8,128)S(1)}, f32[16,24,256]{2,1,0:T(8,128)S(1)}, u32[]{:S(2)}, u32[]{:S(2)}) collective-permute-start(f32[16,24,256]{2,1,0:T(8,128)S(1)} %pad_maximum_fusion.1.rows_ref), channel_id=1, source_target_pairs={{0,8},{1,9},{2,10},{3,11},{4,12},{5,13},{6,14},{7,15},{8,0},{9,1},... | collective-permute-start | bytes 1179656 | tf_op jit(solution)/shard_map/ppermute | solution.py:371
  21.3 1.7 %copy-start.4 = (f32[16,256]{1,0:T(8,128)S(1)}, f32[16,256]{1,0:T(8,128)}, u32[]{:S(2)}) copy-start(f32[16,256]{1,0:T(8,128)} %get-tuple-element.38.aux_ref) | copy-start | bytes 49156
  25.2 2.0 %collective-permute-start.7 = (f32[4,264,128]{2,1,0:T(8,128)S(1)}, f32[4,264,128]{2,1,0:T(8,128)S(1)}, u32[]{:S(2)}, u32[]{:S(2)}) collective-permute-start(f32[4,264,128]{2,1,0:T(8,128)S(1)} %get-tuple-element.53), channel_id=1, source_target_pairs={{0,8},{1,9},{2,10},{3,11},{4,12},{5,13},{6,14},{7,15},{8,0},{9,1},... | collective-permute-start | bytes 1622024 | tf_op jit(solution)/shard_map/ppermute | solution.py:371
  27.3 6.0 %collective-permute-start.10 = (f32[264,128]{1,0:T(8,128)S(1)}, f32[264,128]{1,0:T(8,128)S(1)}, u32[]{:S(2)}, u32[]{:S(2)}) collective-permute-start(f32[264,128]{1,0:T(8,128)S(1)} %get-tuple-element.61), channel_id=1, source_target_pairs={{0,17},{1,16},{2,19},{3,18},{4,21},{5,20},{6,23},{7,22},{8,14},{9,... | collective-permute-start | bytes 405512 | tf_op jit(solution)/shard_map/ppermute | solution.py:371
  29.4 5.3 %collective-permute-start.9 = (f32[264,128]{1,0:T(8,128)S(1)}, f32[264,128]{1,0:T(8,128)S(1)}, u32[]{:S(2)}, u32[]{:S(2)}) collective-permute-start(f32[264,128]{1,0:T(8,128)S(1)} %get-tuple-element.62), channel_id=1, source_target_pairs={{0,16},{1,17},{2,18},{3,19},{4,20},{5,21},{6,22},{7,23},{8,12},{9,... | collective-permute-start | bytes 405512 | tf_op jit(solution)/shard_map/ppermute | solution.py:371
  29.9 5.0 %collective-permute-start.8 = (f32[264,128]{1,0:T(8,128)S(1)}, f32[264,128]{1,0:T(8,128)S(1)}, u32[]{:S(2)}, u32[]{:S(2)}) collective-permute-start(f32[264,128]{1,0:T(8,128)S(1)} %get-tuple-element.63), channel_id=1, source_target_pairs={{0,1},{1,0},{2,3},{3,2},{4,5},{5,4},{6,7},{7,6},{8,10},{9,11},{10,... | collective-permute-start | bytes 405512 | tf_op jit(solution)/shard_map/ppermute | solution.py:371
  35.0 5.1 %collective-permute-start.11 = (f32[264,128]{1,0:T(8,128)S(1)}, f32[264,128]{1,0:T(8,128)S(1)}, u32[]{:S(2)}, u32[]{:S(2)}) collective-permute-start(f32[264,128]{1,0:T(8,128)S(1)} %fusion.1), channel_id=1, source_target_pairs={{0,2},{1,3},{2,0},{3,1},{4,6},{5,7},{6,4},{7,5},{8,9},{9,8},{10,11... | collective-permute-start | bytes 405512 | tf_op jit(solution)/shard_map/ppermute | solution.py:371
  40.1 6.9 %collective-permute-start.12 = (f32[264,128]{1,0:T(8,128)S(1)}, f32[264,128]{1,0:T(8,128)S(1)}, u32[]{:S(2)}, u32[]{:S(2)}) collective-permute-start(f32[264,128]{1,0:T(8,128)S(1)} %add.22), channel_id=1, source_target_pairs={{0,6},{1,7},{2,4},{3,5},{4,2},{5,3},{6,0},{7,1},{8,24},{9,25},{10,... | collective-permute-start | bytes 405512 | tf_op jit(solution)/shard_map/ppermute | solution.py:371
  47.0 6.0 %collective-permute-start.15 = (f32[264,128]{1,0:T(8,128)S(1)}, f32[264,128]{1,0:T(8,128)S(1)}, u32[]{:S(2)}, u32[]{:S(2)}) collective-permute-start(f32[264,128]{1,0:T(8,128)S(1)} %add.23.refs_0_), channel_id=1, source_target_pairs={{0,17},{1,16},{2,19},{3,18},{4,21},{5,20},{6,23},{7,22},{8,14},{9,... | collective-permute-start | bytes 405512 | tf_op jit(solution)/shard_map/ppermute | solution.py:371
  49.0 5.4 %collective-permute-start.14 = (f32[264,128]{1,0:T(8,128)S(1)}, f32[264,128]{1,0:T(8,128)S(1)}, u32[]{:S(2)}, u32[]{:S(2)}) collective-permute-start(f32[264,128]{1,0:T(8,128)S(1)} %add.23.refs_0_), channel_id=1, source_target_pairs={{0,16},{1,17},{2,18},{3,19},{4,20},{5,21},{6,22},{7,23},{8,12},{9,... | collective-permute-start | bytes 405512 | tf_op jit(solution)/shard_map/ppermute | solution.py:371
  49.5 5.0 %collective-permute-start.13 = (f32[264,128]{1,0:T(8,128)S(1)}, f32[264,128]{1,0:T(8,128)S(1)}, u32[]{:S(2)}, u32[]{:S(2)}) collective-permute-start(f32[264,128]{1,0:T(8,128)S(1)} %add.23.refs_0_), channel_id=1, source_target_pairs={{0,1},{1,0},{2,3},{3,2},{4,5},{5,4},{6,7},{7,6},{8,10},{9,11},{10,... | collective-permute-start | bytes 405512 | tf_op jit(solution)/shard_map/ppermute | solution.py:371
  54.5 2.0 %collective-permute-start.16 = (f32[4,264,128]{2,1,0:T(8,128)S(1)}, f32[4,264,128]{2,1,0:T(8,128)S(1)}, u32[]{:S(2)}, u32[]{:S(2)}) collective-permute-start(f32[4,264,128]{2,1,0:T(8,128)S(1)} %pad_maximum_fusion), channel_id=1, source_target_pairs={{0,8},{1,9},{2,10},{3,11},{4,12},{5,13},{6,14},{7,15},{8,0},{9,1},... | collective-permute-start | bytes 1622024 | tf_op jit(solution)/shard_map/ppermute | solution.py:371

commit v5 on v4

--- a/solution.py
+++ b/solution.py
@@ -483,8 +483,8 @@
     mine = total[0]
     arrived = [swap(total[r + 1], a, b) for r, (a, b) in enumerate(zip(flat_masks, line_masks))]
     mine = (mine + arrived[0]) + (arrived[1] + arrived[2])
-    mine = mine + swap(mine, line[0], plane[0])
-    mine = mine + swap(mine, line[0] ^ line[1], plane[1])
+    arrived = [swap(mine, line_masks[r], flat_masks[r]) for r in (1, 0, 2)]
+    mine = (mine + arrived[0]) + (arrived[1] + arrived[2])
     for m in others:
         mine = mine + swap(mine, m)
     quarter = [mine] + [swap(mine, a, b) for a, b in zip(flat_masks, line_masks)]

time: 57.6 us -> 55.4 us (0.962)
  waiting for transfers between devices: 28 us -> 23.5 us
  starting transfers between devices: 18.8 us -> 21.1 us
    ppermute x17 -> x18, waiting for transfers between devices: 28 us -> 23.5 us  [swap(): lax.ppermute(x, AXES, [(i, i ^ masks[i // core & 1]) for i in range(ndev)])]
    ppermute x17 -> x18, starting transfers between devices: 18.8 us -> 21.1 us  [swap(): lax.ppermute(x, AXES, [(i, i ^ masks[i // core & 1]) for i in range(ndev)])]
  transfers between devices with their start and end apart: 17 -> 18, of which waited for: 15 -> 15; matrix products, arithmetic and copies ran while one was open for 0% -> 0% of each run, Pallas kernels for 5% -> 5%
where the time goes in v5:
time: 55.4 us; the launch traced here: 55.2 us
  waiting for transfers between devices  23.5 us (42%)
  starting transfers between devices  21.1 us (38%)
  Pallas kernels  8.74 us (16%)
  local copies, waits for them, and re-layouts  0.83 us (1%)
  between operations  0.79 us (1%)
    ppermute x18, waiting for transfers between devices, swap(): lax.ppermute(x, AXES, [(i, i ^ masks[i // core & 1]) for i in range(ndev)])  23.5 us
    ppermute x18, starting transfers between devices, swap(): lax.ppermute(x, AXES, [(i, i ^ masks[i // core & 1]) for i in range(ndev)])  21.1 us
    pallas_call x1, Pallas kernels, on_device(): pl.pallas_call(functools.partial(embed_kernel, sizes), out_shape=(jax.Sha...  2.93 us
    pallas_call x1, Pallas kernels, on_device(): pl.pallas_call(functools.partial(backward_kernel, sizes, hits_all, points...  2.2 us
    pallas_call x1, Pallas kernels, on_device(): pl.pallas_call(near_kernel, out_shape=partial_sums, in_specs=[VMEM] * 5,...  1.12 us
  transfers between devices with their start and end apart: 18, of which 15 were waited for; matrix products, arithmetic and copies ran while one was open for 0% of the time, Pallas kernels for 5%

profile of v5, /device:TPU:0, one launch (start us, length us, event | category | flops | bytes accessed | tf_op | source)
XLA Modules:
  0.0 55.2 jit_solution(7743588240115398190)
XLA Ops:
  0.6 0.0 copy-start
  0.6 2.9 %embed.1 = (f32[24,256]{1,0:T(8,128)}, f32[16,256]{1,0:T(8,128)}) custom-call(s32[8]{0:T(128)} %hit_hbm.1, bf16[256,256]{1,0:T(8,128)(2,1)} %feat_ref, bf16[4,256,256]{2,1,0:T(8,128)(2,1)} %w_ref, f32[4,256]{1,0:T(4,128)} %b_ref, bf16[16,256]{1,0:T(8,128)(2,1)} %wc_ref.1, bf16[256]{0:T(256)(128)(2,1)} %wb_ref.1, s32[1,256]{1,0:T(1,128)} %bitcast.32, ...), custom_call_target="tpu_custom_call" | custom-call | tf_op jit(solution)/shard_map/embed/pallas_call | solution.py:378
  3.6 0.0 copy-start.1
  3.6 4.1 %collective-permute-start.2 = (f32[1,24,256]{2,1,0:T(8,128)}, f32[1,24,256]{2,1,0:T(8,128)S(1)}, u32[]{:S(2)}, u32[]{:S(2)}) collective-permute-start(f32[1,24,256]{2,1,0:T(8,128)} %bitcast.28), channel_id=1, source_target_pairs={{0,4},{1,5},{2,6},{3,7},{4,0},{5,1},{6,2},{7,3},{8,12},{9,13},{10,... | collective-permute-start | bytes 73736 | tf_op jit(solution)/shard_map/ppermute | solution.py:371
  7.7 1.3 %collective-permute-start.1 = (f32[1,24,256]{2,1,0:T(8,128)}, f32[1,24,256]{2,1,0:T(8,128)S(1)}, u32[]{:S(2)}, u32[]{:S(2)}) collective-permute-start(f32[1,24,256]{2,1,0:T(8,128)} %bitcast.29), channel_id=1, source_target_pairs={{0,6},{1,7},{2,4},{3,5},{4,2},{5,3},{6,0},{7,1},{8,14},{9,15},{10,... | collective-permute-start | bytes 73736 | tf_op jit(solution)/shard_map/ppermute | solution.py:371
  9.0 0.2 collective-permute-start
  9.3 0.0 copy-start.3
  9.3 0.8 %copy-done.3 = f32[24,256]{1,0:T(8,128)S(1)} copy-done((f32[24,256]{1,0:T(8,128)S(1)}, f32[24,256]{1,0:T(8,128)}, u32[]{:S(2)}) %copy-start.3) | copy-done | bytes 24600
  10.0 0.1 spread.1
  10.1 0.0 collective-permute-done.2
  10.1 3.4 %collective-permute-done.1 = f32[1,24,256]{2,1,0:T(8,128)S(1)} collective-permute-done((f32[1,24,256]{2,1,0:T(8,128)}, f32[1,24,256]{2,1,0:T(8,128)S(1)}, u32[]{:S(2)}, u32[]{:S(2)}) %collective-permute-start.1) | collective-permute-done | bytes 24608 | tf_op jit(solution)/shard_map/ppermute | solution.py:371
  13.5 0.0 collective-permute-done
  13.5 0.0 copy-start.2
  13.5 0.0 copy-start.5
  13.5 0.0 copy-start.6
  13.6 1.6 %collective-permute-start.5 = (f32[4,24,256]{2,1,0:T(8,128)S(1)}, f32[4,24,256]{2,1,0:T(8,128)S(1)}, u32[]{:S(2)}, u32[]{:S(2)}) collective-permute-start(f32[4,24,256]{2,1,0:T(8,128)S(1)} %pad_maximum_fusion.2), channel_id=1, source_target_pairs={{0,16},{1,17},{2,18},{3,19},{4,20},{5,21},{6,22},{7,23},{8,24},{9,... | collective-permute-start | bytes 294920 | tf_op jit(solution)/shard_map/ppermute | solution.py:371
  15.2 1.4 %collective-permute-start.4 = (f32[4,24,256]{2,1,0:T(8,128)S(1)}, f32[4,24,256]{2,1,0:T(8,128)S(1)}, u32[]{:S(2)}, u32[]{:S(2)}) collective-permute-start(f32[4,24,256]{2,1,0:T(8,128)S(1)} %pad_maximum_fusion.2), channel_id=1, source_target_pairs={{0,17},{1,16},{2,19},{3,18},{4,21},{5,20},{6,23},{7,22},{8,25},{9,... | collective-permute-start | bytes 294920 | tf_op jit(solution)/shard_map/ppermute | solution.py:371
  16.6 0.5 collective-permute-start.3
  17.1 0.0 copy-done
  17.1 0.0 copy-done.1
  17.1 0.0 copy-done.2
  17.1 0.0 copy-done.5
  17.1 0.0 copy-done.6
  17.1 0.6 %residuals.1 = (f32[4,256,256]{2,1,0:T(8,128)S(1)}, bf16[4,256,256]{2,1,0:T(8,128)(2,1)S(1)}, bf16[256,256]{1,0:T(8,128)(2,1)S(1)}, bf16[3,256,256]{2,1,0:T(8,128)(2,1)S(1)}, bf16[32,256]{1,0:T(8,128)(2,1)S(1)}) custom-call(bf16[256,256]{1,0:T(8,128)(2,1)S(1)} %copy-done.1, bf16[4,256,256]{2,1,0:T(8,128)(2,1)S(1)} %copy-done, f32[4,256]{1,0:T(4,128)S(1)} %copy-done.5, ...), custom_call_target="tpu_custom_call" | custom-call | flops 5242880 | bytes 1572864 | tf_op jit(solution)/shard_map/residuals/pallas_call | solution.py:402
  17.8 1.1 %collective-permute-done.5 = f32[4,24,256]{2,1,0:T(8,128)S(1)} collective-permute-done((f32[4,24,256]{2,1,0:T(8,128)S(1)}, f32[4,24,256]{2,1,0:T(8,128)S(1)}, u32[]{:S(2)}, u32[]{:S(2)}) %collective-permute-start.5) | collective-permute-done | bytes 98336 | tf_op jit(solution)/shard_map/ppermute | solution.py:371
  18.9 1.8 %collective-permute-done.4 = f32[4,24,256]{2,1,0:T(8,128)S(1)} collective-permute-done((f32[4,24,256]{2,1,0:T(8,128)S(1)}, f32[4,24,256]{2,1,0:T(8,128)S(1)}, u32[]{:S(2)}, u32[]{:S(2)}) %collective-permute-start.4) | collective-permute-done | bytes 98336 | tf_op jit(solution)/shard_map/ppermute | solution.py:371
  20.7 0.5 collective-permute-done.3
  21.2 0.1 collective-permute-start.6
  21.3 0.0 copy-start.4
  21.3 1.1 %near_pairs.1 = (f32[17,8,256]{2,1,0:T(8,128)S(1)}, f32[17,8,128]{2,1,0:T(8,128)S(1)}) custom-call(f32[24,256]{1,0:T(8,128)S(1)} %get-tuple-element.34.pay_ref, f32[8,128]{1,0:T(8,128)S(1)} %get-tuple-element.35.own_ref, f32[16,8,256]{2,1,0:T(8,128)S(1)} %get-tuple-element.36.xb, f32[16,8,256]{2,1,0:T(8,128)S(1)} %get-tuple-element.37.yb, ...), custom_call_target="tpu_custom_call" | custom-call | flops 13107200 | bytes 524288 | tf_op jit(solution)/shard_map/near_pairs/pallas_call | solution.py:452
  22.4 0.6 %collective-permute-done.6.rows_ref = f32[16,24,256]{2,1,0:T(8,128)S(1)} collective-permute-done((f32[16,24,256]{2,1,0:T(8,128)S(1)}, f32[16,24,256]{2,1,0:T(8,128)S(1)}, u32[]{:S(2)}, u32[]{:S(2)}) %collective-permute-start.6) | collective-permute-done | bytes 393248 | tf_op jit(solution)/shard_map/ppermute | solution.py:371
  23.0 0.0 copy-done.4
  23.0 2.2 %pairs_backward.1 = (f32[4,264,128]{2,1,0:T(8,128)S(1)}, f32[4,264,128]{2,1,0:T(8,128)S(1)}) custom-call(f32[24,256]{1,0:T(8,128)S(1)} %get-tuple-element.34.pay_ref, f32[8,128]{1,0:T(8,128)S(1)} %get-tuple-element.35.own_ref, f32[16,8,256]{2,1,0:T(8,128)S(1)} %get-tuple-element.36.xb, f32[16,8,256]{2,1,0:T(8,128)S(1)} %get-tuple-element.37.yb, ...), custom_call_target="tpu_custom_call" | custom-call | tf_op jit(solution)/shard_map/pairs_backward/pallas_call | solution.py:468
  25.2 0.2 collective-permute-start.7
  25.4 1.8 %collective-permute-done.7 = f32[4,264,128]{2,1,0:T(8,128)S(1)} collective-permute-done((f32[4,264,128]{2,1,0:T(8,128)S(1)}, f32[4,264,128]{2,1,0:T(8,128)S(1)}, u32[]{:S(2)}, u32[]{:S(2)}) %collective-permute-start.7) | collective-permute-done | bytes 540704 | tf_op jit(solution)/shard_map/ppermute | solution.py:371
  27.2 0.1 add.21
  27.3 2.1 %collective-permute-start.10 = (f32[264,128]{1,0:T(8,128)S(1)}, f32[264,128]{1,0:T(8,128)S(1)}, u32[]{:S(2)}, u32[]{:S(2)}) collective-permute-start(f32[264,128]{1,0:T(8,128)S(1)} %get-tuple-element.61), channel_id=1, source_target_pairs={{0,17},{1,16},{2,19},{3,18},{4,21},{5,20},{6,23},{7,22},{8,14},{9,... | collective-permute-start | bytes 405512 | tf_op jit(solution)/shard_map/ppermute | solution.py:371
  29.4 0.5 collective-permute-start.9
  29.9 1.0 %collective-permute-start.8 = (f32[264,128]{1,0:T(8,128)S(1)}, f32[264,128]{1,0:T(8,128)S(1)}, u32[]{:S(2)}, u32[]{:S(2)}) collective-permute-start(f32[264,128]{1,0:T(8,128)S(1)} %get-tuple-element.63), channel_id=1, source_target_pairs={{0,1},{1,0},{2,3},{3,2},{4,5},{5,4},{6,7},{7,6},{8,10},{9,11},{10,... | collective-permute-start | bytes 405512 | tf_op jit(solution)/shard_map/ppermute | solution.py:371
  30.9 2.5 %collective-permute-done.10 = f32[264,128]{1,0:T(8,128)S(1)} collective-permute-done((f32[264,128]{1,0:T(8,128)S(1)}, f32[264,128]{1,0:T(8,128)S(1)}, u32[]{:S(2)}, u32[]{:S(2)}) %collective-permute-start.10) | collective-permute-done | bytes 135200 | tf_op jit(solution)/shard_map/ppermute | solution.py:371
  33.3 1.4 %collective-permute-done.9 = f32[264,128]{1,0:T(8,128)S(1)} collective-permute-done((f32[264,128]{1,0:T(8,128)S(1)}, f32[264,128]{1,0:T(8,128)S(1)}, u32[]{:S(2)}, u32[]{:S(2)}) %collective-permute-start.9) | collective-permute-done | bytes 135200 | tf_op jit(solution)/shard_map/ppermute | solution.py:371
  34.8 0.2 collective-permute-done.8
  35.0 2.1 %collective-permute-start.13 = (f32[264,128]{1,0:T(8,128)S(1)}, f32[264,128]{1,0:T(8,128)S(1)}, u32[]{:S(2)}, u32[]{:S(2)}) collective-permute-start(f32[264,128]{1,0:T(8,128)S(1)} %fusion.1), channel_id=1, source_target_pairs={{0,6},{1,7},{2,4},{3,5},{4,2},{5,3},{6,0},{7,1},{8,25},{9,24},{10,... | collective-permute-start | bytes 405512 | tf_op jit(solution)/shard_map/ppermute | solution.py:371
  37.0 0.0 collective-permute-start.12
  37.0 2.4 %collective-permute-start.11 = (f32[264,128]{1,0:T(8,128)S(1)}, f32[264,128]{1,0:T(8,128)S(1)}, u32[]{:S(2)}, u32[]{:S(2)}) collective-permute-start(f32[264,128]{1,0:T(8,128)S(1)} %fusion.1), channel_id=1, source_target_pairs={{0,4},{1,5},{2,6},{3,7},{4,0},{5,1},{6,2},{7,3},{8,24},{9,25},{10,... | collective-permute-start | bytes 405512 | tf_op jit(solution)/shard_map/ppermute | solution.py:371
  39.4 2.6 %collective-permute-done.13 = f32[264,128]{1,0:T(8,128)S(1)} collective-permute-done((f32[264,128]{1,0:T(8,128)S(1)}, f32[264,128]{1,0:T(8,128)S(1)}, u32[]{:S(2)}, u32[]{:S(2)}) %collective-permute-start.13) | collective-permute-done | bytes 135200 | tf_op jit(solution)/shard_map/ppermute | solution.py:371
  42.0 2.8 %collective-permute-done.12 = f32[264,128]{1,0:T(8,128)S(1)} collective-permute-done((f32[264,128]{1,0:T(8,128)S(1)}, f32[264,128]{1,0:T(8,128)S(1)}, u32[]{:S(2)}, u32[]{:S(2)}) %collective-permute-start.12) | collective-permute-done | bytes 135200 | tf_op jit(solution)/shard_map/ppermute | solution.py:371
  44.7 0.0 collective-permute-done.11
  44.8 2.0 %collective-permute-start.16 = (f32[264,128]{1,0:T(8,128)S(1)}, f32[264,128]{1,0:T(8,128)S(1)}, u32[]{:S(2)}, u32[]{:S(2)}) collective-permute-start(f32[264,128]{1,0:T(8,128)S(1)} %add_add_fusion.refs_0_), channel_id=1, source_target_pairs={{0,17},{1,16},{2,19},{3,18},{4,21},{5,20},{6,23},{7,22},{8,14},{9,... | collective-permute-start | bytes 405512 | tf_op jit(solution)/shard_map/ppermute | solution.py:371
  46.8 0.5 collective-permute-start.15
  47.3 1.1 %collective-permute-start.14 = (f32[264,128]{1,0:T(8,128)S(1)}, f32[264,128]{1,0:T(8,128)S(1)}, u32[]{:S(2)}, u32[]{:S(2)}) collective-permute-start(f32[264,128]{1,0:T(8,128)S(1)} %add_add_fusion.refs_0_), channel_id=1, source_target_pairs={{0,1},{1,0},{2,3},{3,2},{4,5},{5,4},{6,7},{7,6},{8,10},{9,11},{10,... | collective-permute-start | bytes 405512 | tf_op jit(solution)/shard_map/ppermute | solution.py:371
  48.3 2.5 %collective-permute-done.16.refs_3_ = f32[264,128]{1,0:T(8,128)S(1)} collective-permute-done((f32[264,128]{1,0:T(8,128)S(1)}, f32[264,128]{1,0:T(8,128)S(1)}, u32[]{:S(2)}, u32[]{:S(2)}) %collective-permute-start.16) | collective-permute-done | bytes 135200 | tf_op jit(solution)/shard_map/ppermute | solution.py:371
  50.8 1.4 %collective-permute-done.15.refs_2_ = f32[264,128]{1,0:T(8,128)S(1)} collective-permute-done((f32[264,128]{1,0:T(8,128)S(1)}, f32[264,128]{1,0:T(8,128)S(1)}, u32[]{:S(2)}, u32[]{:S(2)}) %collective-permute-start.15) | collective-permute-done | bytes 135200 | tf_op jit(solution)/shard_map/ppermute | solution.py:371
  52.2 0.1 collective-permute-done.14.refs_1_
  52.3 0.1 pad_maximum_fusion
  52.3 0.1 collective-permute-start.17
  52.4 0.9 %place_near.1 = (f32[8,128,256]{2,1,0:T(8,128)}, f32[4,8,128]{2,1,0:T(8,128)S(1)}) custom-call(f32[264,128]{1,0:T(8,128)S(1)} %add_add_fusion.refs_0_, f32[264,128]{1,0:T(8,128)S(1)} %collective-permute-done.14.refs_1_, f32[264,128]{1,0:T(8,128)S(1)} %collective-permute-done.15.refs_2_, f32[264,128]{1,0:T(8,128)S(1)} %collective-permute-done.16.refs_3_), custom_call_target="tpu_custom_call" | custom-call | bytes 1048576 | tf_op jit(solution)/shard_map/place_near/pallas_call | solution.py:494
  53.3 1.0 %collective-permute-done.17.far_ref = f32[4,264,128]{2,1,0:T(8,128)S(1)} collective-permute-done((f32[4,264,128]{2,1,0:T(8,128)S(1)}, f32[4,264,128]{2,1,0:T(8,128)S(1)}, u32[]{:S(2)}, u32[]{:S(2)}) %collective-permute-start.17) | collective-permute-done | bytes 540704 | tf_op jit(solution)/shard_map/ppermute | solution.py:371
  54.3 0.9 %place_far.1 = (f32[8,128,256]{2,1,0:T(8,128)}, f32[4,256]{1,0:T(4,128)}, f32[16,256]{1,0:T(8,128)}, f32[1,256]{1,0:T(1,128)}, f32[1,1]{1,0:T(1,128)}) custom-call(f32[4,264,128]{2,1,0:T(8,128)S(1)} %collective-permute-done.17.far_ref, f32[4,8,128]{2,1,0:T(8,128)S(1)} %get-tuple-element.54.near_ref, ...), custom_call_target="tpu_custom_call", output_to_operand_aliasing={{0}: (2, {})} | custom-call | tf_op jit(solution)/shard_map/place_far/pallas_call | solution.py:504
  (5 shorter events, 0.1 us)
Async XLA Ops:
  0.6 16.5 %copy-start = (bf16[4,256,256]{2,1,0:T(8,128)(2,1)S(1)}, bf16[4,256,256]{2,1,0:T(8,128)(2,1)}, u32[]{:S(2)}) copy-start(bf16[4,256,256]{2,1,0:T(8,128)(2,1)} %w_ref) | copy-start | bytes 1572868
  3.6 13.5 %copy-start.1 = (bf16[256,256]{1,0:T(8,128)(2,1)S(1)}, bf16[256,256]{1,0:T(8,128)(2,1)}, u32[]{:S(2)}) copy-start(bf16[256,256]{1,0:T(8,128)(2,1)} %feat_ref) | copy-start | bytes 393220
  3.6 6.5 %collective-permute-start.2 = (f32[1,24,256]{2,1,0:T(8,128)}, f32[1,24,256]{2,1,0:T(8,128)S(1)}, u32[]{:S(2)}, u32[]{:S(2)}) collective-permute-start(f32[1,24,256]{2,1,0:T(8,128)} %bitcast.28), channel_id=1, source_target_pairs={{0,4},{1,5},{2,6},{3,7},{4,0},{5,1},{6,2},{7,3},{8,12},{9,13},{10,... | collective-permute-start | bytes 73736 | tf_op jit(solution)/shard_map/ppermute | solution.py:371
  7.7 5.8 %collective-permute-start.1 = (f32[1,24,256]{2,1,0:T(8,128)}, f32[1,24,256]{2,1,0:T(8,128)S(1)}, u32[]{:S(2)}, u32[]{:S(2)}) collective-permute-start(f32[1,24,256]{2,1,0:T(8,128)} %bitcast.29), channel_id=1, source_target_pairs={{0,6},{1,7},{2,4},{3,5},{4,2},{5,3},{6,0},{7,1},{8,14},{9,15},{10,... | collective-permute-start | bytes 73736 | tf_op jit(solution)/shard_map/ppermute | solution.py:371
  9.0 4.5 %collective-permute-start = (f32[1,24,256]{2,1,0:T(8,128)}, f32[1,24,256]{2,1,0:T(8,128)S(1)}, u32[]{:S(2)}, u32[]{:S(2)}) collective-permute-start(f32[1,24,256]{2,1,0:T(8,128)} %bitcast.30), channel_id=1, source_target_pairs={{0,2},{1,3},{2,0},{3,1},{4,6},{5,7},{6,4},{7,5},{8,10},{9,11},{10,... | collective-permute-start | bytes 73736 | tf_op jit(solution)/shard_map/ppermute | solution.py:371
  9.3 0.8 %copy-start.3 = (f32[24,256]{1,0:T(8,128)S(1)}, f32[24,256]{1,0:T(8,128)}, u32[]{:S(2)}) copy-start(f32[24,256]{1,0:T(8,128)} %get-tuple-element.33.pay_ref) | copy-start | bytes 73732
  13.5 3.6 %copy-start.2 = (bf16[16,256]{1,0:T(8,128)(2,1)S(1)}, bf16[16,256]{1,0:T(8,128)(2,1)}, u32[]{:S(2)}) copy-start(bf16[16,256]{1,0:T(8,128)(2,1)} %wc_ref.1) | copy-start | bytes 24580
  13.5 3.6 %copy-start.5 = (f32[4,256]{1,0:T(4,128)S(1)}, f32[4,256]{1,0:T(4,128)}, u32[]{:S(2)}) copy-start(f32[4,256]{1,0:T(4,128)} %b_ref) | copy-start | bytes 12292
  13.5 3.6 %copy-start.6 = (bf16[256]{0:T(256)(128)(2,1)S(1)}, bf16[256]{0:T(256)(128)(2,1)}, u32[]{:S(2)}) copy-start(bf16[256]{0:T(256)(128)(2,1)} %wb_ref.1) | copy-start | bytes 1540
  13.6 5.3 %collective-permute-start.5 = (f32[4,24,256]{2,1,0:T(8,128)S(1)}, f32[4,24,256]{2,1,0:T(8,128)S(1)}, u32[]{:S(2)}, u32[]{:S(2)}) collective-permute-start(f32[4,24,256]{2,1,0:T(8,128)S(1)} %pad_maximum_fusion.2), channel_id=1, source_target_pairs={{0,16},{1,17},{2,18},{3,19},{4,20},{5,21},{6,22},{7,23},{8,24},{9,... | collective-permute-start | bytes 294920 | tf_op jit(solution)/shard_map/ppermute | solution.py:371
  15.2 5.5 %collective-permute-start.4 = (f32[4,24,256]{2,1,0:T(8,128)S(1)}, f32[4,24,256]{2,1,0:T(8,128)S(1)}, u32[]{:S(2)}, u32[]{:S(2)}) collective-permute-start(f32[4,24,256]{2,1,0:T(8,128)S(1)} %pad_maximum_fusion.2), channel_id=1, source_target_pairs={{0,17},{1,16},{2,19},{3,18},{4,21},{5,20},{6,23},{7,22},{8,25},{9,... | collective-permute-start | bytes 294920 | tf_op jit(solution)/shard_map/ppermute | solution.py:371
  16.6 4.6 %collective-permute-start.3 = (f32[4,24,256]{2,1,0:T(8,128)S(1)}, f32[4,24,256]{2,1,0:T(8,128)S(1)}, u32[]{:S(2)}, u32[]{:S(2)}) collective-permute-start(f32[4,24,256]{2,1,0:T(8,128)S(1)} %pad_maximum_fusion.2), channel_id=1, source_target_pairs={{0,1},{1,0},{2,3},{3,2},{4,5},{5,4},{6,7},{7,6},{8,9},{9,8},{10,11... | collective-permute-start | bytes 294920 | tf_op jit(solution)/shard_map/ppermute | solution.py:371
  21.2 1.8 %collective-permute-start.6 = (f32[16,24,256]{2,1,0:T(8,128)S(1)}, f32[16,24,256]{2,1,0:T(8,128)S(1)}, u32[]{:S(2)}, u32[]{:S(2)}) collective-permute-start(f32[16,24,256]{2,1,0:T(8,128)S(1)} %pad_maximum_fusion.1.rows_ref), channel_id=1, source_target_pairs={{0,8},{1,9},{2,10},{3,11},{4,12},{5,13},{6,14},{7,15},{8,0},{9,1},... | collective-permute-start | bytes 1179656 | tf_op jit(solution)/shard_map/ppermute | solution.py:371
  21.3 1.7 %copy-start.4 = (f32[16,256]{1,0:T(8,128)S(1)}, f32[16,256]{1,0:T(8,128)}, u32[]{:S(2)}) copy-start(f32[16,256]{1,0:T(8,128)} %get-tuple-element.38.aux_ref) | copy-start | bytes 49156
  25.2 2.0 %collective-permute-start.7 = (f32[4,264,128]{2,1,0:T(8,128)S(1)}, f32[4,264,128]{2,1,0:T(8,128)S(1)}, u32[]{:S(2)}, u32[]{:S(2)}) collective-permute-start(f32[4,264,128]{2,1,0:T(8,128)S(1)} %get-tuple-element.53), channel_id=1, source_target_pairs={{0,8},{1,9},{2,10},{3,11},{4,12},{5,13},{6,14},{7,15},{8,0},{9,1},... | collective-permute-start | bytes 1622024 | tf_op jit(solution)/shard_map/ppermute | solution.py:371
  27.3 6.0 %collective-permute-start.10 = (f32[264,128]{1,0:T(8,128)S(1)}, f32[264,128]{1,0:T(8,128)S(1)}, u32[]{:S(2)}, u32[]{:S(2)}) collective-permute-start(f32[264,128]{1,0:T(8,128)S(1)} %get-tuple-element.61), channel_id=1, source_target_pairs={{0,17},{1,16},{2,19},{3,18},{4,21},{5,20},{6,23},{7,22},{8,14},{9,... | collective-permute-start | bytes 405512 | tf_op jit(solution)/shard_map/ppermute | solution.py:371
  29.4 5.3 %collective-permute-start.9 = (f32[264,128]{1,0:T(8,128)S(1)}, f32[264,128]{1,0:T(8,128)S(1)}, u32[]{:S(2)}, u32[]{:S(2)}) collective-permute-start(f32[264,128]{1,0:T(8,128)S(1)} %get-tuple-element.62), channel_id=1, source_target_pairs={{0,16},{1,17},{2,18},{3,19},{4,20},{5,21},{6,22},{7,23},{8,12},{9,... | collective-permute-start | bytes 405512 | tf_op jit(solution)/shard_map/ppermute | solution.py:371
  29.9 5.0 %collective-permute-start.8 = (f32[264,128]{1,0:T(8,128)S(1)}, f32[264,128]{1,0:T(8,128)S(1)}, u32[]{:S(2)}, u32[]{:S(2)}) collective-permute-start(f32[264,128]{1,0:T(8,128)S(1)} %get-tuple-element.63), channel_id=1, source_target_pairs={{0,1},{1,0},{2,3},{3,2},{4,5},{5,4},{6,7},{7,6},{8,10},{9,11},{10,... | collective-permute-start | bytes 405512 | tf_op jit(solution)/shard_map/ppermute | solution.py:371
  35.0 7.0 %collective-permute-start.13 = (f32[264,128]{1,0:T(8,128)S(1)}, f32[264,128]{1,0:T(8,128)S(1)}, u32[]{:S(2)}, u32[]{:S(2)}) collective-permute-start(f32[264,128]{1,0:T(8,128)S(1)} %fusion.1), channel_id=1, source_target_pairs={{0,6},{1,7},{2,4},{3,5},{4,2},{5,3},{6,0},{7,1},{8,25},{9,24},{10,... | collective-permute-start | bytes 405512 | tf_op jit(solution)/shard_map/ppermute | solution.py:371
  37.0 7.7 %collective-permute-start.12 = (f32[264,128]{1,0:T(8,128)S(1)}, f32[264,128]{1,0:T(8,128)S(1)}, u32[]{:S(2)}, u32[]{:S(2)}) collective-permute-start(f32[264,128]{1,0:T(8,128)S(1)} %fusion.1), channel_id=1, source_target_pairs={{0,2},{1,3},{2,0},{3,1},{4,6},{5,7},{6,4},{7,5},{8,9},{9,8},{10,11... | collective-permute-start | bytes 405512 | tf_op jit(solution)/shard_map/ppermute | solution.py:371
  37.0 7.7 %collective-permute-start.11 = (f32[264,128]{1,0:T(8,128)S(1)}, f32[264,128]{1,0:T(8,128)S(1)}, u32[]{:S(2)}, u32[]{:S(2)}) collective-permute-start(f32[264,128]{1,0:T(8,128)S(1)} %fusion.1), channel_id=1, source_target_pairs={{0,4},{1,5},{2,6},{3,7},{4,0},{5,1},{6,2},{7,3},{8,24},{9,25},{10,... | collective-permute-start | bytes 405512 | tf_op jit(solution)/shard_map/ppermute | solution.py:371
  44.8 6.0 %collective-permute-start.16 = (f32[264,128]{1,0:T(8,128)S(1)}, f32[264,128]{1,0:T(8,128)S(1)}, u32[]{:S(2)}, u32[]{:S(2)}) collective-permute-start(f32[264,128]{1,0:T(8,128)S(1)} %add_add_fusion.refs_0_), channel_id=1, source_target_pairs={{0,17},{1,16},{2,19},{3,18},{4,21},{5,20},{6,23},{7,22},{8,14},{9,... | collective-permute-start | bytes 405512 | tf_op jit(solution)/shard_map/ppermute | solution.py:371
  46.8 5.4 %collective-permute-start.15 = (f32[264,128]{1,0:T(8,128)S(1)}, f32[264,128]{1,0:T(8,128)S(1)}, u32[]{:S(2)}, u32[]{:S(2)}) collective-permute-start(f32[264,128]{1,0:T(8,128)S(1)} %add_add_fusion.refs_0_), channel_id=1, source_target_pairs={{0,16},{1,17},{2,18},{3,19},{4,20},{5,21},{6,22},{7,23},{8,12},{9,... | collective-permute-start | bytes 405512 | tf_op jit(solution)/shard_map/ppermute | solution.py:371
  47.3 5.0 %collective-permute-start.14 = (f32[264,128]{1,0:T(8,128)S(1)}, f32[264,128]{1,0:T(8,128)S(1)}, u32[]{:S(2)}, u32[]{:S(2)}) collective-permute-start(f32[264,128]{1,0:T(8,128)S(1)} %add_add_fusion.refs_0_), channel_id=1, source_target_pairs={{0,1},{1,0},{2,3},{3,2},{4,5},{5,4},{6,7},{7,6},{8,10},{9,11},{10,... | collective-permute-start | bytes 405512 | tf_op jit(solution)/shard_map/ppermute | solution.py:371
  52.3 2.0 %collective-permute-start.17 = (f32[4,264,128]{2,1,0:T(8,128)S(1)}, f32[4,264,128]{2,1,0:T(8,128)S(1)}, u32[]{:S(2)}, u32[]{:S(2)}) collective-permute-start(f32[4,264,128]{2,1,0:T(8,128)S(1)} %pad_maximum_fusion), channel_id=1, source_target_pairs={{0,8},{1,9},{2,10},{3,11},{4,12},{5,13},{6,14},{7,15},{8,0},{9,1},... | collective-permute-start | bytes 1622024 | tf_op jit(solution)/shard_map/ppermute | solution.py:371

commit v6 on v5

--- a/solution.py
+++ b/solution.py
@@ -315,21 +315,19 @@
         copy.wait()
 
 
-def place_far_kernel(
-    sizes, far_ref, near_ref, gw_in, gw_ref, *rest
-):
+def place_far_kernel(sizes, *refs):
+    blocks, (near_ref, _, gw_ref), rest = refs[:4], refs[4:7], refs[7:]
     outs, scratch, (ext, sems, small_sems) = rest[:4], rest[4:8], rest[8:]
     gb_ref, gc_ref, gbeta_ref, loss_ref = scratch
     rows = gw_ref.shape[1]
-    half = far_ref.shape[0]
+    half = len(blocks)
     dim = gc_ref.shape[0]
     layers = gb_ref.shape[0]
-    blocks = [far_ref.at[r] for r in range(half)]
     (near_first, near_place), (far_first, far_place) = block_places(sizes)
     copies = place_copies(blocks, far_first, far_place, gw_ref, sems)
     for r in range(half):
         ext[near_first + jnp.bitwise_xor(near_place, r)] = near_ref[r]
-        ext[far_first + jnp.bitwise_xor(far_place, r)] = far_ref[r, 2 * rows :, :]
+        ext[far_first + jnp.bitwise_xor(far_place, r)] = blocks[r][2 * rows :, :]
     flat = jnp.concatenate([ext[b] for b in range(2 * half)], 0)
     base = 2 * layers
     for h, col in enumerate([slice(0, 128), slice(128, 256)]):
@@ -488,7 +486,7 @@
     for m in others:
         mine = mine + swap(mine, m)
     quarter = [mine] + [swap(mine, a, b) for a, b in zip(flat_masks, line_masks)]
-    far = swap(jnp.stack(quarter), core)
+    far = [swap(block, core) for block in quarter]
 
     weights = jax.ShapeDtypeStruct((blocks, layers * width // blocks, width), f32)
     gw, near_ext = pl.pallas_call(
@@ -510,7 +508,7 @@
             jax.ShapeDtypeStruct((1, width), f32),
             jax.ShapeDtypeStruct((1, 1), f32),
         ),
-        in_specs=[VMEM, VMEM, HBM],
+        in_specs=[VMEM] * 5 + [HBM],
         out_specs=(HBM,) * 5,
         scratch_shapes=[
             pltpu.VMEM((layers, width), f32),
@@ -521,10 +519,10 @@
             pltpu.SemaphoreType.DMA((blocks,)),
             pltpu.SemaphoreType.DMA((4,)),
         ],
-        input_output_aliases={2: 0},
+        input_output_aliases={5: 0},
         compiler_params=PARAMS,
         name="place_far",
-    )(far, near_ext, gw)
+    )(*far, near_ext, gw)
     return (
         gw.reshape(layers, width, width),
         gb,

time: 55.4 us -> 54.8 us (0.989)
  waiting for transfers between devices: 23.5 us -> 22.6 us
    ppermute x18 -> x21, waiting for transfers between devices: 23.5 us -> 22.6 us  [swap(): lax.ppermute(x, AXES, [(i, i ^ masks[i // core & 1]) for i in range(ndev)])]
    ppermute x18 -> x21, starting transfers between devices: 21.1 us -> 21.5 us  [swap(): lax.ppermute(x, AXES, [(i, i ^ masks[i // core & 1]) for i in range(ndev)])]
  transfers between devices with their start and end apart: 18 -> 21, of which waited for: 15 -> 15; matrix products, arithmetic and copies ran while one was open for 0% -> 0% of each run, Pallas kernels for 5% -> 5%
where the time goes in v6:
time: 54.8 us; the launch traced here: 54.6 us
  waiting for transfers between devices  22.6 us (41%)
  starting transfers between devices  21.5 us (39%)
  Pallas kernels  8.73 us (16%)
  local copies, waits for them, and re-layouts  0.83 us (2%)
  between operations  0.8 us (1%)
    ppermute x21, waiting for transfers between devices, swap(): lax.ppermute(x, AXES, [(i, i ^ masks[i // core & 1]) for i in range(ndev)])  22.6 us
    ppermute x21, starting transfers between devices, swap(): lax.ppermute(x, AXES, [(i, i ^ masks[i // core & 1]) for i in range(ndev)])  21.5 us
    pallas_call x1, Pallas kernels, on_device(): pl.pallas_call(functools.partial(embed_kernel, sizes), out_shape=(jax.Sha...  2.93 us
    pallas_call x1, Pallas kernels, on_device(): pl.pallas_call(functools.partial(backward_kernel, sizes, hits_all, points...  2.2 us
    pallas_call x1, Pallas kernels, on_device(): pl.pallas_call(near_kernel, out_shape=partial_sums, in_specs=[VMEM] * 5,...  1.12 us
  transfers between devices with their start and end apart: 21, of which 15 were waited for; matrix products, arithmetic and copies ran while one was open for 0% of the time, Pallas kernels for 5%

profile of v6, /device:TPU:0, one launch (start us, length us, event | category | flops | bytes accessed | tf_op | source)
XLA Modules:
  0.0 54.6 jit_solution(14883878615831148548)
XLA Ops:
  0.6 0.0 copy-start
  0.6 2.9 %embed.1 = (f32[24,256]{1,0:T(8,128)}, f32[16,256]{1,0:T(8,128)}) custom-call(s32[8]{0:T(128)} %hit_hbm.1, bf16[256,256]{1,0:T(8,128)(2,1)} %feat_ref, bf16[4,256,256]{2,1,0:T(8,128)(2,1)} %w_ref, f32[4,256]{1,0:T(4,128)} %b_ref, bf16[16,256]{1,0:T(8,128)(2,1)} %wc_ref.1, bf16[256]{0:T(256)(128)(2,1)} %wb_ref.1, s32[1,256]{1,0:T(1,128)} %bitcast.24, ...), custom_call_target="tpu_custom_call" | custom-call | tf_op jit(solution)/shard_map/embed/pallas_call | solution.py:376
  3.6 0.0 copy-start.1
  3.6 4.1 %collective-permute-start.2 = (f32[1,24,256]{2,1,0:T(8,128)}, f32[1,24,256]{2,1,0:T(8,128)S(1)}, u32[]{:S(2)}, u32[]{:S(2)}) collective-permute-start(f32[1,24,256]{2,1,0:T(8,128)} %bitcast.20), channel_id=1, source_target_pairs={{0,4},{1,5},{2,6},{3,7},{4,0},{5,1},{6,2},{7,3},{8,12},{9,13},{10,... | collective-permute-start | bytes 73736 | tf_op jit(solution)/shard_map/ppermute | solution.py:369
  7.7 1.3 %collective-permute-start.1 = (f32[1,24,256]{2,1,0:T(8,128)}, f32[1,24,256]{2,1,0:T(8,128)S(1)}, u32[]{:S(2)}, u32[]{:S(2)}) collective-permute-start(f32[1,24,256]{2,1,0:T(8,128)} %bitcast.21), channel_id=1, source_target_pairs={{0,6},{1,7},{2,4},{3,5},{4,2},{5,3},{6,0},{7,1},{8,14},{9,15},{10,... | collective-permute-start | bytes 73736 | tf_op jit(solution)/shard_map/ppermute | solution.py:369
  9.0 0.2 collective-permute-start
  9.3 0.0 copy-start.3
  9.3 0.8 %copy-done.3 = f32[24,256]{1,0:T(8,128)S(1)} copy-done((f32[24,256]{1,0:T(8,128)S(1)}, f32[24,256]{1,0:T(8,128)}, u32[]{:S(2)}) %copy-start.3) | copy-done | bytes 24600
  10.0 0.1 spread.1
  10.1 0.0 collective-permute-done.2
  10.1 3.4 %collective-permute-done.1 = f32[1,24,256]{2,1,0:T(8,128)S(1)} collective-permute-done((f32[1,24,256]{2,1,0:T(8,128)}, f32[1,24,256]{2,1,0:T(8,128)S(1)}, u32[]{:S(2)}, u32[]{:S(2)}) %collective-permute-start.1) | collective-permute-done | bytes 24608 | tf_op jit(solution)/shard_map/ppermute | solution.py:369
  13.5 0.0 collective-permute-done
  13.5 0.0 copy-start.2
  13.5 0.0 copy-start.5
  13.5 0.0 copy-start.6
  13.6 1.6 %collective-permute-start.5 = (f32[4,24,256]{2,1,0:T(8,128)S(1)}, f32[4,24,256]{2,1,0:T(8,128)S(1)}, u32[]{:S(2)}, u32[]{:S(2)}) collective-permute-start(f32[4,24,256]{2,1,0:T(8,128)S(1)} %pad_maximum_fusion.1), channel_id=1, source_target_pairs={{0,16},{1,17},{2,18},{3,19},{4,20},{5,21},{6,22},{7,23},{8,24},{9,... | collective-permute-start | bytes 294920 | tf_op jit(solution)/shard_map/ppermute | solution.py:369
  15.2 1.4 %collective-permute-start.4 = (f32[4,24,256]{2,1,0:T(8,128)S(1)}, f32[4,24,256]{2,1,0:T(8,128)S(1)}, u32[]{:S(2)}, u32[]{:S(2)}) collective-permute-start(f32[4,24,256]{2,1,0:T(8,128)S(1)} %pad_maximum_fusion.1), channel_id=1, source_target_pairs={{0,17},{1,16},{2,19},{3,18},{4,21},{5,20},{6,23},{7,22},{8,25},{9,... | collective-permute-start | bytes 294920 | tf_op jit(solution)/shard_map/ppermute | solution.py:369
  16.6 0.5 collective-permute-start.3
  17.1 0.0 copy-done
  17.1 0.0 copy-done.1
  17.1 0.0 copy-done.2
  17.1 0.0 copy-done.5
  17.1 0.0 copy-done.6
  17.1 0.6 %residuals.1 = (f32[4,256,256]{2,1,0:T(8,128)S(1)}, bf16[4,256,256]{2,1,0:T(8,128)(2,1)S(1)}, bf16[256,256]{1,0:T(8,128)(2,1)S(1)}, bf16[3,256,256]{2,1,0:T(8,128)(2,1)S(1)}, bf16[32,256]{1,0:T(8,128)(2,1)S(1)}) custom-call(bf16[256,256]{1,0:T(8,128)(2,1)S(1)} %copy-done.1, bf16[4,256,256]{2,1,0:T(8,128)(2,1)S(1)} %copy-done, f32[4,256]{1,0:T(4,128)S(1)} %copy-done.5, ...), custom_call_target="tpu_custom_call" | custom-call | flops 5242880 | bytes 1572864 | tf_op jit(solution)/shard_map/residuals/pallas_call | solution.py:400
  17.8 1.1 %collective-permute-done.5 = f32[4,24,256]{2,1,0:T(8,128)S(1)} collective-permute-done((f32[4,24,256]{2,1,0:T(8,128)S(1)}, f32[4,24,256]{2,1,0:T(8,128)S(1)}, u32[]{:S(2)}, u32[]{:S(2)}) %collective-permute-start.5) | collective-permute-done | bytes 98336 | tf_op jit(solution)/shard_map/ppermute | solution.py:369
  18.9 1.8 %collective-permute-done.4 = f32[4,24,256]{2,1,0:T(8,128)S(1)} collective-permute-done((f32[4,24,256]{2,1,0:T(8,128)S(1)}, f32[4,24,256]{2,1,0:T(8,128)S(1)}, u32[]{:S(2)}, u32[]{:S(2)}) %collective-permute-start.4) | collective-permute-done | bytes 98336 | tf_op jit(solution)/shard_map/ppermute | solution.py:369
  20.7 0.5 collective-permute-done.3
  21.2 0.1 collective-permute-start.6
  21.3 0.0 copy-start.4
  21.3 1.1 %near_pairs.1 = (f32[17,8,256]{2,1,0:T(8,128)S(1)}, f32[17,8,128]{2,1,0:T(8,128)S(1)}) custom-call(f32[24,256]{1,0:T(8,128)S(1)} %get-tuple-element.34.pay_ref, f32[8,128]{1,0:T(8,128)S(1)} %get-tuple-element.35.own_ref, f32[16,8,256]{2,1,0:T(8,128)S(1)} %get-tuple-element.36.xb, f32[16,8,256]{2,1,0:T(8,128)S(1)} %get-tuple-element.37.yb, ...), custom_call_target="tpu_custom_call" | custom-call | flops 13107200 | bytes 524288 | tf_op jit(solution)/shard_map/near_pairs/pallas_call | solution.py:450
  22.4 0.6 %collective-permute-done.6.rows_ref = f32[16,24,256]{2,1,0:T(8,128)S(1)} collective-permute-done((f32[16,24,256]{2,1,0:T(8,128)S(1)}, f32[16,24,256]{2,1,0:T(8,128)S(1)}, u32[]{:S(2)}, u32[]{:S(2)}) %collective-permute-start.6) | collective-permute-done | bytes 393248 | tf_op jit(solution)/shard_map/ppermute | solution.py:369
  23.0 0.0 copy-done.4
  23.0 2.2 %pairs_backward.1 = (f32[4,264,128]{2,1,0:T(8,128)S(1)}, f32[4,264,128]{2,1,0:T(8,128)S(1)}) custom-call(f32[24,256]{1,0:T(8,128)S(1)} %get-tuple-element.34.pay_ref, f32[8,128]{1,0:T(8,128)S(1)} %get-tuple-element.35.own_ref, f32[16,8,256]{2,1,0:T(8,128)S(1)} %get-tuple-element.36.xb, f32[16,8,256]{2,1,0:T(8,128)S(1)} %get-tuple-element.37.yb, ...), custom_call_target="tpu_custom_call" | custom-call | tf_op jit(solution)/shard_map/pairs_backward/pallas_call | solution.py:466
  25.2 0.2 collective-permute-start.7
  25.4 1.8 %collective-permute-done.7 = f32[4,264,128]{2,1,0:T(8,128)S(1)} collective-permute-done((f32[4,264,128]{2,1,0:T(8,128)S(1)}, f32[4,264,128]{2,1,0:T(8,128)S(1)}, u32[]{:S(2)}, u32[]{:S(2)}) %collective-permute-start.7) | collective-permute-done | bytes 540704 | tf_op jit(solution)/shard_map/ppermute | solution.py:369
  27.2 0.1 add.21
  27.3 2.1 %collective-permute-start.10 = (f32[264,128]{1,0:T(8,128)S(1)}, f32[264,128]{1,0:T(8,128)S(1)}, u32[]{:S(2)}, u32[]{:S(2)}) collective-permute-start(f32[264,128]{1,0:T(8,128)S(1)} %get-tuple-element.61), channel_id=1, source_target_pairs={{0,17},{1,16},{2,19},{3,18},{4,21},{5,20},{6,23},{7,22},{8,14},{9,... | collective-permute-start | bytes 405512 | tf_op jit(solution)/shard_map/ppermute | solution.py:369
  29.4 0.5 collective-permute-start.9
  29.9 1.0 %collective-permute-start.8 = (f32[264,128]{1,0:T(8,128)S(1)}, f32[264,128]{1,0:T(8,128)S(1)}, u32[]{:S(2)}, u32[]{:S(2)}) collective-permute-start(f32[264,128]{1,0:T(8,128)S(1)} %get-tuple-element.63), channel_id=1, source_target_pairs={{0,1},{1,0},{2,3},{3,2},{4,5},{5,4},{6,7},{7,6},{8,10},{9,11},{10,... | collective-permute-start | bytes 405512 | tf_op jit(solution)/shard_map/ppermute | solution.py:369
  30.9 2.5 %collective-permute-done.10 = f32[264,128]{1,0:T(8,128)S(1)} collective-permute-done((f32[264,128]{1,0:T(8,128)S(1)}, f32[264,128]{1,0:T(8,128)S(1)}, u32[]{:S(2)}, u32[]{:S(2)}) %collective-permute-start.10) | collective-permute-done | bytes 135200 | tf_op jit(solution)/shard_map/ppermute | solution.py:369
  33.4 1.4 %collective-permute-done.9 = f32[264,128]{1,0:T(8,128)S(1)} collective-permute-done((f32[264,128]{1,0:T(8,128)S(1)}, f32[264,128]{1,0:T(8,128)S(1)}, u32[]{:S(2)}, u32[]{:S(2)}) %collective-permute-start.9) | collective-permute-done | bytes 135200 | tf_op jit(solution)/shard_map/ppermute | solution.py:369
  34.8 0.2 collective-permute-done.8
  35.0 2.1 %collective-permute-start.13 = (f32[264,128]{1,0:T(8,128)S(1)}, f32[264,128]{1,0:T(8,128)S(1)}, u32[]{:S(2)}, u32[]{:S(2)}) collective-permute-start(f32[264,128]{1,0:T(8,128)S(1)} %fusion.1), channel_id=1, source_target_pairs={{0,6},{1,7},{2,4},{3,5},{4,2},{5,3},{6,0},{7,1},{8,25},{9,24},{10,... | collective-permute-start | bytes 405512 | tf_op jit(solution)/shard_map/ppermute | solution.py:369
  37.0 0.0 collective-permute-start.12
  37.1 2.4 %collective-permute-start.11 = (f32[264,128]{1,0:T(8,128)S(1)}, f32[264,128]{1,0:T(8,128)S(1)}, u32[]{:S(2)}, u32[]{:S(2)}) collective-permute-start(f32[264,128]{1,0:T(8,128)S(1)} %fusion.1), channel_id=1, source_target_pairs={{0,4},{1,5},{2,6},{3,7},{4,0},{5,1},{6,2},{7,3},{8,24},{9,25},{10,... | collective-permute-start | bytes 405512 | tf_op jit(solution)/shard_map/ppermute | solution.py:369
  39.4 2.6 %collective-permute-done.13 = f32[264,128]{1,0:T(8,128)S(1)} collective-permute-done((f32[264,128]{1,0:T(8,128)S(1)}, f32[264,128]{1,0:T(8,128)S(1)}, u32[]{:S(2)}, u32[]{:S(2)}) %collective-permute-start.13) | collective-permute-done | bytes 135200 | tf_op jit(solution)/shard_map/ppermute | solution.py:369
  42.0 2.8 %collective-permute-done.12 = f32[264,128]{1,0:T(8,128)S(1)} collective-permute-done((f32[264,128]{1,0:T(8,128)S(1)}, f32[264,128]{1,0:T(8,128)S(1)}, u32[]{:S(2)}, u32[]{:S(2)}) %collective-permute-start.12) | collective-permute-done | bytes 135200 | tf_op jit(solution)/shard_map/ppermute | solution.py:369
  44.7 0.0 collective-permute-done.11
  44.8 2.0 %collective-permute-start.19 = (f32[264,128]{1,0:T(8,128)S(1)}, f32[264,128]{1,0:T(8,128)S(1)}, u32[]{:S(2)}, u32[]{:S(2)}) collective-permute-start(f32[264,128]{1,0:T(8,128)S(1)} %add_add_fusion.refs_0_), channel_id=1, source_target_pairs={{0,17},{1,16},{2,19},{3,18},{4,21},{5,20},{6,23},{7,22},{8,14},{9,... | collective-permute-start | bytes 405512 | tf_op jit(solution)/shard_map/ppermute | solution.py:369
  46.8 0.5 collective-permute-start.17
  47.3 1.1 %collective-permute-start.15 = (f32[264,128]{1,0:T(8,128)S(1)}, f32[264,128]{1,0:T(8,128)S(1)}, u32[]{:S(2)}, u32[]{:S(2)}) collective-permute-start(f32[264,128]{1,0:T(8,128)S(1)} %add_add_fusion.refs_0_), channel_id=1, source_target_pairs={{0,1},{1,0},{2,3},{3,2},{4,5},{5,4},{6,7},{7,6},{8,10},{9,11},{10,... | collective-permute-start | bytes 405512 | tf_op jit(solution)/shard_map/ppermute | solution.py:369
  48.3 0.0 collective-permute-start.14
  48.3 2.5 %collective-permute-done.19.refs_3_ = f32[264,128]{1,0:T(8,128)S(1)} collective-permute-done((f32[264,128]{1,0:T(8,128)S(1)}, f32[264,128]{1,0:T(8,128)S(1)}, u32[]{:S(2)}, u32[]{:S(2)}) %collective-permute-start.19) | collective-permute-done | bytes 135200 | tf_op jit(solution)/shard_map/ppermute | solution.py:369
  50.8 0.0 collective-permute-start.20
  50.8 1.4 %collective-permute-done.17.refs_2_ = f32[264,128]{1,0:T(8,128)S(1)} collective-permute-done((f32[264,128]{1,0:T(8,128)S(1)}, f32[264,128]{1,0:T(8,128)S(1)}, u32[]{:S(2)}, u32[]{:S(2)}) %collective-permute-start.17) | collective-permute-done | bytes 135200 | tf_op jit(solution)/shard_map/ppermute | solution.py:369
  52.2 0.0 collective-permute-start.18
  52.2 0.1 collective-permute-done.15.refs_1_
  52.3 0.4 collective-permute-start.16
  52.7 0.8 %place_near.1 = (f32[8,128,256]{2,1,0:T(8,128)}, f32[4,8,128]{2,1,0:T(8,128)S(1)}) custom-call(f32[264,128]{1,0:T(8,128)S(1)} %add_add_fusion.refs_0_, f32[264,128]{1,0:T(8,128)S(1)} %collective-permute-done.15.refs_1_, f32[264,128]{1,0:T(8,128)S(1)} %collective-permute-done.17.refs_2_, f32[264,128]{1,0:T(8,128)S(1)} %collective-permute-done.19.refs_3_), custom_call_target="tpu_custom_call" | custom-call | bytes 1048576 | tf_op jit(solution)/shard_map/place_near/pallas_call | solution.py:492
  53.6 0.0 collective-permute-done.14.refs_0_
  53.6 0.0 collective-permute-done.20.refs_3_
  53.6 0.0 collective-permute-done.18.refs_2_
  53.6 0.1 collective-permute-done.16.refs_1_
  53.8 0.9 %place_far.1 = (f32[8,128,256]{2,1,0:T(8,128)}, f32[4,256]{1,0:T(4,128)}, f32[16,256]{1,0:T(8,128)}, f32[1,256]{1,0:T(1,128)}, f32[1,1]{1,0:T(1,128)}) custom-call(f32[264,128]{1,0:T(8,128)S(1)} %collective-permute-done.14.refs_0_, f32[264,128]{1,0:T(8,128)S(1)} %collective-permute-done.16.refs_1_, ...), custom_call_target="tpu_custom_call", output_to_operand_aliasing={{0}: (5, {})} | custom-call | tf_op jit(solution)/shard_map/place_far/pallas_call | solution.py:502
  (5 shorter events, 0.1 us)
Async XLA Ops:
  0.6 16.5 %copy-start = (bf16[4,256,256]{2,1,0:T(8,128)(2,1)S(1)}, bf16[4,256,256]{2,1,0:T(8,128)(2,1)}, u32[]{:S(2)}) copy-start(bf16[4,256,256]{2,1,0:T(8,128)(2,1)} %w_ref) | copy-start | bytes 1572868
  3.6 13.5 %copy-start.1 = (bf16[256,256]{1,0:T(8,128)(2,1)S(1)}, bf16[256,256]{1,0:T(8,128)(2,1)}, u32[]{:S(2)}) copy-start(bf16[256,256]{1,0:T(8,128)(2,1)} %feat_ref) | copy-start | bytes 393220
  3.6 6.5 %collective-permute-start.2 = (f32[1,24,256]{2,1,0:T(8,128)}, f32[1,24,256]{2,1,0:T(8,128)S(1)}, u32[]{:S(2)}, u32[]{:S(2)}) collective-permute-start(f32[1,24,256]{2,1,0:T(8,128)} %bitcast.20), channel_id=1, source_target_pairs={{0,4},{1,5},{2,6},{3,7},{4,0},{5,1},{6,2},{7,3},{8,12},{9,13},{10,... | collective-permute-start | bytes 73736 | tf_op jit(solution)/shard_map/ppermute | solution.py:369
  7.7 5.8 %collective-permute-start.1 = (f32[1,24,256]{2,1,0:T(8,128)}, f32[1,24,256]{2,1,0:T(8,128)S(1)}, u32[]{:S(2)}, u32[]{:S(2)}) collective-permute-start(f32[1,24,256]{2,1,0:T(8,128)} %bitcast.21), channel_id=1, source_target_pairs={{0,6},{1,7},{2,4},{3,5},{4,2},{5,3},{6,0},{7,1},{8,14},{9,15},{10,... | collective-permute-start | bytes 73736 | tf_op jit(solution)/shard_map/ppermute | solution.py:369
  9.0 4.5 %collective-permute-start = (f32[1,24,256]{2,1,0:T(8,128)}, f32[1,24,256]{2,1,0:T(8,128)S(1)}, u32[]{:S(2)}, u32[]{:S(2)}) collective-permute-start(f32[1,24,256]{2,1,0:T(8,128)} %bitcast.22), channel_id=1, source_target_pairs={{0,2},{1,3},{2,0},{3,1},{4,6},{5,7},{6,4},{7,5},{8,10},{9,11},{10,... | collective-permute-start | bytes 73736 | tf_op jit(solution)/shard_map/ppermute | solution.py:369
  9.3 0.8 %copy-start.3 = (f32[24,256]{1,0:T(8,128)S(1)}, f32[24,256]{1,0:T(8,128)}, u32[]{:S(2)}) copy-start(f32[24,256]{1,0:T(8,128)} %get-tuple-element.33.pay_ref) | copy-start | bytes 73732
  13.5 3.6 %copy-start.2 = (bf16[16,256]{1,0:T(8,128)(2,1)S(1)}, bf16[16,256]{1,0:T(8,128)(2,1)}, u32[]{:S(2)}) copy-start(bf16[16,256]{1,0:T(8,128)(2,1)} %wc_ref.1) | copy-start | bytes 24580
  13.5 3.6 %copy-start.5 = (f32[4,256]{1,0:T(4,128)S(1)}, f32[4,256]{1,0:T(4,128)}, u32[]{:S(2)}) copy-start(f32[4,256]{1,0:T(4,128)} %b_ref) | copy-start | bytes 12292
  13.5 3.6 %copy-start.6 = (bf16[256]{0:T(256)(128)(2,1)S(1)}, bf16[256]{0:T(256)(128)(2,1)}, u32[]{:S(2)}) copy-start(bf16[256]{0:T(256)(128)(2,1)} %wb_ref.1) | copy-start | bytes 1540
  13.6 5.3 %collective-permute-start.5 = (f32[4,24,256]{2,1,0:T(8,128)S(1)}, f32[4,24,256]{2,1,0:T(8,128)S(1)}, u32[]{:S(2)}, u32[]{:S(2)}) collective-permute-start(f32[4,24,256]{2,1,0:T(8,128)S(1)} %pad_maximum_fusion.1), channel_id=1, source_target_pairs={{0,16},{1,17},{2,18},{3,19},{4,20},{5,21},{6,22},{7,23},{8,24},{9,... | collective-permute-start | bytes 294920 | tf_op jit(solution)/shard_map/ppermute | solution.py:369
  15.2 5.5 %collective-permute-start.4 = (f32[4,24,256]{2,1,0:T(8,128)S(1)}, f32[4,24,256]{2,1,0:T(8,128)S(1)}, u32[]{:S(2)}, u32[]{:S(2)}) collective-permute-start(f32[4,24,256]{2,1,0:T(8,128)S(1)} %pad_maximum_fusion.1), channel_id=1, source_target_pairs={{0,17},{1,16},{2,19},{3,18},{4,21},{5,20},{6,23},{7,22},{8,25},{9,... | collective-permute-start | bytes 294920 | tf_op jit(solution)/shard_map/ppermute | solution.py:369
  16.6 4.6 %collective-permute-start.3 = (f32[4,24,256]{2,1,0:T(8,128)S(1)}, f32[4,24,256]{2,1,0:T(8,128)S(1)}, u32[]{:S(2)}, u32[]{:S(2)}) collective-permute-start(f32[4,24,256]{2,1,0:T(8,128)S(1)} %pad_maximum_fusion.1), channel_id=1, source_target_pairs={{0,1},{1,0},{2,3},{3,2},{4,5},{5,4},{6,7},{7,6},{8,9},{9,8},{10,11... | collective-permute-start | bytes 294920 | tf_op jit(solution)/shard_map/ppermute | solution.py:369
  21.2 1.8 %collective-permute-start.6 = (f32[16,24,256]{2,1,0:T(8,128)S(1)}, f32[16,24,256]{2,1,0:T(8,128)S(1)}, u32[]{:S(2)}, u32[]{:S(2)}) collective-permute-start(f32[16,24,256]{2,1,0:T(8,128)S(1)} %pad_maximum_fusion.rows_ref), channel_id=1, source_target_pairs={{0,8},{1,9},{2,10},{3,11},{4,12},{5,13},{6,14},{7,15},{8,0},{9,1},... | collective-permute-start | bytes 1179656 | tf_op jit(solution)/shard_map/ppermute | solution.py:369
  21.3 1.7 %copy-start.4 = (f32[16,256]{1,0:T(8,128)S(1)}, f32[16,256]{1,0:T(8,128)}, u32[]{:S(2)}) copy-start(f32[16,256]{1,0:T(8,128)} %get-tuple-element.38.aux_ref) | copy-start | bytes 49156
  25.2 2.0 %collective-permute-start.7 = (f32[4,264,128]{2,1,0:T(8,128)S(1)}, f32[4,264,128]{2,1,0:T(8,128)S(1)}, u32[]{:S(2)}, u32[]{:S(2)}) collective-permute-start(f32[4,264,128]{2,1,0:T(8,128)S(1)} %get-tuple-element.53), channel_id=1, source_target_pairs={{0,8},{1,9},{2,10},{3,11},{4,12},{5,13},{6,14},{7,15},{8,0},{9,1},... | collective-permute-start | bytes 1622024 | tf_op jit(solution)/shard_map/ppermute | solution.py:369
  27.3 6.0 %collective-permute-start.10 = (f32[264,128]{1,0:T(8,128)S(1)}, f32[264,128]{1,0:T(8,128)S(1)}, u32[]{:S(2)}, u32[]{:S(2)}) collective-permute-start(f32[264,128]{1,0:T(8,128)S(1)} %get-tuple-element.61), channel_id=1, source_target_pairs={{0,17},{1,16},{2,19},{3,18},{4,21},{5,20},{6,23},{7,22},{8,14},{9,... | collective-permute-start | bytes 405512 | tf_op jit(solution)/shard_map/ppermute | solution.py:369
  29.4 5.3 %collective-permute-start.9 = (f32[264,128]{1,0:T(8,128)S(1)}, f32[264,128]{1,0:T(8,128)S(1)}, u32[]{:S(2)}, u32[]{:S(2)}) collective-permute-start(f32[264,128]{1,0:T(8,128)S(1)} %get-tuple-element.62), channel_id=1, source_target_pairs={{0,16},{1,17},{2,18},{3,19},{4,20},{5,21},{6,22},{7,23},{8,12},{9,... | collective-permute-start | bytes 405512 | tf_op jit(solution)/shard_map/ppermute | solution.py:369
  29.9 5.0 %collective-permute-start.8 = (f32[264,128]{1,0:T(8,128)S(1)}, f32[264,128]{1,0:T(8,128)S(1)}, u32[]{:S(2)}, u32[]{:S(2)}) collective-permute-start(f32[264,128]{1,0:T(8,128)S(1)} %get-tuple-element.63), channel_id=1, source_target_pairs={{0,1},{1,0},{2,3},{3,2},{4,5},{5,4},{6,7},{7,6},{8,10},{9,11},{10,... | collective-permute-start | bytes 405512 | tf_op jit(solution)/shard_map/ppermute | solution.py:369
  35.0 7.0 %collective-permute-start.13 = (f32[264,128]{1,0:T(8,128)S(1)}, f32[264,128]{1,0:T(8,128)S(1)}, u32[]{:S(2)}, u32[]{:S(2)}) collective-permute-start(f32[264,128]{1,0:T(8,128)S(1)} %fusion.1), channel_id=1, source_target_pairs={{0,6},{1,7},{2,4},{3,5},{4,2},{5,3},{6,0},{7,1},{8,25},{9,24},{10,... | collective-permute-start | bytes 405512 | tf_op jit(solution)/shard_map/ppermute | solution.py:369
  37.0 7.7 %collective-permute-start.12 = (f32[264,128]{1,0:T(8,128)S(1)}, f32[264,128]{1,0:T(8,128)S(1)}, u32[]{:S(2)}, u32[]{:S(2)}) collective-permute-start(f32[264,128]{1,0:T(8,128)S(1)} %fusion.1), channel_id=1, source_target_pairs={{0,2},{1,3},{2,0},{3,1},{4,6},{5,7},{6,4},{7,5},{8,9},{9,8},{10,11... | collective-permute-start | bytes 405512 | tf_op jit(solution)/shard_map/ppermute | solution.py:369
  37.1 7.7 %collective-permute-start.11 = (f32[264,128]{1,0:T(8,128)S(1)}, f32[264,128]{1,0:T(8,128)S(1)}, u32[]{:S(2)}, u32[]{:S(2)}) collective-permute-start(f32[264,128]{1,0:T(8,128)S(1)} %fusion.1), channel_id=1, source_target_pairs={{0,4},{1,5},{2,6},{3,7},{4,0},{5,1},{6,2},{7,3},{8,24},{9,25},{10,... | collective-permute-start | bytes 405512 | tf_op jit(solution)/shard_map/ppermute | solution.py:369
  44.8 6.0 %collective-permute-start.19 = (f32[264,128]{1,0:T(8,128)S(1)}, f32[264,128]{1,0:T(8,128)S(1)}, u32[]{:S(2)}, u32[]{:S(2)}) collective-permute-start(f32[264,128]{1,0:T(8,128)S(1)} %add_add_fusion.refs_0_), channel_id=1, source_target_pairs={{0,17},{1,16},{2,19},{3,18},{4,21},{5,20},{6,23},{7,22},{8,14},{9,... | collective-permute-start | bytes 405512 | tf_op jit(solution)/shard_map/ppermute | solution.py:369
  46.8 5.4 %collective-permute-start.17 = (f32[264,128]{1,0:T(8,128)S(1)}, f32[264,128]{1,0:T(8,128)S(1)}, u32[]{:S(2)}, u32[]{:S(2)}) collective-permute-start(f32[264,128]{1,0:T(8,128)S(1)} %add_add_fusion.refs_0_), channel_id=1, source_target_pairs={{0,16},{1,17},{2,18},{3,19},{4,20},{5,21},{6,22},{7,23},{8,12},{9,... | collective-permute-start | bytes 405512 | tf_op jit(solution)/shard_map/ppermute | solution.py:369
  47.3 5.0 %collective-permute-start.15 = (f32[264,128]{1,0:T(8,128)S(1)}, f32[264,128]{1,0:T(8,128)S(1)}, u32[]{:S(2)}, u32[]{:S(2)}) collective-permute-start(f32[264,128]{1,0:T(8,128)S(1)} %add_add_fusion.refs_0_), channel_id=1, source_target_pairs={{0,1},{1,0},{2,3},{3,2},{4,5},{5,4},{6,7},{7,6},{8,10},{9,11},{10,... | collective-permute-start | bytes 405512 | tf_op jit(solution)/shard_map/ppermute | solution.py:369
  48.3 5.2 %collective-permute-start.14 = (f32[264,128]{1,0:T(8,128)S(1)}, f32[264,128]{1,0:T(8,128)S(1)}, u32[]{:S(2)}, u32[]{:S(2)}) collective-permute-start(f32[264,128]{1,0:T(8,128)S(1)} %add_add_fusion.refs_0_), channel_id=1, source_target_pairs={{0,8},{1,9},{2,10},{3,11},{4,12},{5,13},{6,14},{7,15},{8,0},{9,1},... | collective-permute-start | bytes 405512 | tf_op jit(solution)/shard_map/ppermute | solution.py:369
  50.8 2.8 %collective-permute-start.20 = (f32[264,128]{1,0:T(8,128)S(1)}, f32[264,128]{1,0:T(8,128)S(1)}, u32[]{:S(2)}, u32[]{:S(2)}) collective-permute-start(f32[264,128]{1,0:T(8,128)S(1)} %collective-permute-done.19.refs_3_), channel_id=1, source_target_pairs={{0,8},{1,9},{2,10},{3,11},{4,12},{5,13},{6,14},{7,15},{8,0},{9,1},... | collective-permute-start | bytes 405512 | tf_op jit(solution)/shard_map/ppermute | solution.py:369
  52.2 1.4 %collective-permute-start.18 = (f32[264,128]{1,0:T(8,128)S(1)}, f32[264,128]{1,0:T(8,128)S(1)}, u32[]{:S(2)}, u32[]{:S(2)}) collective-permute-start(f32[264,128]{1,0:T(8,128)S(1)} %collective-permute-done.17.refs_2_), channel_id=1, source_target_pairs={{0,8},{1,9},{2,10},{3,11},{4,12},{5,13},{6,14},{7,15},{8,0},{9,1},... | collective-permute-start | bytes 405512 | tf_op jit(solution)/shard_map/ppermute | solution.py:369
  52.3 1.5 %collective-permute-start.16 = (f32[264,128]{1,0:T(8,128)S(1)}, f32[264,128]{1,0:T(8,128)S(1)}, u32[]{:S(2)}, u32[]{:S(2)}) collective-permute-start(f32[264,128]{1,0:T(8,128)S(1)} %collective-permute-done.15.refs_1_), channel_id=1, source_target_pairs={{0,8},{1,9},{2,10},{3,11},{4,12},{5,13},{6,14},{7,15},{8,0},{9,1},... | collective-permute-start | bytes 405512 | tf_op jit(solution)/shard_map/ppermute | solution.py:369

commit v7 on v6

--- a/solution.py
+++ b/solution.py
@@ -60,10 +60,8 @@
     hits = feat_ref.shape[0]
     points = hit_ref.shape[0]
     layers = w_ref.shape[0]
-    pairs = [(feat_hbm, feat_ref)] + [(w_hbm.at[l], w_ref.at[l]) for l in range(layers)]
-    pairs = pairs[:2] + [(b_hbm, b_ref)] + pairs[2:]
-    pairs += [(wc_hbm, wc_ref), (wb_hbm, wb_ref), (track_hbm, track_ref)]
-    pairs += [(noise_hbm, noise_ref), (hit_hbm, hit_ref)]
+    pairs = [(feat_hbm, feat_ref), (w_hbm, w_ref), (b_hbm, b_ref), (wc_hbm, wc_ref), (wb_hbm, wb_ref)]
+    pairs += [(track_hbm, track_ref), (noise_hbm, noise_ref), (hit_hbm, hit_ref)]
     copies = [
         pltpu.make_async_copy(src, dst, sems.at[i]) for i, (src, dst) in enumerate(pairs)
     ]
@@ -73,11 +71,9 @@
         copy.wait()
     h = feat_ref[...]
     for l in range(layers):
-        if l > 0:
-            copies[l + 2].wait()
         a = matmul(h, w_ref[l]) + b_ref[l : l + 1, :]
         h = (a * jax.nn.sigmoid(a)).astype(jnp.bfloat16)
-    for copy in copies[layers + 2 :]:
+    for copy in copies[3:]:
         copy.wait()
     xz = matmul(head_rows(wc_ref, wb_ref), h, 1, 1)
     z = xz[dim : dim + 1]
@@ -201,15 +197,19 @@
     return hit_acc, point_acc
 
 
-def near_kernel(pay_ref, own_ref, xb, yb, rows_ref, hit_ref, point_ref):
-    dim = xb.shape[0]
+def pair_kernel(parts, pay_ref, own_ref, xb, yb, *rest):
+    rows, rest = rest[:parts], rest[parts:]
+    hit_ref, point_ref = rest[-2:]
+    if len(rest) > 2:
+        sums = [tuple(ref[c] for c in range(ref.shape[0])) for ref in rest[:2]]
+    else:
+        sums = [(jnp.zeros(ref.shape[1:], jnp.float32),) * ref.shape[0] for ref in rest]
     own = own_ref[...]
-    hit_acc = (jnp.zeros(hit_ref.shape[1:], jnp.float32),) * (dim + 1)
-    point_acc = (jnp.zeros(point_ref.shape[1:], jnp.float32),) * (dim + 1)
-    hit_acc, point_acc = pair_sums(pay_ref, own, rows_ref, xb, yb, hit_acc, point_acc)
-    for c in range(dim + 1):
-        hit_ref[c] = hit_acc[c]
-        point_ref[c] = point_acc[c]
+    for ref in rows:
+        sums = pair_sums(pay_ref, own, ref, xb, yb, *sums)
+    for ref, values in zip((hit_ref, point_ref), sums):
+        for c, value in enumerate(values):
+            ref[c] = value
 
 
 def backward_kernel(
@@ -390,7 +390,7 @@
             pltpu.VMEM(w_beta.shape, low),
             pltpu.VMEM((1, hits), jnp.int32),
             pltpu.VMEM((1, hits), jnp.int32),
-            pltpu.SemaphoreType.DMA((layers + 7,)),
+            pltpu.SemaphoreType.DMA((8,)),
         ],
         compiler_params=pltpu.CompilerParams(vmem_limit_bytes=EMBED_VMEM),
         name="embed",
@@ -438,27 +438,33 @@
     rows_all = jnp.concatenate([kept] + arrived, 0)
     rows_all, *early = lax.optimization_barrier((rows_all, features, w_layers, b_layers))
     arrived = [swap(rows_all, m) for m in (plane[0], plane[0] ^ plane[1], plane[1])]
-    rows_all = jnp.concatenate([rows_all] + arrived, 0)
+    first_far = swap(rows_all, core)
+    rows = jnp.concatenate(arrived, 0)
     slope, ht, last, wt, head = residuals(early + [w_coord, w_beta])
-    rows_all, slope = lax.optimization_barrier((rows_all, slope))
-    rows_far = swap(rows_all, core)
+    rows, first_far, slope = lax.optimization_barrier((rows, first_far, slope))
+    rows_far = swap(rows, core)
 
     partial_sums = (
         jax.ShapeDtypeStruct((dim + 1, 8, hits), f32),
         jax.ShapeDtypeStruct((dim + 1, 8, 128), f32),
     )
-    hit_sums, point_sums = pl.pallas_call(
-        near_kernel,
-        out_shape=partial_sums,
-        in_specs=[VMEM] * 5,
-        out_specs=(VMEM, VMEM),
-        compiler_params=PARAMS,
-        cost_estimate=pl.CostEstimate(
-            flops=200 * points * hits * ndev, bytes_accessed=ndev * hits * 64,
-            transcendentals=2 * points * hits * ndev,
-        ),
-        name="near_pairs",
-    )(pay_own, own, xb, yb, rows_all)
+
+    def pairs(rows, sums=()):
+        count = sum(r.shape[0] for r in rows)
+        return pl.pallas_call(
+            functools.partial(pair_kernel, len(rows)),
+            out_shape=partial_sums,
+            in_specs=[VMEM] * (4 + len(rows) + len(sums)),
+            out_specs=(VMEM, VMEM),
+            compiler_params=PARAMS,
+            cost_estimate=pl.CostEstimate(
+                flops=200 * points * hits * count, bytes_accessed=count * hits * 64,
+                transcendentals=2 * points * hits * count,
+            ),
+            name="pairs",
+        )(pay_own, own, xb, yb, *rows, *sums)
+
+    sums = pairs([rows_all, first_far, rows])
 
     blocks = 8
     block_rows = 2 * (layers * width // blocks) + 8
@@ -475,7 +481,7 @@
         ],
         compiler_params=PARAMS,
         name="pairs_backward",
-    )(pay_own, own, xb, yb, aux, slope, ht, last, wt, head, rows_far, hit_sums, point_sums)
+    )(pay_own, own, xb, yb, aux, slope, ht, last, wt, head, rows_far, *sums)
 
     total = keep + swap(send, core)
     mine = total[0]

time: 54.8 us -> 54.3 us (level)
  waiting for transfers between devices: 22.6 us -> 22 us
    ppermute x21 -> x22, waiting for transfers between devices: 22.6 us -> 22 us  [swap(): lax.ppermute(x, AXES, [(i, i ^ masks[i // core & 1]) for i in range(ndev)])]
    ppermute x21 -> x22, starting transfers between devices: 21.5 us -> 21.7 us  [swap(): lax.ppermute(x, AXES, [(i, i ^ masks[i // core & 1]) for i in range(ndev)])]
  transfers between devices with their start and end apart: 21 -> 22, of which waited for: 15 -> 15; matrix products, arithmetic and copies ran while one was open for 0% -> 0% of each run, Pallas kernels for 5% -> 5%
where the time goes in v7:
time: 54.3 us; the launch traced here: 54.1 us
  waiting for transfers between devices  22 us (41%)
  starting transfers between devices  21.7 us (40%)
  Pallas kernels  8.6 us (16%)
  local copies, waits for them, and re-layouts  0.83 us (2%)
  between operations  0.82 us (2%)
    ppermute x22, waiting for transfers between devices, swap(): lax.ppermute(x, AXES, [(i, i ^ masks[i // core & 1]) for i in range(ndev)])  22 us
    ppermute x22, starting transfers between devices, swap(): lax.ppermute(x, AXES, [(i, i ^ masks[i // core & 1]) for i in range(ndev)])  21.7 us
    pallas_call x1, Pallas kernels, on_device(): pl.pallas_call(functools.partial(embed_kernel, sizes), out_shape=(jax.Sha...  2.75 us
    pallas_call x1, Pallas kernels, on_device(): pl.pallas_call(functools.partial(backward_kernel, sizes, hits_all, points...  2 us
    pallas_call x1, Pallas kernels, pairs(): pl.pallas_call(functools.partial(pair_kernel, len(rows)), out_shape=parti...  1.38 us
  transfers between devices with their start and end apart: 22, of which 15 were waited for; matrix products, arithmetic and copies ran while one was open for 0% of the time, Pallas kernels for 5%

profile of v7, /device:TPU:0, one launch (start us, length us, event | category | flops | bytes accessed | tf_op | source)
XLA Modules:
  0.0 54.1 jit_solution(2798613913142958057)
XLA Ops:
  0.6 0.0 copy-start
  0.6 2.7 %embed.1 = (f32[24,256]{1,0:T(8,128)}, f32[16,256]{1,0:T(8,128)}) custom-call(s32[8]{0:T(128)} %hit_hbm.1, bf16[256,256]{1,0:T(8,128)(2,1)} %feat_ref, bf16[4,256,256]{2,1,0:T(8,128)(2,1)} %w_ref, f32[4,256]{1,0:T(4,128)} %b_ref, bf16[16,256]{1,0:T(8,128)(2,1)} %wc_ref.1, bf16[256]{0:T(256)(128)(2,1)} %wb_ref.1, s32[1,256]{1,0:T(1,128)} %bitcast.24, ...), custom_call_target="tpu_custom_call" | custom-call | tf_op jit(solution)/shard_map/embed/pallas_call | solution.py:376
  3.4 0.0 copy-start.1
  3.4 4.1 %collective-permute-start.2 = (f32[1,24,256]{2,1,0:T(8,128)}, f32[1,24,256]{2,1,0:T(8,128)S(1)}, u32[]{:S(2)}, u32[]{:S(2)}) collective-permute-start(f32[1,24,256]{2,1,0:T(8,128)} %bitcast.20), channel_id=1, source_target_pairs={{0,4},{1,5},{2,6},{3,7},{4,0},{5,1},{6,2},{7,3},{8,12},{9,13},{10,... | collective-permute-start | bytes 73736 | tf_op jit(solution)/shard_map/ppermute | solution.py:369
  7.5 1.3 %collective-permute-start.1 = (f32[1,24,256]{2,1,0:T(8,128)}, f32[1,24,256]{2,1,0:T(8,128)S(1)}, u32[]{:S(2)}, u32[]{:S(2)}) collective-permute-start(f32[1,24,256]{2,1,0:T(8,128)} %bitcast.21), channel_id=1, source_target_pairs={{0,6},{1,7},{2,4},{3,5},{4,2},{5,3},{6,0},{7,1},{8,14},{9,15},{10,... | collective-permute-start | bytes 73736 | tf_op jit(solution)/shard_map/ppermute | solution.py:369
  8.9 0.2 collective-permute-start
  9.1 0.0 copy-start.3
  9.1 0.8 %copy-done.3 = f32[24,256]{1,0:T(8,128)S(1)} copy-done((f32[24,256]{1,0:T(8,128)S(1)}, f32[24,256]{1,0:T(8,128)}, u32[]{:S(2)}) %copy-start.3) | copy-done | bytes 24600
  9.9 0.1 spread.1
  10.0 0.0 collective-permute-done.2
  10.0 3.4 %collective-permute-done.1 = f32[1,24,256]{2,1,0:T(8,128)S(1)} collective-permute-done((f32[1,24,256]{2,1,0:T(8,128)}, f32[1,24,256]{2,1,0:T(8,128)S(1)}, u32[]{:S(2)}, u32[]{:S(2)}) %collective-permute-start.1) | collective-permute-done | bytes 24608 | tf_op jit(solution)/shard_map/ppermute | solution.py:369
  13.3 0.0 collective-permute-done
  13.4 0.0 copy-start.2
  13.4 1.6 %collective-permute-start.5 = (f32[4,24,256]{2,1,0:T(8,128)S(1)}, f32[4,24,256]{2,1,0:T(8,128)S(1)}, u32[]{:S(2)}, u32[]{:S(2)}) collective-permute-start(f32[4,24,256]{2,1,0:T(8,128)S(1)} %pad_maximum_fusion.1.rest_0_), channel_id=1, source_target_pairs={{0,16},{1,17},{2,18},{3,19},{4,20},{5,21},{6,22},{7,23},{8,24},{9,... | collective-permute-start | bytes 294920 | tf_op jit(solution)/shard_map/ppermute | solution.py:369
  15.0 1.4 %collective-permute-start.4 = (f32[4,24,256]{2,1,0:T(8,128)S(1)}, f32[4,24,256]{2,1,0:T(8,128)S(1)}, u32[]{:S(2)}, u32[]{:S(2)}) collective-permute-start(f32[4,24,256]{2,1,0:T(8,128)S(1)} %pad_maximum_fusion.1.rest_0_), channel_id=1, source_target_pairs={{0,17},{1,16},{2,19},{3,18},{4,21},{5,20},{6,23},{7,22},{8,25},{9,... | collective-permute-start | bytes 294920 | tf_op jit(solution)/shard_map/ppermute | solution.py:369
  16.4 0.5 collective-permute-start.3
  16.9 0.0 collective-permute-start.6
  16.9 0.0 copy-done
  16.9 0.0 copy-done.1
  16.9 0.0 copy-done.2
  17.0 0.0 copy-done.5
  17.0 0.0 copy-done.6
  17.0 0.6 %residuals.1 = (f32[4,256,256]{2,1,0:T(8,128)S(1)}, bf16[4,256,256]{2,1,0:T(8,128)(2,1)S(1)}, bf16[256,256]{1,0:T(8,128)(2,1)S(1)}, bf16[3,256,256]{2,1,0:T(8,128)(2,1)S(1)}, bf16[32,256]{1,0:T(8,128)(2,1)S(1)}) custom-call(bf16[256,256]{1,0:T(8,128)(2,1)S(1)} %copy-done.1, bf16[4,256,256]{2,1,0:T(8,128)(2,1)S(1)} %copy-done, f32[4,256]{1,0:T(4,128)S(1)} %copy-done.5, ...), custom_call_target="tpu_custom_call" | custom-call | flops 5242880 | bytes 1572864 | tf_op jit(solution)/shard_map/residuals/pallas_call | solution.py:400
  17.6 1.1 %collective-permute-done.5 = f32[4,24,256]{2,1,0:T(8,128)S(1)} collective-permute-done((f32[4,24,256]{2,1,0:T(8,128)S(1)}, f32[4,24,256]{2,1,0:T(8,128)S(1)}, u32[]{:S(2)}, u32[]{:S(2)}) %collective-permute-start.5) | collective-permute-done | bytes 98336 | tf_op jit(solution)/shard_map/ppermute | solution.py:369
  18.7 1.8 %collective-permute-done.4 = f32[4,24,256]{2,1,0:T(8,128)S(1)} collective-permute-done((f32[4,24,256]{2,1,0:T(8,128)S(1)}, f32[4,24,256]{2,1,0:T(8,128)S(1)}, u32[]{:S(2)}, u32[]{:S(2)}) %collective-permute-start.4) | collective-permute-done | bytes 98336 | tf_op jit(solution)/shard_map/ppermute | solution.py:369
  20.5 0.5 collective-permute-done.3
  21.0 0.0 collective-permute-done.6.rest_1_
  21.1 0.1 collective-permute-start.7
  21.1 0.0 copy-start.4
  21.1 1.4 %pairs.1 = (f32[17,8,256]{2,1,0:T(8,128)S(1)}, f32[17,8,128]{2,1,0:T(8,128)S(1)}) custom-call(f32[24,256]{1,0:T(8,128)S(1)} %get-tuple-element.35.pay_ref, f32[8,128]{1,0:T(8,128)S(1)} %get-tuple-element.36.own_ref, f32[16,8,256]{2,1,0:T(8,128)S(1)} %get-tuple-element.37.xb, f32[16,8,256]{2,1,0:T(8,128)S(1)} %get-tuple-element.38.yb, ...), custom_call_target="tpu_custom_call" | custom-call | flops 8192000 | bytes 327680 | tf_op jit(solution)/shard_map/pairs/pallas_call | solution.py:454
  22.5 0.2 collective-permute-done.7.rows_ref
  22.7 0.0 copy-done.4
  22.7 2.0 %pairs_backward.1 = (f32[4,264,128]{2,1,0:T(8,128)S(1)}, f32[4,264,128]{2,1,0:T(8,128)S(1)}) custom-call(f32[24,256]{1,0:T(8,128)S(1)} %get-tuple-element.35.pay_ref, f32[8,128]{1,0:T(8,128)S(1)} %get-tuple-element.36.own_ref, f32[16,8,256]{2,1,0:T(8,128)S(1)} %get-tuple-element.37.xb, f32[16,8,256]{2,1,0:T(8,128)S(1)} %get-tuple-element.38.yb, ...), custom_call_target="tpu_custom_call" | custom-call | tf_op jit(solution)/shard_map/pairs_backward/pallas_call | solution.py:472
  24.7 0.4 collective-permute-start.8
  25.1 1.6 %collective-permute-done.8 = f32[4,264,128]{2,1,0:T(8,128)S(1)} collective-permute-done((f32[4,264,128]{2,1,0:T(8,128)S(1)}, f32[4,264,128]{2,1,0:T(8,128)S(1)}, u32[]{:S(2)}, u32[]{:S(2)}) %collective-permute-start.8) | collective-permute-done | bytes 540704 | tf_op jit(solution)/shard_map/ppermute | solution.py:369
  26.7 0.1 add.21
  26.8 2.1 %collective-permute-start.11 = (f32[264,128]{1,0:T(8,128)S(1)}, f32[264,128]{1,0:T(8,128)S(1)}, u32[]{:S(2)}, u32[]{:S(2)}) collective-permute-start(f32[264,128]{1,0:T(8,128)S(1)} %get-tuple-element.63), channel_id=1, source_target_pairs={{0,17},{1,16},{2,19},{3,18},{4,21},{5,20},{6,23},{7,22},{8,14},{9,... | collective-permute-start | bytes 405512 | tf_op jit(solution)/shard_map/ppermute | solution.py:369
  28.9 0.5 collective-permute-start.10
  29.4 1.0 %collective-permute-start.9 = (f32[264,128]{1,0:T(8,128)S(1)}, f32[264,128]{1,0:T(8,128)S(1)}, u32[]{:S(2)}, u32[]{:S(2)}) collective-permute-start(f32[264,128]{1,0:T(8,128)S(1)} %get-tuple-element.65), channel_id=1, source_target_pairs={{0,1},{1,0},{2,3},{3,2},{4,5},{5,4},{6,7},{7,6},{8,10},{9,11},{10,... | collective-permute-start | bytes 405512 | tf_op jit(solution)/shard_map/ppermute | solution.py:369
  30.4 2.5 %collective-permute-done.11 = f32[264,128]{1,0:T(8,128)S(1)} collective-permute-done((f32[264,128]{1,0:T(8,128)S(1)}, f32[264,128]{1,0:T(8,128)S(1)}, u32[]{:S(2)}, u32[]{:S(2)}) %collective-permute-start.11) | collective-permute-done | bytes 135200 | tf_op jit(solution)/shard_map/ppermute | solution.py:369
  32.8 1.4 %collective-permute-done.10 = f32[264,128]{1,0:T(8,128)S(1)} collective-permute-done((f32[264,128]{1,0:T(8,128)S(1)}, f32[264,128]{1,0:T(8,128)S(1)}, u32[]{:S(2)}, u32[]{:S(2)}) %collective-permute-start.10) | collective-permute-done | bytes 135200 | tf_op jit(solution)/shard_map/ppermute | solution.py:369
  34.2 0.2 collective-permute-done.9
  34.4 2.1 %collective-permute-start.14 = (f32[264,128]{1,0:T(8,128)S(1)}, f32[264,128]{1,0:T(8,128)S(1)}, u32[]{:S(2)}, u32[]{:S(2)}) collective-permute-start(f32[264,128]{1,0:T(8,128)S(1)} %fusion.1), channel_id=1, source_target_pairs={{0,6},{1,7},{2,4},{3,5},{4,2},{5,3},{6,0},{7,1},{8,25},{9,24},{10,... | collective-permute-start | bytes 405512 | tf_op jit(solution)/shard_map/ppermute | solution.py:369
  36.5 0.0 collective-permute-start.13
  36.5 2.4 %collective-permute-start.12 = (f32[264,128]{1,0:T(8,128)S(1)}, f32[264,128]{1,0:T(8,128)S(1)}, u32[]{:S(2)}, u32[]{:S(2)}) collective-permute-start(f32[264,128]{1,0:T(8,128)S(1)} %fusion.1), channel_id=1, source_target_pairs={{0,4},{1,5},{2,6},{3,7},{4,0},{5,1},{6,2},{7,3},{8,24},{9,25},{10,... | collective-permute-start | bytes 405512 | tf_op jit(solution)/shard_map/ppermute | solution.py:369
  38.9 2.6 %collective-permute-done.14 = f32[264,128]{1,0:T(8,128)S(1)} collective-permute-done((f32[264,128]{1,0:T(8,128)S(1)}, f32[264,128]{1,0:T(8,128)S(1)}, u32[]{:S(2)}, u32[]{:S(2)}) %collective-permute-start.14) | collective-permute-done | bytes 135200 | tf_op jit(solution)/shard_map/ppermute | solution.py:369
  41.5 2.8 %collective-permute-done.13 = f32[264,128]{1,0:T(8,128)S(1)} collective-permute-done((f32[264,128]{1,0:T(8,128)S(1)}, f32[264,128]{1,0:T(8,128)S(1)}, u32[]{:S(2)}, u32[]{:S(2)}) %collective-permute-start.13) | collective-permute-done | bytes 135200 | tf_op jit(solution)/shard_map/ppermute | solution.py:369
  44.2 0.0 collective-permute-done.12
  44.3 2.0 %collective-permute-start.20 = (f32[264,128]{1,0:T(8,128)S(1)}, f32[264,128]{1,0:T(8,128)S(1)}, u32[]{:S(2)}, u32[]{:S(2)}) collective-permute-start(f32[264,128]{1,0:T(8,128)S(1)} %add_add_fusion.refs_0_), channel_id=1, source_target_pairs={{0,17},{1,16},{2,19},{3,18},{4,21},{5,20},{6,23},{7,22},{8,14},{9,... | collective-permute-start | bytes 405512 | tf_op jit(solution)/shard_map/ppermute | solution.py:369
  46.2 0.5 collective-permute-start.18
  46.8 1.1 %collective-permute-start.16 = (f32[264,128]{1,0:T(8,128)S(1)}, f32[264,128]{1,0:T(8,128)S(1)}, u32[]{:S(2)}, u32[]{:S(2)}) collective-permute-start(f32[264,128]{1,0:T(8,128)S(1)} %add_add_fusion.refs_0_), channel_id=1, source_target_pairs={{0,1},{1,0},{2,3},{3,2},{4,5},{5,4},{6,7},{7,6},{8,10},{9,11},{10,... | collective-permute-start | bytes 405512 | tf_op jit(solution)/shard_map/ppermute | solution.py:369
  47.8 0.0 collective-permute-start.15
  47.8 2.5 %collective-permute-done.20.refs_3_ = f32[264,128]{1,0:T(8,128)S(1)} collective-permute-done((f32[264,128]{1,0:T(8,128)S(1)}, f32[264,128]{1,0:T(8,128)S(1)}, u32[]{:S(2)}, u32[]{:S(2)}) %collective-permute-start.20) | collective-permute-done | bytes 135200 | tf_op jit(solution)/shard_map/ppermute | solution.py:369
  50.3 0.0 collective-permute-start.21
  50.3 1.4 %collective-permute-done.18.refs_2_ = f32[264,128]{1,0:T(8,128)S(1)} collective-permute-done((f32[264,128]{1,0:T(8,128)S(1)}, f32[264,128]{1,0:T(8,128)S(1)}, u32[]{:S(2)}, u32[]{:S(2)}) %collective-permute-start.18) | collective-permute-done | bytes 135200 | tf_op jit(solution)/shard_map/ppermute | solution.py:369
  51.7 0.0 collective-permute-start.19
  51.7 0.1 collective-permute-done.16.refs_1_
  51.8 0.4 collective-permute-start.17
  52.2 0.8 %place_near.1 = (f32[8,128,256]{2,1,0:T(8,128)}, f32[4,8,128]{2,1,0:T(8,128)S(1)}) custom-call(f32[264,128]{1,0:T(8,128)S(1)} %add_add_fusion.refs_0_, f32[264,128]{1,0:T(8,128)S(1)} %collective-permute-done.16.refs_1_, f32[264,128]{1,0:T(8,128)S(1)} %collective-permute-done.18.refs_2_, f32[264,128]{1,0:T(8,128)S(1)} %collective-permute-done.20.refs_3_), custom_call_target="tpu_custom_call" | custom-call | bytes 1048576 | tf_op jit(solution)/shard_map/place_near/pallas_call | solution.py:498
  53.1 0.0 collective-permute-done.15.refs_0_
  53.1 0.0 collective-permute-done.21.refs_3_
  53.1 0.0 collective-permute-done.19.refs_2_
  53.1 0.1 collective-permute-done.17.refs_1_
  53.2 0.9 %place_far.1 = (f32[8,128,256]{2,1,0:T(8,128)}, f32[4,256]{1,0:T(4,128)}, f32[16,256]{1,0:T(8,128)}, f32[1,256]{1,0:T(1,128)}, f32[1,1]{1,0:T(1,128)}) custom-call(f32[264,128]{1,0:T(8,128)S(1)} %collective-permute-done.15.refs_0_, f32[264,128]{1,0:T(8,128)S(1)} %collective-permute-done.17.refs_1_, ...), custom_call_target="tpu_custom_call", output_to_operand_aliasing={{0}: (5, {})} | custom-call | tf_op jit(solution)/shard_map/place_far/pallas_call | solution.py:508
  (7 shorter events, 0.1 us)
Async XLA Ops:
  0.6 16.3 %copy-start = (bf16[4,256,256]{2,1,0:T(8,128)(2,1)S(1)}, bf16[4,256,256]{2,1,0:T(8,128)(2,1)}, u32[]{:S(2)}) copy-start(bf16[4,256,256]{2,1,0:T(8,128)(2,1)} %w_ref) | copy-start | bytes 1572868
  3.4 13.5 %copy-start.1 = (bf16[256,256]{1,0:T(8,128)(2,1)S(1)}, bf16[256,256]{1,0:T(8,128)(2,1)}, u32[]{:S(2)}) copy-start(bf16[256,256]{1,0:T(8,128)(2,1)} %feat_ref) | copy-start | bytes 393220
  3.4 6.5 %collective-permute-start.2 = (f32[1,24,256]{2,1,0:T(8,128)}, f32[1,24,256]{2,1,0:T(8,128)S(1)}, u32[]{:S(2)}, u32[]{:S(2)}) collective-permute-start(f32[1,24,256]{2,1,0:T(8,128)} %bitcast.20), channel_id=1, source_target_pairs={{0,4},{1,5},{2,6},{3,7},{4,0},{5,1},{6,2},{7,3},{8,12},{9,13},{10,... | collective-permute-start | bytes 73736 | tf_op jit(solution)/shard_map/ppermute | solution.py:369
  7.5 5.8 %collective-permute-start.1 = (f32[1,24,256]{2,1,0:T(8,128)}, f32[1,24,256]{2,1,0:T(8,128)S(1)}, u32[]{:S(2)}, u32[]{:S(2)}) collective-permute-start(f32[1,24,256]{2,1,0:T(8,128)} %bitcast.21), channel_id=1, source_target_pairs={{0,6},{1,7},{2,4},{3,5},{4,2},{5,3},{6,0},{7,1},{8,14},{9,15},{10,... | collective-permute-start | bytes 73736 | tf_op jit(solution)/shard_map/ppermute | solution.py:369
  8.9 4.5 %collective-permute-start = (f32[1,24,256]{2,1,0:T(8,128)}, f32[1,24,256]{2,1,0:T(8,128)S(1)}, u32[]{:S(2)}, u32[]{:S(2)}) collective-permute-start(f32[1,24,256]{2,1,0:T(8,128)} %bitcast.22), channel_id=1, source_target_pairs={{0,2},{1,3},{2,0},{3,1},{4,6},{5,7},{6,4},{7,5},{8,10},{9,11},{10,... | collective-permute-start | bytes 73736 | tf_op jit(solution)/shard_map/ppermute | solution.py:369
  9.1 0.8 %copy-start.3 = (f32[24,256]{1,0:T(8,128)S(1)}, f32[24,256]{1,0:T(8,128)}, u32[]{:S(2)}) copy-start(f32[24,256]{1,0:T(8,128)} %get-tuple-element.34.pay_ref) | copy-start | bytes 73732
  13.4 3.6 %copy-start.2 = (bf16[16,256]{1,0:T(8,128)(2,1)S(1)}, bf16[16,256]{1,0:T(8,128)(2,1)}, u32[]{:S(2)}) copy-start(bf16[16,256]{1,0:T(8,128)(2,1)} %wc_ref.1) | copy-start | bytes 24580
  13.4 3.6 %copy-start.5 = (f32[4,256]{1,0:T(4,128)S(1)}, f32[4,256]{1,0:T(4,128)}, u32[]{:S(2)}) copy-start(f32[4,256]{1,0:T(4,128)} %b_ref) | copy-start | bytes 12292
  13.4 3.6 %copy-start.6 = (bf16[256]{0:T(256)(128)(2,1)S(1)}, bf16[256]{0:T(256)(128)(2,1)}, u32[]{:S(2)}) copy-start(bf16[256]{0:T(256)(128)(2,1)} %wb_ref.1) | copy-start | bytes 1540
  13.4 5.3 %collective-permute-start.5 = (f32[4,24,256]{2,1,0:T(8,128)S(1)}, f32[4,24,256]{2,1,0:T(8,128)S(1)}, u32[]{:S(2)}, u32[]{:S(2)}) collective-permute-start(f32[4,24,256]{2,1,0:T(8,128)S(1)} %pad_maximum_fusion.1.rest_0_), channel_id=1, source_target_pairs={{0,16},{1,17},{2,18},{3,19},{4,20},{5,21},{6,22},{7,23},{8,24},{9,... | collective-permute-start | bytes 294920 | tf_op jit(solution)/shard_map/ppermute | solution.py:369
  15.0 5.5 %collective-permute-start.4 = (f32[4,24,256]{2,1,0:T(8,128)S(1)}, f32[4,24,256]{2,1,0:T(8,128)S(1)}, u32[]{:S(2)}, u32[]{:S(2)}) collective-permute-start(f32[4,24,256]{2,1,0:T(8,128)S(1)} %pad_maximum_fusion.1.rest_0_), channel_id=1, source_target_pairs={{0,17},{1,16},{2,19},{3,18},{4,21},{5,20},{6,23},{7,22},{8,25},{9,... | collective-permute-start | bytes 294920 | tf_op jit(solution)/shard_map/ppermute | solution.py:369
  16.4 4.6 %collective-permute-start.3 = (f32[4,24,256]{2,1,0:T(8,128)S(1)}, f32[4,24,256]{2,1,0:T(8,128)S(1)}, u32[]{:S(2)}, u32[]{:S(2)}) collective-permute-start(f32[4,24,256]{2,1,0:T(8,128)S(1)} %pad_maximum_fusion.1.rest_0_), channel_id=1, source_target_pairs={{0,1},{1,0},{2,3},{3,2},{4,5},{5,4},{6,7},{7,6},{8,9},{9,8},{10,11... | collective-permute-start | bytes 294920 | tf_op jit(solution)/shard_map/ppermute | solution.py:369
  16.9 4.1 %collective-permute-start.6 = (f32[4,24,256]{2,1,0:T(8,128)S(1)}, f32[4,24,256]{2,1,0:T(8,128)S(1)}, u32[]{:S(2)}, u32[]{:S(2)}) collective-permute-start(f32[4,24,256]{2,1,0:T(8,128)S(1)} %pad_maximum_fusion.1.rest_0_), channel_id=1, source_target_pairs={{0,8},{1,9},{2,10},{3,11},{4,12},{5,13},{6,14},{7,15},{8,0},{9,1},... | collective-permute-start | bytes 294920 | tf_op jit(solution)/shard_map/ppermute | solution.py:369
  21.1 1.6 %collective-permute-start.7 = (f32[12,24,256]{2,1,0:T(8,128)S(1)}, f32[12,24,256]{2,1,0:T(8,128)S(1)}, u32[]{:S(2)}, u32[]{:S(2)}) collective-permute-start(f32[12,24,256]{2,1,0:T(8,128)S(1)} %pad_maximum_fusion.rest_2_), channel_id=1, source_target_pairs={{0,8},{1,9},{2,10},{3,11},{4,12},{5,13},{6,14},{7,15},{8,0},{9,1},... | collective-permute-start | bytes 884744 | tf_op jit(solution)/shard_map/ppermute | solution.py:369
  21.1 1.6 %copy-start.4 = (f32[16,256]{1,0:T(8,128)S(1)}, f32[16,256]{1,0:T(8,128)}, u32[]{:S(2)}) copy-start(f32[16,256]{1,0:T(8,128)} %get-tuple-element.39.aux_ref) | copy-start | bytes 49156
  24.7 2.0 %collective-permute-start.8 = (f32[4,264,128]{2,1,0:T(8,128)S(1)}, f32[4,264,128]{2,1,0:T(8,128)S(1)}, u32[]{:S(2)}, u32[]{:S(2)}) collective-permute-start(f32[4,264,128]{2,1,0:T(8,128)S(1)} %get-tuple-element.55), channel_id=1, source_target_pairs={{0,8},{1,9},{2,10},{3,11},{4,12},{5,13},{6,14},{7,15},{8,0},{9,1},... | collective-permute-start | bytes 1622024 | tf_op jit(solution)/shard_map/ppermute | solution.py:369
  26.8 6.0 %collective-permute-start.11 = (f32[264,128]{1,0:T(8,128)S(1)}, f32[264,128]{1,0:T(8,128)S(1)}, u32[]{:S(2)}, u32[]{:S(2)}) collective-permute-start(f32[264,128]{1,0:T(8,128)S(1)} %get-tuple-element.63), channel_id=1, source_target_pairs={{0,17},{1,16},{2,19},{3,18},{4,21},{5,20},{6,23},{7,22},{8,14},{9,... | collective-permute-start | bytes 405512 | tf_op jit(solution)/shard_map/ppermute | solution.py:369
  28.9 5.4 %collective-permute-start.10 = (f32[264,128]{1,0:T(8,128)S(1)}, f32[264,128]{1,0:T(8,128)S(1)}, u32[]{:S(2)}, u32[]{:S(2)}) collective-permute-start(f32[264,128]{1,0:T(8,128)S(1)} %get-tuple-element.64), channel_id=1, source_target_pairs={{0,16},{1,17},{2,18},{3,19},{4,20},{5,21},{6,22},{7,23},{8,12},{9,... | collective-permute-start | bytes 405512 | tf_op jit(solution)/shard_map/ppermute | solution.py:369
  29.4 5.0 %collective-permute-start.9 = (f32[264,128]{1,0:T(8,128)S(1)}, f32[264,128]{1,0:T(8,128)S(1)}, u32[]{:S(2)}, u32[]{:S(2)}) collective-permute-start(f32[264,128]{1,0:T(8,128)S(1)} %get-tuple-element.65), channel_id=1, source_target_pairs={{0,1},{1,0},{2,3},{3,2},{4,5},{5,4},{6,7},{7,6},{8,10},{9,11},{10,... | collective-permute-start | bytes 405512 | tf_op jit(solution)/shard_map/ppermute | solution.py:369
  34.4 7.0 %collective-permute-start.14 = (f32[264,128]{1,0:T(8,128)S(1)}, f32[264,128]{1,0:T(8,128)S(1)}, u32[]{:S(2)}, u32[]{:S(2)}) collective-permute-start(f32[264,128]{1,0:T(8,128)S(1)} %fusion.1), channel_id=1, source_target_pairs={{0,6},{1,7},{2,4},{3,5},{4,2},{5,3},{6,0},{7,1},{8,25},{9,24},{10,... | collective-permute-start | bytes 405512 | tf_op jit(solution)/shard_map/ppermute | solution.py:369
  36.5 7.7 %collective-permute-start.13 = (f32[264,128]{1,0:T(8,128)S(1)}, f32[264,128]{1,0:T(8,128)S(1)}, u32[]{:S(2)}, u32[]{:S(2)}) collective-permute-start(f32[264,128]{1,0:T(8,128)S(1)} %fusion.1), channel_id=1, source_target_pairs={{0,2},{1,3},{2,0},{3,1},{4,6},{5,7},{6,4},{7,5},{8,9},{9,8},{10,11... | collective-permute-start | bytes 405512 | tf_op jit(solution)/shard_map/ppermute | solution.py:369
  36.5 7.7 %collective-permute-start.12 = (f32[264,128]{1,0:T(8,128)S(1)}, f32[264,128]{1,0:T(8,128)S(1)}, u32[]{:S(2)}, u32[]{:S(2)}) collective-permute-start(f32[264,128]{1,0:T(8,128)S(1)} %fusion.1), channel_id=1, source_target_pairs={{0,4},{1,5},{2,6},{3,7},{4,0},{5,1},{6,2},{7,3},{8,24},{9,25},{10,... | collective-permute-start | bytes 405512 | tf_op jit(solution)/shard_map/ppermute | solution.py:369
  44.3 6.0 %collective-permute-start.20 = (f32[264,128]{1,0:T(8,128)S(1)}, f32[264,128]{1,0:T(8,128)S(1)}, u32[]{:S(2)}, u32[]{:S(2)}) collective-permute-start(f32[264,128]{1,0:T(8,128)S(1)} %add_add_fusion.refs_0_), channel_id=1, source_target_pairs={{0,17},{1,16},{2,19},{3,18},{4,21},{5,20},{6,23},{7,22},{8,14},{9,... | collective-permute-start | bytes 405512 | tf_op jit(solution)/shard_map/ppermute | solution.py:369
  46.2 5.4 %collective-permute-start.18 = (f32[264,128]{1,0:T(8,128)S(1)}, f32[264,128]{1,0:T(8,128)S(1)}, u32[]{:S(2)}, u32[]{:S(2)}) collective-permute-start(f32[264,128]{1,0:T(8,128)S(1)} %add_add_fusion.refs_0_), channel_id=1, source_target_pairs={{0,16},{1,17},{2,18},{3,19},{4,20},{5,21},{6,22},{7,23},{8,12},{9,... | collective-permute-start | bytes 405512 | tf_op jit(solution)/shard_map/ppermute | solution.py:369
  46.8 5.0 %collective-permute-start.16 = (f32[264,128]{1,0:T(8,128)S(1)}, f32[264,128]{1,0:T(8,128)S(1)}, u32[]{:S(2)}, u32[]{:S(2)}) collective-permute-start(f32[264,128]{1,0:T(8,128)S(1)} %add_add_fusion.refs_0_), channel_id=1, source_target_pairs={{0,1},{1,0},{2,3},{3,2},{4,5},{5,4},{6,7},{7,6},{8,10},{9,11},{10,... | collective-permute-start | bytes 405512 | tf_op jit(solution)/shard_map/ppermute | solution.py:369
  47.8 5.2 %collective-permute-start.15 = (f32[264,128]{1,0:T(8,128)S(1)}, f32[264,128]{1,0:T(8,128)S(1)}, u32[]{:S(2)}, u32[]{:S(2)}) collective-permute-start(f32[264,128]{1,0:T(8,128)S(1)} %add_add_fusion.refs_0_), channel_id=1, source_target_pairs={{0,8},{1,9},{2,10},{3,11},{4,12},{5,13},{6,14},{7,15},{8,0},{9,1},... | collective-permute-start | bytes 405512 | tf_op jit(solution)/shard_map/ppermute | solution.py:369
  50.3 2.8 %collective-permute-start.21 = (f32[264,128]{1,0:T(8,128)S(1)}, f32[264,128]{1,0:T(8,128)S(1)}, u32[]{:S(2)}, u32[]{:S(2)}) collective-permute-start(f32[264,128]{1,0:T(8,128)S(1)} %collective-permute-done.20.refs_3_), channel_id=1, source_target_pairs={{0,8},{1,9},{2,10},{3,11},{4,12},{5,13},{6,14},{7,15},{8,0},{9,1},... | collective-permute-start | bytes 405512 | tf_op jit(solution)/shard_map/ppermute | solution.py:369
  51.7 1.4 %collective-permute-start.19 = (f32[264,128]{1,0:T(8,128)S(1)}, f32[264,128]{1,0:T(8,128)S(1)}, u32[]{:S(2)}, u32[]{:S(2)}) collective-permute-start(f32[264,128]{1,0:T(8,128)S(1)} %collective-permute-done.18.refs_2_), channel_id=1, source_target_pairs={{0,8},{1,9},{2,10},{3,11},{4,12},{5,13},{6,14},{7,15},{8,0},{9,1},... | collective-permute-start | bytes 405512 | tf_op jit(solution)/shard_map/ppermute | solution.py:369
  51.8 1.5 %collective-permute-start.17 = (f32[264,128]{1,0:T(8,128)S(1)}, f32[264,128]{1,0:T(8,128)S(1)}, u32[]{:S(2)}, u32[]{:S(2)}) collective-permute-start(f32[264,128]{1,0:T(8,128)S(1)} %collective-permute-done.16.refs_1_), channel_id=1, source_target_pairs={{0,8},{1,9},{2,10},{3,11},{4,12},{5,13},{6,14},{7,15},{8,0},{9,1},... | collective-permute-start | bytes 405512 | tf_op jit(solution)/shard_map/ppermute | solution.py:369

commit v8 on v7

--- a/solution.py
+++ b/solution.py
@@ -11,6 +11,7 @@
 charge_floor = 0.5
 AXES = ("layer", "phi")
 VMEM = pl.BlockSpec(memory_space=pltpu.VMEM)
+SMEM = pl.BlockSpec(memory_space=pltpu.SMEM)
 HBM = pl.BlockSpec(memory_space=pltpu.HBM)
 UNROLL = 16
 EMBED_VMEM = 63400000
@@ -52,29 +53,16 @@
 
 def embed_kernel(
     sizes,
-    hit_hbm, feat_hbm, w_hbm, b_hbm, wc_hbm, wb_hbm, track_hbm, noise_hbm,
-    pay_ref, aux_ref,
-    hit_ref, feat_ref, w_ref, b_ref, wc_ref, wb_ref, track_ref, noise_ref, sems,
+    hit_ref, feat_ref, w_ref, b_ref, wc_ref, wb_ref, track_ref, noise_ref, pay_ref, aux_ref,
 ):
     dim = wc_ref.shape[0]
     hits = feat_ref.shape[0]
     points = hit_ref.shape[0]
     layers = w_ref.shape[0]
-    pairs = [(feat_hbm, feat_ref), (w_hbm, w_ref), (b_hbm, b_ref), (wc_hbm, wc_ref), (wb_hbm, wb_ref)]
-    pairs += [(track_hbm, track_ref), (noise_hbm, noise_ref), (hit_hbm, hit_ref)]
-    copies = [
-        pltpu.make_async_copy(src, dst, sems.at[i]) for i, (src, dst) in enumerate(pairs)
-    ]
-    for copy in copies:
-        copy.start()
-    for copy in copies[:3]:
-        copy.wait()
     h = feat_ref[...]
     for l in range(layers):
         a = matmul(h, w_ref[l]) + b_ref[l : l + 1, :]
         h = (a * jax.nn.sigmoid(a)).astype(jnp.bfloat16)
-    for copy in copies[3:]:
-        copy.wait()
     xz = matmul(head_rows(wc_ref, wb_ref), h, 1, 1)
     z = xz[dim : dim + 1]
     expz = jnp.exp(z)
@@ -379,19 +367,8 @@
             jax.ShapeDtypeStruct((dim + 8, hits), f32),
             jax.ShapeDtypeStruct((16, hits), f32),
         ),
-        in_specs=[HBM] * 8,
+        in_specs=[SMEM] + [VMEM] * 7,
         out_specs=(VMEM,) * 2,
-        scratch_shapes=[
-            pltpu.SMEM((points,), jnp.int32),
-            pltpu.VMEM((hits, width), low),
-            pltpu.VMEM((layers, width, width), low),
-            pltpu.VMEM((layers, width), f32),
-            pltpu.VMEM((dim, width), low),
-            pltpu.VMEM(w_beta.shape, low),
-            pltpu.VMEM((1, hits), jnp.int32),
-            pltpu.VMEM((1, hits), jnp.int32),
-            pltpu.SemaphoreType.DMA((8,)),
-        ],
         compiler_params=pltpu.CompilerParams(vmem_limit_bytes=EMBED_VMEM),
         name="embed",
     )(point_hit, features, w_layers, b_layers, w_coord, w_beta, track, noise)

time: 54.3 us -> 54.1 us (level)
  no operation moved by 1% of the time
where the time goes in v8:
time: 54.1 us; the launch traced here: 53.9 us
  waiting for transfers between devices  22 us (41%)
  starting transfers between devices  21.6 us (40%)
  Pallas kernels  8.46 us (16%)
  local copies, waits for them, and re-layouts  0.82 us (2%)
  between operations  0.81 us (1%)
    ppermute x22, waiting for transfers between devices, swap(): lax.ppermute(x, AXES, [(i, i ^ masks[i // core & 1]) for i in range(ndev)])  22 us
    ppermute x22, starting transfers between devices, swap(): lax.ppermute(x, AXES, [(i, i ^ masks[i // core & 1]) for i in range(ndev)])  21.6 us
    pallas_call x1, Pallas kernels, on_device(): pl.pallas_call(functools.partial(embed_kernel, sizes), out_shape=(jax.Sha...  2.6 us
    pallas_call x1, Pallas kernels, on_device(): pl.pallas_call(functools.partial(backward_kernel, sizes, hits_all, points...  2 us
    pallas_call x1, Pallas kernels, pairs(): pl.pallas_call(functools.partial(pair_kernel, len(rows)), out_shape=parti...  1.38 us
  transfers between devices with their start and end apart: 22, of which 15 were waited for; matrix products, arithmetic and copies ran while one was open for 0% of the time, Pallas kernels for 5%

profile of v8, /device:TPU:0, one launch (start us, length us, event | category | flops | bytes accessed | tf_op | source)
XLA Modules:
  0.0 53.9 jit_solution(3482669864504989182)
XLA Ops:
  0.6 0.0 copy-start
  0.6 2.6 %embed.1 = (f32[24,256]{1,0:T(8,128)}, f32[16,256]{1,0:T(8,128)}) custom-call(s32[8]{0:T(128)} %hit_ref.1, bf16[256,256]{1,0:T(8,128)(2,1)} %feat_ref.2, bf16[4,256,256]{2,1,0:T(8,128)(2,1)} %w_ref.2, f32[4,256]{1,0:T(4,128)} %b_ref.2, bf16[16,256]{1,0:T(8,128)(2,1)} %wc_ref.3, bf16[256]{0:T(256)(128)(2,1)} %wb_ref.3, s32[1,256]{1,0:T(1,128)} %bitcast.24, ...), custom_call_target="tpu_custom_call" | custom-call | tf_op jit(solution)/shard_map/embed/pallas_call | solution.py:364
  3.2 4.0 %collective-permute-start.2 = (f32[1,24,256]{2,1,0:T(8,128)}, f32[1,24,256]{2,1,0:T(8,128)S(1)}, u32[]{:S(2)}, u32[]{:S(2)}) collective-permute-start(f32[1,24,256]{2,1,0:T(8,128)} %bitcast.20), channel_id=1, source_target_pairs={{0,4},{1,5},{2,6},{3,7},{4,0},{5,1},{6,2},{7,3},{8,12},{9,13},{10,... | collective-permute-start | bytes 73736 | tf_op jit(solution)/shard_map/ppermute | solution.py:357
  7.3 1.3 %collective-permute-start.1 = (f32[1,24,256]{2,1,0:T(8,128)}, f32[1,24,256]{2,1,0:T(8,128)S(1)}, u32[]{:S(2)}, u32[]{:S(2)}) collective-permute-start(f32[1,24,256]{2,1,0:T(8,128)} %bitcast.21), channel_id=1, source_target_pairs={{0,6},{1,7},{2,4},{3,5},{4,2},{5,3},{6,0},{7,1},{8,14},{9,15},{10,... | collective-permute-start | bytes 73736 | tf_op jit(solution)/shard_map/ppermute | solution.py:357
  8.6 0.2 collective-permute-start
  8.9 0.0 copy-start.3
  8.9 0.8 %copy-done.3 = f32[24,256]{1,0:T(8,128)S(1)} copy-done((f32[24,256]{1,0:T(8,128)S(1)}, f32[24,256]{1,0:T(8,128)}, u32[]{:S(2)}) %copy-start.3) | copy-done | bytes 24600
  9.6 0.1 spread.1
  9.7 0.0 collective-permute-done.2
  9.7 3.4 %collective-permute-done.1 = f32[1,24,256]{2,1,0:T(8,128)S(1)} collective-permute-done((f32[1,24,256]{2,1,0:T(8,128)}, f32[1,24,256]{2,1,0:T(8,128)S(1)}, u32[]{:S(2)}, u32[]{:S(2)}) %collective-permute-start.1) | collective-permute-done | bytes 24608 | tf_op jit(solution)/shard_map/ppermute | solution.py:357
  13.1 0.0 collective-permute-done
  13.1 0.0 copy-start.2
  13.1 0.0 copy-start.6
  13.2 1.6 %collective-permute-start.5 = (f32[4,24,256]{2,1,0:T(8,128)S(1)}, f32[4,24,256]{2,1,0:T(8,128)S(1)}, u32[]{:S(2)}, u32[]{:S(2)}) collective-permute-start(f32[4,24,256]{2,1,0:T(8,128)S(1)} %pad_maximum_fusion.1.rest_0_), channel_id=1, source_target_pairs={{0,16},{1,17},{2,18},{3,19},{4,20},{5,21},{6,22},{7,23},{8,24},{9,... | collective-permute-start | bytes 294920 | tf_op jit(solution)/shard_map/ppermute | solution.py:357
  14.7 1.4 %collective-permute-start.4 = (f32[4,24,256]{2,1,0:T(8,128)S(1)}, f32[4,24,256]{2,1,0:T(8,128)S(1)}, u32[]{:S(2)}, u32[]{:S(2)}) collective-permute-start(f32[4,24,256]{2,1,0:T(8,128)S(1)} %pad_maximum_fusion.1.rest_0_), channel_id=1, source_target_pairs={{0,17},{1,16},{2,19},{3,18},{4,21},{5,20},{6,23},{7,22},{8,25},{9,... | collective-permute-start | bytes 294920 | tf_op jit(solution)/shard_map/ppermute | solution.py:357
  16.2 0.5 collective-permute-start.3
  16.7 0.0 collective-permute-start.6
  16.7 0.0 copy-done
  16.7 0.0 copy-done.1
  16.7 0.0 copy-done.2
  16.7 0.0 copy-done.5
  16.7 0.0 copy-done.6
  16.8 0.6 %residuals.1 = (f32[4,256,256]{2,1,0:T(8,128)S(1)}, bf16[4,256,256]{2,1,0:T(8,128)(2,1)S(1)}, bf16[256,256]{1,0:T(8,128)(2,1)S(1)}, bf16[3,256,256]{2,1,0:T(8,128)(2,1)S(1)}, bf16[32,256]{1,0:T(8,128)(2,1)S(1)}) custom-call(bf16[256,256]{1,0:T(8,128)(2,1)S(1)} %copy-done.1, bf16[4,256,256]{2,1,0:T(8,128)(2,1)S(1)} %copy-done, f32[4,256]{1,0:T(4,128)S(1)} %copy-done.5, ...), custom_call_target="tpu_custom_call" | custom-call | flops 5242880 | bytes 1572864 | tf_op jit(solution)/shard_map/residuals/pallas_call | solution.py:377
  17.4 1.1 %collective-permute-done.5 = f32[4,24,256]{2,1,0:T(8,128)S(1)} collective-permute-done((f32[4,24,256]{2,1,0:T(8,128)S(1)}, f32[4,24,256]{2,1,0:T(8,128)S(1)}, u32[]{:S(2)}, u32[]{:S(2)}) %collective-permute-start.5) | collective-permute-done | bytes 98336 | tf_op jit(solution)/shard_map/ppermute | solution.py:357
  18.5 1.8 %collective-permute-done.4 = f32[4,24,256]{2,1,0:T(8,128)S(1)} collective-permute-done((f32[4,24,256]{2,1,0:T(8,128)S(1)}, f32[4,24,256]{2,1,0:T(8,128)S(1)}, u32[]{:S(2)}, u32[]{:S(2)}) %collective-permute-start.4) | collective-permute-done | bytes 98336 | tf_op jit(solution)/shard_map/ppermute | solution.py:357
  20.3 0.5 collective-permute-done.3
  20.8 0.0 collective-permute-done.6.rest_1_
  20.8 0.1 collective-permute-start.7
  20.9 0.0 copy-start.4
  20.9 1.4 %pairs.1 = (f32[17,8,256]{2,1,0:T(8,128)S(1)}, f32[17,8,128]{2,1,0:T(8,128)S(1)}) custom-call(f32[24,256]{1,0:T(8,128)S(1)} %get-tuple-element.35.pay_ref, f32[8,128]{1,0:T(8,128)S(1)} %get-tuple-element.36.own_ref, f32[16,8,256]{2,1,0:T(8,128)S(1)} %get-tuple-element.37.xb, f32[16,8,256]{2,1,0:T(8,128)S(1)} %get-tuple-element.38.yb, ...), custom_call_target="tpu_custom_call" | custom-call | flops 8192000 | bytes 327680 | tf_op jit(solution)/shard_map/pairs/pallas_call | solution.py:431
  22.3 0.2 collective-permute-done.7.rows_ref
  22.5 0.0 copy-done.4
  22.5 2.0 %pairs_backward.1 = (f32[4,264,128]{2,1,0:T(8,128)S(1)}, f32[4,264,128]{2,1,0:T(8,128)S(1)}) custom-call(f32[24,256]{1,0:T(8,128)S(1)} %get-tuple-element.35.pay_ref, f32[8,128]{1,0:T(8,128)S(1)} %get-tuple-element.36.own_ref, f32[16,8,256]{2,1,0:T(8,128)S(1)} %get-tuple-element.37.xb, f32[16,8,256]{2,1,0:T(8,128)S(1)} %get-tuple-element.38.yb, ...), custom_call_target="tpu_custom_call" | custom-call | tf_op jit(solution)/shard_map/pairs_backward/pallas_call | solution.py:449
  24.5 0.4 collective-permute-start.8
  24.9 1.6 %collective-permute-done.8 = f32[4,264,128]{2,1,0:T(8,128)S(1)} collective-permute-done((f32[4,264,128]{2,1,0:T(8,128)S(1)}, f32[4,264,128]{2,1,0:T(8,128)S(1)}, u32[]{:S(2)}, u32[]{:S(2)}) %collective-permute-start.8) | collective-permute-done | bytes 540704 | tf_op jit(solution)/shard_map/ppermute | solution.py:357
  26.5 0.1 add.21
  26.6 2.1 %collective-permute-start.11 = (f32[264,128]{1,0:T(8,128)S(1)}, f32[264,128]{1,0:T(8,128)S(1)}, u32[]{:S(2)}, u32[]{:S(2)}) collective-permute-start(f32[264,128]{1,0:T(8,128)S(1)} %get-tuple-element.63), channel_id=1, source_target_pairs={{0,17},{1,16},{2,19},{3,18},{4,21},{5,20},{6,23},{7,22},{8,14},{9,... | collective-permute-start | bytes 405512 | tf_op jit(solution)/shard_map/ppermute | solution.py:357
  28.7 0.5 collective-permute-start.10
  29.2 1.0 %collective-permute-start.9 = (f32[264,128]{1,0:T(8,128)S(1)}, f32[264,128]{1,0:T(8,128)S(1)}, u32[]{:S(2)}, u32[]{:S(2)}) collective-permute-start(f32[264,128]{1,0:T(8,128)S(1)} %get-tuple-element.65), channel_id=1, source_target_pairs={{0,1},{1,0},{2,3},{3,2},{4,5},{5,4},{6,7},{7,6},{8,10},{9,11},{10,... | collective-permute-start | bytes 405512 | tf_op jit(solution)/shard_map/ppermute | solution.py:357
  30.1 2.5 %collective-permute-done.11 = f32[264,128]{1,0:T(8,128)S(1)} collective-permute-done((f32[264,128]{1,0:T(8,128)S(1)}, f32[264,128]{1,0:T(8,128)S(1)}, u32[]{:S(2)}, u32[]{:S(2)}) %collective-permute-start.11) | collective-permute-done | bytes 135200 | tf_op jit(solution)/shard_map/ppermute | solution.py:357
  32.6 1.4 %collective-permute-done.10 = f32[264,128]{1,0:T(8,128)S(1)} collective-permute-done((f32[264,128]{1,0:T(8,128)S(1)}, f32[264,128]{1,0:T(8,128)S(1)}, u32[]{:S(2)}, u32[]{:S(2)}) %collective-permute-start.10) | collective-permute-done | bytes 135200 | tf_op jit(solution)/shard_map/ppermute | solution.py:357
  34.0 0.2 collective-permute-done.9
  34.2 2.1 %collective-permute-start.14 = (f32[264,128]{1,0:T(8,128)S(1)}, f32[264,128]{1,0:T(8,128)S(1)}, u32[]{:S(2)}, u32[]{:S(2)}) collective-permute-start(f32[264,128]{1,0:T(8,128)S(1)} %fusion.1), channel_id=1, source_target_pairs={{0,6},{1,7},{2,4},{3,5},{4,2},{5,3},{6,0},{7,1},{8,25},{9,24},{10,... | collective-permute-start | bytes 405512 | tf_op jit(solution)/shard_map/ppermute | solution.py:357
  36.3 0.0 collective-permute-start.13
  36.3 2.4 %collective-permute-start.12 = (f32[264,128]{1,0:T(8,128)S(1)}, f32[264,128]{1,0:T(8,128)S(1)}, u32[]{:S(2)}, u32[]{:S(2)}) collective-permute-start(f32[264,128]{1,0:T(8,128)S(1)} %fusion.1), channel_id=1, source_target_pairs={{0,4},{1,5},{2,6},{3,7},{4,0},{5,1},{6,2},{7,3},{8,24},{9,25},{10,... | collective-permute-start | bytes 405512 | tf_op jit(solution)/shard_map/ppermute | solution.py:357
  38.7 2.6 %collective-permute-done.14 = f32[264,128]{1,0:T(8,128)S(1)} collective-permute-done((f32[264,128]{1,0:T(8,128)S(1)}, f32[264,128]{1,0:T(8,128)S(1)}, u32[]{:S(2)}, u32[]{:S(2)}) %collective-permute-start.14) | collective-permute-done | bytes 135200 | tf_op jit(solution)/shard_map/ppermute | solution.py:357
  41.2 2.8 %collective-permute-done.13 = f32[264,128]{1,0:T(8,128)S(1)} collective-permute-done((f32[264,128]{1,0:T(8,128)S(1)}, f32[264,128]{1,0:T(8,128)S(1)}, u32[]{:S(2)}, u32[]{:S(2)}) %collective-permute-start.13) | collective-permute-done | bytes 135200 | tf_op jit(solution)/shard_map/ppermute | solution.py:357
  44.0 0.0 collective-permute-done.12
  44.0 2.0 %collective-permute-start.20 = (f32[264,128]{1,0:T(8,128)S(1)}, f32[264,128]{1,0:T(8,128)S(1)}, u32[]{:S(2)}, u32[]{:S(2)}) collective-permute-start(f32[264,128]{1,0:T(8,128)S(1)} %add_add_fusion.refs_0_), channel_id=1, source_target_pairs={{0,17},{1,16},{2,19},{3,18},{4,21},{5,20},{6,23},{7,22},{8,14},{9,... | collective-permute-start | bytes 405512 | tf_op jit(solution)/shard_map/ppermute | solution.py:357
  46.0 0.5 collective-permute-start.18
  46.5 1.1 %collective-permute-start.16 = (f32[264,128]{1,0:T(8,128)S(1)}, f32[264,128]{1,0:T(8,128)S(1)}, u32[]{:S(2)}, u32[]{:S(2)}) collective-permute-start(f32[264,128]{1,0:T(8,128)S(1)} %add_add_fusion.refs_0_), channel_id=1, source_target_pairs={{0,1},{1,0},{2,3},{3,2},{4,5},{5,4},{6,7},{7,6},{8,10},{9,11},{10,... | collective-permute-start | bytes 405512 | tf_op jit(solution)/shard_map/ppermute | solution.py:357
  47.6 0.0 collective-permute-start.15
  47.6 2.5 %collective-permute-done.20.refs_3_ = f32[264,128]{1,0:T(8,128)S(1)} collective-permute-done((f32[264,128]{1,0:T(8,128)S(1)}, f32[264,128]{1,0:T(8,128)S(1)}, u32[]{:S(2)}, u32[]{:S(2)}) %collective-permute-start.20) | collective-permute-done | bytes 135200 | tf_op jit(solution)/shard_map/ppermute | solution.py:357
  50.0 0.0 collective-permute-start.21
  50.1 1.4 %collective-permute-done.18.refs_2_ = f32[264,128]{1,0:T(8,128)S(1)} collective-permute-done((f32[264,128]{1,0:T(8,128)S(1)}, f32[264,128]{1,0:T(8,128)S(1)}, u32[]{:S(2)}, u32[]{:S(2)}) %collective-permute-start.18) | collective-permute-done | bytes 135200 | tf_op jit(solution)/shard_map/ppermute | solution.py:357
  51.5 0.0 collective-permute-start.19
  51.5 0.1 collective-permute-done.16.refs_1_
  51.5 0.4 collective-permute-start.17
  52.0 0.8 %place_near.1 = (f32[8,128,256]{2,1,0:T(8,128)}, f32[4,8,128]{2,1,0:T(8,128)S(1)}) custom-call(f32[264,128]{1,0:T(8,128)S(1)} %add_add_fusion.refs_0_, f32[264,128]{1,0:T(8,128)S(1)} %collective-permute-done.16.refs_1_, f32[264,128]{1,0:T(8,128)S(1)} %collective-permute-done.18.refs_2_, f32[264,128]{1,0:T(8,128)S(1)} %collective-permute-done.20.refs_3_), custom_call_target="tpu_custom_call" | custom-call | bytes 1048576 | tf_op jit(solution)/shard_map/place_near/pallas_call | solution.py:475
  52.8 0.0 collective-permute-done.15.refs_0_
  52.8 0.0 collective-permute-done.21.refs_3_
  52.8 0.0 collective-permute-done.19.refs_2_
  52.9 0.1 collective-permute-done.17.refs_1_
  53.0 0.9 %place_far.1 = (f32[8,128,256]{2,1,0:T(8,128)}, f32[4,256]{1,0:T(4,128)}, f32[16,256]{1,0:T(8,128)}, f32[1,256]{1,0:T(1,128)}, f32[1,1]{1,0:T(1,128)}) custom-call(f32[264,128]{1,0:T(8,128)S(1)} %collective-permute-done.15.refs_0_, f32[264,128]{1,0:T(8,128)S(1)} %collective-permute-done.17.refs_1_, ...), custom_call_target="tpu_custom_call", output_to_operand_aliasing={{0}: (5, {})} | custom-call | tf_op jit(solution)/shard_map/place_far/pallas_call | solution.py:485
  (7 shorter events, 0.1 us)
Async XLA Ops:
  0.6 16.1 %copy-start = (bf16[4,256,256]{2,1,0:T(8,128)(2,1)S(1)}, bf16[4,256,256]{2,1,0:T(8,128)(2,1)}, u32[]{:S(2)}) copy-start(bf16[4,256,256]{2,1,0:T(8,128)(2,1)} %w_ref.2) | copy-start | bytes 1572868
  3.2 13.5 %copy-start.1 = (bf16[256,256]{1,0:T(8,128)(2,1)S(1)}, bf16[256,256]{1,0:T(8,128)(2,1)}, u32[]{:S(2)}) copy-start(bf16[256,256]{1,0:T(8,128)(2,1)} %feat_ref.2) | copy-start | bytes 393220
  3.2 6.5 %collective-permute-start.2 = (f32[1,24,256]{2,1,0:T(8,128)}, f32[1,24,256]{2,1,0:T(8,128)S(1)}, u32[]{:S(2)}, u32[]{:S(2)}) collective-permute-start(f32[1,24,256]{2,1,0:T(8,128)} %bitcast.20), channel_id=1, source_target_pairs={{0,4},{1,5},{2,6},{3,7},{4,0},{5,1},{6,2},{7,3},{8,12},{9,13},{10,... | collective-permute-start | bytes 73736 | tf_op jit(solution)/shard_map/ppermute | solution.py:357
  7.3 5.8 %collective-permute-start.1 = (f32[1,24,256]{2,1,0:T(8,128)}, f32[1,24,256]{2,1,0:T(8,128)S(1)}, u32[]{:S(2)}, u32[]{:S(2)}) collective-permute-start(f32[1,24,256]{2,1,0:T(8,128)} %bitcast.21), channel_id=1, source_target_pairs={{0,6},{1,7},{2,4},{3,5},{4,2},{5,3},{6,0},{7,1},{8,14},{9,15},{10,... | collective-permute-start | bytes 73736 | tf_op jit(solution)/shard_map/ppermute | solution.py:357
  8.6 4.5 %collective-permute-start = (f32[1,24,256]{2,1,0:T(8,128)}, f32[1,24,256]{2,1,0:T(8,128)S(1)}, u32[]{:S(2)}, u32[]{:S(2)}) collective-permute-start(f32[1,24,256]{2,1,0:T(8,128)} %bitcast.22), channel_id=1, source_target_pairs={{0,2},{1,3},{2,0},{3,1},{4,6},{5,7},{6,4},{7,5},{8,10},{9,11},{10,... | collective-permute-start | bytes 73736 | tf_op jit(solution)/shard_map/ppermute | solution.py:357
  8.9 0.8 %copy-start.3 = (f32[24,256]{1,0:T(8,128)S(1)}, f32[24,256]{1,0:T(8,128)}, u32[]{:S(2)}) copy-start(f32[24,256]{1,0:T(8,128)} %get-tuple-element.34.pay_ref) | copy-start | bytes 73732
  13.1 3.6 %copy-start.2 = (bf16[16,256]{1,0:T(8,128)(2,1)S(1)}, bf16[16,256]{1,0:T(8,128)(2,1)}, u32[]{:S(2)}) copy-start(bf16[16,256]{1,0:T(8,128)(2,1)} %wc_ref.3) | copy-start | bytes 24580
  13.1 3.6 %copy-start.5 = (f32[4,256]{1,0:T(4,128)S(1)}, f32[4,256]{1,0:T(4,128)}, u32[]{:S(2)}) copy-start(f32[4,256]{1,0:T(4,128)} %b_ref.2) | copy-start | bytes 12292
  13.1 3.6 %copy-start.6 = (bf16[256]{0:T(256)(128)(2,1)S(1)}, bf16[256]{0:T(256)(128)(2,1)}, u32[]{:S(2)}) copy-start(bf16[256]{0:T(256)(128)(2,1)} %wb_ref.3) | copy-start | bytes 1540
  13.2 5.3 %collective-permute-start.5 = (f32[4,24,256]{2,1,0:T(8,128)S(1)}, f32[4,24,256]{2,1,0:T(8,128)S(1)}, u32[]{:S(2)}, u32[]{:S(2)}) collective-permute-start(f32[4,24,256]{2,1,0:T(8,128)S(1)} %pad_maximum_fusion.1.rest_0_), channel_id=1, source_target_pairs={{0,16},{1,17},{2,18},{3,19},{4,20},{5,21},{6,22},{7,23},{8,24},{9,... | collective-permute-start | bytes 294920 | tf_op jit(solution)/shard_map/ppermute | solution.py:357
  14.7 5.5 %collective-permute-start.4 = (f32[4,24,256]{2,1,0:T(8,128)S(1)}, f32[4,24,256]{2,1,0:T(8,128)S(1)}, u32[]{:S(2)}, u32[]{:S(2)}) collective-permute-start(f32[4,24,256]{2,1,0:T(8,128)S(1)} %pad_maximum_fusion.1.rest_0_), channel_id=1, source_target_pairs={{0,17},{1,16},{2,19},{3,18},{4,21},{5,20},{6,23},{7,22},{8,25},{9,... | collective-permute-start | bytes 294920 | tf_op jit(solution)/shard_map/ppermute | solution.py:357
  16.2 4.6 %collective-permute-start.3 = (f32[4,24,256]{2,1,0:T(8,128)S(1)}, f32[4,24,256]{2,1,0:T(8,128)S(1)}, u32[]{:S(2)}, u32[]{:S(2)}) collective-permute-start(f32[4,24,256]{2,1,0:T(8,128)S(1)} %pad_maximum_fusion.1.rest_0_), channel_id=1, source_target_pairs={{0,1},{1,0},{2,3},{3,2},{4,5},{5,4},{6,7},{7,6},{8,9},{9,8},{10,11... | collective-permute-start | bytes 294920 | tf_op jit(solution)/shard_map/ppermute | solution.py:357
  16.7 4.1 %collective-permute-start.6 = (f32[4,24,256]{2,1,0:T(8,128)S(1)}, f32[4,24,256]{2,1,0:T(8,128)S(1)}, u32[]{:S(2)}, u32[]{:S(2)}) collective-permute-start(f32[4,24,256]{2,1,0:T(8,128)S(1)} %pad_maximum_fusion.1.rest_0_), channel_id=1, source_target_pairs={{0,8},{1,9},{2,10},{3,11},{4,12},{5,13},{6,14},{7,15},{8,0},{9,1},... | collective-permute-start | bytes 294920 | tf_op jit(solution)/shard_map/ppermute | solution.py:357
  20.8 1.6 %collective-permute-start.7 = (f32[12,24,256]{2,1,0:T(8,128)S(1)}, f32[12,24,256]{2,1,0:T(8,128)S(1)}, u32[]{:S(2)}, u32[]{:S(2)}) collective-permute-start(f32[12,24,256]{2,1,0:T(8,128)S(1)} %pad_maximum_fusion.rest_2_), channel_id=1, source_target_pairs={{0,8},{1,9},{2,10},{3,11},{4,12},{5,13},{6,14},{7,15},{8,0},{9,1},... | collective-permute-start | bytes 884744 | tf_op jit(solution)/shard_map/ppermute | solution.py:357
  20.9 1.6 %copy-start.4 = (f32[16,256]{1,0:T(8,128)S(1)}, f32[16,256]{1,0:T(8,128)}, u32[]{:S(2)}) copy-start(f32[16,256]{1,0:T(8,128)} %get-tuple-element.39.aux_ref) | copy-start | bytes 49156
  24.5 2.0 %collective-permute-start.8 = (f32[4,264,128]{2,1,0:T(8,128)S(1)}, f32[4,264,128]{2,1,0:T(8,128)S(1)}, u32[]{:S(2)}, u32[]{:S(2)}) collective-permute-start(f32[4,264,128]{2,1,0:T(8,128)S(1)} %get-tuple-element.55), channel_id=1, source_target_pairs={{0,8},{1,9},{2,10},{3,11},{4,12},{5,13},{6,14},{7,15},{8,0},{9,1},... | collective-permute-start | bytes 1622024 | tf_op jit(solution)/shard_map/ppermute | solution.py:357
  26.6 6.0 %collective-permute-start.11 = (f32[264,128]{1,0:T(8,128)S(1)}, f32[264,128]{1,0:T(8,128)S(1)}, u32[]{:S(2)}, u32[]{:S(2)}) collective-permute-start(f32[264,128]{1,0:T(8,128)S(1)} %get-tuple-element.63), channel_id=1, source_target_pairs={{0,17},{1,16},{2,19},{3,18},{4,21},{5,20},{6,23},{7,22},{8,14},{9,... | collective-permute-start | bytes 405512 | tf_op jit(solution)/shard_map/ppermute | solution.py:357
  28.7 5.3 %collective-permute-start.10 = (f32[264,128]{1,0:T(8,128)S(1)}, f32[264,128]{1,0:T(8,128)S(1)}, u32[]{:S(2)}, u32[]{:S(2)}) collective-permute-start(f32[264,128]{1,0:T(8,128)S(1)} %get-tuple-element.64), channel_id=1, source_target_pairs={{0,16},{1,17},{2,18},{3,19},{4,20},{5,21},{6,22},{7,23},{8,12},{9,... | collective-permute-start | bytes 405512 | tf_op jit(solution)/shard_map/ppermute | solution.py:357
  29.2 5.0 %collective-permute-start.9 = (f32[264,128]{1,0:T(8,128)S(1)}, f32[264,128]{1,0:T(8,128)S(1)}, u32[]{:S(2)}, u32[]{:S(2)}) collective-permute-start(f32[264,128]{1,0:T(8,128)S(1)} %get-tuple-element.65), channel_id=1, source_target_pairs={{0,1},{1,0},{2,3},{3,2},{4,5},{5,4},{6,7},{7,6},{8,10},{9,11},{10,... | collective-permute-start | bytes 405512 | tf_op jit(solution)/shard_map/ppermute | solution.py:357
  34.2 7.0 %collective-permute-start.14 = (f32[264,128]{1,0:T(8,128)S(1)}, f32[264,128]{1,0:T(8,128)S(1)}, u32[]{:S(2)}, u32[]{:S(2)}) collective-permute-start(f32[264,128]{1,0:T(8,128)S(1)} %fusion.1), channel_id=1, source_target_pairs={{0,6},{1,7},{2,4},{3,5},{4,2},{5,3},{6,0},{7,1},{8,25},{9,24},{10,... | collective-permute-start | bytes 405512 | tf_op jit(solution)/shard_map/ppermute | solution.py:357
  36.3 7.7 %collective-permute-start.13 = (f32[264,128]{1,0:T(8,128)S(1)}, f32[264,128]{1,0:T(8,128)S(1)}, u32[]{:S(2)}, u32[]{:S(2)}) collective-permute-start(f32[264,128]{1,0:T(8,128)S(1)} %fusion.1), channel_id=1, source_target_pairs={{0,2},{1,3},{2,0},{3,1},{4,6},{5,7},{6,4},{7,5},{8,9},{9,8},{10,11... | collective-permute-start | bytes 405512 | tf_op jit(solution)/shard_map/ppermute | solution.py:357
  36.3 7.7 %collective-permute-start.12 = (f32[264,128]{1,0:T(8,128)S(1)}, f32[264,128]{1,0:T(8,128)S(1)}, u32[]{:S(2)}, u32[]{:S(2)}) collective-permute-start(f32[264,128]{1,0:T(8,128)S(1)} %fusion.1), channel_id=1, source_target_pairs={{0,4},{1,5},{2,6},{3,7},{4,0},{5,1},{6,2},{7,3},{8,24},{9,25},{10,... | collective-permute-start | bytes 405512 | tf_op jit(solution)/shard_map/ppermute | solution.py:357
  44.0 6.0 %collective-permute-start.20 = (f32[264,128]{1,0:T(8,128)S(1)}, f32[264,128]{1,0:T(8,128)S(1)}, u32[]{:S(2)}, u32[]{:S(2)}) collective-permute-start(f32[264,128]{1,0:T(8,128)S(1)} %add_add_fusion.refs_0_), channel_id=1, source_target_pairs={{0,17},{1,16},{2,19},{3,18},{4,21},{5,20},{6,23},{7,22},{8,14},{9,... | collective-permute-start | bytes 405512 | tf_op jit(solution)/shard_map/ppermute | solution.py:357
  46.0 5.4 %collective-permute-start.18 = (f32[264,128]{1,0:T(8,128)S(1)}, f32[264,128]{1,0:T(8,128)S(1)}, u32[]{:S(2)}, u32[]{:S(2)}) collective-permute-start(f32[264,128]{1,0:T(8,128)S(1)} %add_add_fusion.refs_0_), channel_id=1, source_target_pairs={{0,16},{1,17},{2,18},{3,19},{4,20},{5,21},{6,22},{7,23},{8,12},{9,... | collective-permute-start | bytes 405512 | tf_op jit(solution)/shard_map/ppermute | solution.py:357
  46.5 5.0 %collective-permute-start.16 = (f32[264,128]{1,0:T(8,128)S(1)}, f32[264,128]{1,0:T(8,128)S(1)}, u32[]{:S(2)}, u32[]{:S(2)}) collective-permute-start(f32[264,128]{1,0:T(8,128)S(1)} %add_add_fusion.refs_0_), channel_id=1, source_target_pairs={{0,1},{1,0},{2,3},{3,2},{4,5},{5,4},{6,7},{7,6},{8,10},{9,11},{10,... | collective-permute-start | bytes 405512 | tf_op jit(solution)/shard_map/ppermute | solution.py:357
  47.6 5.2 %collective-permute-start.15 = (f32[264,128]{1,0:T(8,128)S(1)}, f32[264,128]{1,0:T(8,128)S(1)}, u32[]{:S(2)}, u32[]{:S(2)}) collective-permute-start(f32[264,128]{1,0:T(8,128)S(1)} %add_add_fusion.refs_0_), channel_id=1, source_target_pairs={{0,8},{1,9},{2,10},{3,11},{4,12},{5,13},{6,14},{7,15},{8,0},{9,1},... | collective-permute-start | bytes 405512 | tf_op jit(solution)/shard_map/ppermute | solution.py:357
  50.0 2.8 %collective-permute-start.21 = (f32[264,128]{1,0:T(8,128)S(1)}, f32[264,128]{1,0:T(8,128)S(1)}, u32[]{:S(2)}, u32[]{:S(2)}) collective-permute-start(f32[264,128]{1,0:T(8,128)S(1)} %collective-permute-done.20.refs_3_), channel_id=1, source_target_pairs={{0,8},{1,9},{2,10},{3,11},{4,12},{5,13},{6,14},{7,15},{8,0},{9,1},... | collective-permute-start | bytes 405512 | tf_op jit(solution)/shard_map/ppermute | solution.py:357
  51.5 1.4 %collective-permute-start.19 = (f32[264,128]{1,0:T(8,128)S(1)}, f32[264,128]{1,0:T(8,128)S(1)}, u32[]{:S(2)}, u32[]{:S(2)}) collective-permute-start(f32[264,128]{1,0:T(8,128)S(1)} %collective-permute-done.18.refs_2_), channel_id=1, source_target_pairs={{0,8},{1,9},{2,10},{3,11},{4,12},{5,13},{6,14},{7,15},{8,0},{9,1},... | collective-permute-start | bytes 405512 | tf_op jit(solution)/shard_map/ppermute | solution.py:357
  51.5 1.5 %collective-permute-start.17 = (f32[264,128]{1,0:T(8,128)S(1)}, f32[264,128]{1,0:T(8,128)S(1)}, u32[]{:S(2)}, u32[]{:S(2)}) collective-permute-start(f32[264,128]{1,0:T(8,128)S(1)} %collective-permute-done.16.refs_1_), channel_id=1, source_target_pairs={{0,8},{1,9},{2,10},{3,11},{4,12},{5,13},{6,14},{7,15},{8,0},{9,1},... | collective-permute-start | bytes 405512 | tf_op jit(solution)/shard_map/ppermute | solution.py:357

commit v9 on v8

--- a/solution.py
+++ b/solution.py
@@ -464,7 +464,7 @@
     mine = total[0]
     arrived = [swap(total[r + 1], a, b) for r, (a, b) in enumerate(zip(flat_masks, line_masks))]
     mine = (mine + arrived[0]) + (arrived[1] + arrived[2])
-    arrived = [swap(mine, line_masks[r], flat_masks[r]) for r in (1, 0, 2)]
+    arrived = [swap(mine, line_masks[r], flat_masks[r]) for r in (0, 2, 1)]
     mine = (mine + arrived[0]) + (arrived[1] + arrived[2])
     for m in others:
         mine = mine + swap(mine, m)

time: 54.1 us -> 53.9 us (level)
  starting transfers between devices: 21.6 us -> 20.7 us
  waiting for transfers between devices: 22 us -> 22.7 us
    ppermute x22, starting transfers between devices: 21.6 us -> 20.7 us  [swap(): lax.ppermute(x, AXES, [(i, i ^ masks[i // core & 1]) for i in range(ndev)])]
    ppermute x22, waiting for transfers between devices: 22 us -> 22.7 us  [swap(): lax.ppermute(x, AXES, [(i, i ^ masks[i // core & 1]) for i in range(ndev)])]
  transfers between devices with their start and end apart: 22 -> 22, of which waited for: 15 -> 16; matrix products, arithmetic and copies ran while one was open for 0% -> 0% of each run, Pallas kernels for 5% -> 6%
where the time goes in v9:
time: 53.9 us; the launch traced here: 53.7 us
  waiting for transfers between devices  22.7 us (42%)
  starting transfers between devices  20.7 us (38%)
  Pallas kernels  8.46 us (16%)
  local copies, waits for them, and re-layouts  0.82 us (2%)
  between operations  0.81 us (2%)
    ppermute x22, waiting for transfers between devices, swap(): lax.ppermute(x, AXES, [(i, i ^ masks[i // core & 1]) for i in range(ndev)])  22.7 us
    ppermute x22, starting transfers between devices, swap(): lax.ppermute(x, AXES, [(i, i ^ masks[i // core & 1]) for i in range(ndev)])  20.7 us
    pallas_call x1, Pallas kernels, on_device(): pl.pallas_call(functools.partial(embed_kernel, sizes), out_shape=(jax.Sha...  2.6 us
    pallas_call x1, Pallas kernels, on_device(): pl.pallas_call(functools.partial(backward_kernel, sizes, hits_all, points...  2 us
    pallas_call x1, Pallas kernels, pairs(): pl.pallas_call(functools.partial(pair_kernel, len(rows)), out_shape=parti...  1.38 us
  transfers between devices with their start and end apart: 22, of which 16 were waited for; matrix products, arithmetic and copies ran while one was open for 0% of the time, Pallas kernels for 6%

profile of v9, /device:TPU:0, one launch (start us, length us, event | category | flops | bytes accessed | tf_op | source)
XLA Modules:
  0.0 53.7 jit_solution(7317925021470892011)
XLA Ops:
  0.6 0.0 copy-start
  0.6 2.6 %embed.1 = (f32[24,256]{1,0:T(8,128)}, f32[16,256]{1,0:T(8,128)}) custom-call(s32[8]{0:T(128)} %hit_ref.1, bf16[256,256]{1,0:T(8,128)(2,1)} %feat_ref.2, bf16[4,256,256]{2,1,0:T(8,128)(2,1)} %w_ref.2, f32[4,256]{1,0:T(4,128)} %b_ref.2, bf16[16,256]{1,0:T(8,128)(2,1)} %wc_ref.3, bf16[256]{0:T(256)(128)(2,1)} %wb_ref.3, s32[1,256]{1,0:T(1,128)} %bitcast.24, ...), custom_call_target="tpu_custom_call" | custom-call | tf_op jit(solution)/shard_map/embed/pallas_call | solution.py:364
  3.2 0.0 copy-start.1
  3.2 4.0 %collective-permute-start.2 = (f32[1,24,256]{2,1,0:T(8,128)}, f32[1,24,256]{2,1,0:T(8,128)S(1)}, u32[]{:S(2)}, u32[]{:S(2)}) collective-permute-start(f32[1,24,256]{2,1,0:T(8,128)} %bitcast.20), channel_id=1, source_target_pairs={{0,4},{1,5},{2,6},{3,7},{4,0},{5,1},{6,2},{7,3},{8,12},{9,13},{10,... | collective-permute-start | bytes 73736 | tf_op jit(solution)/shard_map/ppermute | solution.py:357
  7.3 1.3 %collective-permute-start.1 = (f32[1,24,256]{2,1,0:T(8,128)}, f32[1,24,256]{2,1,0:T(8,128)S(1)}, u32[]{:S(2)}, u32[]{:S(2)}) collective-permute-start(f32[1,24,256]{2,1,0:T(8,128)} %bitcast.21), channel_id=1, source_target_pairs={{0,6},{1,7},{2,4},{3,5},{4,2},{5,3},{6,0},{7,1},{8,14},{9,15},{10,... | collective-permute-start | bytes 73736 | tf_op jit(solution)/shard_map/ppermute | solution.py:357
  8.6 0.2 collective-permute-start
  8.9 0.0 copy-start.3
  8.9 0.8 %copy-done.3 = f32[24,256]{1,0:T(8,128)S(1)} copy-done((f32[24,256]{1,0:T(8,128)S(1)}, f32[24,256]{1,0:T(8,128)}, u32[]{:S(2)}) %copy-start.3) | copy-done | bytes 24600
  9.6 0.1 spread.1
  9.7 0.0 collective-permute-done.2
  9.7 3.4 %collective-permute-done.1 = f32[1,24,256]{2,1,0:T(8,128)S(1)} collective-permute-done((f32[1,24,256]{2,1,0:T(8,128)}, f32[1,24,256]{2,1,0:T(8,128)S(1)}, u32[]{:S(2)}, u32[]{:S(2)}) %collective-permute-start.1) | collective-permute-done | bytes 24608 | tf_op jit(solution)/shard_map/ppermute | solution.py:357
  13.1 0.0 collective-permute-done
  13.1 0.0 copy-start.2
  13.2 1.6 %collective-permute-start.5 = (f32[4,24,256]{2,1,0:T(8,128)S(1)}, f32[4,24,256]{2,1,0:T(8,128)S(1)}, u32[]{:S(2)}, u32[]{:S(2)}) collective-permute-start(f32[4,24,256]{2,1,0:T(8,128)S(1)} %pad_maximum_fusion.1.rest_0_), channel_id=1, source_target_pairs={{0,16},{1,17},{2,18},{3,19},{4,20},{5,21},{6,22},{7,23},{8,24},{9,... | collective-permute-start | bytes 294920 | tf_op jit(solution)/shard_map/ppermute | solution.py:357
  14.7 1.4 %collective-permute-start.4 = (f32[4,24,256]{2,1,0:T(8,128)S(1)}, f32[4,24,256]{2,1,0:T(8,128)S(1)}, u32[]{:S(2)}, u32[]{:S(2)}) collective-permute-start(f32[4,24,256]{2,1,0:T(8,128)S(1)} %pad_maximum_fusion.1.rest_0_), channel_id=1, source_target_pairs={{0,17},{1,16},{2,19},{3,18},{4,21},{5,20},{6,23},{7,22},{8,25},{9,... | collective-permute-start | bytes 294920 | tf_op jit(solution)/shard_map/ppermute | solution.py:357
  16.2 0.5 collective-permute-start.3
  16.7 0.0 collective-permute-start.6
  16.7 0.0 copy-done
  16.7 0.0 copy-done.1
  16.7 0.0 copy-done.2
  16.7 0.0 copy-done.5
  16.7 0.0 copy-done.6
  16.8 0.6 %residuals.1 = (f32[4,256,256]{2,1,0:T(8,128)S(1)}, bf16[4,256,256]{2,1,0:T(8,128)(2,1)S(1)}, bf16[256,256]{1,0:T(8,128)(2,1)S(1)}, bf16[3,256,256]{2,1,0:T(8,128)(2,1)S(1)}, bf16[32,256]{1,0:T(8,128)(2,1)S(1)}) custom-call(bf16[256,256]{1,0:T(8,128)(2,1)S(1)} %copy-done.1, bf16[4,256,256]{2,1,0:T(8,128)(2,1)S(1)} %copy-done, f32[4,256]{1,0:T(4,128)S(1)} %copy-done.5, ...), custom_call_target="tpu_custom_call" | custom-call | flops 5242880 | bytes 1572864 | tf_op jit(solution)/shard_map/residuals/pallas_call | solution.py:377
  17.4 1.1 %collective-permute-done.5 = f32[4,24,256]{2,1,0:T(8,128)S(1)} collective-permute-done((f32[4,24,256]{2,1,0:T(8,128)S(1)}, f32[4,24,256]{2,1,0:T(8,128)S(1)}, u32[]{:S(2)}, u32[]{:S(2)}) %collective-permute-start.5) | collective-permute-done | bytes 98336 | tf_op jit(solution)/shard_map/ppermute | solution.py:357
  18.5 1.8 %collective-permute-done.4 = f32[4,24,256]{2,1,0:T(8,128)S(1)} collective-permute-done((f32[4,24,256]{2,1,0:T(8,128)S(1)}, f32[4,24,256]{2,1,0:T(8,128)S(1)}, u32[]{:S(2)}, u32[]{:S(2)}) %collective-permute-start.4) | collective-permute-done | bytes 98336 | tf_op jit(solution)/shard_map/ppermute | solution.py:357
  20.3 0.5 collective-permute-done.3
  20.8 0.0 collective-permute-done.6.rest_1_
  20.8 0.1 collective-permute-start.7
  20.9 0.0 copy-start.4
  20.9 1.4 %pairs.1 = (f32[17,8,256]{2,1,0:T(8,128)S(1)}, f32[17,8,128]{2,1,0:T(8,128)S(1)}) custom-call(f32[24,256]{1,0:T(8,128)S(1)} %get-tuple-element.35.pay_ref, f32[8,128]{1,0:T(8,128)S(1)} %get-tuple-element.36.own_ref, f32[16,8,256]{2,1,0:T(8,128)S(1)} %get-tuple-element.37.xb, f32[16,8,256]{2,1,0:T(8,128)S(1)} %get-tuple-element.38.yb, ...), custom_call_target="tpu_custom_call" | custom-call | flops 8192000 | bytes 327680 | tf_op jit(solution)/shard_map/pairs/pallas_call | solution.py:431
  22.3 0.2 collective-permute-done.7.rows_ref
  22.5 0.0 copy-done.4
  22.5 2.0 %pairs_backward.1 = (f32[4,264,128]{2,1,0:T(8,128)S(1)}, f32[4,264,128]{2,1,0:T(8,128)S(1)}) custom-call(f32[24,256]{1,0:T(8,128)S(1)} %get-tuple-element.35.pay_ref, f32[8,128]{1,0:T(8,128)S(1)} %get-tuple-element.36.own_ref, f32[16,8,256]{2,1,0:T(8,128)S(1)} %get-tuple-element.37.xb, f32[16,8,256]{2,1,0:T(8,128)S(1)} %get-tuple-element.38.yb, ...), custom_call_target="tpu_custom_call" | custom-call | tf_op jit(solution)/shard_map/pairs_backward/pallas_call | solution.py:449
  24.5 0.4 collective-permute-start.8
  24.9 1.6 %collective-permute-done.8 = f32[4,264,128]{2,1,0:T(8,128)S(1)} collective-permute-done((f32[4,264,128]{2,1,0:T(8,128)S(1)}, f32[4,264,128]{2,1,0:T(8,128)S(1)}, u32[]{:S(2)}, u32[]{:S(2)}) %collective-permute-start.8) | collective-permute-done | bytes 540704 | tf_op jit(solution)/shard_map/ppermute | solution.py:357
  26.5 0.1 add.21
  26.6 2.1 %collective-permute-start.11 = (f32[264,128]{1,0:T(8,128)S(1)}, f32[264,128]{1,0:T(8,128)S(1)}, u32[]{:S(2)}, u32[]{:S(2)}) collective-permute-start(f32[264,128]{1,0:T(8,128)S(1)} %get-tuple-element.63), channel_id=1, source_target_pairs={{0,17},{1,16},{2,19},{3,18},{4,21},{5,20},{6,23},{7,22},{8,14},{9,... | collective-permute-start | bytes 405512 | tf_op jit(solution)/shard_map/ppermute | solution.py:357
  28.7 0.5 collective-permute-start.10
  29.2 1.0 %collective-permute-start.9 = (f32[264,128]{1,0:T(8,128)S(1)}, f32[264,128]{1,0:T(8,128)S(1)}, u32[]{:S(2)}, u32[]{:S(2)}) collective-permute-start(f32[264,128]{1,0:T(8,128)S(1)} %get-tuple-element.65), channel_id=1, source_target_pairs={{0,1},{1,0},{2,3},{3,2},{4,5},{5,4},{6,7},{7,6},{8,10},{9,11},{10,... | collective-permute-start | bytes 405512 | tf_op jit(solution)/shard_map/ppermute | solution.py:357
  30.1 2.5 %collective-permute-done.11 = f32[264,128]{1,0:T(8,128)S(1)} collective-permute-done((f32[264,128]{1,0:T(8,128)S(1)}, f32[264,128]{1,0:T(8,128)S(1)}, u32[]{:S(2)}, u32[]{:S(2)}) %collective-permute-start.11) | collective-permute-done | bytes 135200 | tf_op jit(solution)/shard_map/ppermute | solution.py:357
  32.6 1.4 %collective-permute-done.10 = f32[264,128]{1,0:T(8,128)S(1)} collective-permute-done((f32[264,128]{1,0:T(8,128)S(1)}, f32[264,128]{1,0:T(8,128)S(1)}, u32[]{:S(2)}, u32[]{:S(2)}) %collective-permute-start.10) | collective-permute-done | bytes 135200 | tf_op jit(solution)/shard_map/ppermute | solution.py:357
  34.0 0.2 collective-permute-done.9
  34.2 1.3 %collective-permute-start.14 = (f32[264,128]{1,0:T(8,128)S(1)}, f32[264,128]{1,0:T(8,128)S(1)}, u32[]{:S(2)}, u32[]{:S(2)}) collective-permute-start(f32[264,128]{1,0:T(8,128)S(1)} %fusion.1), channel_id=1, source_target_pairs={{0,4},{1,5},{2,6},{3,7},{4,0},{5,1},{6,2},{7,3},{8,24},{9,25},{10,... | collective-permute-start | bytes 405512 | tf_op jit(solution)/shard_map/ppermute | solution.py:357
  35.5 0.9 %collective-permute-start.13 = (f32[264,128]{1,0:T(8,128)S(1)}, f32[264,128]{1,0:T(8,128)S(1)}, u32[]{:S(2)}, u32[]{:S(2)}) collective-permute-start(f32[264,128]{1,0:T(8,128)S(1)} %fusion.1), channel_id=1, source_target_pairs={{0,6},{1,7},{2,4},{3,5},{4,2},{5,3},{6,0},{7,1},{8,25},{9,24},{10,... | collective-permute-start | bytes 405512 | tf_op jit(solution)/shard_map/ppermute | solution.py:357
  36.4 1.3 %collective-permute-start.12 = (f32[264,128]{1,0:T(8,128)S(1)}, f32[264,128]{1,0:T(8,128)S(1)}, u32[]{:S(2)}, u32[]{:S(2)}) collective-permute-start(f32[264,128]{1,0:T(8,128)S(1)} %fusion.1), channel_id=1, source_target_pairs={{0,2},{1,3},{2,0},{3,1},{4,6},{5,7},{6,4},{7,5},{8,9},{9,8},{10,11... | collective-permute-start | bytes 405512 | tf_op jit(solution)/shard_map/ppermute | solution.py:357
  37.8 3.2 %collective-permute-done.14 = f32[264,128]{1,0:T(8,128)S(1)} collective-permute-done((f32[264,128]{1,0:T(8,128)S(1)}, f32[264,128]{1,0:T(8,128)S(1)}, u32[]{:S(2)}, u32[]{:S(2)}) %collective-permute-start.14) | collective-permute-done | bytes 135200 | tf_op jit(solution)/shard_map/ppermute | solution.py:357
  41.0 1.5 %collective-permute-done.13 = f32[264,128]{1,0:T(8,128)S(1)} collective-permute-done((f32[264,128]{1,0:T(8,128)S(1)}, f32[264,128]{1,0:T(8,128)S(1)}, u32[]{:S(2)}, u32[]{:S(2)}) %collective-permute-start.13) | collective-permute-done | bytes 135200 | tf_op jit(solution)/shard_map/ppermute | solution.py:357
  42.5 1.3 %collective-permute-done.12 = f32[264,128]{1,0:T(8,128)S(1)} collective-permute-done((f32[264,128]{1,0:T(8,128)S(1)}, f32[264,128]{1,0:T(8,128)S(1)}, u32[]{:S(2)}, u32[]{:S(2)}) %collective-permute-start.12) | collective-permute-done | bytes 135200 | tf_op jit(solution)/shard_map/ppermute | solution.py:357
  43.8 2.0 %collective-permute-start.20 = (f32[264,128]{1,0:T(8,128)S(1)}, f32[264,128]{1,0:T(8,128)S(1)}, u32[]{:S(2)}, u32[]{:S(2)}) collective-permute-start(f32[264,128]{1,0:T(8,128)S(1)} %add_add_fusion.refs_0_), channel_id=1, source_target_pairs={{0,17},{1,16},{2,19},{3,18},{4,21},{5,20},{6,23},{7,22},{8,14},{9,... | collective-permute-start | bytes 405512 | tf_op jit(solution)/shard_map/ppermute | solution.py:357
  45.8 0.5 collective-permute-start.18
  46.3 1.1 %collective-permute-start.16 = (f32[264,128]{1,0:T(8,128)S(1)}, f32[264,128]{1,0:T(8,128)S(1)}, u32[]{:S(2)}, u32[]{:S(2)}) collective-permute-start(f32[264,128]{1,0:T(8,128)S(1)} %add_add_fusion.refs_0_), channel_id=1, source_target_pairs={{0,1},{1,0},{2,3},{3,2},{4,5},{5,4},{6,7},{7,6},{8,10},{9,11},{10,... | collective-permute-start | bytes 405512 | tf_op jit(solution)/shard_map/ppermute | solution.py:357
  47.4 0.0 collective-permute-start.15
  47.4 2.5 %collective-permute-done.20.refs_3_ = f32[264,128]{1,0:T(8,128)S(1)} collective-permute-done((f32[264,128]{1,0:T(8,128)S(1)}, f32[264,128]{1,0:T(8,128)S(1)}, u32[]{:S(2)}, u32[]{:S(2)}) %collective-permute-start.20) | collective-permute-done | bytes 135200 | tf_op jit(solution)/shard_map/ppermute | solution.py:357
  49.8 0.0 collective-permute-start.21
  49.8 1.4 %collective-permute-done.18.refs_2_ = f32[264,128]{1,0:T(8,128)S(1)} collective-permute-done((f32[264,128]{1,0:T(8,128)S(1)}, f32[264,128]{1,0:T(8,128)S(1)}, u32[]{:S(2)}, u32[]{:S(2)}) %collective-permute-start.18) | collective-permute-done | bytes 135200 | tf_op jit(solution)/shard_map/ppermute | solution.py:357
  51.2 0.0 collective-permute-start.19
  51.2 0.1 collective-permute-done.16.refs_1_
  51.3 0.4 collective-permute-start.17
  51.8 0.8 %place_near.1 = (f32[8,128,256]{2,1,0:T(8,128)}, f32[4,8,128]{2,1,0:T(8,128)S(1)}) custom-call(f32[264,128]{1,0:T(8,128)S(1)} %add_add_fusion.refs_0_, f32[264,128]{1,0:T(8,128)S(1)} %collective-permute-done.16.refs_1_, f32[264,128]{1,0:T(8,128)S(1)} %collective-permute-done.18.refs_2_, f32[264,128]{1,0:T(8,128)S(1)} %collective-permute-done.20.refs_3_), custom_call_target="tpu_custom_call" | custom-call | bytes 1048576 | tf_op jit(solution)/shard_map/place_near/pallas_call | solution.py:475
  52.6 0.0 collective-permute-done.15.refs_0_
  52.6 0.0 collective-permute-done.21.refs_3_
  52.6 0.0 collective-permute-done.19.refs_2_
  52.6 0.1 collective-permute-done.17.refs_1_
  52.8 0.9 %place_far.1 = (f32[8,128,256]{2,1,0:T(8,128)}, f32[4,256]{1,0:T(4,128)}, f32[16,256]{1,0:T(8,128)}, f32[1,256]{1,0:T(1,128)}, f32[1,1]{1,0:T(1,128)}) custom-call(f32[264,128]{1,0:T(8,128)S(1)} %collective-permute-done.15.refs_0_, f32[264,128]{1,0:T(8,128)S(1)} %collective-permute-done.17.refs_1_, ...), custom_call_target="tpu_custom_call", output_to_operand_aliasing={{0}: (5, {})} | custom-call | tf_op jit(solution)/shard_map/place_far/pallas_call | solution.py:485
  (7 shorter events, 0.1 us)
Async XLA Ops:
  0.6 16.1 %copy-start = (bf16[4,256,256]{2,1,0:T(8,128)(2,1)S(1)}, bf16[4,256,256]{2,1,0:T(8,128)(2,1)}, u32[]{:S(2)}) copy-start(bf16[4,256,256]{2,1,0:T(8,128)(2,1)} %w_ref.2) | copy-start | bytes 1572868
  3.2 13.5 %copy-start.1 = (bf16[256,256]{1,0:T(8,128)(2,1)S(1)}, bf16[256,256]{1,0:T(8,128)(2,1)}, u32[]{:S(2)}) copy-start(bf16[256,256]{1,0:T(8,128)(2,1)} %feat_ref.2) | copy-start | bytes 393220
  3.2 6.5 %collective-permute-start.2 = (f32[1,24,256]{2,1,0:T(8,128)}, f32[1,24,256]{2,1,0:T(8,128)S(1)}, u32[]{:S(2)}, u32[]{:S(2)}) collective-permute-start(f32[1,24,256]{2,1,0:T(8,128)} %bitcast.20), channel_id=1, source_target_pairs={{0,4},{1,5},{2,6},{3,7},{4,0},{5,1},{6,2},{7,3},{8,12},{9,13},{10,... | collective-permute-start | bytes 73736 | tf_op jit(solution)/shard_map/ppermute | solution.py:357
  7.3 5.8 %collective-permute-start.1 = (f32[1,24,256]{2,1,0:T(8,128)}, f32[1,24,256]{2,1,0:T(8,128)S(1)}, u32[]{:S(2)}, u32[]{:S(2)}) collective-permute-start(f32[1,24,256]{2,1,0:T(8,128)} %bitcast.21), channel_id=1, source_target_pairs={{0,6},{1,7},{2,4},{3,5},{4,2},{5,3},{6,0},{7,1},{8,14},{9,15},{10,... | collective-permute-start | bytes 73736 | tf_op jit(solution)/shard_map/ppermute | solution.py:357
  8.6 4.5 %collective-permute-start = (f32[1,24,256]{2,1,0:T(8,128)}, f32[1,24,256]{2,1,0:T(8,128)S(1)}, u32[]{:S(2)}, u32[]{:S(2)}) collective-permute-start(f32[1,24,256]{2,1,0:T(8,128)} %bitcast.22), channel_id=1, source_target_pairs={{0,2},{1,3},{2,0},{3,1},{4,6},{5,7},{6,4},{7,5},{8,10},{9,11},{10,... | collective-permute-start | bytes 73736 | tf_op jit(solution)/shard_map/ppermute | solution.py:357
  8.9 0.8 %copy-start.3 = (f32[24,256]{1,0:T(8,128)S(1)}, f32[24,256]{1,0:T(8,128)}, u32[]{:S(2)}) copy-start(f32[24,256]{1,0:T(8,128)} %get-tuple-element.34.pay_ref) | copy-start | bytes 73732
  13.1 3.6 %copy-start.2 = (bf16[16,256]{1,0:T(8,128)(2,1)S(1)}, bf16[16,256]{1,0:T(8,128)(2,1)}, u32[]{:S(2)}) copy-start(bf16[16,256]{1,0:T(8,128)(2,1)} %wc_ref.3) | copy-start | bytes 24580
  13.1 3.6 %copy-start.5 = (f32[4,256]{1,0:T(4,128)S(1)}, f32[4,256]{1,0:T(4,128)}, u32[]{:S(2)}) copy-start(f32[4,256]{1,0:T(4,128)} %b_ref.2) | copy-start | bytes 12292
  13.1 3.6 %copy-start.6 = (bf16[256]{0:T(256)(128)(2,1)S(1)}, bf16[256]{0:T(256)(128)(2,1)}, u32[]{:S(2)}) copy-start(bf16[256]{0:T(256)(128)(2,1)} %wb_ref.3) | copy-start | bytes 1540
  13.2 5.3 %collective-permute-start.5 = (f32[4,24,256]{2,1,0:T(8,128)S(1)}, f32[4,24,256]{2,1,0:T(8,128)S(1)}, u32[]{:S(2)}, u32[]{:S(2)}) collective-permute-start(f32[4,24,256]{2,1,0:T(8,128)S(1)} %pad_maximum_fusion.1.rest_0_), channel_id=1, source_target_pairs={{0,16},{1,17},{2,18},{3,19},{4,20},{5,21},{6,22},{7,23},{8,24},{9,... | collective-permute-start | bytes 294920 | tf_op jit(solution)/shard_map/ppermute | solution.py:357
  14.7 5.5 %collective-permute-start.4 = (f32[4,24,256]{2,1,0:T(8,128)S(1)}, f32[4,24,256]{2,1,0:T(8,128)S(1)}, u32[]{:S(2)}, u32[]{:S(2)}) collective-permute-start(f32[4,24,256]{2,1,0:T(8,128)S(1)} %pad_maximum_fusion.1.rest_0_), channel_id=1, source_target_pairs={{0,17},{1,16},{2,19},{3,18},{4,21},{5,20},{6,23},{7,22},{8,25},{9,... | collective-permute-start | bytes 294920 | tf_op jit(solution)/shard_map/ppermute | solution.py:357
  16.2 4.6 %collective-permute-start.3 = (f32[4,24,256]{2,1,0:T(8,128)S(1)}, f32[4,24,256]{2,1,0:T(8,128)S(1)}, u32[]{:S(2)}, u32[]{:S(2)}) collective-permute-start(f32[4,24,256]{2,1,0:T(8,128)S(1)} %pad_maximum_fusion.1.rest_0_), channel_id=1, source_target_pairs={{0,1},{1,0},{2,3},{3,2},{4,5},{5,4},{6,7},{7,6},{8,9},{9,8},{10,11... | collective-permute-start | bytes 294920 | tf_op jit(solution)/shard_map/ppermute | solution.py:357
  16.7 4.1 %collective-permute-start.6 = (f32[4,24,256]{2,1,0:T(8,128)S(1)}, f32[4,24,256]{2,1,0:T(8,128)S(1)}, u32[]{:S(2)}, u32[]{:S(2)}) collective-permute-start(f32[4,24,256]{2,1,0:T(8,128)S(1)} %pad_maximum_fusion.1.rest_0_), channel_id=1, source_target_pairs={{0,8},{1,9},{2,10},{3,11},{4,12},{5,13},{6,14},{7,15},{8,0},{9,1},... | collective-permute-start | bytes 294920 | tf_op jit(solution)/shard_map/ppermute | solution.py:357
  20.8 1.6 %collective-permute-start.7 = (f32[12,24,256]{2,1,0:T(8,128)S(1)}, f32[12,24,256]{2,1,0:T(8,128)S(1)}, u32[]{:S(2)}, u32[]{:S(2)}) collective-permute-start(f32[12,24,256]{2,1,0:T(8,128)S(1)} %pad_maximum_fusion.rest_2_), channel_id=1, source_target_pairs={{0,8},{1,9},{2,10},{3,11},{4,12},{5,13},{6,14},{7,15},{8,0},{9,1},... | collective-permute-start | bytes 884744 | tf_op jit(solution)/shard_map/ppermute | solution.py:357
  20.9 1.6 %copy-start.4 = (f32[16,256]{1,0:T(8,128)S(1)}, f32[16,256]{1,0:T(8,128)}, u32[]{:S(2)}) copy-start(f32[16,256]{1,0:T(8,128)} %get-tuple-element.39.aux_ref) | copy-start | bytes 49156
  24.5 2.0 %collective-permute-start.8 = (f32[4,264,128]{2,1,0:T(8,128)S(1)}, f32[4,264,128]{2,1,0:T(8,128)S(1)}, u32[]{:S(2)}, u32[]{:S(2)}) collective-permute-start(f32[4,264,128]{2,1,0:T(8,128)S(1)} %get-tuple-element.55), channel_id=1, source_target_pairs={{0,8},{1,9},{2,10},{3,11},{4,12},{5,13},{6,14},{7,15},{8,0},{9,1},... | collective-permute-start | bytes 1622024 | tf_op jit(solution)/shard_map/ppermute | solution.py:357
  26.6 6.0 %collective-permute-start.11 = (f32[264,128]{1,0:T(8,128)S(1)}, f32[264,128]{1,0:T(8,128)S(1)}, u32[]{:S(2)}, u32[]{:S(2)}) collective-permute-start(f32[264,128]{1,0:T(8,128)S(1)} %get-tuple-element.63), channel_id=1, source_target_pairs={{0,17},{1,16},{2,19},{3,18},{4,21},{5,20},{6,23},{7,22},{8,14},{9,... | collective-permute-start | bytes 405512 | tf_op jit(solution)/shard_map/ppermute | solution.py:357
  28.7 5.3 %collective-permute-start.10 = (f32[264,128]{1,0:T(8,128)S(1)}, f32[264,128]{1,0:T(8,128)S(1)}, u32[]{:S(2)}, u32[]{:S(2)}) collective-permute-start(f32[264,128]{1,0:T(8,128)S(1)} %get-tuple-element.64), channel_id=1, source_target_pairs={{0,16},{1,17},{2,18},{3,19},{4,20},{5,21},{6,22},{7,23},{8,12},{9,... | collective-permute-start | bytes 405512 | tf_op jit(solution)/shard_map/ppermute | solution.py:357
  29.2 5.0 %collective-permute-start.9 = (f32[264,128]{1,0:T(8,128)S(1)}, f32[264,128]{1,0:T(8,128)S(1)}, u32[]{:S(2)}, u32[]{:S(2)}) collective-permute-start(f32[264,128]{1,0:T(8,128)S(1)} %get-tuple-element.65), channel_id=1, source_target_pairs={{0,1},{1,0},{2,3},{3,2},{4,5},{5,4},{6,7},{7,6},{8,10},{9,11},{10,... | collective-permute-start | bytes 405512 | tf_op jit(solution)/shard_map/ppermute | solution.py:357
  34.2 6.8 %collective-permute-start.14 = (f32[264,128]{1,0:T(8,128)S(1)}, f32[264,128]{1,0:T(8,128)S(1)}, u32[]{:S(2)}, u32[]{:S(2)}) collective-permute-start(f32[264,128]{1,0:T(8,128)S(1)} %fusion.1), channel_id=1, source_target_pairs={{0,4},{1,5},{2,6},{3,7},{4,0},{5,1},{6,2},{7,3},{8,24},{9,25},{10,... | collective-permute-start | bytes 405512 | tf_op jit(solution)/shard_map/ppermute | solution.py:357
  35.5 7.0 %collective-permute-start.13 = (f32[264,128]{1,0:T(8,128)S(1)}, f32[264,128]{1,0:T(8,128)S(1)}, u32[]{:S(2)}, u32[]{:S(2)}) collective-permute-start(f32[264,128]{1,0:T(8,128)S(1)} %fusion.1), channel_id=1, source_target_pairs={{0,6},{1,7},{2,4},{3,5},{4,2},{5,3},{6,0},{7,1},{8,25},{9,24},{10,... | collective-permute-start | bytes 405512 | tf_op jit(solution)/shard_map/ppermute | solution.py:357
  36.4 7.3 %collective-permute-start.12 = (f32[264,128]{1,0:T(8,128)S(1)}, f32[264,128]{1,0:T(8,128)S(1)}, u32[]{:S(2)}, u32[]{:S(2)}) collective-permute-start(f32[264,128]{1,0:T(8,128)S(1)} %fusion.1), channel_id=1, source_target_pairs={{0,2},{1,3},{2,0},{3,1},{4,6},{5,7},{6,4},{7,5},{8,9},{9,8},{10,11... | collective-permute-start | bytes 405512 | tf_op jit(solution)/shard_map/ppermute | solution.py:357
  43.8 6.0 %collective-permute-start.20 = (f32[264,128]{1,0:T(8,128)S(1)}, f32[264,128]{1,0:T(8,128)S(1)}, u32[]{:S(2)}, u32[]{:S(2)}) collective-permute-start(f32[264,128]{1,0:T(8,128)S(1)} %add_add_fusion.refs_0_), channel_id=1, source_target_pairs={{0,17},{1,16},{2,19},{3,18},{4,21},{5,20},{6,23},{7,22},{8,14},{9,... | collective-permute-start | bytes 405512 | tf_op jit(solution)/shard_map/ppermute | solution.py:357
  45.8 5.4 %collective-permute-start.18 = (f32[264,128]{1,0:T(8,128)S(1)}, f32[264,128]{1,0:T(8,128)S(1)}, u32[]{:S(2)}, u32[]{:S(2)}) collective-permute-start(f32[264,128]{1,0:T(8,128)S(1)} %add_add_fusion.refs_0_), channel_id=1, source_target_pairs={{0,16},{1,17},{2,18},{3,19},{4,20},{5,21},{6,22},{7,23},{8,12},{9,... | collective-permute-start | bytes 405512 | tf_op jit(solution)/shard_map/ppermute | solution.py:357
  46.3 5.0 %collective-permute-start.16 = (f32[264,128]{1,0:T(8,128)S(1)}, f32[264,128]{1,0:T(8,128)S(1)}, u32[]{:S(2)}, u32[]{:S(2)}) collective-permute-start(f32[264,128]{1,0:T(8,128)S(1)} %add_add_fusion.refs_0_), channel_id=1, source_target_pairs={{0,1},{1,0},{2,3},{3,2},{4,5},{5,4},{6,7},{7,6},{8,10},{9,11},{10,... | collective-permute-start | bytes 405512 | tf_op jit(solution)/shard_map/ppermute | solution.py:357
  47.4 5.2 %collective-permute-start.15 = (f32[264,128]{1,0:T(8,128)S(1)}, f32[264,128]{1,0:T(8,128)S(1)}, u32[]{:S(2)}, u32[]{:S(2)}) collective-permute-start(f32[264,128]{1,0:T(8,128)S(1)} %add_add_fusion.refs_0_), channel_id=1, source_target_pairs={{0,8},{1,9},{2,10},{3,11},{4,12},{5,13},{6,14},{7,15},{8,0},{9,1},... | collective-permute-start | bytes 405512 | tf_op jit(solution)/shard_map/ppermute | solution.py:357
  49.8 2.8 %collective-permute-start.21 = (f32[264,128]{1,0:T(8,128)S(1)}, f32[264,128]{1,0:T(8,128)S(1)}, u32[]{:S(2)}, u32[]{:S(2)}) collective-permute-start(f32[264,128]{1,0:T(8,128)S(1)} %collective-permute-done.20.refs_3_), channel_id=1, source_target_pairs={{0,8},{1,9},{2,10},{3,11},{4,12},{5,13},{6,14},{7,15},{8,0},{9,1},... | collective-permute-start | bytes 405512 | tf_op jit(solution)/shard_map/ppermute | solution.py:357
  51.2 1.4 %collective-permute-start.19 = (f32[264,128]{1,0:T(8,128)S(1)}, f32[264,128]{1,0:T(8,128)S(1)}, u32[]{:S(2)}, u32[]{:S(2)}) collective-permute-start(f32[264,128]{1,0:T(8,128)S(1)} %collective-permute-done.18.refs_2_), channel_id=1, source_target_pairs={{0,8},{1,9},{2,10},{3,11},{4,12},{5,13},{6,14},{7,15},{8,0},{9,1},... | collective-permute-start | bytes 405512 | tf_op jit(solution)/shard_map/ppermute | solution.py:357
  51.3 1.5 %collective-permute-start.17 = (f32[264,128]{1,0:T(8,128)S(1)}, f32[264,128]{1,0:T(8,128)S(1)}, u32[]{:S(2)}, u32[]{:S(2)}) collective-permute-start(f32[264,128]{1,0:T(8,128)S(1)} %collective-permute-done.16.refs_1_), channel_id=1, source_target_pairs={{0,8},{1,9},{2,10},{3,11},{4,12},{5,13},{6,14},{7,15},{8,0},{9,1},... | collective-permute-start | bytes 405512 | tf_op jit(solution)/shard_map/ppermute | solution.py:357

commit v10 on v9

--- a/solution.py
+++ b/solution.py
@@ -59,10 +59,12 @@
     hits = feat_ref.shape[0]
     points = hit_ref.shape[0]
     layers = w_ref.shape[0]
-    h = feat_ref[...]
+    half = hits // 2
+    parts = [feat_ref[0:half, :], feat_ref[half:, :]]
     for l in range(layers):
-        a = matmul(h, w_ref[l]) + b_ref[l : l + 1, :]
-        h = (a * jax.nn.sigmoid(a)).astype(jnp.bfloat16)
+        pre = [matmul(h, w_ref[l]) + b_ref[l : l + 1, :] for h in parts]
+        parts = [(a * jax.nn.sigmoid(a)).astype(jnp.bfloat16) for a in pre]
+    h = jnp.concatenate(parts, 0)
     xz = matmul(head_rows(wc_ref, wb_ref), h, 1, 1)
     z = xz[dim : dim + 1]
     expz = jnp.exp(z)

time: 53.9 us -> 53.9 us (level)
  no operation moved by 1% of the time
where the time goes in v10:
time: 53.9 us; the launch traced here: 53.7 us
  waiting for transfers between devices  22.7 us (42%)
  starting transfers between devices  20.7 us (38%)
  Pallas kernels  8.46 us (16%)
  local copies, waits for them, and re-layouts  0.82 us (2%)
  between operations  0.81 us (2%)
    ppermute x22, waiting for transfers between devices, swap(): lax.ppermute(x, AXES, [(i, i ^ masks[i // core & 1]) for i in range(ndev)])  22.7 us
    ppermute x22, starting transfers between devices, swap(): lax.ppermute(x, AXES, [(i, i ^ masks[i // core & 1]) for i in range(ndev)])  20.7 us
    pallas_call x1, Pallas kernels, on_device(): pl.pallas_call(functools.partial(embed_kernel, sizes), out_shape=(jax.Sha...  2.61 us
    pallas_call x1, Pallas kernels, on_device(): pl.pallas_call(functools.partial(backward_kernel, sizes, hits_all, points...  2 us
    pallas_call x1, Pallas kernels, pairs(): pl.pallas_call(functools.partial(pair_kernel, len(rows)), out_shape=parti...  1.38 us
  transfers between devices with their start and end apart: 22, of which 16 were waited for; matrix products, arithmetic and copies ran while one was open for 0% of the time, Pallas kernels for 6%

profile of v10, /device:TPU:0, one launch (start us, length us, event | category | flops | bytes accessed | tf_op | source)
XLA Modules:
  0.0 53.7 jit_solution(16471518382571258390)
XLA Ops:
  0.6 0.0 copy-start
  0.6 2.6 %embed.1 = (f32[24,256]{1,0:T(8,128)}, f32[16,256]{1,0:T(8,128)}) custom-call(s32[8]{0:T(128)} %hit_ref.1, bf16[256,256]{1,0:T(8,128)(2,1)} %feat_ref.2, bf16[4,256,256]{2,1,0:T(8,128)(2,1)} %w_ref.2, f32[4,256]{1,0:T(4,128)} %b_ref.2, bf16[16,256]{1,0:T(8,128)(2,1)} %wc_ref.3, bf16[256]{0:T(256)(128)(2,1)} %wb_ref.3, s32[1,256]{1,0:T(1,128)} %bitcast.24, ...), custom_call_target="tpu_custom_call" | custom-call | tf_op jit(solution)/shard_map/embed/pallas_call | solution.py:366
  3.2 0.0 copy-start.1
  3.3 4.0 %collective-permute-start.2 = (f32[1,24,256]{2,1,0:T(8,128)}, f32[1,24,256]{2,1,0:T(8,128)S(1)}, u32[]{:S(2)}, u32[]{:S(2)}) collective-permute-start(f32[1,24,256]{2,1,0:T(8,128)} %bitcast.20), channel_id=1, source_target_pairs={{0,4},{1,5},{2,6},{3,7},{4,0},{5,1},{6,2},{7,3},{8,12},{9,13},{10,... | collective-permute-start | bytes 73736 | tf_op jit(solution)/shard_map/ppermute | solution.py:359
  7.3 1.3 %collective-permute-start.1 = (f32[1,24,256]{2,1,0:T(8,128)}, f32[1,24,256]{2,1,0:T(8,128)S(1)}, u32[]{:S(2)}, u32[]{:S(2)}) collective-permute-start(f32[1,24,256]{2,1,0:T(8,128)} %bitcast.21), channel_id=1, source_target_pairs={{0,6},{1,7},{2,4},{3,5},{4,2},{5,3},{6,0},{7,1},{8,14},{9,15},{10,... | collective-permute-start | bytes 73736 | tf_op jit(solution)/shard_map/ppermute | solution.py:359
  8.6 0.2 collective-permute-start
  8.9 0.0 copy-start.3
  8.9 0.8 %copy-done.3 = f32[24,256]{1,0:T(8,128)S(1)} copy-done((f32[24,256]{1,0:T(8,128)S(1)}, f32[24,256]{1,0:T(8,128)}, u32[]{:S(2)}) %copy-start.3) | copy-done | bytes 24600
  9.6 0.1 spread.1
  9.7 0.0 collective-permute-done.2
  9.7 3.4 %collective-permute-done.1 = f32[1,24,256]{2,1,0:T(8,128)S(1)} collective-permute-done((f32[1,24,256]{2,1,0:T(8,128)}, f32[1,24,256]{2,1,0:T(8,128)S(1)}, u32[]{:S(2)}, u32[]{:S(2)}) %collective-permute-start.1) | collective-permute-done | bytes 24608 | tf_op jit(solution)/shard_map/ppermute | solution.py:359
  13.1 0.0 collective-permute-done
  13.1 0.0 copy-start.2
  13.2 1.6 %collective-permute-start.5 = (f32[4,24,256]{2,1,0:T(8,128)S(1)}, f32[4,24,256]{2,1,0:T(8,128)S(1)}, u32[]{:S(2)}, u32[]{:S(2)}) collective-permute-start(f32[4,24,256]{2,1,0:T(8,128)S(1)} %pad_maximum_fusion.1.rest_0_), channel_id=1, source_target_pairs={{0,16},{1,17},{2,18},{3,19},{4,20},{5,21},{6,22},{7,23},{8,24},{9,... | collective-permute-start | bytes 294920 | tf_op jit(solution)/shard_map/ppermute | solution.py:359
  14.7 1.4 %collective-permute-start.4 = (f32[4,24,256]{2,1,0:T(8,128)S(1)}, f32[4,24,256]{2,1,0:T(8,128)S(1)}, u32[]{:S(2)}, u32[]{:S(2)}) collective-permute-start(f32[4,24,256]{2,1,0:T(8,128)S(1)} %pad_maximum_fusion.1.rest_0_), channel_id=1, source_target_pairs={{0,17},{1,16},{2,19},{3,18},{4,21},{5,20},{6,23},{7,22},{8,25},{9,... | collective-permute-start | bytes 294920 | tf_op jit(solution)/shard_map/ppermute | solution.py:359
  16.2 0.5 collective-permute-start.3
  16.7 0.0 collective-permute-start.6
  16.7 0.0 copy-done
  16.7 0.0 copy-done.1
  16.7 0.0 copy-done.2
  16.7 0.0 copy-done.5
  16.7 0.0 copy-done.6
  16.8 0.6 %residuals.1 = (f32[4,256,256]{2,1,0:T(8,128)S(1)}, bf16[4,256,256]{2,1,0:T(8,128)(2,1)S(1)}, bf16[256,256]{1,0:T(8,128)(2,1)S(1)}, bf16[3,256,256]{2,1,0:T(8,128)(2,1)S(1)}, bf16[32,256]{1,0:T(8,128)(2,1)S(1)}) custom-call(bf16[256,256]{1,0:T(8,128)(2,1)S(1)} %copy-done.1, bf16[4,256,256]{2,1,0:T(8,128)(2,1)S(1)} %copy-done, f32[4,256]{1,0:T(4,128)S(1)} %copy-done.5, ...), custom_call_target="tpu_custom_call" | custom-call | flops 5242880 | bytes 1572864 | tf_op jit(solution)/shard_map/residuals/pallas_call | solution.py:379
  17.4 1.1 %collective-permute-done.5 = f32[4,24,256]{2,1,0:T(8,128)S(1)} collective-permute-done((f32[4,24,256]{2,1,0:T(8,128)S(1)}, f32[4,24,256]{2,1,0:T(8,128)S(1)}, u32[]{:S(2)}, u32[]{:S(2)}) %collective-permute-start.5) | collective-permute-done | bytes 98336 | tf_op jit(solution)/shard_map/ppermute | solution.py:359
  18.5 1.8 %collective-permute-done.4 = f32[4,24,256]{2,1,0:T(8,128)S(1)} collective-permute-done((f32[4,24,256]{2,1,0:T(8,128)S(1)}, f32[4,24,256]{2,1,0:T(8,128)S(1)}, u32[]{:S(2)}, u32[]{:S(2)}) %collective-permute-start.4) | collective-permute-done | bytes 98336 | tf_op jit(solution)/shard_map/ppermute | solution.py:359
  20.3 0.5 collective-permute-done.3
  20.8 0.0 collective-permute-done.6.rest_1_
  20.8 0.1 collective-permute-start.7
  20.9 0.0 copy-start.4
  20.9 1.4 %pairs.1 = (f32[17,8,256]{2,1,0:T(8,128)S(1)}, f32[17,8,128]{2,1,0:T(8,128)S(1)}) custom-call(f32[24,256]{1,0:T(8,128)S(1)} %get-tuple-element.35.pay_ref, f32[8,128]{1,0:T(8,128)S(1)} %get-tuple-element.36.own_ref, f32[16,8,256]{2,1,0:T(8,128)S(1)} %get-tuple-element.37.xb, f32[16,8,256]{2,1,0:T(8,128)S(1)} %get-tuple-element.38.yb, ...), custom_call_target="tpu_custom_call" | custom-call | flops 8192000 | bytes 327680 | tf_op jit(solution)/shard_map/pairs/pallas_call | solution.py:433
  22.3 0.2 collective-permute-done.7.rows_ref
  22.5 0.0 copy-done.4
  22.5 2.0 %pairs_backward.1 = (f32[4,264,128]{2,1,0:T(8,128)S(1)}, f32[4,264,128]{2,1,0:T(8,128)S(1)}) custom-call(f32[24,256]{1,0:T(8,128)S(1)} %get-tuple-element.35.pay_ref, f32[8,128]{1,0:T(8,128)S(1)} %get-tuple-element.36.own_ref, f32[16,8,256]{2,1,0:T(8,128)S(1)} %get-tuple-element.37.xb, f32[16,8,256]{2,1,0:T(8,128)S(1)} %get-tuple-element.38.yb, ...), custom_call_target="tpu_custom_call" | custom-call | tf_op jit(solution)/shard_map/pairs_backward/pallas_call | solution.py:451
  24.5 0.4 collective-permute-start.8
  24.9 1.6 %collective-permute-done.8 = f32[4,264,128]{2,1,0:T(8,128)S(1)} collective-permute-done((f32[4,264,128]{2,1,0:T(8,128)S(1)}, f32[4,264,128]{2,1,0:T(8,128)S(1)}, u32[]{:S(2)}, u32[]{:S(2)}) %collective-permute-start.8) | collective-permute-done | bytes 540704 | tf_op jit(solution)/shard_map/ppermute | solution.py:359
  26.5 0.1 add.21
  26.6 2.1 %collective-permute-start.11 = (f32[264,128]{1,0:T(8,128)S(1)}, f32[264,128]{1,0:T(8,128)S(1)}, u32[]{:S(2)}, u32[]{:S(2)}) collective-permute-start(f32[264,128]{1,0:T(8,128)S(1)} %get-tuple-element.63), channel_id=1, source_target_pairs={{0,17},{1,16},{2,19},{3,18},{4,21},{5,20},{6,23},{7,22},{8,14},{9,... | collective-permute-start | bytes 405512 | tf_op jit(solution)/shard_map/ppermute | solution.py:359
  28.7 0.5 collective-permute-start.10
  29.2 1.0 %collective-permute-start.9 = (f32[264,128]{1,0:T(8,128)S(1)}, f32[264,128]{1,0:T(8,128)S(1)}, u32[]{:S(2)}, u32[]{:S(2)}) collective-permute-start(f32[264,128]{1,0:T(8,128)S(1)} %get-tuple-element.65), channel_id=1, source_target_pairs={{0,1},{1,0},{2,3},{3,2},{4,5},{5,4},{6,7},{7,6},{8,10},{9,11},{10,... | collective-permute-start | bytes 405512 | tf_op jit(solution)/shard_map/ppermute | solution.py:359
  30.1 2.5 %collective-permute-done.11 = f32[264,128]{1,0:T(8,128)S(1)} collective-permute-done((f32[264,128]{1,0:T(8,128)S(1)}, f32[264,128]{1,0:T(8,128)S(1)}, u32[]{:S(2)}, u32[]{:S(2)}) %collective-permute-start.11) | collective-permute-done | bytes 135200 | tf_op jit(solution)/shard_map/ppermute | solution.py:359
  32.6 1.4 %collective-permute-done.10 = f32[264,128]{1,0:T(8,128)S(1)} collective-permute-done((f32[264,128]{1,0:T(8,128)S(1)}, f32[264,128]{1,0:T(8,128)S(1)}, u32[]{:S(2)}, u32[]{:S(2)}) %collective-permute-start.10) | collective-permute-done | bytes 135200 | tf_op jit(solution)/shard_map/ppermute | solution.py:359
  34.0 0.2 collective-permute-done.9
  34.2 1.3 %collective-permute-start.14 = (f32[264,128]{1,0:T(8,128)S(1)}, f32[264,128]{1,0:T(8,128)S(1)}, u32[]{:S(2)}, u32[]{:S(2)}) collective-permute-start(f32[264,128]{1,0:T(8,128)S(1)} %fusion.1), channel_id=1, source_target_pairs={{0,4},{1,5},{2,6},{3,7},{4,0},{5,1},{6,2},{7,3},{8,24},{9,25},{10,... | collective-permute-start | bytes 405512 | tf_op jit(solution)/shard_map/ppermute | solution.py:359
  35.5 0.9 %collective-permute-start.13 = (f32[264,128]{1,0:T(8,128)S(1)}, f32[264,128]{1,0:T(8,128)S(1)}, u32[]{:S(2)}, u32[]{:S(2)}) collective-permute-start(f32[264,128]{1,0:T(8,128)S(1)} %fusion.1), channel_id=1, source_target_pairs={{0,6},{1,7},{2,4},{3,5},{4,2},{5,3},{6,0},{7,1},{8,25},{9,24},{10,... | collective-permute-start | bytes 405512 | tf_op jit(solution)/shard_map/ppermute | solution.py:359
  36.4 1.3 %collective-permute-start.12 = (f32[264,128]{1,0:T(8,128)S(1)}, f32[264,128]{1,0:T(8,128)S(1)}, u32[]{:S(2)}, u32[]{:S(2)}) collective-permute-start(f32[264,128]{1,0:T(8,128)S(1)} %fusion.1), channel_id=1, source_target_pairs={{0,2},{1,3},{2,0},{3,1},{4,6},{5,7},{6,4},{7,5},{8,9},{9,8},{10,11... | collective-permute-start | bytes 405512 | tf_op jit(solution)/shard_map/ppermute | solution.py:359
  37.8 3.2 %collective-permute-done.14 = f32[264,128]{1,0:T(8,128)S(1)} collective-permute-done((f32[264,128]{1,0:T(8,128)S(1)}, f32[264,128]{1,0:T(8,128)S(1)}, u32[]{:S(2)}, u32[]{:S(2)}) %collective-permute-start.14) | collective-permute-done | bytes 135200 | tf_op jit(solution)/shard_map/ppermute | solution.py:359
  41.0 1.5 %collective-permute-done.13 = f32[264,128]{1,0:T(8,128)S(1)} collective-permute-done((f32[264,128]{1,0:T(8,128)S(1)}, f32[264,128]{1,0:T(8,128)S(1)}, u32[]{:S(2)}, u32[]{:S(2)}) %collective-permute-start.13) | collective-permute-done | bytes 135200 | tf_op jit(solution)/shard_map/ppermute | solution.py:359
  42.5 1.3 %collective-permute-done.12 = f32[264,128]{1,0:T(8,128)S(1)} collective-permute-done((f32[264,128]{1,0:T(8,128)S(1)}, f32[264,128]{1,0:T(8,128)S(1)}, u32[]{:S(2)}, u32[]{:S(2)}) %collective-permute-start.12) | collective-permute-done | bytes 135200 | tf_op jit(solution)/shard_map/ppermute | solution.py:359
  43.8 2.0 %collective-permute-start.20 = (f32[264,128]{1,0:T(8,128)S(1)}, f32[264,128]{1,0:T(8,128)S(1)}, u32[]{:S(2)}, u32[]{:S(2)}) collective-permute-start(f32[264,128]{1,0:T(8,128)S(1)} %add_add_fusion.refs_0_), channel_id=1, source_target_pairs={{0,17},{1,16},{2,19},{3,18},{4,21},{5,20},{6,23},{7,22},{8,14},{9,... | collective-permute-start | bytes 405512 | tf_op jit(solution)/shard_map/ppermute | solution.py:359
  45.8 0.5 collective-permute-start.18
  46.3 1.1 %collective-permute-start.16 = (f32[264,128]{1,0:T(8,128)S(1)}, f32[264,128]{1,0:T(8,128)S(1)}, u32[]{:S(2)}, u32[]{:S(2)}) collective-permute-start(f32[264,128]{1,0:T(8,128)S(1)} %add_add_fusion.refs_0_), channel_id=1, source_target_pairs={{0,1},{1,0},{2,3},{3,2},{4,5},{5,4},{6,7},{7,6},{8,10},{9,11},{10,... | collective-permute-start | bytes 405512 | tf_op jit(solution)/shard_map/ppermute | solution.py:359
  47.4 0.0 collective-permute-start.15
  47.4 2.5 %collective-permute-done.20.refs_3_ = f32[264,128]{1,0:T(8,128)S(1)} collective-permute-done((f32[264,128]{1,0:T(8,128)S(1)}, f32[264,128]{1,0:T(8,128)S(1)}, u32[]{:S(2)}, u32[]{:S(2)}) %collective-permute-start.20) | collective-permute-done | bytes 135200 | tf_op jit(solution)/shard_map/ppermute | solution.py:359
  49.8 0.0 collective-permute-start.21
  49.8 1.4 %collective-permute-done.18.refs_2_ = f32[264,128]{1,0:T(8,128)S(1)} collective-permute-done((f32[264,128]{1,0:T(8,128)S(1)}, f32[264,128]{1,0:T(8,128)S(1)}, u32[]{:S(2)}, u32[]{:S(2)}) %collective-permute-start.18) | collective-permute-done | bytes 135200 | tf_op jit(solution)/shard_map/ppermute | solution.py:359
  51.2 0.0 collective-permute-start.19
  51.2 0.1 collective-permute-done.16.refs_1_
  51.3 0.4 collective-permute-start.17
  51.8 0.8 %place_near.1 = (f32[8,128,256]{2,1,0:T(8,128)}, f32[4,8,128]{2,1,0:T(8,128)S(1)}) custom-call(f32[264,128]{1,0:T(8,128)S(1)} %add_add_fusion.refs_0_, f32[264,128]{1,0:T(8,128)S(1)} %collective-permute-done.16.refs_1_, f32[264,128]{1,0:T(8,128)S(1)} %collective-permute-done.18.refs_2_, f32[264,128]{1,0:T(8,128)S(1)} %collective-permute-done.20.refs_3_), custom_call_target="tpu_custom_call" | custom-call | bytes 1048576 | tf_op jit(solution)/shard_map/place_near/pallas_call | solution.py:477
  52.6 0.0 collective-permute-done.15.refs_0_
  52.6 0.0 collective-permute-done.21.refs_3_
  52.6 0.0 collective-permute-done.19.refs_2_
  52.6 0.1 collective-permute-done.17.refs_1_
  52.8 0.9 %place_far.1 = (f32[8,128,256]{2,1,0:T(8,128)}, f32[4,256]{1,0:T(4,128)}, f32[16,256]{1,0:T(8,128)}, f32[1,256]{1,0:T(1,128)}, f32[1,1]{1,0:T(1,128)}) custom-call(f32[264,128]{1,0:T(8,128)S(1)} %collective-permute-done.15.refs_0_, f32[264,128]{1,0:T(8,128)S(1)} %collective-permute-done.17.refs_1_, ...), custom_call_target="tpu_custom_call", output_to_operand_aliasing={{0}: (5, {})} | custom-call | tf_op jit(solution)/shard_map/place_far/pallas_call | solution.py:487
  (7 shorter events, 0.1 us)
Async XLA Ops:
  0.6 16.1 %copy-start = (bf16[4,256,256]{2,1,0:T(8,128)(2,1)S(1)}, bf16[4,256,256]{2,1,0:T(8,128)(2,1)}, u32[]{:S(2)}) copy-start(bf16[4,256,256]{2,1,0:T(8,128)(2,1)} %w_ref.2) | copy-start | bytes 1572868
  3.2 13.5 %copy-start.1 = (bf16[256,256]{1,0:T(8,128)(2,1)S(1)}, bf16[256,256]{1,0:T(8,128)(2,1)}, u32[]{:S(2)}) copy-start(bf16[256,256]{1,0:T(8,128)(2,1)} %feat_ref.2) | copy-start | bytes 393220
  3.3 6.5 %collective-permute-start.2 = (f32[1,24,256]{2,1,0:T(8,128)}, f32[1,24,256]{2,1,0:T(8,128)S(1)}, u32[]{:S(2)}, u32[]{:S(2)}) collective-permute-start(f32[1,24,256]{2,1,0:T(8,128)} %bitcast.20), channel_id=1, source_target_pairs={{0,4},{1,5},{2,6},{3,7},{4,0},{5,1},{6,2},{7,3},{8,12},{9,13},{10,... | collective-permute-start | bytes 73736 | tf_op jit(solution)/shard_map/ppermute | solution.py:359
  7.3 5.8 %collective-permute-start.1 = (f32[1,24,256]{2,1,0:T(8,128)}, f32[1,24,256]{2,1,0:T(8,128)S(1)}, u32[]{:S(2)}, u32[]{:S(2)}) collective-permute-start(f32[1,24,256]{2,1,0:T(8,128)} %bitcast.21), channel_id=1, source_target_pairs={{0,6},{1,7},{2,4},{3,5},{4,2},{5,3},{6,0},{7,1},{8,14},{9,15},{10,... | collective-permute-start | bytes 73736 | tf_op jit(solution)/shard_map/ppermute | solution.py:359
  8.6 4.5 %collective-permute-start = (f32[1,24,256]{2,1,0:T(8,128)}, f32[1,24,256]{2,1,0:T(8,128)S(1)}, u32[]{:S(2)}, u32[]{:S(2)}) collective-permute-start(f32[1,24,256]{2,1,0:T(8,128)} %bitcast.22), channel_id=1, source_target_pairs={{0,2},{1,3},{2,0},{3,1},{4,6},{5,7},{6,4},{7,5},{8,10},{9,11},{10,... | collective-permute-start | bytes 73736 | tf_op jit(solution)/shard_map/ppermute | solution.py:359
  8.9 0.8 %copy-start.3 = (f32[24,256]{1,0:T(8,128)S(1)}, f32[24,256]{1,0:T(8,128)}, u32[]{:S(2)}) copy-start(f32[24,256]{1,0:T(8,128)} %get-tuple-element.34.pay_ref) | copy-start | bytes 73732
  13.1 3.6 %copy-start.2 = (bf16[16,256]{1,0:T(8,128)(2,1)S(1)}, bf16[16,256]{1,0:T(8,128)(2,1)}, u32[]{:S(2)}) copy-start(bf16[16,256]{1,0:T(8,128)(2,1)} %wc_ref.3) | copy-start | bytes 24580
  13.1 3.6 %copy-start.5 = (f32[4,256]{1,0:T(4,128)S(1)}, f32[4,256]{1,0:T(4,128)}, u32[]{:S(2)}) copy-start(f32[4,256]{1,0:T(4,128)} %b_ref.2) | copy-start | bytes 12292
  13.1 3.6 %copy-start.6 = (bf16[256]{0:T(256)(128)(2,1)S(1)}, bf16[256]{0:T(256)(128)(2,1)}, u32[]{:S(2)}) copy-start(bf16[256]{0:T(256)(128)(2,1)} %wb_ref.3) | copy-start | bytes 1540
  13.2 5.3 %collective-permute-start.5 = (f32[4,24,256]{2,1,0:T(8,128)S(1)}, f32[4,24,256]{2,1,0:T(8,128)S(1)}, u32[]{:S(2)}, u32[]{:S(2)}) collective-permute-start(f32[4,24,256]{2,1,0:T(8,128)S(1)} %pad_maximum_fusion.1.rest_0_), channel_id=1, source_target_pairs={{0,16},{1,17},{2,18},{3,19},{4,20},{5,21},{6,22},{7,23},{8,24},{9,... | collective-permute-start | bytes 294920 | tf_op jit(solution)/shard_map/ppermute | solution.py:359
  14.7 5.5 %collective-permute-start.4 = (f32[4,24,256]{2,1,0:T(8,128)S(1)}, f32[4,24,256]{2,1,0:T(8,128)S(1)}, u32[]{:S(2)}, u32[]{:S(2)}) collective-permute-start(f32[4,24,256]{2,1,0:T(8,128)S(1)} %pad_maximum_fusion.1.rest_0_), channel_id=1, source_target_pairs={{0,17},{1,16},{2,19},{3,18},{4,21},{5,20},{6,23},{7,22},{8,25},{9,... | collective-permute-start | bytes 294920 | tf_op jit(solution)/shard_map/ppermute | solution.py:359
  16.2 4.6 %collective-permute-start.3 = (f32[4,24,256]{2,1,0:T(8,128)S(1)}, f32[4,24,256]{2,1,0:T(8,128)S(1)}, u32[]{:S(2)}, u32[]{:S(2)}) collective-permute-start(f32[4,24,256]{2,1,0:T(8,128)S(1)} %pad_maximum_fusion.1.rest_0_), channel_id=1, source_target_pairs={{0,1},{1,0},{2,3},{3,2},{4,5},{5,4},{6,7},{7,6},{8,9},{9,8},{10,11... | collective-permute-start | bytes 294920 | tf_op jit(solution)/shard_map/ppermute | solution.py:359
  16.7 4.1 %collective-permute-start.6 = (f32[4,24,256]{2,1,0:T(8,128)S(1)}, f32[4,24,256]{2,1,0:T(8,128)S(1)}, u32[]{:S(2)}, u32[]{:S(2)}) collective-permute-start(f32[4,24,256]{2,1,0:T(8,128)S(1)} %pad_maximum_fusion.1.rest_0_), channel_id=1, source_target_pairs={{0,8},{1,9},{2,10},{3,11},{4,12},{5,13},{6,14},{7,15},{8,0},{9,1},... | collective-permute-start | bytes 294920 | tf_op jit(solution)/shard_map/ppermute | solution.py:359
  20.8 1.6 %collective-permute-start.7 = (f32[12,24,256]{2,1,0:T(8,128)S(1)}, f32[12,24,256]{2,1,0:T(8,128)S(1)}, u32[]{:S(2)}, u32[]{:S(2)}) collective-permute-start(f32[12,24,256]{2,1,0:T(8,128)S(1)} %pad_maximum_fusion.rest_2_), channel_id=1, source_target_pairs={{0,8},{1,9},{2,10},{3,11},{4,12},{5,13},{6,14},{7,15},{8,0},{9,1},... | collective-permute-start | bytes 884744 | tf_op jit(solution)/shard_map/ppermute | solution.py:359
  20.9 1.6 %copy-start.4 = (f32[16,256]{1,0:T(8,128)S(1)}, f32[16,256]{1,0:T(8,128)}, u32[]{:S(2)}) copy-start(f32[16,256]{1,0:T(8,128)} %get-tuple-element.39.aux_ref) | copy-start | bytes 49156
  24.5 2.0 %collective-permute-start.8 = (f32[4,264,128]{2,1,0:T(8,128)S(1)}, f32[4,264,128]{2,1,0:T(8,128)S(1)}, u32[]{:S(2)}, u32[]{:S(2)}) collective-permute-start(f32[4,264,128]{2,1,0:T(8,128)S(1)} %get-tuple-element.55), channel_id=1, source_target_pairs={{0,8},{1,9},{2,10},{3,11},{4,12},{5,13},{6,14},{7,15},{8,0},{9,1},... | collective-permute-start | bytes 1622024 | tf_op jit(solution)/shard_map/ppermute | solution.py:359
  26.6 6.0 %collective-permute-start.11 = (f32[264,128]{1,0:T(8,128)S(1)}, f32[264,128]{1,0:T(8,128)S(1)}, u32[]{:S(2)}, u32[]{:S(2)}) collective-permute-start(f32[264,128]{1,0:T(8,128)S(1)} %get-tuple-element.63), channel_id=1, source_target_pairs={{0,17},{1,16},{2,19},{3,18},{4,21},{5,20},{6,23},{7,22},{8,14},{9,... | collective-permute-start | bytes 405512 | tf_op jit(solution)/shard_map/ppermute | solution.py:359
  28.7 5.3 %collective-permute-start.10 = (f32[264,128]{1,0:T(8,128)S(1)}, f32[264,128]{1,0:T(8,128)S(1)}, u32[]{:S(2)}, u32[]{:S(2)}) collective-permute-start(f32[264,128]{1,0:T(8,128)S(1)} %get-tuple-element.64), channel_id=1, source_target_pairs={{0,16},{1,17},{2,18},{3,19},{4,20},{5,21},{6,22},{7,23},{8,12},{9,... | collective-permute-start | bytes 405512 | tf_op jit(solution)/shard_map/ppermute | solution.py:359
  29.2 5.0 %collective-permute-start.9 = (f32[264,128]{1,0:T(8,128)S(1)}, f32[264,128]{1,0:T(8,128)S(1)}, u32[]{:S(2)}, u32[]{:S(2)}) collective-permute-start(f32[264,128]{1,0:T(8,128)S(1)} %get-tuple-element.65), channel_id=1, source_target_pairs={{0,1},{1,0},{2,3},{3,2},{4,5},{5,4},{6,7},{7,6},{8,10},{9,11},{10,... | collective-permute-start | bytes 405512 | tf_op jit(solution)/shard_map/ppermute | solution.py:359
  34.2 6.8 %collective-permute-start.14 = (f32[264,128]{1,0:T(8,128)S(1)}, f32[264,128]{1,0:T(8,128)S(1)}, u32[]{:S(2)}, u32[]{:S(2)}) collective-permute-start(f32[264,128]{1,0:T(8,128)S(1)} %fusion.1), channel_id=1, source_target_pairs={{0,4},{1,5},{2,6},{3,7},{4,0},{5,1},{6,2},{7,3},{8,24},{9,25},{10,... | collective-permute-start | bytes 405512 | tf_op jit(solution)/shard_map/ppermute | solution.py:359
  35.5 7.0 %collective-permute-start.13 = (f32[264,128]{1,0:T(8,128)S(1)}, f32[264,128]{1,0:T(8,128)S(1)}, u32[]{:S(2)}, u32[]{:S(2)}) collective-permute-start(f32[264,128]{1,0:T(8,128)S(1)} %fusion.1), channel_id=1, source_target_pairs={{0,6},{1,7},{2,4},{3,5},{4,2},{5,3},{6,0},{7,1},{8,25},{9,24},{10,... | collective-permute-start | bytes 405512 | tf_op jit(solution)/shard_map/ppermute | solution.py:359
  36.4 7.3 %collective-permute-start.12 = (f32[264,128]{1,0:T(8,128)S(1)}, f32[264,128]{1,0:T(8,128)S(1)}, u32[]{:S(2)}, u32[]{:S(2)}) collective-permute-start(f32[264,128]{1,0:T(8,128)S(1)} %fusion.1), channel_id=1, source_target_pairs={{0,2},{1,3},{2,0},{3,1},{4,6},{5,7},{6,4},{7,5},{8,9},{9,8},{10,11... | collective-permute-start | bytes 405512 | tf_op jit(solution)/shard_map/ppermute | solution.py:359
  43.8 6.0 %collective-permute-start.20 = (f32[264,128]{1,0:T(8,128)S(1)}, f32[264,128]{1,0:T(8,128)S(1)}, u32[]{:S(2)}, u32[]{:S(2)}) collective-permute-start(f32[264,128]{1,0:T(8,128)S(1)} %add_add_fusion.refs_0_), channel_id=1, source_target_pairs={{0,17},{1,16},{2,19},{3,18},{4,21},{5,20},{6,23},{7,22},{8,14},{9,... | collective-permute-start | bytes 405512 | tf_op jit(solution)/shard_map/ppermute | solution.py:359
  45.8 5.4 %collective-permute-start.18 = (f32[264,128]{1,0:T(8,128)S(1)}, f32[264,128]{1,0:T(8,128)S(1)}, u32[]{:S(2)}, u32[]{:S(2)}) collective-permute-start(f32[264,128]{1,0:T(8,128)S(1)} %add_add_fusion.refs_0_), channel_id=1, source_target_pairs={{0,16},{1,17},{2,18},{3,19},{4,20},{5,21},{6,22},{7,23},{8,12},{9,... | collective-permute-start | bytes 405512 | tf_op jit(solution)/shard_map/ppermute | solution.py:359
  46.3 5.0 %collective-permute-start.16 = (f32[264,128]{1,0:T(8,128)S(1)}, f32[264,128]{1,0:T(8,128)S(1)}, u32[]{:S(2)}, u32[]{:S(2)}) collective-permute-start(f32[264,128]{1,0:T(8,128)S(1)} %add_add_fusion.refs_0_), channel_id=1, source_target_pairs={{0,1},{1,0},{2,3},{3,2},{4,5},{5,4},{6,7},{7,6},{8,10},{9,11},{10,... | collective-permute-start | bytes 405512 | tf_op jit(solution)/shard_map/ppermute | solution.py:359
  47.4 5.2 %collective-permute-start.15 = (f32[264,128]{1,0:T(8,128)S(1)}, f32[264,128]{1,0:T(8,128)S(1)}, u32[]{:S(2)}, u32[]{:S(2)}) collective-permute-start(f32[264,128]{1,0:T(8,128)S(1)} %add_add_fusion.refs_0_), channel_id=1, source_target_pairs={{0,8},{1,9},{2,10},{3,11},{4,12},{5,13},{6,14},{7,15},{8,0},{9,1},... | collective-permute-start | bytes 405512 | tf_op jit(solution)/shard_map/ppermute | solution.py:359
  49.8 2.8 %collective-permute-start.21 = (f32[264,128]{1,0:T(8,128)S(1)}, f32[264,128]{1,0:T(8,128)S(1)}, u32[]{:S(2)}, u32[]{:S(2)}) collective-permute-start(f32[264,128]{1,0:T(8,128)S(1)} %collective-permute-done.20.refs_3_), channel_id=1, source_target_pairs={{0,8},{1,9},{2,10},{3,11},{4,12},{5,13},{6,14},{7,15},{8,0},{9,1},... | collective-permute-start | bytes 405512 | tf_op jit(solution)/shard_map/ppermute | solution.py:359
  51.2 1.4 %collective-permute-start.19 = (f32[264,128]{1,0:T(8,128)S(1)}, f32[264,128]{1,0:T(8,128)S(1)}, u32[]{:S(2)}, u32[]{:S(2)}) collective-permute-start(f32[264,128]{1,0:T(8,128)S(1)} %collective-permute-done.18.refs_2_), channel_id=1, source_target_pairs={{0,8},{1,9},{2,10},{3,11},{4,12},{5,13},{6,14},{7,15},{8,0},{9,1},... | collective-permute-start | bytes 405512 | tf_op jit(solution)/shard_map/ppermute | solution.py:359
  51.3 1.5 %collective-permute-start.17 = (f32[264,128]{1,0:T(8,128)S(1)}, f32[264,128]{1,0:T(8,128)S(1)}, u32[]{:S(2)}, u32[]{:S(2)}) collective-permute-start(f32[264,128]{1,0:T(8,128)S(1)} %collective-permute-done.16.refs_1_), channel_id=1, source_target_pairs={{0,8},{1,9},{2,10},{3,11},{4,12},{5,13},{6,14},{7,15},{8,0},{9,1},... | collective-permute-start | bytes 405512 | tf_op jit(solution)/shard_map/ppermute | solution.py:359
